TPU v7x, 32 devices: a whole 2x2x4 slice. The times are simulated.
32 devices in a mesh: groups: 2 (over y), dom: 4 (over z), sample: 2 (over x), sub: 2 (over core).
Axes of the slice: x: 2, y: 2, z: 4, core: 2. Of those that a mesh axis runs over, the one named last changes fastest.
Arguments:
- node_in: bfloat16 [4, 8192, 128], P(('groups', 'sample'), ('dom', 'sub')), parts along dimension 0, may hold values from -6 to 6
- edge_in: bfloat16 [4, 24576, 128], P(('groups', 'sample'), ('dom', 'sub')), parts along dimension 0, may hold values from -6 to 6
- senders: int32 [24576], P(('dom', 'sub')), may hold values from 0 to 1023
- receivers: int32 [24576], P(('dom', 'sub')), may hold values from 0 to 1279, as said below
- send_list: int32 [8, 2, 128], P(('dom', 'sub')), may hold values from 0 to 1023, as said below
- w_edge_first: bfloat16 [384, 128], replicated, may hold values from -0.3125 to 0.3125
- b_edge_first: float32 [128], replicated, may hold values from -3 to 3
- w_edge_second: bfloat16 [128, 128], replicated, may hold values from -0.5 to 0.5
- b_edge_second: float32 [128], replicated, may hold values from -3 to 3
- edge_gain: float32 [128], replicated, may hold values from 0.5 to 1.5
- edge_shift: float32 [128], replicated, may hold values from -3 to 3
- w_node_first: bfloat16 [256, 128], replicated, may hold values from -0.375 to 0.375
- b_node_first: float32 [128], replicated, may hold values from -3 to 3
- w_node_second: bfloat16 [128, 128], replicated, may hold values from -0.5 to 0.5
- b_node_second: float32 [128], replicated, may hold values from -3 to 3
- node_gain: float32 [128], replicated, may hold values from 0.5 to 1.5
- node_shift: float32 [128], replicated, may hold values from -3 to 3
- node_cotangent: bfloat16 [4, 8192, 128], P(('groups', 'sample'), ('dom', 'sub')), parts along dimension 0, may hold values from -6 to 6
- edge_cotangent: bfloat16 [4, 24576, 128], P(('groups', 'sample'), ('dom', 'sub')), parts along dimension 0, may hold values from -6 to 6
Outputs:
- node_out: bfloat16 [4, 8192, 128], P(('groups', 'sample'), ('dom', 'sub')), parts along dimension 0
- edge_out: bfloat16 [4, 24576, 128], P(('groups', 'sample'), ('dom', 'sub')), parts along dimension 0
- node_grad: bfloat16 [4, 8192, 128], P(('groups', 'sample'), ('dom', 'sub')), parts along dimension 0
- edge_grad: bfloat16 [4, 24576, 128], P(('groups', 'sample'), ('dom', 'sub')), parts along dimension 0
- g_edge_first: float32 [768, 128], P('groups'), parts along dimension 0
- g_b_edge_first: float32 [256], P('groups'), parts along dimension 0
- g_edge_second: float32 [256, 128], P('groups'), parts along dimension 0
- g_b_edge_second: float32 [256], P('groups'), parts along dimension 0
- g_edge_gain: float32 [256], P('groups'), parts along dimension 0
- g_edge_shift: float32 [256], P('groups'), parts along dimension 0
- g_node_first: float32 [512, 128], P('groups'), parts along dimension 0
- g_b_node_first: float32 [256], P('groups'), parts along dimension 0
- g_node_second: float32 [256, 128], P('groups'), parts along dimension 0
- g_b_node_second: float32 [256], P('groups'), parts along dimension 0
- g_node_gain: float32 [256], P('groups'), parts along dimension 0
- g_node_shift: float32 [256], P('groups'), parts along dimension 0
There are 2 independent parts, one for each index of `groups`. A program takes and returns all parts, laid end to end along the dimension named above; an argument that names none is the same for every part. Nothing has to cross between parts.
Inputs may be any that keep to these rules, and one draw needn't show every extreme that they name: Values of 1024 and above name halo slots: slot k below 128 is the left neighbour's send_list row 1, entry k; the rest are the right neighbour's row 0. The first partition has no left slots and the last none on the right. In every other partition exactly 512 edges have halo receivers and every slot receives at least one edge. `send_list`: each row holds 128 distinct nodes of the partition.
All inputs are finite; a program needn't handle non-finite values.
Results may differ from a plain program's by a relative error of at most 0.0078.
Values may be sent and summed in bfloat16 or wider, within the bound.
No kernel may reach another device: no remote copies, remote signals or barrier semaphores. Data moves between devices by JAX's collectives and lax.ppermute only.
A program may use at most 64 MiB of HBM per device.

v0:
```python
import math

import jax
import jax.numpy as jnp
from jax import lax
from jax.sharding import PartitionSpec as P

epsilon = 1e-05
rows_dims = (((0,), (0,)), ((), ()))
back_dims = (((1,), (1,)), ((), ()))


def with_halo(block, sides, width):
    for axis, dim in sides:
        count = lax.axis_size(axis)
        forward = [(i, i + 1) for i in range(count - 1)]
        backward = [(target, source) for source, target in forward]
        low = lax.ppermute(
            lax.slice_in_dim(block, block.shape[dim] - width, None, axis=dim), axis, forward
        )
        high = lax.ppermute(lax.slice_in_dim(block, 0, width, axis=dim), axis, backward)
        block = jnp.concatenate([low, block, high], axis=dim)
    return block


def block_forward(inputs, w_first, b_first, w_second, b_second, gain, shift):
    hidden_pre = jnp.dot(inputs, w_first, preferred_element_type=jnp.float32) + b_first
    hidden_act = jax.nn.silu(hidden_pre).astype(jnp.bfloat16)
    second = jnp.dot(hidden_act, w_second, preferred_element_type=jnp.float32) + b_second
    center = second - jnp.mean(second, axis=-1, keepdims=True)
    scale_inv = lax.rsqrt(jnp.mean(center * center, axis=-1, keepdims=True) + epsilon)
    normed = center * scale_inv
    return (normed * gain + shift, (hidden_pre, hidden_act, normed, scale_inv))


def block_backward(inputs, saved, w_first, w_second, gain, upstream):
    hidden_pre, hidden_act, normed, scale_inv = saved
    d_gain = jnp.sum(upstream * normed, axis=0)
    d_shift = jnp.sum(upstream, axis=0)
    d_normed = upstream * gain
    d_second = scale_inv * (
        d_normed
        - jnp.mean(d_normed, axis=-1, keepdims=True)
        - normed * jnp.mean(d_normed * normed, axis=-1, keepdims=True)
    )
    d_second_b = d_second.astype(jnp.bfloat16)
    g_second = lax.dot_general(
        hidden_act, d_second_b, rows_dims, preferred_element_type=jnp.float32
    )
    g_bias_second = jnp.sum(d_second, axis=0)
    d_act = lax.dot_general(d_second_b, w_second, back_dims, preferred_element_type=jnp.float32)
    sigmoid_value = jax.nn.sigmoid(hidden_pre)
    d_pre = d_act * sigmoid_value * (1.0 + hidden_pre * (1.0 - sigmoid_value))
    d_pre_b = d_pre.astype(jnp.bfloat16)
    g_first = lax.dot_general(inputs, d_pre_b, rows_dims, preferred_element_type=jnp.float32)
    g_bias_first = jnp.sum(d_pre, axis=0)
    d_inputs = lax.dot_general(d_pre_b, w_first, back_dims, preferred_element_type=jnp.float32)
    return (d_inputs, (g_first, g_bias_first, g_second, g_bias_second, d_gain, d_shift))


def segment_rows(values, indices, row_count):
    edge_count = values.shape[0]
    block_rows = math.gcd(edge_count, 512)
    block_count = edge_count // block_rows
    value_blocks = values.reshape(block_count, block_rows, values.shape[1])
    index_blocks = indices.reshape(block_count, block_rows)
    targets = lax.broadcasted_iota(jnp.int32, (block_rows, row_count), 1)

    def add_block(running, portion):
        block_values, block_ids = portion
        one_hot = (block_ids[:, None] == targets).astype(jnp.bfloat16)
        return (
            running
            + lax.dot_general(one_hot, block_values, rows_dims, preferred_element_type=jnp.float32),
            None,
        )

    running, unused = lax.scan(
        add_block,
        jnp.zeros((row_count, values.shape[1]), jnp.float32),
        (value_blocks, index_blocks),
    )
    return running


def rim_rows(matrix, lists):
    return jnp.concatenate(
        [jnp.take(matrix, lists[0], axis=0), jnp.take(matrix, lists[1], axis=0)], axis=0
    )


def on_device(
    node_in,
    edge_in,
    senders,
    receivers,
    send_list,
    w_edge_first,
    b_edge_first,
    w_edge_second,
    b_edge_second,
    edge_gain,
    edge_shift,
    w_node_first,
    b_node_first,
    w_node_second,
    b_node_second,
    node_gain,
    node_shift,
    node_cotangent,
    edge_cotangent,
):
    node_rows = node_in[0]
    edge_rows = edge_in[0]
    lists = send_list[0]
    node_count = node_rows.shape[0]
    latent = node_rows.shape[1]
    rim_width = lists.shape[1]
    arrived = with_halo(rim_rows(node_rows, lists), ((("dom", "sub"), 0),), rim_width)
    extended = jnp.concatenate([node_rows, arrived[:rim_width], arrived[3 * rim_width :]], axis=0)
    edge_inputs = jnp.concatenate(
        [edge_rows, jnp.take(node_rows, senders, axis=0), jnp.take(extended, receivers, axis=0)],
        axis=1,
    )
    edge_update, edge_saved = block_forward(
        edge_inputs, w_edge_first, b_edge_first, w_edge_second, b_edge_second, edge_gain, edge_shift
    )
    edge_out = (edge_rows.astype(jnp.float32) + edge_update).astype(jnp.bfloat16)
    messages = edge_update.astype(jnp.bfloat16)
    gathered_sum = segment_rows(messages, receivers, node_count + 2 * rim_width)
    returned = with_halo(
        gathered_sum[node_count:].astype(jnp.bfloat16), ((("dom", "sub"), 0),), rim_width
    ).astype(jnp.float32)
    aggregate = gathered_sum[:node_count].at[lists[0]].add(returned[:rim_width])
    aggregate = aggregate.at[lists[1]].add(returned[3 * rim_width :])
    node_inputs = jnp.concatenate([node_rows, aggregate.astype(jnp.bfloat16)], axis=1)
    node_update, node_saved = block_forward(
        node_inputs, w_node_first, b_node_first, w_node_second, b_node_second, node_gain, node_shift
    )
    node_out = (node_rows.astype(jnp.float32) + node_update).astype(jnp.bfloat16)
    node_upstream = node_cotangent[0].astype(jnp.float32)
    node_back, node_terms = block_backward(
        node_inputs, node_saved, w_node_first, w_node_second, node_gain, node_upstream
    )
    aggregate_grad = node_back[:, latent:].astype(jnp.bfloat16)
    adjoint_in = with_halo(rim_rows(aggregate_grad, lists), ((("dom", "sub"), 0),), rim_width)
    adjoint_ext = jnp.concatenate(
        [aggregate_grad, adjoint_in[:rim_width], adjoint_in[3 * rim_width :]], axis=0
    )
    edge_upstream = edge_cotangent[0].astype(jnp.float32) + jnp.take(
        adjoint_ext, receivers, axis=0
    ).astype(jnp.float32)
    edge_back, edge_terms = block_backward(
        edge_inputs, edge_saved, w_edge_first, w_edge_second, edge_gain, edge_upstream
    )
    edge_grad = (edge_cotangent[0].astype(jnp.float32) + edge_back[:, :latent]).astype(jnp.bfloat16)
    sender_grad = edge_back[:, latent : 2 * latent].astype(jnp.bfloat16)
    receiver_grad = edge_back[:, 2 * latent :].astype(jnp.bfloat16)
    sender_sum = segment_rows(sender_grad, senders, node_count)
    receiver_sum = segment_rows(receiver_grad, receivers, node_count + 2 * rim_width)
    returned_grad = with_halo(
        receiver_sum[node_count:].astype(jnp.bfloat16), ((("dom", "sub"), 0),), rim_width
    ).astype(jnp.float32)
    owned = receiver_sum[:node_count].at[lists[0]].add(returned_grad[:rim_width])
    owned = owned.at[lists[1]].add(returned_grad[3 * rim_width :])
    node_grad = (node_upstream + node_back[:, :latent] + sender_sum + owned).astype(jnp.bfloat16)
    totals = lax.psum(
        (
            edge_terms[0],
            edge_terms[1],
            edge_terms[2],
            edge_terms[3],
            edge_terms[4],
            edge_terms[5],
            node_terms[0],
            node_terms[1],
            node_terms[2],
            node_terms[3],
            node_terms[4],
            node_terms[5],
        ),
        ("dom", "sample", "sub"),
    )
    return (
        node_out[None],
        edge_out[None],
        node_grad[None],
        edge_grad[None],
        totals[0],
        totals[1],
        totals[2],
        totals[3],
        totals[4],
        totals[5],
        totals[6],
        totals[7],
        totals[8],
        totals[9],
        totals[10],
        totals[11],
    )


def solution(mesh):
    return jax.shard_map(
        on_device,
        mesh=mesh,
        in_specs=(
            P(("groups", "sample"), ("dom", "sub"), None),
            P(("groups", "sample"), ("dom", "sub"), None),
            P(("dom", "sub")),
            P(("dom", "sub")),
            P(("dom", "sub"), None, None),
            P(),
            P(),
            P(),
            P(),
            P(),
            P(),
            P(),
            P(),
            P(),
            P(),
            P(),
            P(),
            P(("groups", "sample"), ("dom", "sub"), None),
            P(("groups", "sample"), ("dom", "sub"), None),
        ),
        out_specs=(
            P(("groups", "sample"), ("dom", "sub"), None),
            P(("groups", "sample"), ("dom", "sub"), None),
            P(("groups", "sample"), ("dom", "sub"), None),
            P(("groups", "sample"), ("dom", "sub"), None),
            P("groups", None),
            P("groups"),
            P("groups", None),
            P("groups"),
            P("groups"),
            P("groups"),
            P("groups", None),
            P("groups"),
            P("groups", None),
            P("groups"),
            P("groups"),
            P("groups"),
        ),
        check_vma=False,
    )
```

profile of v0, /device:TPU:1, one launch (start us, length us, event | category | flops | bytes accessed | tf_op | source)
XLA Modules:
  0.0 274.9 jit_solution(9462295321944375404)
XLA Ops:
  10.4 4.6 %collective-permute-start = (bf16[128,128]{0,1:T(8,128)(2,1)S(1)}, bf16[128,128]{0,1:T(8,128)(2,1)S(1)}, u32[]{:S(2)}, u32[]{:S(2)}) collective-permute-start(bf16[128,128]{0,1:T(8,128)(2,1)S(1)} %broadcast_select_fusion.6), channel_id=1, source_target_pairs={{0,1},{1,4},{4,5},{5,8},{8,9},{9,12},{12,13},{2,3},{3,6},{6,7},{7,... | collective-permute-start | bytes 98312 | tf_op jit(solution)/shard_map/ppermute | solution.py:18
  22.2 9.2 %gather_fusion = bf16[3072,128]{1,0:T(8,128)(2,1)S(1)} fusion(bf16[1024,128]{1,0:T(8,128)(2,1)S(1)} %bitcast.117, s32[3072]{0:T(1024)S(1)} %fusion.80), kind=kCustom, calls=%fused_computation.6 | custom fusion | bytes 1585152 | tf_op jit(solution)/shard_map/jit(_take)/gather | solution.py:122
  34.7 9.2 %gather_fusion.3 = bf16[3072,128]{1,0:T(8,128)(2,1)S(1)} fusion(bf16[1280,128]{1,0:T(8,128)(2,1)S(1)} %copy.57, s32[3072]{0:T(1024)S(1)} %fusion.81), kind=kCustom, calls=%fused_computation.1.clone | custom fusion | bytes 1585152 | tf_op jit(solution)/shard_map/jit(_take)/gather | solution.py:122
  48.5 2.6 fusion.32
  51.1 12.6 %while.33 = (s32[]{:T(128)}, f32[1280,128]{1,0:T(8,128)S(1)}, s32[6,512]{1,0:T(8,128)S(1)}, bf16[6,512,128]{2,1,0:T(8,128)(2,1)}, s32[]{:T(128)}, /*index=5*/s32[]{:T(128)}) while((s32[]{:T(128)}, f32[1280,128]{1,0:T(8,128)S(1)}, s32[6,512]{1,0:T(8,128)S(1)}, bf16[6,512,128]{2,1,0:T(8,128)(2,1)}, s32[]{:T(128)}, ...), condition=%wide.region_3.6_spmd.clone, body=%wide.region_2.5_spmd.clone.sunk | while | flops 168755200 | bytes 1448031 | solution.py:78
  51.1 2.1 fusion.121
  53.2 2.1 fusion.121
  55.3 2.1 fusion.121
  57.4 2.1 fusion.121
  59.5 2.1 fusion.121
  61.6 2.1 fusion.121
  65.1 3.6 %collective-permute-start.2 = (bf16[128,128]{1,0:T(8,128)(2,1)}, bf16[128,128]{1,0:T(8,128)(2,1)S(1)}, u32[]{:S(2)}, u32[]{:S(2)}) collective-permute-start(bf16[128,128]{1,0:T(8,128)(2,1)} %get-tuple-element.242), channel_id=1, source_target_pairs={{0,1},{1,4},{4,5},{5,8},{8,9},{9,12},{12,13},{2,3},{3,6},{6,7},{7,... | collective-permute-start | bytes 98312 | tf_op jit(solution)/shard_map/ppermute | solution.py:18
  87.3 2.5 collective-permute-start.4
  89.8 2.5 collective-permute-start.5
  98.1 11.5 %gather_fusion.6 = bf16[3072,128]{1,0:T(8,128)(2,1)} fusion(bf16[1280,128]{1,0:T(8,128)(2,1)S(1)} %pad_maximum_fusion.7, s32[3072]{0:T(1024)S(1)} %fusion.81), kind=kCustom, calls=%fused_computation.5.clone | custom fusion | bytes 1585152 | tf_op jit(solution)/shard_map/jit(_take)/gather | solution.py:150
  109.7 5.0 %multiply_reduce_fusion = (f32[128]{0:T(128)}, f32[3072]{0:T(1024)S(1)}, f32[3072]{0:T(1024)S(1)}, f32[128]{0:T(128)}) fusion(f32[3072,128]{1,0:T(8,128)S(1)} %get-tuple-element.250, bf16[1,3072,128]{2,1,0:T(8,128)(2,1)S(1)} %copy-done.2, f32[3072]{0:T(1024)S(1)} %add_rsqrt_fusion, f32[3072]{0:T(1024)S(1)} %broadcast_multiply_fusion.2, ...), kind=kLoop, calls=%fused_computation.46 | loop fusion | flops 5105408 | bytes 3199488 | tf_op jit(solution)/shard_map/reduce_sum | solution.py:38
  114.6 3.6 %fusion.91 = (f32[128]{0:T(128)}, bf16[3072,128]{1,0:T(8,128)(2,1)S(1)}) fusion(f32[3072]{0:T(1024)S(1)} %broadcast_multiply_fusion, f32[3072,128]{1,0:T(8,128)S(1)} %get-tuple-element.250, f32[3072]{0:T(1024)S(1)} %broadcast_multiply_fusion.2, f32[3072]{0:T(1024)S(1)} %broadcast_multiply_fusion.1, f32[128]{0:T(128)S(1)} %copy-done.36, ...), kind=kLoop, calls=%fused_computation.164 | loop fusion | flops 5111680 | bytes 3985408 | tf_op jit(solution)/shard_map/reduce_sum | solution.py:50
  123.2 4.1 %fusion.97 = (bf16[3072,384]{1,0:T(8,128)(2,1)S(1)}, f32[3072,384]{1,0:T(8,128)}) fusion(bf16[384,128]{1,0:T(8,128)(2,1)S(1)} %copy-done, bf16[3072,128]{1,0:T(8,128)(2,1)} %copy-done.16), kind=kOutput, calls=%fused_computation.170 | convolution fusion | flops 303169536 | bytes 7962624 | tf_op jit(solution)/shard_map/dot_general | solution.py:57
  128.5 11.3 %while.35 = (s32[]{:T(128)}, f32[1280,128]{1,0:T(8,128)S(1)}, s32[6,512]{1,0:T(8,128)}, bf16[6,512,128]{2,1,0:T(8,128)(2,1)S(1)}, s32[]{:T(128)}, /*index=5*/s32[]{:T(128)}) while((s32[]{:T(128)}, f32[1280,128]{1,0:T(8,128)S(1)}, s32[6,512]{1,0:T(8,128)}, bf16[6,512,128]{2,1,0:T(8,128)(2,1)S(1)}, s32[]{:T(128)}, ...), condition=%wide.region_15.18_spmd.clone, body=%wide.region_14.17_spmd.clone.sunk | while | flops 168755200 | bytes 1448031 | solution.py:78
  141.0 15.7 %while.34 = (s32[]{:T(128)}, f32[1024,128]{1,0:T(8,128)S(1)}, s32[6,512]{1,0:T(8,128)}, bf16[6,512,128]{2,1,0:T(8,128)(2,1)}, s32[]{:T(128)}, /*index=5*/s32[]{:T(128)}) while((s32[]{:T(128)}, f32[1024,128]{1,0:T(8,128)S(1)}, s32[6,512]{1,0:T(8,128)}, bf16[6,512,128]{2,1,0:T(8,128)(2,1)}, s32[]{:T(128)}, ...), condition=%wide.region_13.16_spmd.clone, body=%wide.region_12.15_spmd.clone.sunk | while | flops 135004160 | bytes 1185887 | solution.py:78
  159.5 3.2 %collective-permute-start.6 = (bf16[128,128]{1,0:T(8,128)(2,1)S(1)}, bf16[128,128]{1,0:T(8,128)(2,1)S(1)}, u32[]{:S(2)}, u32[]{:S(2)}) collective-permute-start(bf16[128,128]{1,0:T(8,128)(2,1)S(1)} %get-tuple-element.240), channel_id=1, source_target_pairs={{0,1},{1,4},{4,5},{5,8},{8,9},{9,12},{12,13},{2,3},{3,6},{6,7},{7,... | collective-permute-start | bytes 98312 | tf_op jit(solution)/shard_map/ppermute | solution.py:18
  164.7 2.5 fusion.33
  169.8 30.2 %all-reduce = (f32[128]{0:T(128)}, f32[128]{0:T(128)}, f32[128]{0:T(128)}, f32[128]{0:T(128)}, f32[128]{0:T(128)}, /*index=5*/f32[128]{0:T(128)}, f32[128]{0:T(128)}, f32[128]{0:T(128)}) all-reduce(f32[128]{0:T(128)S(1)} %copy-done.49, ...), channel_id=1, replica_groups=mesh['groups'=2,'dom'=4,'sample'=2,'sub'=2] {'dom','sample','sub'}, use_global_device_ids=true, to_apply=%region_20.23 | all-reduce | flops 1024 | bytes 8192 | tf_op jit(solution)/shard_map/psum | solution.py:167
  203.9 58.0 %all-reduce.4.cloned.1.call-done = (f32[384,128]{1,0:T(8,128)}, f32[128,128]{1,0:T(8,128)}, f32[256,128]{1,0:T(8,128)}, f32[128,128]{1,0:T(8,128)}) async-done(((f32[384,128]{1,0:T(8,128)}, f32[128,128]{1,0:T(8,128)}, f32[256,128]{1,0:T(8,128)}, f32[128,128]{1,0:T(8,128)}), (f32[384,128]{1,0:T(8,128)}, f32[128,128]{1,0:T(8,128)}, f32[256,128]{1,0:T(8,128)}, ...) | async-done | bytes 458768 | tf_op jit(solution)/shard_map/psum | solution.py:167
  (239 shorter events, 94.8 us)
Async XLA Ops:
  7.2 38.4 %copy-start = (bf16[384,128]{1,0:T(8,128)(2,1)S(1)}, bf16[384,128]{1,0:T(8,128)(2,1)}, u32[]{:S(2)}) copy-start(bf16[384,128]{1,0:T(8,128)(2,1)} %param.34) | copy-start | bytes 294916
  7.2 15.0 %copy-start.1 = (bf16[1,1024,128]{2,1,0:T(8,128)(2,1)S(1)}, bf16[1,1024,128]{2,1,0:T(8,128)(2,1)}, u32[]{:S(2)}) copy-start(bf16[1,1024,128]{2,1,0:T(8,128)(2,1)} %param.29) | copy-start | bytes 786436
  7.2 254.8 %all-reduce.4.cloned.1.call-start = ((), (), s32[]{:S(2)}) async-start(), calls=%async_computation | async-start | bytes 917504 | tf_op jit(solution)/shard_map/psum | solution.py:167
  8.0 13.4 %copy-start.33 = (pred[128]{0:T(512)(128)(4,1)}, pred[128]{0:T(512)(128)(4,1)S(1)}, u32[]{:S(2)}) copy-start(pred[128]{0:T(512)(128)(4,1)S(1)} %get-tuple-element.231) | copy-start | bytes 388
  8.0 13.4 %copy-start.34 = (pred[128]{0:T(512)(128)(4,1)}, pred[128]{0:T(512)(128)(4,1)S(1)}, u32[]{:S(2)}) copy-start(pred[128]{0:T(512)(128)(4,1)S(1)} %get-tuple-element.247) | copy-start | bytes 388
  10.4 24.1 %collective-permute-start = (bf16[128,128]{0,1:T(8,128)(2,1)S(1)}, bf16[128,128]{0,1:T(8,128)(2,1)S(1)}, u32[]{:S(2)}, u32[]{:S(2)}) collective-permute-start(bf16[128,128]{0,1:T(8,128)(2,1)S(1)} %broadcast_select_fusion.6), channel_id=1, source_target_pairs={{0,1},{1,4},{4,5},{5,8},{8,9},{9,12},{12,13},{2,3},{3,6},{6,7},{7,... | collective-permute-start | bytes 98312 | tf_op jit(solution)/shard_map/ppermute | solution.py:18
  17.4 17.1 %collective-permute-start.1 = (bf16[128,128]{0,1:T(8,128)(2,1)S(1)}, bf16[128,128]{0,1:T(8,128)(2,1)S(1)}, u32[]{:S(2)}, u32[]{:S(2)}) collective-permute-start(bf16[128,128]{0,1:T(8,128)(2,1)S(1)} %broadcast_select_fusion.5), channel_id=1, source_target_pairs={{1,0},{4,1},{5,4},{8,5},{9,8},{12,9},{13,12},{3,2},{6,3},{7,6},{10... | collective-permute-start | bytes 98312 | tf_op jit(solution)/shard_map/ppermute | solution.py:21
  33.0 12.5 %copy-start.12 = (bf16[3072,128]{1,0:T(8,128)(2,1)}, bf16[3072,128]{1,0:T(8,128)(2,1)S(1)}, u32[]{:S(2)}) copy-start(bf16[3072,128]{1,0:T(8,128)(2,1)S(1)} %broadcast_select_fusion.2) | copy-start | bytes 2359300
  33.0 40.9 %copy-start.47 = (s32[128]{0:T(128)}, s32[128]{0:T(128)S(1)}, u32[]{:S(2)}) copy-start(s32[128]{0:T(128)S(1)} %get-tuple-element.246) | copy-start | bytes 1540
  33.0 42.4 %copy-start.46 = (s32[128]{0:T(128)}, s32[128]{0:T(128)S(1)}, u32[]{:S(2)}) copy-start(s32[128]{0:T(128)S(1)} %get-tuple-element.245) | copy-start | bytes 1540
  33.2 43.9 %copy-start.7 = (bf16[1,1024,128]{1,2,0:T(8,128)(2,1)}, bf16[1,1024,128]{1,2,0:T(8,128)(2,1)S(1)}, u32[]{:S(2)}) copy-start(bf16[1,1024,128]{1,2,0:T(8,128)(2,1)S(1)} %copy.51) | copy-start | bytes 786436
  34.5 45.0 %copy-start.4 = (bf16[1,1024,128]{1,2,0:T(8,128)(2,1)}, bf16[1,1024,128]{1,2,0:T(8,128)(2,1)S(1)}, u32[]{:S(2)}) copy-start(bf16[1,1024,128]{1,2,0:T(8,128)(2,1)S(1)} %copy.59) | copy-start | bytes 786436
  51.1 20.2 %copy-start.23 = (s32[3072]{0:T(1024)S(1)}, s32[3072]{0:T(1024)}, u32[]{:S(2)}) copy-start(s32[3072]{0:T(1024)} %param.31) | copy-start | bytes 36868
  63.7 11.7 %copy-start.24 = (s32[6,512]{1,0:T(8,128)}, s32[6,512]{1,0:T(8,128)S(1)}, u32[]{:S(2)}) copy-start(s32[6,512]{1,0:T(8,128)S(1)} %get-tuple-element.430) | copy-start | bytes 36868
  65.1 7.7 %collective-permute-start.2 = (bf16[128,128]{1,0:T(8,128)(2,1)}, bf16[128,128]{1,0:T(8,128)(2,1)S(1)}, u32[]{:S(2)}, u32[]{:S(2)}) collective-permute-start(bf16[128,128]{1,0:T(8,128)(2,1)} %get-tuple-element.242), channel_id=1, source_target_pairs={{0,1},{1,4},{4,5},{5,8},{8,9},{9,12},{12,13},{2,3},{3,6},{6,7},{7,... | collective-permute-start | bytes 98312 | tf_op jit(solution)/shard_map/ppermute | solution.py:18
  68.7 5.2 %collective-permute-start.3 = (bf16[128,128]{1,0:T(8,128)(2,1)S(1)}, bf16[128,128]{1,0:T(8,128)(2,1)S(1)}, u32[]{:S(2)}, u32[]{:S(2)}) collective-permute-start(bf16[128,128]{1,0:T(8,128)(2,1)S(1)} %get-tuple-element.243), channel_id=1, source_target_pairs={{1,0},{4,1},{5,4},{8,5},{9,8},{12,9},{13,12},{3,2},{6,3},{7,6},{10... | collective-permute-start | bytes 98312 | tf_op jit(solution)/shard_map/ppermute | solution.py:21
  71.9 5.2 %copy-start.55 = (f32[128]{0:T(128)S(1)}, f32[128]{0:T(128)}, u32[]{:S(2)}) copy-start(f32[128]{0:T(128)} %param.41) | copy-start | bytes 1540
  71.9 5.2 %copy-start.25 = (bf16[256,128]{1,0:T(8,128)(2,1)S(1)}, bf16[256,128]{1,0:T(8,128)(2,1)}, u32[]{:S(2)}) copy-start(bf16[256,128]{1,0:T(8,128)(2,1)} %param.40) | copy-start | bytes 196612
  87.3 10.0 %collective-permute-start.4 = (bf16[128,128]{1,0:T(8,128)(2,1)}, bf16[128,128]{1,0:T(8,128)(2,1)}, u32[]{:S(2)}, u32[]{:S(2)}) collective-permute-start(bf16[128,128]{1,0:T(8,128)(2,1)} %broadcast_select_fusion.4), channel_id=1, source_target_pairs={{0,1},{1,4},{4,5},{5,8},{8,9},{9,12},{12,13},{2,3},{3,6},{6,7},{7,... | collective-permute-start | bytes 98312 | tf_op jit(solution)/shard_map/ppermute | solution.py:18
  89.8 7.5 %collective-permute-start.5 = (bf16[128,128]{1,0:T(8,128)(2,1)}, bf16[128,128]{1,0:T(8,128)(2,1)}, u32[]{:S(2)}, u32[]{:S(2)}) collective-permute-start(bf16[128,128]{1,0:T(8,128)(2,1)} %broadcast_select_fusion.3), channel_id=1, source_target_pairs={{1,0},{4,1},{5,4},{8,5},{9,8},{12,9},{13,12},{3,2},{6,3},{7,6},{10... | collective-permute-start | bytes 98312 | tf_op jit(solution)/shard_map/ppermute | solution.py:21
  98.1 11.6 %copy-start.2 = (bf16[1,3072,128]{2,1,0:T(8,128)(2,1)S(1)}, bf16[1,3072,128]{2,1,0:T(8,128)(2,1)}, u32[]{:S(2)}) copy-start(bf16[1,3072,128]{2,1,0:T(8,128)(2,1)} %param.47) | copy-start | bytes 2359300
  98.1 11.6 %copy-start.36 = (f32[128]{0:T(128)S(1)}, f32[128]{0:T(128)}, u32[]{:S(2)}) copy-start(f32[128]{0:T(128)} %param.38) | copy-start | bytes 1540
  159.5 40.5 %collective-permute-start.6 = (bf16[128,128]{1,0:T(8,128)(2,1)S(1)}, bf16[128,128]{1,0:T(8,128)(2,1)S(1)}, u32[]{:S(2)}, u32[]{:S(2)}) collective-permute-start(bf16[128,128]{1,0:T(8,128)(2,1)S(1)} %get-tuple-element.240), channel_id=1, source_target_pairs={{0,1},{1,4},{4,5},{5,8},{8,9},{9,12},{12,13},{2,3},{3,6},{6,7},{7,... | collective-permute-start | bytes 98312 | tf_op jit(solution)/shard_map/ppermute | solution.py:18
  162.7 37.3 %collective-permute-start.7 = (bf16[128,128]{1,0:T(8,128)(2,1)S(1)}, bf16[128,128]{1,0:T(8,128)(2,1)S(1)}, u32[]{:S(2)}, u32[]{:S(2)}) collective-permute-start(bf16[128,128]{1,0:T(8,128)(2,1)S(1)} %get-tuple-element.241), channel_id=1, source_target_pairs={{1,0},{4,1},{5,4},{8,5},{9,8},{12,9},{13,12},{3,2},{6,3},{7,6},{10... | collective-permute-start | bytes 98312 | tf_op jit(solution)/shard_map/ppermute | solution.py:21
  (44 other events, 77.7 us)
Sparse Core Ops, SparseCore 0:
  169.9 92.0 all-reduce.3
where the time goes:
time: 278 us; the launch traced here: 275 us
  local copies, waits for them, and re-layouts  68.7 us (25%)
  waiting for transfers between devices  59.2 us (21%)
  matrix products  44.9 us (16%)
  other arithmetic  34.2 us (12%)
  blocking collectives  30.2 us (11%)
  starting transfers between devices  22.3 us (8%)
  between operations  15 us (5%)
    psum x1, waiting for transfers between devices, on_device(): lax.psum((edge_terms[0], edge_terms[1], edge_terms[2], edge_terms[3], edg...  58 us
    dot_general x18, matrix products, add_block(): lax.dot_general(one_hot, block_values, rows_dims, preferred_element_type=...  30.4 us
    psum x1, blocking collectives, on_device(): lax.psum((edge_terms[0], edge_terms[1], edge_terms[2], edge_terms[3], edg...  30.2 us
    unnamed x126, local copies, waits for them, and re-layouts  16.1 us
    ppermute x4, starting transfers between devices, with_halo(): lax.ppermute(lax.slice_in_dim(block, block.shape[dim] - width, None, axis...  13.9 us
    gather x1, local copies, waits for them, and re-layouts, on_device(): jnp.take(adjoint_ext, receivers, axis=0).astype(jnp.float32)  11.5 us
    gather x1, local copies, waits for them, and re-layouts, on_device(): jnp.take(extended, receivers, axis=0)  9.16 us
    gather x1, local copies, waits for them, and re-layouts, on_device(): jnp.take(node_rows, senders, axis=0)  9.15 us
  transfers between devices with their start and end apart: 9, of which 2 were waited for; matrix products, arithmetic and copies ran while one was open for 12% of the time, Pallas kernels for 0%

commit v1 on v0

v1 whole, which is shorter than its diff:
```python
import jax
import jax.numpy as jnp
from jax import lax
from jax.experimental import pallas as pl
from jax.experimental.pallas import tpu as pltpu
from jax.sharding import PartitionSpec as P

epsilon = 1e-05
rows_dims = (((0,), (0,)), ((), ()))
back_dims = (((1,), (1,)), ((), ()))
f32 = jnp.float32
bf16 = jnp.bfloat16
lane = 128
edge_tile = 512
vmem_limit = 32 * 1024 * 1024
sum_rows = 16


def dot(left, right):
    return jnp.dot(left, right, preferred_element_type=f32)


def dot_rows(left, right):
    return lax.dot_general(left, right, rows_dims, preferred_element_type=f32)


def dot_back(left, right):
    return lax.dot_general(left, right, back_dims, preferred_element_type=f32)


def column_of(row):
    return jnp.broadcast_to(row, (lane, lane)).T


def hot_columns(ids, width):
    targets = lax.broadcasted_iota(jnp.int32, ids.shape, 1)
    parts = [
        jnp.where(ids == targets + at, 1.0, 0.0).astype(bf16) for at in range(0, width, lane)
    ]
    return jnp.concatenate(parts, axis=1)


def hot_rows(row, height):
    targets = lax.broadcasted_iota(jnp.int32, (height, lane), 0)
    return jnp.where(row == targets, 1.0, 0.0).astype(bf16)


def fold(ids, half):
    upper = ids >= half
    return upper, jnp.where(upper, ids - half, ids)


def side_by_side(rows):
    half = rows.shape[0] // 2
    return jnp.concatenate([rows[:half], rows[half:]], axis=1)


def pick(ids, table):
    half = table.shape[0]
    upper, low = fold(ids, half)
    both = dot(hot_columns(low, half), table)
    return jnp.where(upper, both[:, lane:], both[:, :lane])


def spread(ids_ref, first, count, half, ids, values):
    upper, unused = fold(ids, half)
    paired = jnp.concatenate(
        [jnp.where(upper, 0.0, values).astype(bf16), jnp.where(upper, values, 0.0).astype(bf16)],
        axis=1,
    )
    parts = []
    for k in range(count):
        row = ids_ref[pl.ds(first + k, 1), :]
        unused, low = fold(row, half)
        parts.append(hot_rows(low, half))
    return dot(jnp.concatenate(parts, axis=1), paired)


def sigmoid(z):
    return 0.5 * jnp.tanh(0.5 * z) + 0.5


def centred_second(w_ref, b_ref):
    w = w_ref[...].astype(f32)
    w = w - jnp.mean(w, axis=1, keepdims=True)
    high = w.astype(bf16)
    low = (w - high.astype(f32)).astype(bf16)
    b = b_ref[...]
    return jnp.concatenate([high, low], axis=1), b - jnp.mean(b, axis=1, keepdims=True)


def normed_of(act, w_pair, b_centred):
    both = dot(act, w_pair)
    center = both[:, :lane] + both[:, lane:] + b_centred
    scale_inv = lax.rsqrt(jnp.mean(center * center, axis=1, keepdims=True) + epsilon)
    return center * scale_inv, scale_inv


def back_norm(upstream, normed, scale_inv, gain):
    d_normed = upstream * gain
    return scale_inv * (
        d_normed
        - jnp.mean(d_normed, axis=1, keepdims=True)
        - normed * jnp.mean(d_normed * normed, axis=1, keepdims=True)
    )


def column_sum(values):
    return jnp.sum(values, axis=0, keepdims=True)


def fill_columns(ids_ref, out_ref):
    for k in range(ids_ref.shape[0]):
        out_ref[k * lane : (k + 1) * lane, :] = column_of(ids_ref[k : k + 1, :])


def rim_kernel(node_ref, list_ref, low_ref, high_ref):
    node = node_ref[...]
    for side, out_ref in ((0, low_ref), (1, high_ref)):
        hot = hot_columns(column_of(list_ref[side : side + 1, :]), node.shape[0])
        out_ref[...] = dot(hot, node).astype(bf16)


def edge_forward_kernel(
    node_ref,
    low_ref,
    high_ref,
    edge_ref,
    snd_ref,
    rcv_ref,
    w1_ref,
    b1_ref,
    w2_ref,
    b2_ref,
    gain_ref,
    shift_ref,
    out_ref,
    z_ref,
    agg_ref,
    agg_low_ref,
    agg_high_ref,
    snd_table,
    rcv_table,
    snd_column,
    rcv_column,
    w2_pair,
    total,
):
    nodes = node_ref.shape[0]
    rim = low_ref.shape[0]
    half = rcv_table.shape[0]
    w1_edge = w1_ref[:lane]
    b1 = b1_ref[...]
    gain = gain_ref[...]
    shift = shift_ref[...]
    snd_table[...] = side_by_side(dot(node_ref[...], w1_ref[lane : 2 * lane]).astype(bf16))
    extended = jnp.concatenate([node_ref[...], low_ref[...], high_ref[...]], axis=0)
    rcv_table[...] = side_by_side(dot(extended, w1_ref[2 * lane :]).astype(bf16))
    pair, b2 = centred_second(w2_ref, b2_ref)
    w2_pair[...] = pair
    fill_columns(snd_ref, snd_column)
    fill_columns(rcv_ref, rcv_column)
    total[...] = jnp.zeros_like(total)

    def tile(i, carry):
        rows = pl.ds(pl.multiple_of(i * edge_tile, edge_tile), edge_tile)
        x = edge_ref[rows, :]
        rcv = rcv_column[rows, :]
        z = dot(x, w1_edge) + b1
        z = z + pick(snd_column[rows, :], snd_table[...])
        z = z + pick(rcv, rcv_table[...])
        z_ref[rows, :] = z
        act = (z * sigmoid(z)).astype(bf16)
        normed, unused = normed_of(act, w2_pair[...], b2)
        update = normed * gain + shift
        out_ref[rows, :] = (x.astype(f32) + update).astype(bf16)
        total[...] += spread(rcv_ref, i * (edge_tile // lane), edge_tile // lane, half, rcv, update)
        return carry

    lax.fori_loop(0, edge_ref.shape[0] // edge_tile, tile, 0)
    agg_ref[:half, :] = total[:, :lane]
    agg_ref[half:, :] = total[: nodes - half, lane:]
    agg_low_ref[...] = total[nodes - half : nodes - half + rim, lane:].astype(bf16)
    agg_high_ref[...] = total[nodes - half + rim :, lane:].astype(bf16)


def node_kernel(
    node_ref,
    agg_ref,
    low_ref,
    high_ref,
    list_ref,
    w1_ref,
    b1_ref,
    w2_ref,
    b2_ref,
    gain_ref,
    shift_ref,
    cot_ref,
    out_ref,
    base_ref,
    dagg_ref,
    rim_low_ref,
    rim_high_ref,
    grads_ref,
):
    nodes = node_ref.shape[0]
    node = node_ref[...]
    hot = jnp.concatenate(
        [hot_rows(list_ref[0:1, :], nodes), hot_rows(list_ref[1:2, :], nodes)], axis=1
    )
    returned = jnp.concatenate([low_ref[...], high_ref[...]], axis=0)
    agg = (agg_ref[...] + dot(hot, returned)).astype(bf16)
    x = jnp.concatenate([node, agg], axis=1)
    w1 = w1_ref[...]
    z = dot(x, w1) + b1_ref[...]
    sig = sigmoid(z)
    act = (z * sig).astype(bf16)
    pair, b2 = centred_second(w2_ref, b2_ref)
    normed, scale_inv = normed_of(act, pair, b2)
    gain = gain_ref[...]
    out_ref[...] = (node.astype(f32) + normed * gain + shift_ref[...]).astype(bf16)
    upstream = cot_ref[...].astype(f32)
    dz2 = back_norm(upstream, normed, scale_inv, gain)
    dz2b = dz2.astype(bf16)
    da = dot_back(dz2b, w2_ref[...])
    dz1 = da * sig * (1.0 + z * (1.0 - sig))
    dz1b = dz1.astype(bf16)
    dx = dot_back(dz1b, w1)
    base_ref[...] = upstream + dx[:, :lane]
    dagg = dx[:, lane:].astype(bf16)
    dagg_ref[...] = dagg
    for side, rim_ref in ((0, rim_low_ref), (1, rim_high_ref)):
        picked = hot_columns(column_of(list_ref[side : side + 1, :]), nodes)
        rim_ref[...] = dot(picked, dagg).astype(bf16)
    first = 2 * lane
    second = first + lane
    grads_ref[:first, :] = dot_rows(x, dz1b).astype(bf16)
    grads_ref[first:second, :] = dot_rows(act, dz2b).astype(bf16)
    sums = [column_sum(dz1), column_sum(dz2), column_sum(upstream * normed), column_sum(upstream)]
    sums.append(jnp.zeros((sum_rows - len(sums), lane), f32))
    grads_ref[second:, :] = jnp.concatenate(sums, axis=0).astype(bf16)


def edge_backward_kernel(
    z_ref,
    cot_ref,
    edge_ref,
    snd_ref,
    rcv_ref,
    node_ref,
    low_ref,
    high_ref,
    dagg_ref,
    dagg_low_ref,
    dagg_high_ref,
    base_ref,
    w1_ref,
    w2_ref,
    b2_ref,
    gain_ref,
    node_grads_ref,
    grad_ref,
    acc_ref,
    back_low_ref,
    back_high_ref,
    grads_ref,
    table,
    snd_column,
    rcv_column,
    w2_pair,
    snd_total,
    rcv_total,
    squares,
    sums,
):
    nodes = node_ref.shape[0]
    rim = low_ref.shape[0]
    snd_half = snd_total.shape[0]
    rcv_half = rcv_total.shape[0]
    w1_edge = w1_ref[:lane]
    w2 = w2_ref[...]
    gain = gain_ref[...]
    table[...] = side_by_side(
        jnp.concatenate([dagg_ref[...], dagg_low_ref[...], dagg_high_ref[...]], axis=0)
    )
    pair, b2 = centred_second(w2_ref, b2_ref)
    w2_pair[...] = pair
    fill_columns(snd_ref, snd_column)
    fill_columns(rcv_ref, rcv_column)
    snd_total[...] = jnp.zeros_like(snd_total)
    rcv_total[...] = jnp.zeros_like(rcv_total)
    squares[...] = jnp.zeros_like(squares)
    sums[...] = jnp.zeros_like(sums)

    def tile(i, carry):
        rows = pl.ds(pl.multiple_of(i * edge_tile, edge_tile), edge_tile)
        chunk = edge_tile // lane
        rcv = rcv_column[rows, :]
        snd = snd_column[rows, :]
        x = edge_ref[rows, :]
        z = z_ref[rows, :]
        cot = cot_ref[rows, :].astype(f32)
        upstream = cot + pick(rcv, table[...])
        sig = sigmoid(z)
        act = (z * sig).astype(bf16)
        normed, scale_inv = normed_of(act, w2_pair[...], b2)
        dz2 = back_norm(upstream, normed, scale_inv, gain)
        dz2b = dz2.astype(bf16)
        da = dot_back(dz2b, w2)
        dz1 = da * sig * (1.0 + z * (1.0 - sig))
        dz1b = dz1.astype(bf16)
        grad_ref[rows, :] = (cot + dot_back(dz1b, w1_edge)).astype(bf16)
        squares[:lane, :] += dot_rows(x, dz1b)
        squares[lane:, :] += dot_rows(act, dz2b)
        sums[0:1, :] += column_sum(dz1)
        sums[1:2, :] += column_sum(dz2)
        sums[2:3, :] += column_sum(upstream * normed)
        sums[3:4, :] += column_sum(upstream)
        snd_total[...] += spread(snd_ref, i * chunk, chunk, snd_half, snd, dz1)
        rcv_total[...] += spread(rcv_ref, i * chunk, chunk, rcv_half, rcv, dz1)
        return carry

    lax.fori_loop(0, edge_ref.shape[0] // edge_tile, tile, 0)
    snd_sum = jnp.concatenate([snd_total[:, :lane], snd_total[:, lane:]], axis=0).astype(bf16)
    rcv_sum = jnp.concatenate([rcv_total[:, :lane], rcv_total[:, lane:]], axis=0).astype(bf16)
    w1_snd = w1_ref[lane : 2 * lane]
    w1_rcv = w1_ref[2 * lane :]
    acc_ref[...] = base_ref[...] + dot_back(snd_sum, w1_snd) + dot_back(rcv_sum[:nodes], w1_rcv)
    back = dot_back(rcv_sum[nodes:], w1_rcv).astype(bf16)
    back_low_ref[...] = back[:rim]
    back_high_ref[...] = back[rim:]
    extended = jnp.concatenate([node_ref[...], low_ref[...], high_ref[...]], axis=0)
    grads_ref[:lane, :] = squares[:lane, :].astype(bf16)
    grads_ref[lane : 2 * lane, :] = dot_rows(node_ref[...], snd_sum).astype(bf16)
    grads_ref[2 * lane : 3 * lane, :] = dot_rows(extended, rcv_sum).astype(bf16)
    grads_ref[3 * lane : 4 * lane, :] = squares[lane:, :].astype(bf16)
    node_rows = node_grads_ref.shape[0] - sum_rows
    grads_ref[4 * lane : 4 * lane + node_rows, :] = node_grads_ref[:node_rows, :]
    node_sums = node_grads_ref[node_rows:, :].astype(f32)
    grads_ref[4 * lane + node_rows :, :] = jnp.concatenate(
        [sums[0:4, :], node_sums[0:4, :], jnp.zeros((sum_rows - 8, lane), f32)], axis=0
    ).astype(bf16)


def node_grad_kernel(acc_ref, low_ref, high_ref, list_ref, out_ref):
    nodes = acc_ref.shape[0]
    hot = jnp.concatenate(
        [hot_rows(list_ref[0:1, :], nodes), hot_rows(list_ref[1:2, :], nodes)], axis=1
    )
    returned = jnp.concatenate([low_ref[...], high_ref[...]], axis=0)
    out_ref[...] = (acc_ref[...] + dot(hot, returned)).astype(bf16)


def finish_kernel(own_ref, other_ref, *out_refs):
    total = own_ref[...].astype(f32) + other_ref[...].astype(f32)
    at = 0
    for out_ref in out_refs[:4]:
        out_ref[...] = total[at : at + out_ref.shape[0]]
        at += out_ref.shape[0]
    for k, out_ref in enumerate(out_refs[4:]):
        out_ref[...] = total[at + k : at + k + 1]


def call(kernel, outs, scratch, *operands, flops=0):
    held = sum(x.size * x.dtype.itemsize for x in operands)
    return pl.pallas_call(
        kernel,
        out_shape=[jax.ShapeDtypeStruct(shape, dtype) for shape, dtype in outs],
        in_specs=[pl.BlockSpec(memory_space=pltpu.VMEM)] * len(operands),
        out_specs=[pl.BlockSpec(memory_space=pltpu.VMEM)] * len(outs),
        scratch_shapes=[pltpu.VMEM(shape, dtype) for shape, dtype in scratch],
        compiler_params=pltpu.CompilerParams(vmem_limit_bytes=vmem_limit),
        cost_estimate=pl.CostEstimate(flops=flops, bytes_accessed=held, transcendentals=0),
    )(*operands)


def neighbours(low, high):
    axis = ("dom", "sub")
    count = lax.axis_size("dom") * lax.axis_size("sub")
    forward = [(i, i + 1) for i in range(count - 1)]
    backward = [(target, source) for source, target in forward]
    return lax.ppermute(high, axis, forward), lax.ppermute(low, axis, backward)


def sum_rounds():
    for axis in ("sub", "sample", "dom"):
        count = lax.axis_size(axis)
        step = 1
        while step < count:
            yield axis, [(i, i ^ step) for i in range(count)]
            step *= 2


def on_device(
    node_in,
    edge_in,
    senders,
    receivers,
    send_list,
    w_edge_first,
    b_edge_first,
    w_edge_second,
    b_edge_second,
    edge_gain,
    edge_shift,
    w_node_first,
    b_node_first,
    w_node_second,
    b_node_second,
    node_gain,
    node_shift,
    node_cotangent,
    edge_cotangent,
):
    node = node_in[0]
    edge = edge_in[0]
    lists = send_list[0]
    nodes = node.shape[0]
    edges = edge.shape[0]
    rim = lists.shape[1]
    snd = senders.reshape(edges // lane, lane)
    rcv = receivers.reshape(edges // lane, lane)
    row = lambda vector: vector.reshape(1, vector.shape[0])
    rim_shape = ((rim, lane), bf16)
    snd_half = nodes // 2
    rcv_half = (nodes + 2 * rim) // 2

    rim_low, rim_high = call(rim_kernel, [rim_shape] * 2, [], node, lists)
    low, high = neighbours(rim_low, rim_high)
    edge_out, z, agg, agg_low, agg_high = call(
        edge_forward_kernel,
        [((edges, lane), bf16), ((edges, lane), f32), ((nodes, lane), f32), rim_shape, rim_shape],
        [
            ((snd_half, 2 * lane), bf16),
            ((rcv_half, 2 * lane), bf16),
            ((edges, lane), jnp.int32),
            ((edges, lane), jnp.int32),
            ((lane, 2 * lane), bf16),
            ((rcv_half, 2 * lane), f32),
        ],
        node,
        low,
        high,
        edge,
        snd,
        rcv,
        w_edge_first,
        row(b_edge_first),
        w_edge_second,
        row(b_edge_second),
        row(edge_gain),
        row(edge_shift),
    )
    back_low, back_high = neighbours(agg_low, agg_high)
    node_out, base, dagg, dagg_rim_low, dagg_rim_high, node_grads = call(
        node_kernel,
        [
            ((nodes, lane), bf16),
            ((nodes, lane), f32),
            ((nodes, lane), bf16),
            rim_shape,
            rim_shape,
            ((3 * lane + sum_rows, lane), bf16),
        ],
        [],
        node,
        agg,
        back_low,
        back_high,
        lists,
        w_node_first,
        row(b_node_first),
        w_node_second,
        row(b_node_second),
        row(node_gain),
        row(node_shift),
        node_cotangent[0],
    )
    dagg_low, dagg_high = neighbours(dagg_rim_low, dagg_rim_high)
    edge_grad, acc, grad_low, grad_high, grads = call(
        edge_backward_kernel,
        [
            ((edges, lane), bf16),
            ((nodes, lane), f32),
            rim_shape,
            rim_shape,
            ((7 * lane + sum_rows, lane), bf16),
        ],
        [
            ((rcv_half, 2 * lane), bf16),
            ((edges, lane), jnp.int32),
            ((edges, lane), jnp.int32),
            ((lane, 2 * lane), bf16),
            ((snd_half, 2 * lane), f32),
            ((rcv_half, 2 * lane), f32),
            ((2 * lane, lane), f32),
            ((8, lane), f32),
        ],
        z,
        edge_cotangent[0],
        edge,
        snd,
        rcv,
        node,
        low,
        high,
        dagg,
        dagg_low,
        dagg_high,
        base,
        w_edge_first,
        w_edge_second,
        row(b_edge_second),
        row(edge_gain),
        node_grads,
    )
    returned_low, returned_high = neighbours(grad_low, grad_high)
    (node_grad,) = call(
        node_grad_kernel, [((nodes, lane), bf16)], [], acc, returned_low, returned_high, lists
    )
    rounds = list(sum_rounds())
    for axis, pairs in rounds[:-1]:
        other = lax.ppermute(grads, axis, pairs)
        grads = (grads.astype(f32) + other.astype(f32)).astype(bf16)
    axis, pairs = rounds[-1]
    other = lax.ppermute(grads, axis, pairs)
    matrices = [3 * lane, lane, 2 * lane, lane]
    totals = call(
        finish_kernel,
        [((height, lane), f32) for height in matrices] + [((1, lane), f32)] * 8,
        [],
        grads,
        other,
    )
    flat = [total.reshape(lane) for total in totals[4:]]
    return (
        node_out[None],
        edge_out[None],
        node_grad[None],
        edge_grad[None],
        totals[0],
        flat[0],
        totals[1],
        flat[1],
        flat[2],
        flat[3],
        totals[2],
        flat[4],
        totals[3],
        flat[5],
        flat[6],
        flat[7],
    )


def solution(mesh):
    node_spec = P(("groups", "sample"), ("dom", "sub"), None)
    ids_spec = P(("dom", "sub"))
    return jax.shard_map(
        on_device,
        mesh=mesh,
        in_specs=(
            (node_spec, node_spec, ids_spec, ids_spec, P(("dom", "sub"), None, None))
            + (P(),) * 12
            + (node_spec, node_spec)
        ),
        out_specs=(
            (node_spec,) * 4
            + (P("groups", None), P("groups"), P("groups", None), P("groups"), P("groups"), P("groups"))
            * 2
        ),
        check_vma=False,
    )
```

time: 278 us -> 88.5 us (0.32)
  local copies, waits for them, and re-layouts: 68.7 us -> 12 us
  matrix products: 44.9 us -> 0 us
  other arithmetic: 34.2 us -> 0.19 us
  waiting for transfers between devices: 59.2 us -> 26.8 us
  blocking collectives: 30.2 us -> 0 us
  Pallas kernels: 0 us -> 22 us
  between operations: 15 us -> 0.83 us
  starting transfers between devices: 22.3 us -> 26 us
    psum x1 -> x0, waiting for transfers between devices: 58 us -> none  [on_device(): lax.psum((edge_terms[0], edge_terms[1], edge_terms[2], edge_terms[3], edg...]
    dot_general x30 -> x0, matrix products: 44.9 us -> none  [the longest x18 30.4 us: add_block(): lax.dot_general(one_hot, block_values, rows_dims, preferred_element_type=...]
    gather x9 -> x0, local copies, waits for them, and re-layouts: 36.2 us -> none  [the longest x1 11.5 us: on_device(): jnp.take(adjoint_ext, receivers, axis=0).astype(jnp.float32)]
    psum x1 -> x0, blocking collectives: 30.2 us -> none  [on_device(): lax.psum((edge_terms[0], edge_terms[1], edge_terms[2], edge_terms[3], edg...]
    ppermute x8 -> x12, waiting for transfers between devices: 1.14 us -> 26.8 us  [the longest x4 14.4 us: neighbours(): lax.ppermute(low, axis, backward)]
    pallas_call x0 -> x6, Pallas kernels: none -> 22 us  [call(): pl.pallas_call(kernel, out_shape=[jax.ShapeDtypeStruct(shape, dtype) for...]
    reduce_sum x7 -> x0, other arithmetic: 10.8 us -> none  [the longest x2 5.42 us: block_backward(): d_gain = jnp.sum(upstream * normed, axis=0)]
    dynamic_slice x18 -> x0, local copies, waits for them, and re-layouts: 8.76 us -> none  [segment_rows(): lax.scan(add_block, jnp.zeros((row_count, values.shape[1]), jnp.float32),...]
  transfers between devices with their start and end apart: 9 -> 12, of which waited for: 2 -> 7; matrix products, arithmetic and copies ran while one was open for 12% -> 0% of each run, Pallas kernels for 0% -> 1%
where the time goes in v1:
time: 88.5 us; the launch traced here: 87.9 us
  waiting for transfers between devices  26.8 us (30%)
  starting transfers between devices  26 us (29%)
  Pallas kernels  22 us (25%)
  local copies, waits for them, and re-layouts  12 us (14%)
    pallas_call x6, Pallas kernels, call(): pl.pallas_call(kernel, out_shape=[jax.ShapeDtypeStruct(shape, dtype) for...  22 us
    ppermute x4, waiting for transfers between devices, neighbours(): lax.ppermute(low, axis, backward)  14.4 us
    ppermute x4, waiting for transfers between devices, on_device(): other = lax.ppermute(grads, axis, pairs)  12.4 us
    ppermute x4, starting transfers between devices, neighbours(): lax.ppermute(high, axis, forward)  12.4 us
    unnamed x46, local copies, waits for them, and re-layouts  12 us
    ppermute x4, starting transfers between devices, neighbours(): lax.ppermute(low, axis, backward)  8.65 us
    ppermute x4, starting transfers between devices, on_device(): other = lax.ppermute(grads, axis, pairs)  5 us
  transfers between devices with their start and end apart: 12, of which 7 were waited for; matrix products, arithmetic and copies ran while one was open for 0% of the time, Pallas kernels for 1%

profile of v1, /device:TPU:1, one launch (start us, length us, event | category | flops | bytes accessed | tf_op | source)
XLA Modules:
  0.0 87.9 jit_solution(6085332553127018632)
XLA Ops:
  2.7 4.6 %collective-permute-start = (bf16[128,128]{1,0:T(8,128)(2,1)S(1)}, bf16[128,128]{1,0:T(8,128)(2,1)S(1)}, u32[]{:S(2)}, u32[]{:S(2)}) collective-permute-start(bf16[128,128]{1,0:T(8,128)(2,1)S(1)} %get-tuple-element.46), channel_id=1, source_target_pairs={{0,1},{1,4},{4,5},{5,8},{8,9},{9,12},{12,13},{2,3},{3,6},{6,7},{7,... | collective-permute-start | bytes 98312 | tf_op jit(solution)/shard_map/ppermute | solution.py:383
  7.3 1.9 %collective-permute-start.1 = (bf16[128,128]{1,0:T(8,128)(2,1)S(1)}, bf16[128,128]{1,0:T(8,128)(2,1)S(1)}, u32[]{:S(2)}, u32[]{:S(2)}) collective-permute-start(bf16[128,128]{1,0:T(8,128)(2,1)S(1)} %get-tuple-element.47), channel_id=1, source_target_pairs={{1,0},{4,1},{5,4},{8,5},{9,8},{12,9},{13,12},{3,2},{6,3},{7,6},{10... | collective-permute-start | bytes 98312 | tf_op jit(solution)/shard_map/ppermute | solution.py:383
  9.2 3.3 %collective-permute-done.1.high_ref = bf16[128,128]{1,0:T(8,128)(2,1)S(1)} collective-permute-done((bf16[128,128]{1,0:T(8,128)(2,1)S(1)}, bf16[128,128]{1,0:T(8,128)(2,1)S(1)}, u32[]{:S(2)}, u32[]{:S(2)}) %collective-permute-start.1) | collective-permute-done | bytes 32800 | tf_op jit(solution)/shard_map/ppermute | solution.py:383
  12.5 1.1 %copy-done.1 = bf16[1,3072,128]{2,1,0:T(8,128)(2,1)S(1)} copy-done((bf16[1,3072,128]{2,1,0:T(8,128)(2,1)S(1)}, bf16[1,3072,128]{2,1,0:T(8,128)(2,1)}, u32[]{:S(2)}) %copy-start.1) | copy-done | bytes 786456
  19.3 8.1 %shard_map.307 = (bf16[3072,128]{1,0:T(8,128)(2,1)}, f32[3072,128]{1,0:T(8,128)S(1)}, f32[1024,128]{1,0:T(8,128)S(1)}, bf16[128,128]{1,0:T(8,128)(2,1)S(1)}, bf16[128,128]{1,0:T(8,128)(2,1)S(1)}) custom-call(bf16[1024,128]{1,0:T(8,128)(2,1)S(1)} %bitcast.28, bf16[128,128]{1,0:T(8,128)(2,1)S(1)} %collective-permute-done.low_ref, ...), custom_call_target="tpu_custom_call" | custom-call | bytes 1271808 | tf_op jit(solution)/shard_map/pallas_call | solution.py:367
  27.5 1.9 %collective-permute-start.2 = (bf16[128,128]{1,0:T(8,128)(2,1)S(1)}, bf16[128,128]{1,0:T(8,128)(2,1)S(1)}, u32[]{:S(2)}, u32[]{:S(2)}) collective-permute-start(bf16[128,128]{1,0:T(8,128)(2,1)S(1)} %get-tuple-element.49), channel_id=1, source_target_pairs={{0,1},{1,4},{4,5},{5,8},{8,9},{9,12},{12,13},{2,3},{3,6},{6,7},{7,... | collective-permute-start | bytes 98312 | tf_op jit(solution)/shard_map/ppermute | solution.py:383
  29.4 2.4 %collective-permute-start.3 = (bf16[128,128]{1,0:T(8,128)(2,1)S(1)}, bf16[128,128]{1,0:T(8,128)(2,1)S(1)}, u32[]{:S(2)}, u32[]{:S(2)}) collective-permute-start(bf16[128,128]{1,0:T(8,128)(2,1)S(1)} %get-tuple-element.50), channel_id=1, source_target_pairs={{1,0},{4,1},{5,4},{8,5},{9,8},{12,9},{13,12},{3,2},{6,3},{7,6},{10... | collective-permute-start | bytes 98312 | tf_op jit(solution)/shard_map/ppermute | solution.py:383
  31.8 2.8 %collective-permute-done.3.high_ref = bf16[128,128]{1,0:T(8,128)(2,1)S(1)} collective-permute-done((bf16[128,128]{1,0:T(8,128)(2,1)S(1)}, bf16[128,128]{1,0:T(8,128)(2,1)S(1)}, u32[]{:S(2)}, u32[]{:S(2)}) %collective-permute-start.3) | collective-permute-done | bytes 32800 | tf_op jit(solution)/shard_map/ppermute | solution.py:383
  34.7 0.9 %copy-done.6 = bf16[1,1024,128]{2,1,0:T(8,128)(2,1)S(1)} copy-done((bf16[1,1024,128]{2,1,0:T(8,128)(2,1)S(1)}, bf16[1,1024,128]{2,1,0:T(8,128)(2,1)}, u32[]{:S(2)}) %copy-start.6) | copy-done | bytes 262168
  38.2 1.8 %shard_map.308 = (bf16[1024,128]{1,0:T(8,128)(2,1)}, f32[1024,128]{1,0:T(8,128)S(1)}, bf16[1024,128]{1,0:T(8,128)(2,1)S(1)}, bf16[128,128]{1,0:T(8,128)(2,1)S(1)...) custom-call(bf16[1024,128]{1,0:T(8,128)(2,1)S(1)} %bitcast.29, f32[1024,128]{1,0:T(8,128)S(1)} %get-tuple-element.48.agg_ref, ...), custom_call_target="tpu_custom_call" | custom-call | bytes 1215488 | tf_op jit(solution)/shard_map/pallas_call | solution.py:367
  40.0 1.9 %collective-permute-start.4 = (bf16[128,128]{1,0:T(8,128)(2,1)S(1)}, bf16[128,128]{1,0:T(8,128)(2,1)S(1)}, u32[]{:S(2)}, u32[]{:S(2)}) collective-permute-start(bf16[128,128]{1,0:T(8,128)(2,1)S(1)} %get-tuple-element.55), channel_id=1, source_target_pairs={{0,1},{1,4},{4,5},{5,8},{8,9},{9,12},{12,13},{2,3},{3,6},{6,7},{7,... | collective-permute-start | bytes 98312 | tf_op jit(solution)/shard_map/ppermute | solution.py:383
  41.9 2.4 %collective-permute-start.5 = (bf16[128,128]{1,0:T(8,128)(2,1)S(1)}, bf16[128,128]{1,0:T(8,128)(2,1)S(1)}, u32[]{:S(2)}, u32[]{:S(2)}) collective-permute-start(bf16[128,128]{1,0:T(8,128)(2,1)S(1)} %get-tuple-element.56), channel_id=1, source_target_pairs={{1,0},{4,1},{5,4},{8,5},{9,8},{12,9},{13,12},{3,2},{6,3},{7,6},{10... | collective-permute-start | bytes 98312 | tf_op jit(solution)/shard_map/ppermute | solution.py:383
  44.4 2.8 %collective-permute-done.5.dagg_high_ref = bf16[128,128]{1,0:T(8,128)(2,1)S(1)} collective-permute-done((bf16[128,128]{1,0:T(8,128)(2,1)S(1)}, bf16[128,128]{1,0:T(8,128)(2,1)S(1)}, u32[]{:S(2)}, u32[]{:S(2)}) %collective-permute-start.5) | collective-permute-done | bytes 32800 | tf_op jit(solution)/shard_map/ppermute | solution.py:383
  47.2 9.9 %shard_map.309 = (bf16[3072,128]{1,0:T(8,128)(2,1)}, f32[1024,128]{1,0:T(8,128)S(1)}, bf16[128,128]{1,0:T(8,128)(2,1)S(1)}, bf16[128,128]{1,0:T(8,128)(2,1)S(1)}, bf16[912,128]{1,0:T(8,128)(2,1)S(1)}) custom-call(f32[3072,128]{1,0:T(8,128)S(1)} %get-tuple-element.53.z_ref, bf16[3072,128]{1,0:T(8,128)(2,1)S(1)} %bitcast.33, bf16[3072,128]{1,0:T(8,128)(2,1)S(1)} %bitcast.32, ...), custom_call_target="tpu_custom_call" | custom-call | bytes 4584448 | tf_op jit(solution)/shard_map/pallas_call | solution.py:367
  57.1 1.5 %collective-permute-done.8 = bf16[912,128]{1,0:T(8,128)(2,1)S(1)} collective-permute-done((bf16[912,128]{1,0:T(8,128)(2,1)S(1)}, bf16[912,128]{1,0:T(8,128)(2,1)S(1)}, u32[]{:S(2)}, u32[]{:S(2)}) %collective-permute-start.8) | collective-permute-done | bytes 233504 | tf_op jit(solution)/shard_map/ppermute | solution.py:524
  58.6 1.3 %collective-permute-start.9 = (bf16[912,128]{1,0:T(8,128)(2,1)S(1)}, bf16[912,128]{1,0:T(8,128)(2,1)S(1)}, u32[]{:S(2)}, u32[]{:S(2)}) collective-permute-start(bf16[912,128]{1,0:T(8,128)(2,1)S(1)} %add_convert_fusion.2), channel_id=1, source_target_pairs={{0,2},{2,0},{1,3},{3,1},{4,6},{6,4},{5,7},{7,5},{8,10},{10,8},{9,1... | collective-permute-start | bytes 700424 | tf_op jit(solution)/shard_map/ppermute | solution.py:524
  59.9 6.0 %collective-permute-done.9 = bf16[912,128]{1,0:T(8,128)(2,1)S(1)} collective-permute-done((bf16[912,128]{1,0:T(8,128)(2,1)S(1)}, bf16[912,128]{1,0:T(8,128)(2,1)S(1)}, u32[]{:S(2)}, u32[]{:S(2)}) %collective-permute-start.9) | collective-permute-done | bytes 233504 | tf_op jit(solution)/shard_map/ppermute | solution.py:524
  65.9 1.4 %collective-permute-start.10 = (bf16[912,128]{1,0:T(8,128)(2,1)S(1)}, bf16[912,128]{1,0:T(8,128)(2,1)S(1)}, u32[]{:S(2)}, u32[]{:S(2)}) collective-permute-start(bf16[912,128]{1,0:T(8,128)(2,1)S(1)} %add_convert_fusion.1), channel_id=1, source_target_pairs={{0,4},{4,0},{8,12},{12,8},{1,5},{5,1},{9,13},{13,9},{2,6},{6,2},{1... | collective-permute-start | bytes 700424 | tf_op jit(solution)/shard_map/ppermute | solution.py:524
  67.3 5.0 %collective-permute-done.10 = bf16[912,128]{1,0:T(8,128)(2,1)S(1)} collective-permute-done((bf16[912,128]{1,0:T(8,128)(2,1)S(1)}, bf16[912,128]{1,0:T(8,128)(2,1)S(1)}, u32[]{:S(2)}, u32[]{:S(2)}) %collective-permute-start.10) | collective-permute-done | bytes 233504 | tf_op jit(solution)/shard_map/ppermute | solution.py:524
  72.3 2.4 %collective-permute-start.11 = (bf16[912,128]{1,0:T(8,128)(2,1)S(1)}, bf16[912,128]{1,0:T(8,128)(2,1)S(1)}, u32[]{:S(2)}, u32[]{:S(2)}) collective-permute-start(bf16[912,128]{1,0:T(8,128)(2,1)S(1)} %add_convert_fusion.own_ref), channel_id=1, source_target_pairs={{0,8},{4,12},{8,0},{12,4},{1,9},{5,13},{9,1},{13,5},{2,10},{6,14},... | collective-permute-start | bytes 700424 | tf_op jit(solution)/shard_map/ppermute | solution.py:527
  74.7 3.9 %collective-permute-start.6 = (bf16[128,128]{1,0:T(8,128)(2,1)S(1)}, bf16[128,128]{1,0:T(8,128)(2,1)S(1)}, u32[]{:S(2)}, u32[]{:S(2)}) collective-permute-start(bf16[128,128]{1,0:T(8,128)(2,1)S(1)} %get-tuple-element.60), channel_id=1, source_target_pairs={{0,1},{1,4},{4,5},{5,8},{8,9},{9,12},{12,13},{2,3},{3,6},{6,7},{7,... | collective-permute-start | bytes 98312 | tf_op jit(solution)/shard_map/ppermute | solution.py:383
  78.6 1.9 %collective-permute-start.7 = (bf16[128,128]{1,0:T(8,128)(2,1)S(1)}, bf16[128,128]{1,0:T(8,128)(2,1)S(1)}, u32[]{:S(2)}, u32[]{:S(2)}) collective-permute-start(bf16[128,128]{1,0:T(8,128)(2,1)S(1)} %get-tuple-element.61), channel_id=1, source_target_pairs={{1,0},{4,1},{5,4},{8,5},{9,8},{12,9},{13,12},{3,2},{6,3},{7,6},{10... | collective-permute-start | bytes 98312 | tf_op jit(solution)/shard_map/ppermute | solution.py:383
  80.5 5.5 %collective-permute-done.7.high_ref = bf16[128,128]{1,0:T(8,128)(2,1)S(1)} collective-permute-done((bf16[128,128]{1,0:T(8,128)(2,1)S(1)}, bf16[128,128]{1,0:T(8,128)(2,1)S(1)}, u32[]{:S(2)}, u32[]{:S(2)}) %collective-permute-start.7) | collective-permute-done | bytes 32800 | tf_op jit(solution)/shard_map/ppermute | solution.py:383
  86.0 1.0 %shard_map.310 = bf16[1024,128]{1,0:T(8,128)(2,1)} custom-call(f32[1024,128]{1,0:T(8,128)S(1)} %get-tuple-element.59.acc_ref, bf16[128,128]{1,0:T(8,128)(2,1)S(1)} %collective-permute-done.6.low_ref, bf16[128,128]{1,0:T(8,128)(2,1)S(1)} %collective-permute-done.7.high_ref, s32[2,128]{1,0:T(2,128)S(1)} %bitcast.41), custom_call_target="tpu_custom_call" | custom-call | bytes 590848 | tf_op jit(solution)/shard_map/pallas_call | solution.py:367
  (55 shorter events, 11.4 us)
Async XLA Ops:
  0.6 46.5 %copy-start.15 = (f32[128]{0:T(128)S(1)}, f32[128]{0:T(128)}, u32[]{:S(2)}) copy-start(f32[128]{0:T(128)} %param.27) | copy-start | bytes 1540
  0.7 1.0 %copy-start = (bf16[1,1024,128]{2,1,0:T(8,128)(2,1)S(1)}, bf16[1,1024,128]{2,1,0:T(8,128)(2,1)}, u32[]{:S(2)}) copy-start(bf16[1,1024,128]{2,1,0:T(8,128)(2,1)} %param.19) | copy-start | bytes 786436
  2.3 32.4 %copy-start.9 = (bf16[256,128]{1,0:T(8,128)(2,1)S(1)}, bf16[256,128]{1,0:T(8,128)(2,1)}, u32[]{:S(2)}) copy-start(bf16[256,128]{1,0:T(8,128)(2,1)} %w1_ref.4) | copy-start | bytes 196612
  2.3 32.4 %copy-start.12 = (bf16[128,128]{1,0:T(8,128)(2,1)S(1)}, bf16[128,128]{1,0:T(8,128)(2,1)}, u32[]{:S(2)}) copy-start(bf16[128,128]{1,0:T(8,128)(2,1)} %w2_ref.4) | copy-start | bytes 98308
  2.3 44.9 %copy-start.5 = (bf16[384,128]{1,0:T(8,128)(2,1)S(1)}, bf16[384,128]{1,0:T(8,128)(2,1)}, u32[]{:S(2)}) copy-start(bf16[384,128]{1,0:T(8,128)(2,1)} %w1_ref.5) | copy-start | bytes 294916
  2.3 44.9 %copy-start.8 = (bf16[128,128]{1,0:T(8,128)(2,1)S(1)}, bf16[128,128]{1,0:T(8,128)(2,1)}, u32[]{:S(2)}) copy-start(bf16[128,128]{1,0:T(8,128)(2,1)} %w2_ref.5) | copy-start | bytes 98308
  2.7 6.5 %collective-permute-start = (bf16[128,128]{1,0:T(8,128)(2,1)S(1)}, bf16[128,128]{1,0:T(8,128)(2,1)S(1)}, u32[]{:S(2)}, u32[]{:S(2)}) collective-permute-start(bf16[128,128]{1,0:T(8,128)(2,1)S(1)} %get-tuple-element.46), channel_id=1, source_target_pairs={{0,1},{1,4},{4,5},{5,8},{8,9},{9,12},{12,13},{2,3},{3,6},{6,7},{7,... | collective-permute-start | bytes 98312 | tf_op jit(solution)/shard_map/ppermute | solution.py:383
  7.3 5.2 %collective-permute-start.1 = (bf16[128,128]{1,0:T(8,128)(2,1)S(1)}, bf16[128,128]{1,0:T(8,128)(2,1)S(1)}, u32[]{:S(2)}, u32[]{:S(2)}) collective-permute-start(bf16[128,128]{1,0:T(8,128)(2,1)S(1)} %get-tuple-element.47), channel_id=1, source_target_pairs={{1,0},{4,1},{5,4},{8,5},{9,8},{12,9},{13,12},{3,2},{6,3},{7,6},{10... | collective-permute-start | bytes 98312 | tf_op jit(solution)/shard_map/ppermute | solution.py:383
  12.5 1.1 %copy-start.1 = (bf16[1,3072,128]{2,1,0:T(8,128)(2,1)S(1)}, bf16[1,3072,128]{2,1,0:T(8,128)(2,1)}, u32[]{:S(2)}) copy-start(bf16[1,3072,128]{2,1,0:T(8,128)(2,1)} %param.20) | copy-start | bytes 2359300
  13.7 0.9 %copy-start.4 = (bf16[384,128]{1,0:T(8,128)(2,1)S(1)}, bf16[384,128]{1,0:T(8,128)(2,1)}, u32[]{:S(2)}) copy-start(bf16[384,128]{1,0:T(8,128)(2,1)} %w1_ref.5) | copy-start | bytes 294916
  14.5 0.8 copy-start.7
  19.3 27.8 %copy-start.2 = (bf16[1,3072,128]{2,1,0:T(8,128)(2,1)S(1)}, bf16[1,3072,128]{2,1,0:T(8,128)(2,1)}, u32[]{:S(2)}) copy-start(bf16[1,3072,128]{2,1,0:T(8,128)(2,1)} %param.20) | copy-start | bytes 2359300
  19.3 27.9 %copy-start.3 = (bf16[1,3072,128]{2,1,0:T(8,128)(2,1)S(1)}, bf16[1,3072,128]{2,1,0:T(8,128)(2,1)}, u32[]{:S(2)}) copy-start(bf16[1,3072,128]{2,1,0:T(8,128)(2,1)} %param.37) | copy-start | bytes 2359300
  27.5 4.3 %collective-permute-start.2 = (bf16[128,128]{1,0:T(8,128)(2,1)S(1)}, bf16[128,128]{1,0:T(8,128)(2,1)S(1)}, u32[]{:S(2)}, u32[]{:S(2)}) collective-permute-start(bf16[128,128]{1,0:T(8,128)(2,1)S(1)} %get-tuple-element.49), channel_id=1, source_target_pairs={{0,1},{1,4},{4,5},{5,8},{8,9},{9,12},{12,13},{2,3},{3,6},{6,7},{7,... | collective-permute-start | bytes 98312 | tf_op jit(solution)/shard_map/ppermute | solution.py:383
  29.4 5.2 %collective-permute-start.3 = (bf16[128,128]{1,0:T(8,128)(2,1)S(1)}, bf16[128,128]{1,0:T(8,128)(2,1)S(1)}, u32[]{:S(2)}, u32[]{:S(2)}) collective-permute-start(bf16[128,128]{1,0:T(8,128)(2,1)S(1)} %get-tuple-element.50), channel_id=1, source_target_pairs={{1,0},{4,1},{5,4},{8,5},{9,8},{12,9},{13,12},{3,2},{6,3},{7,6},{10... | collective-permute-start | bytes 98312 | tf_op jit(solution)/shard_map/ppermute | solution.py:383
  34.7 1.0 %copy-start.6 = (bf16[1,1024,128]{2,1,0:T(8,128)(2,1)S(1)}, bf16[1,1024,128]{2,1,0:T(8,128)(2,1)}, u32[]{:S(2)}) copy-start(bf16[1,1024,128]{2,1,0:T(8,128)(2,1)} %param.36) | copy-start | bytes 786436
  40.0 4.3 %collective-permute-start.4 = (bf16[128,128]{1,0:T(8,128)(2,1)S(1)}, bf16[128,128]{1,0:T(8,128)(2,1)S(1)}, u32[]{:S(2)}, u32[]{:S(2)}) collective-permute-start(bf16[128,128]{1,0:T(8,128)(2,1)S(1)} %get-tuple-element.55), channel_id=1, source_target_pairs={{0,1},{1,4},{4,5},{5,8},{8,9},{9,12},{12,13},{2,3},{3,6},{6,7},{7,... | collective-permute-start | bytes 98312 | tf_op jit(solution)/shard_map/ppermute | solution.py:383
  41.9 5.2 %collective-permute-start.5 = (bf16[128,128]{1,0:T(8,128)(2,1)S(1)}, bf16[128,128]{1,0:T(8,128)(2,1)S(1)}, u32[]{:S(2)}, u32[]{:S(2)}) collective-permute-start(bf16[128,128]{1,0:T(8,128)(2,1)S(1)} %get-tuple-element.56), channel_id=1, source_target_pairs={{1,0},{4,1},{5,4},{8,5},{9,8},{12,9},{13,12},{3,2},{6,3},{7,6},{10... | collective-permute-start | bytes 98312 | tf_op jit(solution)/shard_map/ppermute | solution.py:383
  57.1 1.5 %collective-permute-start.8 = (bf16[912,128]{1,0:T(8,128)(2,1)S(1)}, bf16[912,128]{1,0:T(8,128)(2,1)S(1)}, u32[]{:S(2)}, u32[]{:S(2)}) collective-permute-start(bf16[912,128]{1,0:T(8,128)(2,1)S(1)} %get-tuple-element.63), channel_id=1, source_target_pairs={{0,1},{1,0},{2,3},{3,2},{4,5},{5,4},{6,7},{7,6},{8,9},{9,8},{10,11... | collective-permute-start | bytes 700424 | tf_op jit(solution)/shard_map/ppermute | solution.py:524
  58.6 7.2 %collective-permute-start.9 = (bf16[912,128]{1,0:T(8,128)(2,1)S(1)}, bf16[912,128]{1,0:T(8,128)(2,1)S(1)}, u32[]{:S(2)}, u32[]{:S(2)}) collective-permute-start(bf16[912,128]{1,0:T(8,128)(2,1)S(1)} %add_convert_fusion.2), channel_id=1, source_target_pairs={{0,2},{2,0},{1,3},{3,1},{4,6},{6,4},{5,7},{7,5},{8,10},{10,8},{9,1... | collective-permute-start | bytes 700424 | tf_op jit(solution)/shard_map/ppermute | solution.py:524
  65.9 6.3 %collective-permute-start.10 = (bf16[912,128]{1,0:T(8,128)(2,1)S(1)}, bf16[912,128]{1,0:T(8,128)(2,1)S(1)}, u32[]{:S(2)}, u32[]{:S(2)}) collective-permute-start(bf16[912,128]{1,0:T(8,128)(2,1)S(1)} %add_convert_fusion.1), channel_id=1, source_target_pairs={{0,4},{4,0},{8,12},{12,8},{1,5},{5,1},{9,13},{13,9},{2,6},{6,2},{1... | collective-permute-start | bytes 700424 | tf_op jit(solution)/shard_map/ppermute | solution.py:524
  72.3 14.7 %collective-permute-start.11 = (bf16[912,128]{1,0:T(8,128)(2,1)S(1)}, bf16[912,128]{1,0:T(8,128)(2,1)S(1)}, u32[]{:S(2)}, u32[]{:S(2)}) collective-permute-start(bf16[912,128]{1,0:T(8,128)(2,1)S(1)} %add_convert_fusion.own_ref), channel_id=1, source_target_pairs={{0,8},{4,12},{8,0},{12,4},{1,9},{5,13},{9,1},{13,5},{2,10},{6,14},... | collective-permute-start | bytes 700424 | tf_op jit(solution)/shard_map/ppermute | solution.py:527
  74.7 5.9 %collective-permute-start.6 = (bf16[128,128]{1,0:T(8,128)(2,1)S(1)}, bf16[128,128]{1,0:T(8,128)(2,1)S(1)}, u32[]{:S(2)}, u32[]{:S(2)}) collective-permute-start(bf16[128,128]{1,0:T(8,128)(2,1)S(1)} %get-tuple-element.60), channel_id=1, source_target_pairs={{0,1},{1,4},{4,5},{5,8},{8,9},{9,12},{12,13},{2,3},{3,6},{6,7},{7,... | collective-permute-start | bytes 98312 | tf_op jit(solution)/shard_map/ppermute | solution.py:383
  78.6 7.4 %collective-permute-start.7 = (bf16[128,128]{1,0:T(8,128)(2,1)S(1)}, bf16[128,128]{1,0:T(8,128)(2,1)S(1)}, u32[]{:S(2)}, u32[]{:S(2)}) collective-permute-start(bf16[128,128]{1,0:T(8,128)(2,1)S(1)} %get-tuple-element.61), channel_id=1, source_target_pairs={{1,0},{4,1},{5,4},{8,5},{9,8},{12,9},{13,12},{3,2},{6,3},{7,6},{10... | collective-permute-start | bytes 98312 | tf_op jit(solution)/shard_map/ppermute | solution.py:383
  (11 other events, 7.3 us)

commit v2 on v1

v2 whole, which is shorter than its diff:
```python
import functools
import math

import jax
import jax.numpy as jnp
from jax import lax
from jax.experimental import pallas as pl
from jax.experimental.pallas import tpu as pltpu
from jax.sharding import PartitionSpec as P

epsilon = 1e-05
rows_dims = (((0,), (0,)), ((), ()))
back_dims = (((1,), (1,)), ((), ()))
f32 = jnp.float32
bf16 = jnp.bfloat16
lane = 128
edge_tile = 512
vmem_limit = 32 * 1024 * 1024
sum_rows = 16
chain = ("dom", "sub")


def dot(left, right):
    return jnp.dot(left, right, preferred_element_type=f32)


def dot_rows(left, right):
    return lax.dot_general(left, right, rows_dims, preferred_element_type=f32)


def dot_back(left, right):
    return lax.dot_general(left, right, back_dims, preferred_element_type=f32)


def column_of(row):
    return jnp.broadcast_to(row, (lane, lane)).T


def hot_columns(ids, width):
    targets = lax.broadcasted_iota(jnp.int32, ids.shape, 1)
    parts = [
        jnp.where(ids == targets + at, 1.0, 0.0).astype(bf16) for at in range(0, width, lane)
    ]
    return jnp.concatenate(parts, axis=1)


def hot_rows(row, height):
    targets = lax.broadcasted_iota(jnp.int32, (height, lane), 0)
    return jnp.where(row == targets, 1.0, 0.0).astype(bf16)


def fold(ids, half):
    upper = ids >= half
    return upper, jnp.where(upper, ids - half, ids)


def side_by_side(rows):
    half = rows.shape[0] // 2
    return jnp.concatenate([rows[:half], rows[half:]], axis=1)


def pick(ids, table):
    half = table.shape[0]
    upper, low = fold(ids, half)
    both = dot(hot_columns(low, half), table)
    return jnp.where(upper, both[:, lane:], both[:, :lane])


def spread(ids_ref, first, count, half, ids, values):
    upper, unused = fold(ids, half)
    paired = jnp.concatenate(
        [jnp.where(upper, 0.0, values).astype(bf16), jnp.where(upper, values, 0.0).astype(bf16)],
        axis=1,
    )
    parts = []
    for k in range(count):
        row = ids_ref[pl.ds(first + k, 1), :]
        unused, low = fold(row, half)
        parts.append(hot_rows(low, half))
    return dot(jnp.concatenate(parts, axis=1), paired)


def sigmoid(z):
    return 0.5 * jnp.tanh(0.5 * z) + 0.5


def vector(vectors_ref, k):
    return vectors_ref[k : k + 1, :]


def centred_second(w, b):
    w = w.astype(f32)
    w = w - jnp.mean(w, axis=1, keepdims=True)
    high = w.astype(bf16)
    low = (w - high.astype(f32)).astype(bf16)
    return jnp.concatenate([high, low], axis=1), b - jnp.mean(b, axis=1, keepdims=True)


def normed_of(act, w_pair, b_centred):
    both = dot(act, w_pair)
    center = both[:, :lane] + both[:, lane:] + b_centred
    scale_inv = lax.rsqrt(jnp.mean(center * center, axis=1, keepdims=True) + epsilon)
    return center * scale_inv, scale_inv


def back_norm(upstream, normed, scale_inv, gain):
    d_normed = upstream * gain
    return scale_inv * (
        d_normed
        - jnp.mean(d_normed, axis=1, keepdims=True)
        - normed * jnp.mean(d_normed * normed, axis=1, keepdims=True)
    )


def column_sum(values):
    return jnp.sum(values, axis=0, keepdims=True)


def parity_of_place():
    return lax.axis_index(chain) % 2


def rim_kernel(node_ref, ids_ref, near_ref, far_ref):
    parity = parity_of_place()
    node = node_ref[...]
    first = ids_ref.shape[0] - 2
    for side, out_ref in ((1 - parity, near_ref), (parity, far_ref)):
        hot = hot_columns(column_of(ids_ref[pl.ds(first + side, 1), :]), node.shape[0])
        out_ref[...] = dot(hot, node).astype(bf16)


def prepare_kernel(
    ids_ref,
    node_ref,
    weights_ref,
    edge_ref,
    edge_cot_ref,
    node_cot_ref,
    edge_out,
    edge_cot_out,
    node_cot_out,
    snd_column,
    rcv_column,
    snd_table,
    rcv_local,
    sems,
):
    copies = [
        pltpu.make_async_copy(source, target, sems.at[k])
        for k, (source, target) in enumerate(
            ((edge_ref, edge_out), (edge_cot_ref, edge_cot_out), (node_cot_ref, node_cot_out))
        )
    ]
    for copy in copies:
        copy.start()
    chunks = snd_column.shape[0] // lane
    for k in range(chunks):
        at = slice(k * lane, (k + 1) * lane)
        snd_column[at, :] = column_of(ids_ref[k : k + 1, :])
        rcv_column[at, :] = column_of(ids_ref[chunks + k : chunks + k + 1, :])
    node = node_ref[...]
    snd_table[...] = side_by_side(dot(node, weights_ref[lane : 2 * lane]).astype(bf16))
    rcv_local[...] = dot(node, weights_ref[2 * lane : 3 * lane]).astype(bf16)
    for copy in copies:
        copy.wait()


def edge_forward_kernel(
    near_ref,
    far_ref,
    edge_ref,
    ids_ref,
    weights_ref,
    vectors_ref,
    snd_column,
    rcv_column,
    snd_table,
    rcv_local,
    out_ref,
    z_ref,
    agg_ref,
    agg_near_ref,
    agg_far_ref,
    halo,
    rcv_table,
    w2_pair,
    total,
):
    nodes = rcv_local.shape[0]
    rim = near_ref.shape[0]
    half = rcv_table.shape[0]
    parity = parity_of_place()
    near_at = pl.multiple_of((1 - parity) * rim, rim)
    far_at = pl.multiple_of(parity * rim, rim)
    w1_edge = weights_ref[:lane]
    w1_rcv = weights_ref[2 * lane : 3 * lane]
    b1, gain, shift = vector(vectors_ref, 0), vector(vectors_ref, 2), vector(vectors_ref, 3)
    halo[pl.ds(near_at, rim), :] = dot(near_ref[...], w1_rcv).astype(bf16)
    halo[pl.ds(far_at, rim), :] = dot(far_ref[...], w1_rcv).astype(bf16)
    rcv_table[:, :lane] = rcv_local[:half, :]
    rcv_table[: nodes - half, lane:] = rcv_local[half:, :]
    rcv_table[nodes - half :, lane:] = halo[...]
    pair, b2 = centred_second(weights_ref[3 * lane : 4 * lane], vector(vectors_ref, 1))
    w2_pair[...] = pair
    total[...] = jnp.zeros_like(total)

    def tile(i, carry):
        rows = pl.ds(pl.multiple_of(i * edge_tile, edge_tile), edge_tile)
        x = edge_ref[rows, :]
        rcv = rcv_column[rows, :]
        z = dot(x, w1_edge) + b1
        z = z + pick(snd_column[rows, :], snd_table[...])
        z = z + pick(rcv, rcv_table[...])
        z_ref[rows, :] = z
        act = (z * sigmoid(z)).astype(bf16)
        normed, unused = normed_of(act, w2_pair[...], b2)
        update = normed * gain + shift
        out_ref[rows, :] = (x.astype(f32) + update).astype(bf16)
        first = (rcv_column.shape[0] + i * edge_tile) // lane
        total[...] += spread(ids_ref, first, edge_tile // lane, half, rcv, update)
        return carry

    lax.fori_loop(0, edge_ref.shape[0] // edge_tile, tile, 0)
    agg_ref[:half, :] = total[:, :lane]
    agg_ref[half:, :] = total[: nodes - half, lane:]
    agg_near_ref[...] = total[pl.ds(nodes - half + near_at, rim), lane:].astype(bf16)
    agg_far_ref[...] = total[pl.ds(nodes - half + far_at, rim), lane:].astype(bf16)


def hot_lists(ids_ref, nodes):
    parity = parity_of_place()
    first = ids_ref.shape[0] - 2
    near = ids_ref[pl.ds(first + 1 - parity, 1), :]
    far = ids_ref[pl.ds(first + parity, 1), :]
    return jnp.concatenate([hot_rows(near, nodes), hot_rows(far, nodes)], axis=1)


def node_kernel(
    node_ref,
    agg_ref,
    near_ref,
    far_ref,
    ids_ref,
    weights_ref,
    vectors_ref,
    cot_ref,
    out_ref,
    base_ref,
    dagg_ref,
    rim_near_ref,
    rim_far_ref,
    grads_ref,
):
    nodes = node_ref.shape[0]
    node = node_ref[...]
    returned = jnp.concatenate([near_ref[...], far_ref[...]], axis=0)
    agg = (agg_ref[...] + dot(hot_lists(ids_ref, nodes), returned)).astype(bf16)
    x = jnp.concatenate([node, agg], axis=1)
    w1 = weights_ref[4 * lane : 6 * lane]
    w2 = weights_ref[6 * lane :]
    z = dot(x, w1) + vector(vectors_ref, 4)
    sig = sigmoid(z)
    act = (z * sig).astype(bf16)
    pair, b2 = centred_second(w2, vector(vectors_ref, 5))
    normed, scale_inv = normed_of(act, pair, b2)
    gain = vector(vectors_ref, 6)
    out_ref[...] = (node.astype(f32) + normed * gain + vector(vectors_ref, 7)).astype(bf16)
    upstream = cot_ref[...].astype(f32)
    dz2 = back_norm(upstream, normed, scale_inv, gain)
    dz2b = dz2.astype(bf16)
    da = dot_back(dz2b, w2)
    dz1 = da * sig * (1.0 + z * (1.0 - sig))
    dz1b = dz1.astype(bf16)
    dx = dot_back(dz1b, w1)
    base_ref[...] = upstream + dx[:, :lane]
    dagg = dx[:, lane:].astype(bf16)
    dagg_ref[...] = dagg
    parity = parity_of_place()
    first = ids_ref.shape[0] - 2
    for side, rim_ref in ((1 - parity, rim_near_ref), (parity, rim_far_ref)):
        picked = hot_columns(column_of(ids_ref[pl.ds(first + side, 1), :]), nodes)
        rim_ref[...] = dot(picked, dagg).astype(bf16)
    first = 2 * lane
    second = first + lane
    grads_ref[:first, :] = dot_rows(x, dz1b).astype(bf16)
    grads_ref[first:second, :] = dot_rows(act, dz2b).astype(bf16)
    sums = [column_sum(dz1), column_sum(dz2), column_sum(upstream * normed), column_sum(upstream)]
    sums.append(jnp.zeros((sum_rows - len(sums), lane), f32))
    grads_ref[second:, :] = jnp.concatenate(sums, axis=0).astype(bf16)


def edge_backward_kernel(
    z_ref,
    cot_ref,
    edge_ref,
    ids_ref,
    node_ref,
    near_ref,
    far_ref,
    dagg_ref,
    dagg_near_ref,
    dagg_far_ref,
    base_ref,
    weights_ref,
    vectors_ref,
    node_grads_ref,
    snd_column,
    rcv_column,
    grad_ref,
    acc_ref,
    back_near_ref,
    back_far_ref,
    grads_ref,
    halo,
    table,
    w2_pair,
    snd_total,
    rcv_total,
    squares,
    sums,
):
    nodes = node_ref.shape[0]
    rim = near_ref.shape[0]
    snd_half = snd_total.shape[0]
    rcv_half = rcv_total.shape[0]
    parity = parity_of_place()
    near_at = pl.multiple_of((1 - parity) * rim, rim)
    far_at = pl.multiple_of(parity * rim, rim)
    w1_edge = weights_ref[:lane]
    w2 = weights_ref[3 * lane : 4 * lane]
    gain = vector(vectors_ref, 2)
    table[:, :lane] = dagg_ref[:rcv_half, :]
    table[: nodes - rcv_half, lane:] = dagg_ref[rcv_half:, :]
    table[pl.ds(nodes - rcv_half + near_at, rim), lane:] = dagg_near_ref[...]
    table[pl.ds(nodes - rcv_half + far_at, rim), lane:] = dagg_far_ref[...]
    halo[pl.ds(near_at, rim), :] = near_ref[...]
    halo[pl.ds(far_at, rim), :] = far_ref[...]
    pair, b2 = centred_second(w2, vector(vectors_ref, 1))
    w2_pair[...] = pair
    snd_total[...] = jnp.zeros_like(snd_total)
    rcv_total[...] = jnp.zeros_like(rcv_total)
    squares[...] = jnp.zeros_like(squares)
    sums[...] = jnp.zeros_like(sums)

    def tile(i, carry):
        rows = pl.ds(pl.multiple_of(i * edge_tile, edge_tile), edge_tile)
        chunk = edge_tile // lane
        rcv = rcv_column[rows, :]
        snd = snd_column[rows, :]
        x = edge_ref[rows, :]
        z = z_ref[rows, :]
        cot = cot_ref[rows, :].astype(f32)
        upstream = cot + pick(rcv, table[...])
        sig = sigmoid(z)
        act = (z * sig).astype(bf16)
        normed, scale_inv = normed_of(act, w2_pair[...], b2)
        dz2 = back_norm(upstream, normed, scale_inv, gain)
        dz2b = dz2.astype(bf16)
        da = dot_back(dz2b, w2)
        dz1 = da * sig * (1.0 + z * (1.0 - sig))
        dz1b = dz1.astype(bf16)
        grad_ref[rows, :] = (cot + dot_back(dz1b, w1_edge)).astype(bf16)
        squares[:lane, :] += dot_rows(x, dz1b)
        squares[lane:, :] += dot_rows(act, dz2b)
        sums[0:1, :] += column_sum(dz1)
        sums[1:2, :] += column_sum(dz2)
        sums[2:3, :] += column_sum(upstream * normed)
        sums[3:4, :] += column_sum(upstream)
        first = rcv_column.shape[0] // lane + i * chunk
        snd_total[...] += spread(ids_ref, i * chunk, chunk, snd_half, snd, dz1)
        rcv_total[...] += spread(ids_ref, first, chunk, rcv_half, rcv, dz1)
        return carry

    lax.fori_loop(0, edge_ref.shape[0] // edge_tile, tile, 0)
    snd_sum = jnp.concatenate([snd_total[:, :lane], snd_total[:, lane:]], axis=0).astype(bf16)
    rcv_sum = jnp.concatenate([rcv_total[:, :lane], rcv_total[:, lane:]], axis=0).astype(bf16)
    w1_snd = weights_ref[lane : 2 * lane]
    w1_rcv = weights_ref[2 * lane : 3 * lane]
    acc_ref[...] = base_ref[...] + dot_back(snd_sum, w1_snd) + dot_back(rcv_sum[:nodes], w1_rcv)
    for at, back_ref in ((near_at, back_near_ref), (far_at, back_far_ref)):
        returned = rcv_total[pl.ds(nodes - rcv_half + at, rim), lane:].astype(bf16)
        back_ref[...] = dot_back(returned, w1_rcv).astype(bf16)
    extended = jnp.concatenate([node_ref[...], halo[...]], axis=0)
    grads_ref[:lane, :] = squares[:lane, :].astype(bf16)
    grads_ref[lane : 2 * lane, :] = dot_rows(node_ref[...], snd_sum).astype(bf16)
    grads_ref[2 * lane : 3 * lane, :] = dot_rows(extended, rcv_sum).astype(bf16)
    grads_ref[3 * lane : 4 * lane, :] = squares[lane:, :].astype(bf16)
    node_rows = node_grads_ref.shape[0] - sum_rows
    grads_ref[4 * lane : 4 * lane + node_rows, :] = node_grads_ref[:node_rows, :]
    node_sums = node_grads_ref[node_rows:, :].astype(f32)
    last = 4 * lane + node_rows
    grads_ref[last : last + sum_rows, :] = jnp.concatenate(
        [sums[0:4, :], node_sums[0:4, :], jnp.zeros((sum_rows - 8, lane), f32)], axis=0
    ).astype(bf16)
    if last + sum_rows < grads_ref.shape[0]:
        grads_ref[last + sum_rows :, :] = jnp.zeros(
            (grads_ref.shape[0] - last - sum_rows, lane), bf16
        )


def node_grad_kernel(acc_ref, near_ref, far_ref, ids_ref, out_ref):
    returned = jnp.concatenate([near_ref[...], far_ref[...]], axis=0)
    hot = hot_lists(ids_ref, acc_ref.shape[0])
    out_ref[...] = (acc_ref[...] + dot(hot, returned)).astype(bf16)


def share_kernel(parts_ref, out_ref):
    count = parts_ref.shape[0]
    total = parts_ref[0].astype(f32)
    for k in range(1, count):
        total = total + parts_ref[k].astype(f32)
    total = total.astype(bf16)
    for k in range(count):
        out_ref[k] = total


def finish_kernel(total_ref, *out_refs):
    at = 0
    for out_ref in out_refs[:4]:
        out_ref[...] = total_ref[at : at + out_ref.shape[0], :].astype(f32)
        at += out_ref.shape[0]
    last = total_ref[at : at + sum_rows, :].astype(f32)
    for k, out_ref in enumerate(out_refs[4:]):
        out_ref[...] = last[k : k + 1]


def call(kernel, outs, scratch, *operands, anywhere=0, sems=0):
    moved = sum(x.size * x.dtype.itemsize for x in operands)
    inside = [pl.BlockSpec(memory_space=pltpu.VMEM)] * (len(operands) - anywhere)
    outside = [pl.BlockSpec(memory_space=pl.ANY)] * anywhere
    scratch_shapes = [pltpu.VMEM(shape, dtype) for shape, dtype in scratch]
    if sems:
        scratch_shapes.append(pltpu.SemaphoreType.DMA((sems,)))
    return pl.pallas_call(
        kernel,
        out_shape=[jax.ShapeDtypeStruct(shape, dtype) for shape, dtype in outs],
        in_specs=inside + outside,
        out_specs=[pl.BlockSpec(memory_space=pltpu.VMEM)] * len(outs),
        scratch_shapes=scratch_shapes,
        compiler_params=pltpu.CompilerParams(vmem_limit_bytes=vmem_limit),
        cost_estimate=pl.CostEstimate(flops=0, bytes_accessed=moved, transcendentals=0),
    )(*operands)


def swap(near, far):
    count = lax.axis_size("dom") * lax.axis_size("sub")
    outer = [(i, i + 1) for i in range(1, count - 1, 2)]
    inner = [(i, i + 1) for i in range(0, count - 1, 2)]
    outer += [(target, source) for source, target in outer]
    inner += [(target, source) for source, target in inner]
    far = lax.ppermute(far, chain, outer)
    return lax.ppermute(near, chain, inner), far


def on_device(
    node_in,
    edge_in,
    senders,
    receivers,
    send_list,
    w_edge_first,
    b_edge_first,
    w_edge_second,
    b_edge_second,
    edge_gain,
    edge_shift,
    w_node_first,
    b_node_first,
    w_node_second,
    b_node_second,
    node_gain,
    node_shift,
    node_cotangent,
    edge_cotangent,
):
    node = node_in[0]
    edge = edge_in[0]
    nodes = node.shape[0]
    edges = edge.shape[0]
    rim = send_list.shape[2]
    rim_shape = ((rim, lane), bf16)
    snd_half = nodes // 2
    rcv_half = (nodes + 2 * rim) // 2
    members = ("dom", "sample", "sub")
    sharers = math.prod(lax.axis_size(axis) for axis in members)
    grad_rows = 7 * lane + sum_rows
    share = -(-grad_rows // (sharers * sum_rows)) * sum_rows
    ids = jnp.concatenate([senders, receivers, send_list.reshape(2 * rim)]).reshape(-1, lane)
    weights = jnp.concatenate([w_edge_first, w_edge_second, w_node_first, w_node_second], axis=0)
    vectors = jnp.stack(
        [
            b_edge_first,
            b_edge_second,
            edge_gain,
            edge_shift,
            b_node_first,
            b_node_second,
            node_gain,
            node_shift,
        ]
    )

    rim_near, rim_far = call(rim_kernel, [rim_shape, rim_shape], [], node, ids)
    near, far = swap(rim_near, rim_far)
    edge, edge_cot, node_cot, snd_column, rcv_column, snd_table, rcv_local = call(
        prepare_kernel,
        [
            ((edges, lane), bf16),
            ((edges, lane), bf16),
            ((nodes, lane), bf16),
            ((edges, lane), jnp.int32),
            ((edges, lane), jnp.int32),
            ((snd_half, 2 * lane), bf16),
            ((nodes, lane), bf16),
        ],
        [],
        ids,
        node,
        weights,
        edge,
        edge_cotangent[0],
        node_cotangent[0],
        anywhere=3,
        sems=3,
    )
    edge_out, z, agg, agg_near, agg_far = call(
        edge_forward_kernel,
        [((edges, lane), bf16), ((edges, lane), f32), ((nodes, lane), f32), rim_shape, rim_shape],
        [
            ((2 * rim, lane), bf16),
            ((rcv_half, 2 * lane), bf16),
            ((lane, 2 * lane), bf16),
            ((rcv_half, 2 * lane), f32),
        ],
        near,
        far,
        edge,
        ids,
        weights,
        vectors,
        snd_column,
        rcv_column,
        snd_table,
        rcv_local,
    )
    back_near, back_far = swap(agg_near, agg_far)
    node_out, base, dagg, dagg_rim_near, dagg_rim_far, node_grads = call(
        node_kernel,
        [
            ((nodes, lane), bf16),
            ((nodes, lane), f32),
            ((nodes, lane), bf16),
            rim_shape,
            rim_shape,
            ((3 * lane + sum_rows, lane), bf16),
        ],
        [],
        node,
        agg,
        back_near,
        back_far,
        ids,
        weights,
        vectors,
        node_cot,
    )
    dagg_near, dagg_far = swap(dagg_rim_near, dagg_rim_far)
    edge_grad, acc, grad_near, grad_far, grads = call(
        edge_backward_kernel,
        [
            ((edges, lane), bf16),
            ((nodes, lane), f32),
            rim_shape,
            rim_shape,
            ((sharers * share, lane), bf16),
        ],
        [
            ((2 * rim, lane), bf16),
            ((rcv_half, 2 * lane), bf16),
            ((lane, 2 * lane), bf16),
            ((snd_half, 2 * lane), f32),
            ((rcv_half, 2 * lane), f32),
            ((2 * lane, lane), f32),
            ((8, lane), f32),
        ],
        z,
        edge_cot,
        edge,
        ids,
        node,
        near,
        far,
        dagg,
        dagg_near,
        dagg_far,
        base,
        weights,
        vectors,
        node_grads,
        snd_column,
        rcv_column,
    )
    returned_near, returned_far = swap(grad_near, grad_far)
    (node_grad,) = call(
        node_grad_kernel, [((nodes, lane), bf16)], [], acc, returned_near, returned_far, ids
    )
    parts = lax.all_to_all(grads.reshape(sharers, share, lane), members, 0, 0, tiled=True)
    (shares,) = call(share_kernel, [(parts.shape, bf16)], [], parts)
    shares = lax.all_to_all(shares, members, 0, 0, tiled=True)
    matrices = [3 * lane, lane, 2 * lane, lane]
    totals = call(
        finish_kernel,
        [((height, lane), f32) for height in matrices] + [((1, lane), f32)] * 8,
        [],
        shares.reshape(sharers * share, lane),
    )
    flat = [total.reshape(lane) for total in totals[4:]]
    return (
        node_out[None],
        edge_out[None],
        node_grad[None],
        edge_grad[None],
        totals[0],
        flat[0],
        totals[1],
        flat[1],
        flat[2],
        flat[3],
        totals[2],
        flat[4],
        totals[3],
        flat[5],
        flat[6],
        flat[7],
    )


def solution(mesh):
    node_spec = P(("groups", "sample"), ("dom", "sub"), None)
    ids_spec = P(("dom", "sub"))
    return jax.shard_map(
        on_device,
        mesh=mesh,
        in_specs=(
            (node_spec, node_spec, ids_spec, ids_spec, P(("dom", "sub"), None, None))
            + (P(),) * 12
            + (node_spec, node_spec)
        ),
        out_specs=(
            (node_spec,) * 4
            + (P("groups", None), P("groups"), P("groups", None), P("groups"), P("groups"), P("groups"))
            * 2
        ),
        check_vma=False,
    )
```

time: 88.5 us -> 83.9 us (0.948)
  waiting for transfers between devices: 26.8 us -> 8.25 us
  blocking collectives: 0 us -> 14.7 us
  starting transfers between devices: 26 us -> 19.6 us
  local copies, waits for them, and re-layouts: 12 us -> 15.9 us
    ppermute x12 -> x8, waiting for transfers between devices: 26.8 us -> 5.95 us  [the longest x4 5.94 us: swap(): far = lax.ppermute(far, chain, outer)]
    all_to_all x0 -> x1, blocking collectives: none -> 14.7 us  [on_device(): lax.all_to_all(grads.reshape(sharers, share, lane), members, 0, 0, tiled=...]
    ppermute x12 -> x8, starting transfers between devices: 26 us -> 15.6 us  [the longest x4 15.1 us: swap(): far = lax.ppermute(far, chain, outer)]
    all_to_all x0 -> x1, starting transfers between devices: none -> 3.97 us  [on_device(): shares = lax.all_to_all(shares, members, 0, 0, tiled=True)]
    unnamed x46 -> x45, local copies, waits for them, and re-layouts: 12 us -> 14.4 us
    all_to_all x0 -> x1, waiting for transfers between devices: none -> 2.3 us  [on_device(): shares = lax.all_to_all(shares, members, 0, 0, tiled=True)]
    pallas_call x6 -> x8, Pallas kernels: 22 us -> 22.4 us  [call(): pl.pallas_call(kernel, out_shape=[jax.ShapeDtypeStruct(shape, dtype) for...]
  transfers between devices with their start and end apart: 12 -> 9, of which waited for: 7 -> 4; matrix products, arithmetic and copies ran while one was open for 0% -> 5% of each run, Pallas kernels for 1% -> 2%
where the time goes in v2:
time: 83.9 us; the launch traced here: 82.4 us
  Pallas kernels  22.4 us (27%)
  starting transfers between devices  19.6 us (23%)
  local copies, waits for them, and re-layouts  15.9 us (19%)
  blocking collectives  14.7 us (18%)
  waiting for transfers between devices  8.25 us (10%)
    pallas_call x8, Pallas kernels, call(): pl.pallas_call(kernel, out_shape=[jax.ShapeDtypeStruct(shape, dtype) for...  22.4 us
    ppermute x4, starting transfers between devices, swap(): far = lax.ppermute(far, chain, outer)  15.1 us
    all_to_all x1, blocking collectives, on_device(): lax.all_to_all(grads.reshape(sharers, share, lane), members, 0, 0, tiled=...  14.7 us
    unnamed x45, local copies, waits for them, and re-layouts  14.4 us
    ppermute x4, waiting for transfers between devices, swap(): far = lax.ppermute(far, chain, outer)  5.94 us
    all_to_all x1, starting transfers between devices, on_device(): shares = lax.all_to_all(shares, members, 0, 0, tiled=True)  3.97 us
    all_to_all x1, waiting for transfers between devices, on_device(): shares = lax.all_to_all(shares, members, 0, 0, tiled=True)  2.3 us
  transfers between devices with their start and end apart: 9, of which 4 were waited for; matrix products, arithmetic and copies ran while one was open for 5% of the time, Pallas kernels for 2%

profile of v2, /device:TPU:1, one launch (start us, length us, event | category | flops | bytes accessed | tf_op | source)
XLA Modules:
  0.0 82.4 jit_solution(16802336164116520540)
XLA Ops:
  1.4 1.0 %copy-done = bf16[1,1024,128]{2,1,0:T(8,128)(2,1)S(1)} copy-done((bf16[1,1024,128]{2,1,0:T(8,128)(2,1)S(1)}, bf16[1,1024,128]{2,1,0:T(8,128)(2,1)}, u32[]{:S(2)}) %copy-start) | copy-done | bytes 262168
  2.9 4.6 %collective-permute-start.1 = (bf16[128,128]{1,0:T(8,128)(2,1)S(1)}, bf16[128,128]{1,0:T(8,128)(2,1)S(1)}, u32[]{:S(2)}, u32[]{:S(2)}) collective-permute-start(bf16[128,128]{1,0:T(8,128)(2,1)S(1)} %get-tuple-element.54), channel_id=1, source_target_pairs={{1,4},{5,8},{9,12},{4,1},{8,5},{12,9},{3,6},{7,10},{11,14},{6,3},{... | collective-permute-start | bytes 98312 | tf_op jit(solution)/shard_map/ppermute | solution.py:451
  7.5 0.9 %constant_dynamic-update-slice_fusion.3 = bf16[896,128]{1,0:T(8,128)(2,1)S(1)} fusion(bf16[384,128]{1,0:T(8,128)(2,1)} %param.24), kind=kLoop, calls=%fused_computation.4 | loop fusion | bytes 196608
  10.8 1.1 %copy-done.6 = bf16[1,3072,128]{2,1,0:T(8,128)(2,1)S(1)} copy-done((bf16[1,3072,128]{2,1,0:T(8,128)(2,1)S(1)}, bf16[1,3072,128]{2,1,0:T(8,128)(2,1)}, u32[]{:S(2)}) %copy-start.6) | copy-done | bytes 786456
  11.9 1.1 %copy-done.7 = bf16[1,3072,128]{2,1,0:T(8,128)(2,1)S(1)} copy-done((bf16[1,3072,128]{2,1,0:T(8,128)(2,1)S(1)}, bf16[1,3072,128]{2,1,0:T(8,128)(2,1)}, u32[]{:S(2)}) %copy-start.7) | copy-done | bytes 786456
  13.0 0.9 %copy-done.10 = bf16[1,1024,128]{2,1,0:T(8,128)(2,1)S(1)} copy-done((bf16[1,1024,128]{2,1,0:T(8,128)(2,1)S(1)}, bf16[1,1024,128]{2,1,0:T(8,128)(2,1)}, u32[]{:S(2)}) %copy-start.10) | copy-done | bytes 262168
  14.0 1.1 %shard_map.307 = (bf16[3072,128]{1,0:T(8,128)(2,1)S(1)}, bf16[3072,128]{1,0:T(8,128)(2,1)S(1)}, bf16[1024,128]{1,0:T(8,128)(2,1)S(1)}, s32[3072,128]{1,0:T(8,128...) custom-call(s32[50,128]{1,0:T(8,128)S(1)} %add_bitcast_fusion.ids_ref, ...), custom_call_target="tpu_custom_call" | custom-call | bytes 2352128 | tf_op jit(solution)/shard_map/pallas_call | solution.py:434
  15.9 0.9 %copy-done.4 = bf16[3072,128]{1,0:T(8,128)(2,1)} copy-done((bf16[3072,128]{1,0:T(8,128)(2,1)}, bf16[3072,128]{1,0:T(8,128)(2,1)S(1)}, u32[]{:S(2)}) %copy-start.4) | copy-done | bytes 786456
  19.7 1.1 %copy-done.3 = bf16[3072,128]{1,0:T(8,128)(2,1)S(1)} copy-done((bf16[3072,128]{1,0:T(8,128)(2,1)S(1)}, bf16[3072,128]{1,0:T(8,128)(2,1)}, u32[]{:S(2)}) %copy-start.3) | copy-done | bytes 786456
  20.8 0.9 %copy-done.12 = bf16[512,256]{1,0:T(8,128)(2,1)S(1)} copy-done((bf16[512,256]{1,0:T(8,128)(2,1)S(1)}, bf16[512,256]{1,0:T(8,128)(2,1)}, u32[]{:S(2)}) %copy-start.12) | copy-done | bytes 262168
  21.8 0.9 %copy-done.14 = bf16[1024,128]{1,0:T(8,128)(2,1)S(1)} copy-done((bf16[1024,128]{1,0:T(8,128)(2,1)S(1)}, bf16[1024,128]{1,0:T(8,128)(2,1)}, u32[]{:S(2)}) %copy-start.14) | copy-done | bytes 262168
  22.7 7.4 %shard_map.308 = (bf16[3072,128]{1,0:T(8,128)(2,1)}, f32[3072,128]{1,0:T(8,128)S(1)}, f32[1024,128]{1,0:T(8,128)S(1)}, bf16[128,128]{1,0:T(8,128)(2,1)S(1)}, bf16[128,128]{1,0:T(8,128)(2,1)S(1)}) custom-call(bf16[128,128]{1,0:T(8,128)(2,1)S(1)} %collective-permute-done.near_ref, bf16[128,128]{1,0:T(8,128)(2,1)S(1)} %collective-permute-done.1.far_ref, ...), custom_call_target="tpu_custom_call" | custom-call | bytes 4781056 | tf_op jit(solution)/shard_map/pallas_call | solution.py:434
  30.2 3.6 %collective-permute-start.3 = (bf16[128,128]{1,0:T(8,128)(2,1)S(1)}, bf16[128,128]{1,0:T(8,128)(2,1)S(1)}, u32[]{:S(2)}, u32[]{:S(2)}) collective-permute-start(bf16[128,128]{1,0:T(8,128)(2,1)S(1)} %get-tuple-element.62), channel_id=1, source_target_pairs={{1,4},{5,8},{9,12},{4,1},{8,5},{12,9},{3,6},{7,10},{11,14},{6,3},{... | collective-permute-start | bytes 98312 | tf_op jit(solution)/shard_map/ppermute | solution.py:451
  33.8 1.8 %collective-permute-done.3.far_ref = bf16[128,128]{1,0:T(8,128)(2,1)S(1)} collective-permute-done((bf16[128,128]{1,0:T(8,128)(2,1)S(1)}, bf16[128,128]{1,0:T(8,128)(2,1)S(1)}, u32[]{:S(2)}, u32[]{:S(2)}) %collective-permute-start.3) | collective-permute-done | bytes 32800 | tf_op jit(solution)/shard_map/ppermute | solution.py:451
  35.5 1.8 %shard_map.309 = (bf16[1024,128]{1,0:T(8,128)(2,1)}, f32[1024,128]{1,0:T(8,128)S(1)}, bf16[1024,128]{1,0:T(8,128)(2,1)S(1)}, bf16[128,128]{1,0:T(8,128)(2,1)S(1)...) custom-call(bf16[1024,128]{1,0:T(8,128)(2,1)S(1)} %bitcast.31, f32[1024,128]{1,0:T(8,128)S(1)} %get-tuple-element.60.agg_ref, ...), custom_call_target="tpu_custom_call" | custom-call | bytes 1373184 | tf_op jit(solution)/shard_map/pallas_call | solution.py:434
  37.4 3.6 %collective-permute-start.5 = (bf16[128,128]{1,0:T(8,128)(2,1)S(1)}, bf16[128,128]{1,0:T(8,128)(2,1)S(1)}, u32[]{:S(2)}, u32[]{:S(2)}) collective-permute-start(bf16[128,128]{1,0:T(8,128)(2,1)S(1)} %get-tuple-element.70), channel_id=1, source_target_pairs={{1,4},{5,8},{9,12},{4,1},{8,5},{12,9},{3,6},{7,10},{11,14},{6,3},{... | collective-permute-start | bytes 98312 | tf_op jit(solution)/shard_map/ppermute | solution.py:451
  41.0 1.6 %collective-permute-done.5.dagg_far_ref = bf16[128,128]{1,0:T(8,128)(2,1)S(1)} collective-permute-done((bf16[128,128]{1,0:T(8,128)(2,1)S(1)}, bf16[128,128]{1,0:T(8,128)(2,1)S(1)}, u32[]{:S(2)}, u32[]{:S(2)}) %collective-permute-start.5) | collective-permute-done | bytes 32800 | tf_op jit(solution)/shard_map/ppermute | solution.py:451
  42.6 9.2 %shard_map.310 = (bf16[3072,128]{1,0:T(8,128)(2,1)}, f32[1024,128]{1,0:T(8,128)S(1)}, bf16[128,128]{1,0:T(8,128)(2,1)S(1)}, bf16[128,128]{1,0:T(8,128)(2,1)S(1)}, bf16[1024,128]{1,0:T(8,128)(2,1)S(1)}) custom-call(f32[3072,128]{1,0:T(8,128)S(1)} %get-tuple-element.66.z_ref, bf16[3072,128]{1,0:T(8,128)(2,1)S(1)} %copy-done.5, ...), custom_call_target="tpu_custom_call" | custom-call | bytes 7832576 | tf_op jit(solution)/shard_map/pallas_call | solution.py:434
  52.6 14.7 %all_to_all.10.parts_ref = bf16[16,64,128]{2,1,0:T(8,128)(2,1)S(1)} all-to-all(bf16[16,64,128]{2,1,0:T(8,128)(2,1)S(1)} %bitcast.37), channel_id=1, replica_groups=mesh['groups'=2,'dom'=4,'sample'=2,'sub'=2] {'dom','sample','sub'}, dimensions={0} | all-to-all | bytes 524288 | tf_op jit(solution)/shard_map/all_to_all | solution.py:607
  68.1 4.0 %all-to-all-start.1 = ((bf16[16,64,128]{2,1,0:T(8,128)(2,1)}), bf16[16,64,128]{2,1,0:T(8,128)(2,1)S(1)}, u32[]{:S(2)}, u32[]{:S(2)}) async-start(bf16[16,64,128]{2,1,0:T(8,128)(2,1)} %shard_map.312), calls=%async_computation.1 | async-start | bytes 524288 | tf_op jit(solution)/shard_map/all_to_all | solution.py:609
  72.4 3.4 %collective-permute-start.7 = (bf16[128,128]{1,0:T(8,128)(2,1)S(1)}, bf16[128,128]{1,0:T(8,128)(2,1)S(1)}, u32[]{:S(2)}, u32[]{:S(2)}) collective-permute-start(bf16[128,128]{1,0:T(8,128)(2,1)S(1)} %get-tuple-element.75), channel_id=1, source_target_pairs={{1,4},{5,8},{9,12},{4,1},{8,5},{12,9},{3,6},{7,10},{11,14},{6,3},{... | collective-permute-start | bytes 98312 | tf_op jit(solution)/shard_map/ppermute | solution.py:451
  75.8 2.5 %collective-permute-done.7.far_ref = bf16[128,128]{1,0:T(8,128)(2,1)S(1)} collective-permute-done((bf16[128,128]{1,0:T(8,128)(2,1)S(1)}, bf16[128,128]{1,0:T(8,128)(2,1)S(1)}, u32[]{:S(2)}, u32[]{:S(2)}) %collective-permute-start.7) | collective-permute-done | bytes 32800 | tf_op jit(solution)/shard_map/ppermute | solution.py:451
  78.3 1.0 %shard_map.311 = bf16[1024,128]{1,0:T(8,128)(2,1)} custom-call(f32[1024,128]{1,0:T(8,128)S(1)} %copy-done.9, bf16[128,128]{1,0:T(8,128)(2,1)S(1)} %collective-permute-done.6.near_ref, bf16[128,128]{1,0:T(8,128)(2,1)S(1)} %collective-permute-done.7.far_ref, s32[50,128]{1,0:T(8,128)S(1)} %add_bitcast_fusion.ids_ref), custom_call_target="tpu_custom_call" | custom-call | bytes 615424 | tf_op jit(solution)/shard_map/pallas_call | solution.py:434
  79.3 2.3 %all-to-all-done.1 = bf16[16,64,128]{2,1,0:T(8,128)(2,1)S(1)} async-done(((bf16[16,64,128]{2,1,0:T(8,128)(2,1)}), bf16[16,64,128]{2,1,0:T(8,128)(2,1)S(1)}, u32[]{:S(2)}, u32[]{:S(2)}) %all-to-all-start.1) | async-done | bytes 262176 | tf_op jit(solution)/shard_map/all_to_all | solution.py:609
  (51 shorter events, 10.1 us)
Async XLA Ops:
  1.4 17.5 %copy-start.17 = (f32[128]{0:T(128)S(1)}, f32[128]{0:T(128)}, u32[]{:S(2)}) copy-start(f32[128]{0:T(128)} %param.25) | copy-start | bytes 1540
  1.4 17.5 %copy-start.18 = (f32[128]{0:T(128)S(1)}, f32[128]{0:T(128)}, u32[]{:S(2)}) copy-start(f32[128]{0:T(128)} %param.27) | copy-start | bytes 1540
  1.4 17.5 %copy-start.19 = (f32[128]{0:T(128)S(1)}, f32[128]{0:T(128)}, u32[]{:S(2)}) copy-start(f32[128]{0:T(128)} %param.28) | copy-start | bytes 1540
  1.4 1.0 %copy-start = (bf16[1,1024,128]{2,1,0:T(8,128)(2,1)S(1)}, bf16[1,1024,128]{2,1,0:T(8,128)(2,1)}, u32[]{:S(2)}) copy-start(bf16[1,1024,128]{2,1,0:T(8,128)(2,1)} %param.19) | copy-start | bytes 786436
  2.4 16.6 %copy-start.20 = (f32[128]{0:T(128)S(1)}, f32[128]{0:T(128)}, u32[]{:S(2)}) copy-start(f32[128]{0:T(128)} %param.29) | copy-start | bytes 1540
  2.8 16.9 %collective-permute-start = (bf16[128,128]{1,0:T(8,128)(2,1)S(1)}, bf16[128,128]{1,0:T(8,128)(2,1)S(1)}, u32[]{:S(2)}, u32[]{:S(2)}) collective-permute-start(bf16[128,128]{1,0:T(8,128)(2,1)S(1)} %get-tuple-element.53), channel_id=1, source_target_pairs={{0,1},{4,5},{8,9},{12,13},{1,0},{5,4},{9,8},{13,12},{2,3},{6,7},{1... | collective-permute-start | bytes 98312 | tf_op jit(solution)/shard_map/ppermute | solution.py:452
  2.9 16.8 %collective-permute-start.1 = (bf16[128,128]{1,0:T(8,128)(2,1)S(1)}, bf16[128,128]{1,0:T(8,128)(2,1)S(1)}, u32[]{:S(2)}, u32[]{:S(2)}) collective-permute-start(bf16[128,128]{1,0:T(8,128)(2,1)S(1)} %get-tuple-element.54), channel_id=1, source_target_pairs={{1,4},{5,8},{9,12},{4,1},{8,5},{12,9},{3,6},{7,10},{11,14},{6,3},{... | collective-permute-start | bytes 98312 | tf_op jit(solution)/shard_map/ppermute | solution.py:451
  10.8 1.1 %copy-start.6 = (bf16[1,3072,128]{2,1,0:T(8,128)(2,1)S(1)}, bf16[1,3072,128]{2,1,0:T(8,128)(2,1)}, u32[]{:S(2)}) copy-start(bf16[1,3072,128]{2,1,0:T(8,128)(2,1)} %param.20) | copy-start | bytes 2359300
  11.9 1.1 %copy-start.7 = (bf16[1,3072,128]{2,1,0:T(8,128)(2,1)S(1)}, bf16[1,3072,128]{2,1,0:T(8,128)(2,1)}, u32[]{:S(2)}) copy-start(bf16[1,3072,128]{2,1,0:T(8,128)(2,1)} %param.37) | copy-start | bytes 2359300
  13.0 0.9 %copy-start.10 = (bf16[1,1024,128]{2,1,0:T(8,128)(2,1)S(1)}, bf16[1,1024,128]{2,1,0:T(8,128)(2,1)}, u32[]{:S(2)}) copy-start(bf16[1,1024,128]{2,1,0:T(8,128)(2,1)} %param.36) | copy-start | bytes 786436
  19.7 1.1 %copy-start.3 = (bf16[3072,128]{1,0:T(8,128)(2,1)S(1)}, bf16[3072,128]{1,0:T(8,128)(2,1)}, u32[]{:S(2)}) copy-start(bf16[3072,128]{1,0:T(8,128)(2,1)} %copy-done.2) | copy-start | bytes 2359300
  20.8 0.9 %copy-start.12 = (bf16[512,256]{1,0:T(8,128)(2,1)S(1)}, bf16[512,256]{1,0:T(8,128)(2,1)}, u32[]{:S(2)}) copy-start(bf16[512,256]{1,0:T(8,128)(2,1)} %copy-done.11) | copy-start | bytes 786436
  21.8 0.9 %copy-start.14 = (bf16[1024,128]{1,0:T(8,128)(2,1)S(1)}, bf16[1024,128]{1,0:T(8,128)(2,1)}, u32[]{:S(2)}) copy-start(bf16[1024,128]{1,0:T(8,128)(2,1)} %copy-done.13) | copy-start | bytes 786436
  22.7 12.8 %copy-start.1 = (bf16[1,1024,128]{2,1,0:T(8,128)(2,1)S(1)}, bf16[1,1024,128]{2,1,0:T(8,128)(2,1)}, u32[]{:S(2)}) copy-start(bf16[1,1024,128]{2,1,0:T(8,128)(2,1)} %param.19) | copy-start | bytes 786436
  22.7 12.8 %copy-start.16 = (bf16[1024,128]{1,0:T(8,128)(2,1)S(1)}, bf16[1024,128]{1,0:T(8,128)(2,1)}, u32[]{:S(2)}) copy-start(bf16[1024,128]{1,0:T(8,128)(2,1)} %copy-done.15) | copy-start | bytes 786436
  30.2 12.5 %copy-start.5 = (bf16[3072,128]{1,0:T(8,128)(2,1)S(1)}, bf16[3072,128]{1,0:T(8,128)(2,1)}, u32[]{:S(2)}) copy-start(bf16[3072,128]{1,0:T(8,128)(2,1)} %copy-done.4) | copy-start | bytes 2359300
  30.2 3.6 %collective-permute-start.2 = (bf16[128,128]{1,0:T(8,128)(2,1)S(1)}, bf16[128,128]{1,0:T(8,128)(2,1)S(1)}, u32[]{:S(2)}, u32[]{:S(2)}) collective-permute-start(bf16[128,128]{1,0:T(8,128)(2,1)S(1)} %get-tuple-element.61), channel_id=1, source_target_pairs={{0,1},{4,5},{8,9},{12,13},{1,0},{5,4},{9,8},{13,12},{2,3},{6,7},{1... | collective-permute-start | bytes 98312 | tf_op jit(solution)/shard_map/ppermute | solution.py:452
  30.2 5.4 %collective-permute-start.3 = (bf16[128,128]{1,0:T(8,128)(2,1)S(1)}, bf16[128,128]{1,0:T(8,128)(2,1)S(1)}, u32[]{:S(2)}, u32[]{:S(2)}) collective-permute-start(bf16[128,128]{1,0:T(8,128)(2,1)S(1)} %get-tuple-element.62), channel_id=1, source_target_pairs={{1,4},{5,8},{9,12},{4,1},{8,5},{12,9},{3,6},{7,10},{11,14},{6,3},{... | collective-permute-start | bytes 98312 | tf_op jit(solution)/shard_map/ppermute | solution.py:451
  37.3 3.7 %collective-permute-start.4 = (bf16[128,128]{1,0:T(8,128)(2,1)S(1)}, bf16[128,128]{1,0:T(8,128)(2,1)S(1)}, u32[]{:S(2)}, u32[]{:S(2)}) collective-permute-start(bf16[128,128]{1,0:T(8,128)(2,1)S(1)} %get-tuple-element.69), channel_id=1, source_target_pairs={{0,1},{4,5},{8,9},{12,13},{1,0},{5,4},{9,8},{13,12},{2,3},{6,7},{1... | collective-permute-start | bytes 98312 | tf_op jit(solution)/shard_map/ppermute | solution.py:452
  37.4 5.2 %collective-permute-start.5 = (bf16[128,128]{1,0:T(8,128)(2,1)S(1)}, bf16[128,128]{1,0:T(8,128)(2,1)S(1)}, u32[]{:S(2)}, u32[]{:S(2)}) collective-permute-start(bf16[128,128]{1,0:T(8,128)(2,1)S(1)} %get-tuple-element.70), channel_id=1, source_target_pairs={{1,4},{5,8},{9,12},{4,1},{8,5},{12,9},{3,6},{7,10},{11,14},{6,3},{... | collective-permute-start | bytes 98312 | tf_op jit(solution)/shard_map/ppermute | solution.py:451
  52.6 25.7 %copy-start.9 = (f32[1024,128]{1,0:T(8,128)S(1)}, f32[1024,128]{1,0:T(8,128)}, u32[]{:S(2)}) copy-start(f32[1024,128]{1,0:T(8,128)} %copy-done.8) | copy-start | bytes 1572868
  68.1 13.5 %all-to-all-start.1 = ((bf16[16,64,128]{2,1,0:T(8,128)(2,1)}), bf16[16,64,128]{2,1,0:T(8,128)(2,1)S(1)}, u32[]{:S(2)}, u32[]{:S(2)}) async-start(bf16[16,64,128]{2,1,0:T(8,128)(2,1)} %shard_map.312), calls=%async_computation.1 | async-start | bytes 524288 | tf_op jit(solution)/shard_map/all_to_all | solution.py:609
  72.1 3.7 %collective-permute-start.6 = (bf16[128,128]{1,0:T(8,128)(2,1)S(1)}, bf16[128,128]{1,0:T(8,128)(2,1)S(1)}, u32[]{:S(2)}, u32[]{:S(2)}) collective-permute-start(bf16[128,128]{1,0:T(8,128)(2,1)S(1)} %get-tuple-element.74), channel_id=1, source_target_pairs={{0,1},{4,5},{8,9},{12,13},{1,0},{5,4},{9,8},{13,12},{2,3},{6,7},{1... | collective-permute-start | bytes 98312 | tf_op jit(solution)/shard_map/ppermute | solution.py:452
  72.4 6.0 %collective-permute-start.7 = (bf16[128,128]{1,0:T(8,128)(2,1)S(1)}, bf16[128,128]{1,0:T(8,128)(2,1)S(1)}, u32[]{:S(2)}, u32[]{:S(2)}) collective-permute-start(bf16[128,128]{1,0:T(8,128)(2,1)S(1)} %get-tuple-element.75), channel_id=1, source_target_pairs={{1,4},{5,8},{9,12},{4,1},{8,5},{12,9},{3,6},{7,10},{11,14},{6,3},{... | collective-permute-start | bytes 98312 | tf_op jit(solution)/shard_map/ppermute | solution.py:451
  (6 other events, 4.7 us)

commit v3 on v2

--- a/solution.py
+++ b/solution.py
@@ -120,39 +120,62 @@
     return lax.axis_index(chain) % 2
 
 
-def rim_kernel(node_ref, ids_ref, near_ref, far_ref):
+def first_kernel(
+    node_hbm,
+    snd_hbm,
+    rcv_hbm,
+    list_hbm,
+    edge_hbm,
+    edge_cot_hbm,
+    node_cot_hbm,
+    *refs,
+):
+    small = refs[:12]
+    node_ref, ids_ref, edge_ref, edge_cot_ref, node_cot_ref, weights_ref, vectors_ref = refs[12:19]
+    near_ref, far_ref, sems = refs[19:]
+    chunks = snd_hbm.shape[0]
+    moves = [
+        (node_hbm, node_ref),
+        (list_hbm, ids_ref.at[2 * chunks : 2 * chunks + 2]),
+        (snd_hbm, ids_ref.at[:chunks]),
+        (rcv_hbm, ids_ref.at[chunks : 2 * chunks]),
+    ]
+    at = 0
+    for source in small[:4]:
+        moves.append((source, weights_ref.at[at : at + source.shape[0]]))
+        at += source.shape[0]
+    for k, source in enumerate(small[4:]):
+        moves.append((source, vectors_ref.at[k : k + 1]))
+    moves += [(edge_hbm, edge_ref), (edge_cot_hbm, edge_cot_ref), (node_cot_hbm, node_cot_ref)]
+    copies = [
+        pltpu.make_async_copy(source, target, sems.at[k])
+        for k, (source, target) in enumerate(moves)
+    ]
+    for copy in copies:
+        copy.start()
+    for copy in copies[:2]:
+        copy.wait()
     parity = parity_of_place()
     node = node_ref[...]
-    first = ids_ref.shape[0] - 2
     for side, out_ref in ((1 - parity, near_ref), (parity, far_ref)):
-        hot = hot_columns(column_of(ids_ref[pl.ds(first + side, 1), :]), node.shape[0])
+        hot = hot_columns(column_of(ids_ref[pl.ds(2 * chunks + side, 1), :]), node.shape[0])
         out_ref[...] = dot(hot, node).astype(bf16)
+    for copy in copies[2:]:
+        copy.wait()
 
 
 def prepare_kernel(
     ids_ref,
     node_ref,
     weights_ref,
+    vectors_ref,
     edge_ref,
-    edge_cot_ref,
-    node_cot_ref,
-    edge_out,
-    edge_cot_out,
-    node_cot_out,
     snd_column,
     rcv_column,
+    z_ref,
+    rcv_local,
     snd_table,
-    rcv_local,
-    sems,
 ):
-    copies = [
-        pltpu.make_async_copy(source, target, sems.at[k])
-        for k, (source, target) in enumerate(
-            ((edge_ref, edge_out), (edge_cot_ref, edge_cot_out), (node_cot_ref, node_cot_out))
-        )
-    ]
-    for copy in copies:
-        copy.start()
     chunks = snd_column.shape[0] // lane
     for k in range(chunks):
         at = slice(k * lane, (k + 1) * lane)
@@ -161,8 +184,16 @@
     node = node_ref[...]
     snd_table[...] = side_by_side(dot(node, weights_ref[lane : 2 * lane]).astype(bf16))
     rcv_local[...] = dot(node, weights_ref[2 * lane : 3 * lane]).astype(bf16)
-    for copy in copies:
-        copy.wait()
+    w1_edge = weights_ref[:lane]
+    b1 = vector(vectors_ref, 0)
+
+    def tile(i, carry):
+        rows = pl.ds(pl.multiple_of(i * edge_tile, edge_tile), edge_tile)
+        z = dot(edge_ref[rows, :], w1_edge) + b1
+        z_ref[rows, :] = z + pick(snd_column[rows, :], snd_table[...])
+        return carry
+
+    lax.fori_loop(0, edge_ref.shape[0] // edge_tile, tile, 0)
 
 
 def edge_forward_kernel(
@@ -172,9 +203,8 @@
     ids_ref,
     weights_ref,
     vectors_ref,
-    snd_column,
     rcv_column,
-    snd_table,
+    z_sent,
     rcv_local,
     out_ref,
     z_ref,
@@ -192,9 +222,8 @@
     parity = parity_of_place()
     near_at = pl.multiple_of((1 - parity) * rim, rim)
     far_at = pl.multiple_of(parity * rim, rim)
-    w1_edge = weights_ref[:lane]
     w1_rcv = weights_ref[2 * lane : 3 * lane]
-    b1, gain, shift = vector(vectors_ref, 0), vector(vectors_ref, 2), vector(vectors_ref, 3)
+    gain, shift = vector(vectors_ref, 2), vector(vectors_ref, 3)
     halo[pl.ds(near_at, rim), :] = dot(near_ref[...], w1_rcv).astype(bf16)
     halo[pl.ds(far_at, rim), :] = dot(far_ref[...], w1_rcv).astype(bf16)
     rcv_table[:, :lane] = rcv_local[:half, :]
@@ -208,9 +237,7 @@
         rows = pl.ds(pl.multiple_of(i * edge_tile, edge_tile), edge_tile)
         x = edge_ref[rows, :]
         rcv = rcv_column[rows, :]
-        z = dot(x, w1_edge) + b1
-        z = z + pick(snd_column[rows, :], snd_table[...])
-        z = z + pick(rcv, rcv_table[...])
+        z = z_sent[rows, :] + pick(rcv, rcv_table[...])
         z_ref[rows, :] = z
         act = (z * sigmoid(z)).astype(bf16)
         normed, unused = normed_of(act, w2_pair[...], b2)
@@ -282,11 +309,11 @@
         rim_ref[...] = dot(picked, dagg).astype(bf16)
     first = 2 * lane
     second = first + lane
-    grads_ref[:first, :] = dot_rows(x, dz1b).astype(bf16)
-    grads_ref[first:second, :] = dot_rows(act, dz2b).astype(bf16)
+    grads_ref[:first, :] = dot_rows(x, dz1b)
+    grads_ref[first:second, :] = dot_rows(act, dz2b)
     sums = [column_sum(dz1), column_sum(dz2), column_sum(upstream * normed), column_sum(upstream)]
     sums.append(jnp.zeros((sum_rows - len(sums), lane), f32))
-    grads_ref[second:, :] = jnp.concatenate(sums, axis=0).astype(bf16)
+    grads_ref[second:, :] = jnp.concatenate(sums, axis=0)
 
 
 def edge_backward_kernel(
@@ -308,10 +335,11 @@
     rcv_column,
     grad_ref,
     acc_ref,
-    back_near_ref,
-    back_far_ref,
+    far_back_ref,
+    kept_ref,
+    sent_ref,
+    halo,
     grads_ref,
-    halo,
     table,
     w2_pair,
     snd_total,
@@ -377,31 +405,42 @@
     w1_snd = weights_ref[lane : 2 * lane]
     w1_rcv = weights_ref[2 * lane : 3 * lane]
     acc_ref[...] = base_ref[...] + dot_back(snd_sum, w1_snd) + dot_back(rcv_sum[:nodes], w1_rcv)
-    for at, back_ref in ((near_at, back_near_ref), (far_at, back_far_ref)):
+    kept = kept_ref.shape[0]
+    for at, back_ref in ((near_at, sent_ref.at[kept:]), (far_at, far_back_ref)):
         returned = rcv_total[pl.ds(nodes - rcv_half + at, rim), lane:].astype(bf16)
         back_ref[...] = dot_back(returned, w1_rcv).astype(bf16)
     extended = jnp.concatenate([node_ref[...], halo[...]], axis=0)
-    grads_ref[:lane, :] = squares[:lane, :].astype(bf16)
-    grads_ref[lane : 2 * lane, :] = dot_rows(node_ref[...], snd_sum).astype(bf16)
-    grads_ref[2 * lane : 3 * lane, :] = dot_rows(extended, rcv_sum).astype(bf16)
-    grads_ref[3 * lane : 4 * lane, :] = squares[lane:, :].astype(bf16)
+    grads_ref[:lane, :] = squares[:lane, :]
+    grads_ref[lane : 2 * lane, :] = dot_rows(node_ref[...], snd_sum)
+    grads_ref[2 * lane : 3 * lane, :] = dot_rows(extended, rcv_sum)
+    grads_ref[3 * lane : 4 * lane, :] = squares[lane:, :]
     node_rows = node_grads_ref.shape[0] - sum_rows
-    grads_ref[4 * lane : 4 * lane + node_rows, :] = node_grads_ref[:node_rows, :]
-    node_sums = node_grads_ref[node_rows:, :].astype(f32)
     last = 4 * lane + node_rows
+    grads_ref[4 * lane : last, :] = node_grads_ref[:node_rows, :]
     grads_ref[last : last + sum_rows, :] = jnp.concatenate(
-        [sums[0:4, :], node_sums[0:4, :], jnp.zeros((sum_rows - 8, lane), f32)], axis=0
-    ).astype(bf16)
+        [sums[0:4, :], node_grads_ref[node_rows : node_rows + 4, :], jnp.zeros((8, lane), f32)],
+        axis=0,
+    )
     if last + sum_rows < grads_ref.shape[0]:
         grads_ref[last + sum_rows :, :] = jnp.zeros(
-            (grads_ref.shape[0] - last - sum_rows, lane), bf16
+            (grads_ref.shape[0] - last - sum_rows, lane), f32
         )
+    own = lax.axis_index("sub")
+    kept_ref[...] = grads_ref[pl.ds(pl.multiple_of(own * kept, kept), kept), :]
+    other = pl.multiple_of((1 - own) * kept, kept)
+    sent_ref[:kept, :] = grads_ref[pl.ds(other, kept), :].astype(bf16)
 
 
 def node_grad_kernel(acc_ref, near_ref, far_ref, ids_ref, out_ref):
-    returned = jnp.concatenate([near_ref[...], far_ref[...]], axis=0)
+    rim = far_ref.shape[0]
+    returned = jnp.concatenate([near_ref[near_ref.shape[0] - rim :, :], far_ref[...]], axis=0)
     hot = hot_lists(ids_ref, acc_ref.shape[0])
     out_ref[...] = (acc_ref[...] + dot(hot, returned)).astype(bf16)
+
+
+def halves_kernel(kept_ref, other_ref, out_ref):
+    kept = kept_ref.shape[0]
+    out_ref[...] = (kept_ref[...] + other_ref[:kept, :].astype(f32)).astype(bf16)
 
 
 def share_kernel(parts_ref, out_ref):
@@ -414,18 +453,26 @@
         out_ref[k] = total
 
 
-def finish_kernel(total_ref, *out_refs):
+def finish_kernel(own_ref, other_ref, *refs):
+    out_refs, total_ref = refs[:-1], refs[-1]
+    kept = own_ref.shape[0]
+    own = lax.axis_index("sub")
+    total_ref[pl.ds(pl.multiple_of(own * kept, kept), kept), :] = own_ref[...].astype(f32)
+    other = pl.multiple_of((1 - own) * kept, kept)
+    total_ref[pl.ds(other, kept), :] = other_ref[...].astype(f32)
     at = 0
     for out_ref in out_refs[:4]:
-        out_ref[...] = total_ref[at : at + out_ref.shape[0], :].astype(f32)
+        out_ref[...] = total_ref[at : at + out_ref.shape[0], :]
         at += out_ref.shape[0]
-    last = total_ref[at : at + sum_rows, :].astype(f32)
     for k, out_ref in enumerate(out_refs[4:]):
-        out_ref[...] = last[k : k + 1]
+        out_ref[...] = total_ref[at + k : at + k + 1, :]
 
 
 def call(kernel, outs, scratch, *operands, anywhere=0, sems=0):
     moved = sum(x.size * x.dtype.itemsize for x in operands)
+    held = operands[len(operands) - anywhere :]
+    operands = operands[: len(operands) - anywhere]
+    operands += tuple(pltpu.with_memory_space_constraint(x, pltpu.HBM) for x in held)
     inside = [pl.BlockSpec(memory_space=pltpu.VMEM)] * (len(operands) - anywhere)
     outside = [pl.BlockSpec(memory_space=pl.ANY)] * anywhere
     scratch_shapes = [pltpu.VMEM(shape, dtype) for shape, dtype in scratch]
@@ -481,47 +528,58 @@
     rim_shape = ((rim, lane), bf16)
     snd_half = nodes // 2
     rcv_half = (nodes + 2 * rim) // 2
-    members = ("dom", "sample", "sub")
+    members = ("dom", "sample")
     sharers = math.prod(lax.axis_size(axis) for axis in members)
     grad_rows = 7 * lane + sum_rows
-    share = -(-grad_rows // (sharers * sum_rows)) * sum_rows
-    ids = jnp.concatenate([senders, receivers, send_list.reshape(2 * rim)]).reshape(-1, lane)
-    weights = jnp.concatenate([w_edge_first, w_edge_second, w_node_first, w_node_second], axis=0)
-    vectors = jnp.stack(
+    share = -(-grad_rows // (2 * sharers * sum_rows)) * sum_rows
+    kept = sharers * share
+    row = lambda x: x.reshape(1, lane)
+    small = [w_edge_first, w_edge_second, w_node_first, w_node_second]
+    small += [row(b_edge_first), row(b_edge_second), row(edge_gain), row(edge_shift)]
+    small += [row(b_node_first), row(b_node_second), row(node_gain), row(node_shift)]
+    chunks = edges // lane
+    sources = [
+        node,
+        senders.reshape(chunks, lane),
+        receivers.reshape(chunks, lane),
+        send_list[0],
+        edge,
+        edge_cotangent[0],
+        node_cotangent[0],
+    ] + small
+    node, ids, edge, edge_cot, node_cot, weights, vectors, rim_near, rim_far = call(
+        first_kernel,
         [
-            b_edge_first,
-            b_edge_second,
-            edge_gain,
-            edge_shift,
-            b_node_first,
-            b_node_second,
-            node_gain,
-            node_shift,
-        ]
-    )
-
-    rim_near, rim_far = call(rim_kernel, [rim_shape, rim_shape], [], node, ids)
-    near, far = swap(rim_near, rim_far)
-    edge, edge_cot, node_cot, snd_column, rcv_column, snd_table, rcv_local = call(
-        prepare_kernel,
-        [
+            ((nodes, lane), bf16),
+            ((2 * chunks + 2, lane), jnp.int32),
             ((edges, lane), bf16),
             ((edges, lane), bf16),
             ((nodes, lane), bf16),
+            ((7 * lane, lane), bf16),
+            ((8, lane), f32),
+            rim_shape,
+            rim_shape,
+        ],
+        [],
+        *sources,
+        anywhere=len(sources),
+        sems=len(sources),
+    )
+    near, far = swap(rim_near, rim_far)
+    snd_column, rcv_column, z_sent, rcv_local = call(
+        prepare_kernel,
+        [
             ((edges, lane), jnp.int32),
             ((edges, lane), jnp.int32),
-            ((snd_half, 2 * lane), bf16),
+            ((edges, lane), f32),
             ((nodes, lane), bf16),
         ],
-        [],
+        [((snd_half, 2 * lane), bf16)],
         ids,
         node,
         weights,
+        vectors,
         edge,
-        edge_cotangent[0],
-        node_cotangent[0],
-        anywhere=3,
-        sems=3,
     )
     edge_out, z, agg, agg_near, agg_far = call(
         edge_forward_kernel,
@@ -538,9 +596,8 @@
         ids,
         weights,
         vectors,
-        snd_column,
         rcv_column,
-        snd_table,
+        z_sent,
         rcv_local,
     )
     back_near, back_far = swap(agg_near, agg_far)
@@ -552,7 +609,7 @@
             ((nodes, lane), bf16),
             rim_shape,
             rim_shape,
-            ((3 * lane + sum_rows, lane), bf16),
+            ((3 * lane + sum_rows, lane), f32),
         ],
         [],
         node,
@@ -565,17 +622,18 @@
         node_cot,
     )
     dagg_near, dagg_far = swap(dagg_rim_near, dagg_rim_far)
-    edge_grad, acc, grad_near, grad_far, grads = call(
+    edge_grad, acc, grad_far, grads_kept, grads_sent = call(
         edge_backward_kernel,
         [
             ((edges, lane), bf16),
             ((nodes, lane), f32),
             rim_shape,
-            rim_shape,
-            ((sharers * share, lane), bf16),
+            ((kept, lane), f32),
+            ((kept + rim, lane), bf16),
         ],
         [
             ((2 * rim, lane), bf16),
+            ((2 * kept, lane), f32),
             ((rcv_half, 2 * lane), bf16),
             ((lane, 2 * lane), bf16),
             ((snd_half, 2 * lane), f32),
@@ -600,19 +658,22 @@
         snd_column,
         rcv_column,
     )
-    returned_near, returned_far = swap(grad_near, grad_far)
+    returned_near, returned_far = swap(grads_sent, grad_far)
+    (halves,) = call(halves_kernel, [((kept, lane), bf16)], [], grads_kept, returned_near)
+    parts = lax.all_to_all(halves.reshape(sharers, share, lane), members, 0, 0, tiled=True)
+    (shares,) = call(share_kernel, [(parts.shape, bf16)], [], parts)
+    shares = lax.all_to_all(shares, members, 0, 0, tiled=True).reshape(kept, lane)
     (node_grad,) = call(
         node_grad_kernel, [((nodes, lane), bf16)], [], acc, returned_near, returned_far, ids
     )
-    parts = lax.all_to_all(grads.reshape(sharers, share, lane), members, 0, 0, tiled=True)
-    (shares,) = call(share_kernel, [(parts.shape, bf16)], [], parts)
-    shares = lax.all_to_all(shares, members, 0, 0, tiled=True)
+    others = lax.ppermute(shares, "sub", [(0, 1), (1, 0)])
     matrices = [3 * lane, lane, 2 * lane, lane]
     totals = call(
         finish_kernel,
         [((height, lane), f32) for height in matrices] + [((1, lane), f32)] * 8,
-        [],
-        shares.reshape(sharers * share, lane),
+        [((2 * kept, lane), f32)],
+        shares,
+        others,
     )
     flat = [total.reshape(lane) for total in totals[4:]]
     return (

time: 83.9 us -> 70.8 us (0.84); the launches traced: 82.4 us -> 70.5 us
  local copies, waits for them, and re-layouts: 15.9 us -> 0 us
  blocking collectives: 14.7 us -> 20.5 us
  starting transfers between devices: 19.6 us -> 16 us
  Pallas kernels: 22.4 us -> 25.3 us
    unnamed x45 -> x0, local copies, waits for them, and re-layouts: 14.4 us -> none
    all_to_all x1 -> x2, blocking collectives: 14.7 us -> 20.5 us  [the longest x1 10.9 us: on_device(): lax.all_to_all(halves.reshape(sharers, share, lane), members, 0, 0, tiled...]
    all_to_all x1 -> x0, starting transfers between devices: 3.97 us -> none  [on_device(): shares = lax.all_to_all(shares, members, 0, 0, tiled=True)]
    pallas_call x8 -> x9, Pallas kernels: 22.4 us -> 25.3 us  [call(): pl.pallas_call(kernel, out_shape=[jax.ShapeDtypeStruct(shape, dtype) for...]
    all_to_all x1 -> x0, waiting for transfers between devices: 2.3 us -> none  [on_device(): shares = lax.all_to_all(shares, members, 0, 0, tiled=True)]
    ppermute x0 -> x1, starting transfers between devices: none -> 2.07 us  [on_device(): others = lax.ppermute(shares, 'sub', [(0, 1), (1, 0)])]
    ppermute x4, waiting for transfers between devices: 0.01 us -> 1.4 us  [swap(): return (lax.ppermute(near, chain, inner), far)]
    ppermute x4, starting transfers between devices: 15.1 us -> 13.7 us  [swap(): far = lax.ppermute(far, chain, outer)]
  transfers between devices with their start and end apart: 9 -> 9, of which waited for: 4 -> 4; matrix products, arithmetic and copies ran while one was open for 5% -> 0% of each run, Pallas kernels for 2% -> 6%
where the time goes in v3:
time: 70.8 us; the launch traced here: 70.5 us
  Pallas kernels  25.3 us (36%)
  blocking collectives  20.5 us (29%)
  starting transfers between devices  16 us (23%)
  waiting for transfers between devices  7.9 us (11%)
  between operations  0.76 us (1%)
    pallas_call x9, Pallas kernels, call(): pl.pallas_call(kernel, out_shape=[jax.ShapeDtypeStruct(shape, dtype) for...  25.3 us
    ppermute x4, starting transfers between devices, swap(): far = lax.ppermute(far, chain, outer)  13.7 us
    all_to_all x1, blocking collectives, on_device(): lax.all_to_all(halves.reshape(sharers, share, lane), members, 0, 0, tiled...  10.9 us
    all_to_all x1, blocking collectives, on_device(): lax.all_to_all(shares, members, 0, 0, tiled=True).reshape(kept, lane)  9.52 us
    ppermute x4, waiting for transfers between devices, swap(): far = lax.ppermute(far, chain, outer)  6.5 us
    ppermute x1, starting transfers between devices, on_device(): others = lax.ppermute(shares, 'sub', [(0, 1), (1, 0)])  2.07 us
  transfers between devices with their start and end apart: 9, of which 4 were waited for; matrix products, arithmetic and copies ran while one was open for 0% of the time, Pallas kernels for 6%

profile of v3, /device:TPU:1, one launch (start us, length us, event | category | flops | bytes accessed | tf_op | source)
XLA Modules:
  0.0 70.5 jit_solution(16242479003238761142)
XLA Ops:
  0.7 1.9 %shard_map.306 = (bf16[1024,128]{1,0:T(8,128)(2,1)S(1)}, s32[50,128]{1,0:T(8,128)S(1)}, bf16[3072,128]{1,0:T(8,128)(2,1)S(1)}, bf16[3072,128]{1,0:T(8,128)(2,1)S...) custom-call(bf16[1024,128]{1,0:T(8,128)(2,1)} %bitcast.34, ...), custom_call_target="tpu_custom_call" | custom-call | bytes 2356224 | tf_op jit(solution)/shard_map/pallas_call | solution.py:481
  2.5 0.1 collective-permute-start
  2.7 4.6 %collective-permute-start.1 = (bf16[128,128]{1,0:T(8,128)(2,1)S(1)}, bf16[128,128]{1,0:T(8,128)(2,1)S(1)}, u32[]{:S(2)}, u32[]{:S(2)}) collective-permute-start(bf16[128,128]{1,0:T(8,128)(2,1)S(1)} %get-tuple-element.59), channel_id=1, source_target_pairs={{1,4},{5,8},{9,12},{4,1},{8,5},{12,9},{3,6},{7,10},{11,14},{6,3},{... | collective-permute-start | bytes 98312 | tf_op jit(solution)/shard_map/ppermute | solution.py:498
  7.2 2.9 %shard_map.307 = (s32[3072,128]{1,0:T(8,128)S(1)}, s32[3072,128]{1,0:T(8,128)S(1)}, f32[3072,128]{1,0:T(8,128)S(1)}, bf16[1024,128]{1,0:T(8,128)(2,1)S(1)}) custom-call(s32[50,128]{1,0:T(8,128)S(1)} %get-tuple-element.61.ids_ref, bf16[1024,128]{1,0:T(8,128)(2,1)S(1)} %get-tuple-element.57.node_ref, bf16[896,128]{1,0:T(8,128)(2,1)S(1)} %get-tuple-element.62.weights_ref, ...), custom_call_target="tpu_custom_call" | custom-call | bytes 1307648 | tf_op jit(solution)/shard_map/pallas_call | solution.py:481
  10.1 0.0 collective-permute-done.near_ref
  10.1 0.0 collective-permute-done.1.far_ref
  10.1 7.7 %shard_map.308 = (bf16[3072,128]{1,0:T(8,128)(2,1)}, f32[3072,128]{1,0:T(8,128)S(1)}, f32[1024,128]{1,0:T(8,128)S(1)}, bf16[128,128]{1,0:T(8,128)(2,1)S(1)}, bf16[128,128]{1,0:T(8,128)(2,1)S(1)}) custom-call(bf16[128,128]{1,0:T(8,128)(2,1)S(1)} %collective-permute-done.near_ref, bf16[128,128]{1,0:T(8,128)(2,1)S(1)} %collective-permute-done.1.far_ref, ...), custom_call_target="tpu_custom_call" | custom-call | bytes 4518912 | tf_op jit(solution)/shard_map/pallas_call | solution.py:481
  17.8 0.0 collective-permute-start.2
  17.8 3.6 %collective-permute-start.3 = (bf16[128,128]{1,0:T(8,128)(2,1)S(1)}, bf16[128,128]{1,0:T(8,128)(2,1)S(1)}, u32[]{:S(2)}, u32[]{:S(2)}) collective-permute-start(bf16[128,128]{1,0:T(8,128)(2,1)S(1)} %get-tuple-element.69), channel_id=1, source_target_pairs={{1,4},{5,8},{9,12},{4,1},{8,5},{12,9},{3,6},{7,10},{11,14},{6,3},{... | collective-permute-start | bytes 98312 | tf_op jit(solution)/shard_map/ppermute | solution.py:498
  21.4 0.0 collective-permute-done.2.near_ref
  21.4 1.6 %collective-permute-done.3.far_ref = bf16[128,128]{1,0:T(8,128)(2,1)S(1)} collective-permute-done((bf16[128,128]{1,0:T(8,128)(2,1)S(1)}, bf16[128,128]{1,0:T(8,128)(2,1)S(1)}, u32[]{:S(2)}, u32[]{:S(2)}) %collective-permute-start.3) | collective-permute-done | bytes 32800 | tf_op jit(solution)/shard_map/ppermute | solution.py:498
  23.0 1.8 %shard_map.309 = (bf16[1024,128]{1,0:T(8,128)(2,1)}, f32[1024,128]{1,0:T(8,128)S(1)}, bf16[1024,128]{1,0:T(8,128)(2,1)S(1)}, bf16[128,128]{1,0:T(8,128)(2,1)S(1)...) custom-call(bf16[1024,128]{1,0:T(8,128)(2,1)S(1)} %get-tuple-element.57.node_ref, ...), custom_call_target="tpu_custom_call" | custom-call | bytes 1373184 | tf_op jit(solution)/shard_map/pallas_call | solution.py:481
  24.8 0.1 collective-permute-start.4
  24.9 3.7 %collective-permute-start.5 = (bf16[128,128]{1,0:T(8,128)(2,1)S(1)}, bf16[128,128]{1,0:T(8,128)(2,1)S(1)}, u32[]{:S(2)}, u32[]{:S(2)}) collective-permute-start(bf16[128,128]{1,0:T(8,128)(2,1)S(1)} %get-tuple-element.77), channel_id=1, source_target_pairs={{1,4},{5,8},{9,12},{4,1},{8,5},{12,9},{3,6},{7,10},{11,14},{6,3},{... | collective-permute-start | bytes 98312 | tf_op jit(solution)/shard_map/ppermute | solution.py:498
  28.6 1.6 %collective-permute-done.5.dagg_far_ref = bf16[128,128]{1,0:T(8,128)(2,1)S(1)} collective-permute-done((bf16[128,128]{1,0:T(8,128)(2,1)S(1)}, bf16[128,128]{1,0:T(8,128)(2,1)S(1)}, u32[]{:S(2)}, u32[]{:S(2)}) %collective-permute-start.5) | collective-permute-done | bytes 32800 | tf_op jit(solution)/shard_map/ppermute | solution.py:498
  30.2 9.3 %shard_map.310 = (bf16[3072,128]{1,0:T(8,128)(2,1)}, f32[1024,128]{1,0:T(8,128)S(1)}, bf16[128,128]{1,0:T(8,128)(2,1)S(1)}, f32[512,128]{1,0:T(8,128)S(1)}, bf16[640,128]{1,0:T(8,128)(2,1)S(1)}) custom-call(f32[3072,128]{1,0:T(8,128)S(1)} %get-tuple-element.73.z_ref, bf16[3072,128]{1,0:T(8,128)(2,1)S(1)} %get-tuple-element.74.cot_ref, ...), custom_call_target="tpu_custom_call" | custom-call | bytes 7934976 | tf_op jit(solution)/shard_map/pallas_call | solution.py:481
  39.4 1.4 %collective-permute-done.6.near_ref.other_ref = bf16[640,128]{1,0:T(8,128)(2,1)S(1)} collective-permute-done((bf16[640,128]{1,0:T(8,128)(2,1)S(1)}, bf16[640,128]{1,0:T(8,128)(2,1)S(1)}, u32[]{:S(2)}, u32[]{:S(2)}) %collective-permute-start.6) | collective-permute-done | bytes 163872 | tf_op jit(solution)/shard_map/ppermute | solution.py:499
  40.8 10.9 %all_to_all.10.parts_ref = bf16[8,64,128]{2,1,0:T(8,128)(2,1)S(1)} all-to-all(bf16[8,64,128]{2,1,0:T(8,128)(2,1)S(1)} %bitcast.29), channel_id=1, replica_groups=mesh['groups'=2,'dom'=4,'sample'=2,'sub'=2] {'dom','sample'}, dimensions={0} | all-to-all | bytes 262144 | tf_op jit(solution)/shard_map/all_to_all | solution.py:663
  51.8 9.5 %all_to_all.11 = bf16[8,64,128]{2,1,0:T(8,128)(2,1)S(1)} all-to-all(bf16[8,64,128]{2,1,0:T(8,128)(2,1)S(1)} %shard_map.313), channel_id=1, replica_groups=mesh['groups'=2,'dom'=4,'sample'=2,'sub'=2] {'dom','sample'}, dimensions={0} | all-to-all | bytes 262144 | tf_op jit(solution)/shard_map/all_to_all | solution.py:665
  61.3 2.1 %collective-permute-start.8 = (bf16[512,128]{1,0:T(8,128)(2,1)S(1)}, bf16[512,128]{1,0:T(8,128)(2,1)S(1)}, u32[]{:S(2)}, u32[]{:S(2)}) collective-permute-start(bf16[512,128]{1,0:T(8,128)(2,1)S(1)} %bitcast.30), channel_id=1, source_target_pairs={{0,1},{1,0},{2,3},{3,2},{4,5},{5,4},{6,7},{7,6},{8,9},{9,8},{10,11... | collective-permute-start | bytes 393224 | tf_op jit(solution)/shard_map/ppermute | solution.py:669
  63.4 1.9 %collective-permute-start.7 = (bf16[128,128]{1,0:T(8,128)(2,1)S(1)}, bf16[128,128]{1,0:T(8,128)(2,1)S(1)}, u32[]{:S(2)}, u32[]{:S(2)}) collective-permute-start(bf16[128,128]{1,0:T(8,128)(2,1)S(1)} %get-tuple-element.83), channel_id=1, source_target_pairs={{1,4},{5,8},{9,12},{4,1},{8,5},{12,9},{3,6},{7,10},{11,14},{6,3},{... | collective-permute-start | bytes 98312 | tf_op jit(solution)/shard_map/ppermute | solution.py:498
  65.3 3.3 %collective-permute-done.7.far_ref = bf16[128,128]{1,0:T(8,128)(2,1)S(1)} collective-permute-done((bf16[128,128]{1,0:T(8,128)(2,1)S(1)}, bf16[128,128]{1,0:T(8,128)(2,1)S(1)}, u32[]{:S(2)}, u32[]{:S(2)}) %collective-permute-start.7) | collective-permute-done | bytes 32800 | tf_op jit(solution)/shard_map/ppermute | solution.py:498
  68.6 1.0 %shard_map.311 = bf16[1024,128]{1,0:T(8,128)(2,1)} custom-call(f32[1024,128]{1,0:T(8,128)S(1)} %get-tuple-element.81.acc_ref, bf16[640,128]{1,0:T(8,128)(2,1)S(1)} %collective-permute-done.6.near_ref.other_ref, bf16[128,128]{1,0:T(8,128)(2,1)S(1)} %collective-permute-done.7.far_ref, s32[50,128]{1,0:T(8,128)S(1)} %get-tuple-element.61.ids_ref), custom_call_target="tpu_custom_call" | custom-call | bytes 746496 | tf_op jit(solution)/shard_map/pallas_call | solution.py:481
  69.6 0.8 %shard_map.314 = (f32[384,128]{1,0:T(8,128)}, f32[128,128]{1,0:T(8,128)}, f32[256,128]{1,0:T(8,128)}, f32[128,128]{1,0:T(8,128)}, f32[1,128]{1,0:T(1,128)}, /*in...) custom-call(bf16[512,128]{1,0:T(8,128)(2,1)S(1)} %bitcast.31, ...), custom_call_target="tpu_custom_call" | custom-call | bytes 262144 | tf_op jit(solution)/shard_map/pallas_call | solution.py:481
  (5 shorter events, 0.1 us)
Async XLA Ops:
  2.5 7.6 %collective-permute-start = (bf16[128,128]{1,0:T(8,128)(2,1)S(1)}, bf16[128,128]{1,0:T(8,128)(2,1)S(1)}, u32[]{:S(2)}, u32[]{:S(2)}) collective-permute-start(bf16[128,128]{1,0:T(8,128)(2,1)S(1)} %get-tuple-element.58), channel_id=1, source_target_pairs={{0,1},{4,5},{8,9},{12,13},{1,0},{5,4},{9,8},{13,12},{2,3},{6,7},{1... | collective-permute-start | bytes 98312 | tf_op jit(solution)/shard_map/ppermute | solution.py:499
  2.7 7.5 %collective-permute-start.1 = (bf16[128,128]{1,0:T(8,128)(2,1)S(1)}, bf16[128,128]{1,0:T(8,128)(2,1)S(1)}, u32[]{:S(2)}, u32[]{:S(2)}) collective-permute-start(bf16[128,128]{1,0:T(8,128)(2,1)S(1)} %get-tuple-element.59), channel_id=1, source_target_pairs={{1,4},{5,8},{9,12},{4,1},{8,5},{12,9},{3,6},{7,10},{11,14},{6,3},{... | collective-permute-start | bytes 98312 | tf_op jit(solution)/shard_map/ppermute | solution.py:498
  17.8 3.6 %collective-permute-start.2 = (bf16[128,128]{1,0:T(8,128)(2,1)S(1)}, bf16[128,128]{1,0:T(8,128)(2,1)S(1)}, u32[]{:S(2)}, u32[]{:S(2)}) collective-permute-start(bf16[128,128]{1,0:T(8,128)(2,1)S(1)} %get-tuple-element.68), channel_id=1, source_target_pairs={{0,1},{4,5},{8,9},{12,13},{1,0},{5,4},{9,8},{13,12},{2,3},{6,7},{1... | collective-permute-start | bytes 98312 | tf_op jit(solution)/shard_map/ppermute | solution.py:499
  17.8 5.2 %collective-permute-start.3 = (bf16[128,128]{1,0:T(8,128)(2,1)S(1)}, bf16[128,128]{1,0:T(8,128)(2,1)S(1)}, u32[]{:S(2)}, u32[]{:S(2)}) collective-permute-start(bf16[128,128]{1,0:T(8,128)(2,1)S(1)} %get-tuple-element.69), channel_id=1, source_target_pairs={{1,4},{5,8},{9,12},{4,1},{8,5},{12,9},{3,6},{7,10},{11,14},{6,3},{... | collective-permute-start | bytes 98312 | tf_op jit(solution)/shard_map/ppermute | solution.py:498
  24.8 3.8 %collective-permute-start.4 = (bf16[128,128]{1,0:T(8,128)(2,1)S(1)}, bf16[128,128]{1,0:T(8,128)(2,1)S(1)}, u32[]{:S(2)}, u32[]{:S(2)}) collective-permute-start(bf16[128,128]{1,0:T(8,128)(2,1)S(1)} %get-tuple-element.76), channel_id=1, source_target_pairs={{0,1},{4,5},{8,9},{12,13},{1,0},{5,4},{9,8},{13,12},{2,3},{6,7},{1... | collective-permute-start | bytes 98312 | tf_op jit(solution)/shard_map/ppermute | solution.py:499
  24.9 5.3 %collective-permute-start.5 = (bf16[128,128]{1,0:T(8,128)(2,1)S(1)}, bf16[128,128]{1,0:T(8,128)(2,1)S(1)}, u32[]{:S(2)}, u32[]{:S(2)}) collective-permute-start(bf16[128,128]{1,0:T(8,128)(2,1)S(1)} %get-tuple-element.77), channel_id=1, source_target_pairs={{1,4},{5,8},{9,12},{4,1},{8,5},{12,9},{3,6},{7,10},{11,14},{6,3},{... | collective-permute-start | bytes 98312 | tf_op jit(solution)/shard_map/ppermute | solution.py:498
  39.4 1.4 %collective-permute-start.6 = (bf16[640,128]{1,0:T(8,128)(2,1)S(1)}, bf16[640,128]{1,0:T(8,128)(2,1)S(1)}, u32[]{:S(2)}, u32[]{:S(2)}) collective-permute-start(bf16[640,128]{1,0:T(8,128)(2,1)S(1)} %get-tuple-element.82), channel_id=1, source_target_pairs={{0,1},{4,5},{8,9},{12,13},{1,0},{5,4},{9,8},{13,12},{2,3},{6,7},{1... | collective-permute-start | bytes 491528 | tf_op jit(solution)/shard_map/ppermute | solution.py:499
  61.3 8.3 %collective-permute-start.8 = (bf16[512,128]{1,0:T(8,128)(2,1)S(1)}, bf16[512,128]{1,0:T(8,128)(2,1)S(1)}, u32[]{:S(2)}, u32[]{:S(2)}) collective-permute-start(bf16[512,128]{1,0:T(8,128)(2,1)S(1)} %bitcast.30), channel_id=1, source_target_pairs={{0,1},{1,0},{2,3},{3,2},{4,5},{5,4},{6,7},{7,6},{8,9},{9,8},{10,11... | collective-permute-start | bytes 393224 | tf_op jit(solution)/shard_map/ppermute | solution.py:669
  63.4 5.2 %collective-permute-start.7 = (bf16[128,128]{1,0:T(8,128)(2,1)S(1)}, bf16[128,128]{1,0:T(8,128)(2,1)S(1)}, u32[]{:S(2)}, u32[]{:S(2)}) collective-permute-start(bf16[128,128]{1,0:T(8,128)(2,1)S(1)} %get-tuple-element.83), channel_id=1, source_target_pairs={{1,4},{5,8},{9,12},{4,1},{8,5},{12,9},{3,6},{7,10},{11,14},{6,3},{... | collective-permute-start | bytes 98312 | tf_op jit(solution)/shard_map/ppermute | solution.py:498

commit v4 on v3

--- a/solution.py
+++ b/solution.py
@@ -1,6 +1,3 @@
-import functools
-import math
-
 import jax
 import jax.numpy as jnp
 from jax import lax
@@ -208,7 +205,7 @@
     rcv_local,
     out_ref,
     z_ref,
-    agg_ref,
+    message_ref,
     agg_near_ref,
     agg_far_ref,
     halo,
@@ -243,15 +240,35 @@
         normed, unused = normed_of(act, w2_pair[...], b2)
         update = normed * gain + shift
         out_ref[rows, :] = (x.astype(f32) + update).astype(bf16)
+        message = update.astype(bf16)
+        message_ref[rows, :] = message
         first = (rcv_column.shape[0] + i * edge_tile) // lane
-        total[...] += spread(ids_ref, first, edge_tile // lane, half, rcv, update)
+        parts = [
+            hot_rows(ids_ref[pl.ds(first + k, 1), :] - nodes, 2 * rim)
+            for k in range(edge_tile // lane)
+        ]
+        total[...] += dot(jnp.concatenate(parts, axis=1), message)
         return carry
 
     lax.fori_loop(0, edge_ref.shape[0] // edge_tile, tile, 0)
+    agg_near_ref[...] = total[pl.ds(near_at, rim), :].astype(bf16)
+    agg_far_ref[...] = total[pl.ds(far_at, rim), :].astype(bf16)
+
+
+def collect_kernel(ids_ref, rcv_column, message_ref, agg_ref, total):
+    half = total.shape[0]
+    total[...] = jnp.zeros_like(total)
+
+    def tile(i, carry):
+        rows = pl.ds(pl.multiple_of(i * edge_tile, edge_tile), edge_tile)
+        first = (rcv_column.shape[0] + i * edge_tile) // lane
+        message = message_ref[rows, :].astype(f32)
+        total[...] += spread(ids_ref, first, edge_tile // lane, half, rcv_column[rows, :], message)
+        return carry
+
+    lax.fori_loop(0, rcv_column.shape[0] // edge_tile, tile, 0)
     agg_ref[:half, :] = total[:, :lane]
-    agg_ref[half:, :] = total[: nodes - half, lane:]
-    agg_near_ref[...] = total[pl.ds(nodes - half + near_at, rim), lane:].astype(bf16)
-    agg_far_ref[...] = total[pl.ds(nodes - half + far_at, rim), lane:].astype(bf16)
+    agg_ref[half:, :] = total[:, lane:]
 
 
 def hot_lists(ids_ref, nodes):
@@ -316,25 +333,35 @@
     grads_ref[second:, :] = jnp.concatenate(sums, axis=0)
 
 
+def upstream_kernel(rcv_column, dagg_ref, cot_ref, up_ref, table):
+    table[...] = side_by_side(dagg_ref[...])
+
+    def tile(i, carry):
+        rows = pl.ds(pl.multiple_of(i * edge_tile, edge_tile), edge_tile)
+        up_ref[rows, :] = cot_ref[rows, :].astype(f32) + pick(rcv_column[rows, :], table[...])
+        return carry
+
+    lax.fori_loop(0, cot_ref.shape[0] // edge_tile, tile, 0)
+
+
 def edge_backward_kernel(
     z_ref,
-    cot_ref,
+    up_ref,
     edge_ref,
     ids_ref,
     node_ref,
     near_ref,
     far_ref,
-    dagg_ref,
     dagg_near_ref,
     dagg_far_ref,
-    base_ref,
     weights_ref,
     vectors_ref,
     node_grads_ref,
     snd_column,
     rcv_column,
-    grad_ref,
-    acc_ref,
+    dz_ref,
+    snd_sum_ref,
+    rcv_sum_ref,
     far_back_ref,
     kept_ref,
     sent_ref,
@@ -354,13 +381,10 @@
     parity = parity_of_place()
     near_at = pl.multiple_of((1 - parity) * rim, rim)
     far_at = pl.multiple_of(parity * rim, rim)
-    w1_edge = weights_ref[:lane]
     w2 = weights_ref[3 * lane : 4 * lane]
     gain = vector(vectors_ref, 2)
-    table[:, :lane] = dagg_ref[:rcv_half, :]
-    table[: nodes - rcv_half, lane:] = dagg_ref[rcv_half:, :]
-    table[pl.ds(nodes - rcv_half + near_at, rim), lane:] = dagg_near_ref[...]
-    table[pl.ds(nodes - rcv_half + far_at, rim), lane:] = dagg_far_ref[...]
+    table[pl.ds(near_at, rim), :] = dagg_near_ref[...]
+    table[pl.ds(far_at, rim), :] = dagg_far_ref[...]
     halo[pl.ds(near_at, rim), :] = near_ref[...]
     halo[pl.ds(far_at, rim), :] = far_ref[...]
     pair, b2 = centred_second(w2, vector(vectors_ref, 1))
@@ -377,8 +401,7 @@
         snd = snd_column[rows, :]
         x = edge_ref[rows, :]
         z = z_ref[rows, :]
-        cot = cot_ref[rows, :].astype(f32)
-        upstream = cot + pick(rcv, table[...])
+        upstream = up_ref[rows, :] + dot(hot_columns(rcv - nodes, 2 * rim), table[...])
         sig = sigmoid(z)
         act = (z * sig).astype(bf16)
         normed, scale_inv = normed_of(act, w2_pair[...], b2)
@@ -387,7 +410,7 @@
         da = dot_back(dz2b, w2)
         dz1 = da * sig * (1.0 + z * (1.0 - sig))
         dz1b = dz1.astype(bf16)
-        grad_ref[rows, :] = (cot + dot_back(dz1b, w1_edge)).astype(bf16)
+        dz_ref[rows, :] = dz1b
         squares[:lane, :] += dot_rows(x, dz1b)
         squares[lane:, :] += dot_rows(act, dz2b)
         sums[0:1, :] += column_sum(dz1)
@@ -402,9 +425,9 @@
     lax.fori_loop(0, edge_ref.shape[0] // edge_tile, tile, 0)
     snd_sum = jnp.concatenate([snd_total[:, :lane], snd_total[:, lane:]], axis=0).astype(bf16)
     rcv_sum = jnp.concatenate([rcv_total[:, :lane], rcv_total[:, lane:]], axis=0).astype(bf16)
-    w1_snd = weights_ref[lane : 2 * lane]
+    snd_sum_ref[...] = snd_sum
+    rcv_sum_ref[...] = rcv_sum[:nodes]
     w1_rcv = weights_ref[2 * lane : 3 * lane]
-    acc_ref[...] = base_ref[...] + dot_back(snd_sum, w1_snd) + dot_back(rcv_sum[:nodes], w1_rcv)
     kept = kept_ref.shape[0]
     for at, back_ref in ((near_at, sent_ref.at[kept:]), (far_at, far_back_ref)):
         returned = rcv_total[pl.ds(nodes - rcv_half + at, rim), lane:].astype(bf16)
@@ -426,39 +449,45 @@
             (grads_ref.shape[0] - last - sum_rows, lane), f32
         )
     own = lax.axis_index("sub")
-    kept_ref[...] = grads_ref[pl.ds(pl.multiple_of(own * kept, kept), kept), :]
-    other = pl.multiple_of((1 - own) * kept, kept)
+    kept_ref[...] = grads_ref[pl.ds(pl.multiple_of(own * kept, sum_rows), kept), :]
+    other = pl.multiple_of((1 - own) * kept, sum_rows)
     sent_ref[:kept, :] = grads_ref[pl.ds(other, kept), :].astype(bf16)
 
 
-def node_grad_kernel(acc_ref, near_ref, far_ref, ids_ref, out_ref):
+def edge_grad_kernel(dz_ref, cot_ref, weights_ref, out_ref):
+    w1_edge = weights_ref[:lane]
+
+    def tile(i, carry):
+        rows = pl.ds(pl.multiple_of(i * edge_tile, edge_tile), edge_tile)
+        cot = cot_ref[rows, :].astype(f32)
+        out_ref[rows, :] = (cot + dot_back(dz_ref[rows, :], w1_edge)).astype(bf16)
+        return carry
+
+    lax.fori_loop(0, cot_ref.shape[0] // edge_tile, tile, 0)
+
+
+def node_grad_kernel(
+    base_ref, snd_sum_ref, rcv_sum_ref, weights_ref, near_ref, far_ref, ids_ref, out_ref
+):
     rim = far_ref.shape[0]
     returned = jnp.concatenate([near_ref[near_ref.shape[0] - rim :, :], far_ref[...]], axis=0)
-    hot = hot_lists(ids_ref, acc_ref.shape[0])
-    out_ref[...] = (acc_ref[...] + dot(hot, returned)).astype(bf16)
-
-
-def halves_kernel(kept_ref, other_ref, out_ref):
-    kept = kept_ref.shape[0]
-    out_ref[...] = (kept_ref[...] + other_ref[:kept, :].astype(f32)).astype(bf16)
-
-
-def share_kernel(parts_ref, out_ref):
-    count = parts_ref.shape[0]
-    total = parts_ref[0].astype(f32)
-    for k in range(1, count):
-        total = total + parts_ref[k].astype(f32)
-    total = total.astype(bf16)
-    for k in range(count):
-        out_ref[k] = total
+    total = base_ref[...] + dot_back(snd_sum_ref[...], weights_ref[lane : 2 * lane])
+    total = total + dot_back(rcv_sum_ref[...], weights_ref[2 * lane : 3 * lane])
+    hot = hot_lists(ids_ref, base_ref.shape[0])
+    out_ref[...] = (total + dot(hot, returned)).astype(bf16)
+
+
+def add_kernel(own_ref, other_ref, *refs):
+    own = own_ref[...].astype(f32)
+    refs[-1][...] = (own + other_ref[: own.shape[0], :].astype(f32)).astype(bf16)
 
 
 def finish_kernel(own_ref, other_ref, *refs):
     out_refs, total_ref = refs[:-1], refs[-1]
     kept = own_ref.shape[0]
     own = lax.axis_index("sub")
-    total_ref[pl.ds(pl.multiple_of(own * kept, kept), kept), :] = own_ref[...].astype(f32)
-    other = pl.multiple_of((1 - own) * kept, kept)
+    total_ref[pl.ds(pl.multiple_of(own * kept, sum_rows), kept), :] = own_ref[...].astype(f32)
+    other = pl.multiple_of((1 - own) * kept, sum_rows)
     total_ref[pl.ds(other, kept), :] = other_ref[...].astype(f32)
     at = 0
     for out_ref in out_refs[:4]:
@@ -497,6 +526,15 @@
     inner += [(target, source) for source, target in inner]
     far = lax.ppermute(far, chain, outer)
     return lax.ppermute(near, chain, inner), far
+
+
+def sum_rounds():
+    for axis in ("sample", "dom"):
+        count = lax.axis_size(axis)
+        step = 1
+        while step < count:
+            yield axis, [(i, i ^ step) for i in range(count)]
+            step *= 2
 
 
 def on_device(
@@ -528,11 +566,7 @@
     rim_shape = ((rim, lane), bf16)
     snd_half = nodes // 2
     rcv_half = (nodes + 2 * rim) // 2
-    members = ("dom", "sample")
-    sharers = math.prod(lax.axis_size(axis) for axis in members)
-    grad_rows = 7 * lane + sum_rows
-    share = -(-grad_rows // (2 * sharers * sum_rows)) * sum_rows
-    kept = sharers * share
+    kept = -(-(7 * lane + sum_rows) // (2 * sum_rows)) * sum_rows
     row = lambda x: x.reshape(1, lane)
     small = [w_edge_first, w_edge_second, w_node_first, w_node_second]
     small += [row(b_edge_first), row(b_edge_second), row(edge_gain), row(edge_shift)]
@@ -581,14 +615,14 @@
         vectors,
         edge,
     )
-    edge_out, z, agg, agg_near, agg_far = call(
+    edge_out, z, message, agg_near, agg_far = call(
         edge_forward_kernel,
-        [((edges, lane), bf16), ((edges, lane), f32), ((nodes, lane), f32), rim_shape, rim_shape],
+        [((edges, lane), bf16), ((edges, lane), f32), ((edges, lane), bf16), rim_shape, rim_shape],
         [
             ((2 * rim, lane), bf16),
             ((rcv_half, 2 * lane), bf16),
             ((lane, 2 * lane), bf16),
-            ((rcv_half, 2 * lane), f32),
+            ((2 * rim, lane), f32),
         ],
         near,
         far,
@@ -601,6 +635,14 @@
         rcv_local,
     )
     back_near, back_far = swap(agg_near, agg_far)
+    (agg,) = call(
+        collect_kernel,
+        [((nodes, lane), f32)],
+        [((snd_half, 2 * lane), f32)],
+        ids,
+        rcv_column,
+        message,
+    )
     node_out, base, dagg, dagg_rim_near, dagg_rim_far, node_grads = call(
         node_kernel,
         [
@@ -622,11 +664,20 @@
         node_cot,
     )
     dagg_near, dagg_far = swap(dagg_rim_near, dagg_rim_far)
-    edge_grad, acc, grad_far, grads_kept, grads_sent = call(
+    (upstream,) = call(
+        upstream_kernel,
+        [((edges, lane), f32)],
+        [((snd_half, 2 * lane), bf16)],
+        rcv_column,
+        dagg,
+        edge_cot,
+    )
+    dz, snd_sum, rcv_sum, grad_far, grads_kept, grads_sent = call(
         edge_backward_kernel,
         [
             ((edges, lane), bf16),
-            ((nodes, lane), f32),
+            ((nodes, lane), bf16),
+            ((nodes, lane), bf16),
             rim_shape,
             ((kept, lane), f32),
             ((kept + rim, lane), bf16),
@@ -634,7 +685,7 @@
         [
             ((2 * rim, lane), bf16),
             ((2 * kept, lane), f32),
-            ((rcv_half, 2 * lane), bf16),
+            ((2 * rim, lane), bf16),
             ((lane, 2 * lane), bf16),
             ((snd_half, 2 * lane), f32),
             ((rcv_half, 2 * lane), f32),
@@ -642,16 +693,14 @@
             ((8, lane), f32),
         ],
         z,
-        edge_cot,
+        upstream,
         edge,
         ids,
         node,
         near,
         far,
-        dagg,
         dagg_near,
         dagg_far,
-        base,
         weights,
         vectors,
         node_grads,
@@ -659,20 +708,36 @@
         rcv_column,
     )
     returned_near, returned_far = swap(grads_sent, grad_far)
-    (halves,) = call(halves_kernel, [((kept, lane), bf16)], [], grads_kept, returned_near)
-    parts = lax.all_to_all(halves.reshape(sharers, share, lane), members, 0, 0, tiled=True)
-    (shares,) = call(share_kernel, [(parts.shape, bf16)], [], parts)
-    shares = lax.all_to_all(shares, members, 0, 0, tiled=True).reshape(kept, lane)
+    (edge_grad,) = call(
+        edge_grad_kernel, [((edges, lane), bf16)], [], dz, edge_cot, weights
+    )
     (node_grad,) = call(
-        node_grad_kernel, [((nodes, lane), bf16)], [], acc, returned_near, returned_far, ids
-    )
-    others = lax.ppermute(shares, "sub", [(0, 1), (1, 0)])
+        node_grad_kernel,
+        [((nodes, lane), bf16)],
+        [],
+        base,
+        snd_sum,
+        rcv_sum,
+        weights,
+        returned_near,
+        returned_far,
+        ids,
+    )
+    half_shape = ((kept, lane), bf16)
+    (grads,) = call(add_kernel, [half_shape], [], grads_kept, returned_near)
+    between = [[returned_far, edge_grad], [node_grad]]
+    for number, (axis, pairs) in enumerate(sum_rounds()):
+        other = lax.ppermute(grads, axis, pairs)
+        early = between[number] if number < len(between) else []
+        written = 1 if early else 0
+        (grads,) = call(add_kernel, [half_shape], [], grads, other, *early, anywhere=written)
+    others = lax.ppermute(grads, "sub", [(0, 1), (1, 0)])
     matrices = [3 * lane, lane, 2 * lane, lane]
     totals = call(
         finish_kernel,
         [((height, lane), f32) for height in matrices] + [((1, lane), f32)] * 8,
         [((2 * kept, lane), f32)],
-        shares,
+        grads,
         others,
     )
     flat = [total.reshape(lane) for total in totals[4:]]

time: 70.8 us -> 62.5 us (0.88)
  blocking collectives: 20.5 us -> 0 us
  waiting for transfers between devices: 7.9 us -> 13 us
  starting transfers between devices: 16 us -> 19.5 us
  Pallas kernels: 25.3 us -> 28.7 us
    all_to_all x2 -> x0, blocking collectives: 20.5 us -> none  [the longest x1 10.9 us: on_device(): lax.all_to_all(halves.reshape(sharers, share, lane), members, 0, 0, tiled...]
    ppermute x1 -> x4, waiting for transfers between devices: 0.01 us -> 11.6 us  [the longest x3 10.7 us: on_device(): other = lax.ppermute(grads, axis, pairs)]
    ppermute x4, waiting for transfers between devices: 6.5 us -> 0.01 us  [swap(): far = lax.ppermute(far, chain, outer)]
    pallas_call x9 -> x14, Pallas kernels: 25.3 us -> 28.7 us  [call(): pl.pallas_call(kernel, out_shape=[jax.ShapeDtypeStruct(shape, dtype) for...]
    ppermute x1 -> x4, starting transfers between devices: 2.07 us -> 3.88 us  [the longest x3 3.32 us: on_device(): other = lax.ppermute(grads, axis, pairs)]
    ppermute x4, starting transfers between devices: 13.7 us -> 15.3 us  [swap(): far = lax.ppermute(far, chain, outer)]
  transfers between devices with their start and end apart: 9 -> 12, of which waited for: 4 -> 4; matrix products, arithmetic and copies ran while one was open for 0% -> 0% of each run, Pallas kernels for 6% -> 16%
where the time goes in v4:
time: 62.5 us; the launch traced here: 62 us
  Pallas kernels  28.7 us (46%)
  starting transfers between devices  19.5 us (31%)
  waiting for transfers between devices  13 us (21%)
  between operations  0.81 us (1%)
    pallas_call x14, Pallas kernels, call(): pl.pallas_call(kernel, out_shape=[jax.ShapeDtypeStruct(shape, dtype) for...  28.7 us
    ppermute x4, starting transfers between devices, swap(): far = lax.ppermute(far, chain, outer)  15.3 us
    ppermute x3, waiting for transfers between devices, on_device(): other = lax.ppermute(grads, axis, pairs)  10.7 us
    ppermute x3, starting transfers between devices, on_device(): other = lax.ppermute(grads, axis, pairs)  3.32 us
    ppermute x4, waiting for transfers between devices, swap(): return (lax.ppermute(near, chain, inner), far)  1.37 us
  transfers between devices with their start and end apart: 12, of which 4 were waited for; matrix products, arithmetic and copies ran while one was open for 0% of the time, Pallas kernels for 16%

profile of v4, /device:TPU:1, one launch (start us, length us, event | category | flops | bytes accessed | tf_op | source)
XLA Modules:
  0.0 62.0 jit_solution(15963057312292194497)
XLA Ops:
  0.7 1.9 %shard_map.306 = (bf16[1024,128]{1,0:T(8,128)(2,1)S(1)}, s32[50,128]{1,0:T(8,128)S(1)}, bf16[3072,128]{1,0:T(8,128)(2,1)S(1)}, bf16[3072,128]{1,0:T(8,128)(2,1)S...) custom-call(bf16[1024,128]{1,0:T(8,128)(2,1)} %bitcast.31, ...), custom_call_target="tpu_custom_call" | custom-call | bytes 2356224 | tf_op jit(solution)/shard_map/pallas_call | solution.py:510
  2.5 0.1 collective-permute-start
  2.7 4.6 %collective-permute-start.1 = (bf16[128,128]{1,0:T(8,128)(2,1)S(1)}, bf16[128,128]{1,0:T(8,128)(2,1)S(1)}, u32[]{:S(2)}, u32[]{:S(2)}) collective-permute-start(bf16[128,128]{1,0:T(8,128)(2,1)S(1)} %get-tuple-element.65), channel_id=1, source_target_pairs={{1,4},{5,8},{9,12},{4,1},{8,5},{12,9},{3,6},{7,10},{11,14},{6,3},{... | collective-permute-start | bytes 98312 | tf_op jit(solution)/shard_map/ppermute | solution.py:527
  7.2 2.9 %shard_map.307 = (s32[3072,128]{1,0:T(8,128)S(1)}, s32[3072,128]{1,0:T(8,128)S(1)}, f32[3072,128]{1,0:T(8,128)S(1)}, bf16[1024,128]{1,0:T(8,128)(2,1)S(1)}) custom-call(s32[50,128]{1,0:T(8,128)S(1)} %get-tuple-element.59.ids_ref, bf16[1024,128]{1,0:T(8,128)(2,1)S(1)} %get-tuple-element.58.node_ref, bf16[896,128]{1,0:T(8,128)(2,1)S(1)} %get-tuple-element.60.weights_ref, ...), custom_call_target="tpu_custom_call" | custom-call | bytes 1307648 | tf_op jit(solution)/shard_map/pallas_call | solution.py:510
  10.2 6.7 %shard_map.308 = (bf16[3072,128]{1,0:T(8,128)(2,1)}, f32[3072,128]{1,0:T(8,128)S(1)}, bf16[3072,128]{1,0:T(8,128)(2,1)S(1)}, bf16[128,128]{1,0:T(8,128)(2,1)S(1)}, bf16[128,128]{1,0:T(8,128)(2,1)S(1)}) custom-call(bf16[128,128]{1,0:T(8,128)(2,1)S(1)} %collective-permute-done.near_ref, bf16[128,128]{1,0:T(8,128)(2,1)S(1)} %collective-permute-done.1.far_ref, ...), custom_call_target="tpu_custom_call" | custom-call | bytes 4518912 | tf_op jit(solution)/shard_map/pallas_call | solution.py:510
  16.9 3.6 %collective-permute-start.3 = (bf16[128,128]{1,0:T(8,128)(2,1)S(1)}, bf16[128,128]{1,0:T(8,128)(2,1)S(1)}, u32[]{:S(2)}, u32[]{:S(2)}) collective-permute-start(bf16[128,128]{1,0:T(8,128)(2,1)S(1)} %get-tuple-element.70), channel_id=1, source_target_pairs={{1,4},{5,8},{9,12},{4,1},{8,5},{12,9},{3,6},{7,10},{11,14},{6,3},{... | collective-permute-start | bytes 98312 | tf_op jit(solution)/shard_map/ppermute | solution.py:527
  20.5 2.1 %shard_map.309.agg_ref = f32[1024,128]{1,0:T(8,128)S(1)} custom-call(s32[50,128]{1,0:T(8,128)S(1)} %get-tuple-element.59.ids_ref, s32[3072,128]{1,0:T(8,128)S(1)} %get-tuple-element.63.rcv_column, bf16[3072,128]{1,0:T(8,128)(2,1)S(1)} %get-tuple-element.68.message_ref), custom_call_target="tpu_custom_call" | custom-call | bytes 2384896 | tf_op jit(solution)/shard_map/pallas_call | solution.py:510
  22.6 1.8 %shard_map.310 = (bf16[1024,128]{1,0:T(8,128)(2,1)}, f32[1024,128]{1,0:T(8,128)S(1)}, bf16[1024,128]{1,0:T(8,128)(2,1)S(1)}, bf16[128,128]{1,0:T(8,128)(2,1)S(1)...) custom-call(bf16[1024,128]{1,0:T(8,128)(2,1)S(1)} %get-tuple-element.58.node_ref, ...), custom_call_target="tpu_custom_call" | custom-call | bytes 1373184 | tf_op jit(solution)/shard_map/pallas_call | solution.py:510
  24.4 0.1 collective-permute-start.4
  24.5 3.6 %collective-permute-start.5 = (bf16[128,128]{1,0:T(8,128)(2,1)S(1)}, bf16[128,128]{1,0:T(8,128)(2,1)S(1)}, u32[]{:S(2)}, u32[]{:S(2)}) collective-permute-start(bf16[128,128]{1,0:T(8,128)(2,1)S(1)} %get-tuple-element.79), channel_id=1, source_target_pairs={{1,4},{5,8},{9,12},{4,1},{8,5},{12,9},{3,6},{7,10},{11,14},{6,3},{... | collective-permute-start | bytes 98312 | tf_op jit(solution)/shard_map/ppermute | solution.py:527
  28.0 1.8 %shard_map.311.up_ref = f32[3072,128]{1,0:T(8,128)S(1)} custom-call(s32[3072,128]{1,0:T(8,128)S(1)} %get-tuple-element.63.rcv_column, bf16[1024,128]{1,0:T(8,128)(2,1)S(1)} %get-tuple-element.76.dagg_ref, bf16[3072,128]{1,0:T(8,128)(2,1)S(1)} %get-tuple-element.77.cot_ref), custom_call_target="tpu_custom_call" | custom-call | bytes 2621440 | tf_op jit(solution)/shard_map/pallas_call | solution.py:510
  29.9 7.3 %shard_map.312 = (bf16[3072,128]{1,0:T(8,128)(2,1)S(1)}, bf16[1024,128]{1,0:T(8,128)(2,1)S(1)}, bf16[1024,128]{1,0:T(8,128)(2,1)S(1)}, bf16[128,128]{1,0:T(8,128...) custom-call(f32[3072,128]{1,0:T(8,128)S(1)} %get-tuple-element.75.z_ref, ...), custom_call_target="tpu_custom_call" | custom-call | bytes 7934976 | tf_op jit(solution)/shard_map/pallas_call | solution.py:510
  37.3 1.4 %collective-permute-done.6.near_ref.other_ref = bf16[592,128]{1,0:T(8,128)(2,1)S(1)} collective-permute-done((bf16[592,128]{1,0:T(8,128)(2,1)S(1)}, bf16[592,128]{1,0:T(8,128)(2,1)S(1)}, u32[]{:S(2)}, u32[]{:S(2)}) %collective-permute-start.6) | collective-permute-done | bytes 151584 | tf_op jit(solution)/shard_map/ppermute | solution.py:528
  38.7 1.3 %collective-permute-start.8 = (bf16[464,128]{1,0:T(8,128)(2,1)S(1)}, bf16[464,128]{1,0:T(8,128)(2,1)S(1)}, u32[]{:S(2)}, u32[]{:S(2)}) collective-permute-start(bf16[464,128]{1,0:T(8,128)(2,1)S(1)} %shard_map.315.own_ref), channel_id=1, source_target_pairs={{0,2},{2,0},{1,3},{3,1},{4,6},{6,4},{5,7},{7,5},{8,10},{10,8},{9,1... | collective-permute-start | bytes 356360 | tf_op jit(solution)/shard_map/ppermute | solution.py:730
  40.0 3.6 %collective-permute-start.7 = (bf16[128,128]{1,0:T(8,128)(2,1)S(1)}, bf16[128,128]{1,0:T(8,128)(2,1)S(1)}, u32[]{:S(2)}, u32[]{:S(2)}) collective-permute-start(bf16[128,128]{1,0:T(8,128)(2,1)S(1)} %get-tuple-element.85), channel_id=1, source_target_pairs={{1,4},{5,8},{9,12},{4,1},{8,5},{12,9},{3,6},{7,10},{11,14},{6,3},{... | collective-permute-start | bytes 98312 | tf_op jit(solution)/shard_map/ppermute | solution.py:527
  43.6 2.0 %shard_map.314.refs_1_ = bf16[3072,128]{1,0:T(8,128)(2,1)} custom-call(bf16[3072,128]{1,0:T(8,128)(2,1)S(1)} %get-tuple-element.86.dz_ref, bf16[3072,128]{1,0:T(8,128)(2,1)S(1)} %get-tuple-element.77.cot_ref, bf16[896,128]{1,0:T(8,128)(2,1)S(1)} %get-tuple-element.60.weights_ref), custom_call_target="tpu_custom_call" | custom-call | bytes 1802240 | tf_op jit(solution)/shard_map/pallas_call | solution.py:510
  45.7 1.1 %collective-permute-start.9 = (bf16[464,128]{1,0:T(8,128)(2,1)S(1)}, bf16[464,128]{1,0:T(8,128)(2,1)S(1)}, u32[]{:S(2)}, u32[]{:S(2)}) collective-permute-start(bf16[464,128]{1,0:T(8,128)(2,1)S(1)} %shard_map.316.own_ref), channel_id=1, source_target_pairs={{0,4},{4,0},{8,12},{12,8},{1,5},{5,1},{9,13},{13,9},{2,6},{6,2},{1... | collective-permute-start | bytes 356360 | tf_op jit(solution)/shard_map/ppermute | solution.py:730
  46.8 1.1 %shard_map.313.refs_0_ = bf16[1024,128]{1,0:T(8,128)(2,1)} custom-call(f32[1024,128]{1,0:T(8,128)S(1)} %get-tuple-element.74.base_ref, bf16[1024,128]{1,0:T(8,128)(2,1)S(1)} %get-tuple-element.82.snd_sum_ref, bf16[1024,128]{1,0:T(8,128)(2,1)S(1)} %get-tuple-element.83.rcv_sum_ref, bf16[896,128]{1,0:T(8,128)(2,1)S(1)} %get-tuple-element.60.weights_ref, ...), custom_call_target="tpu_custom_call" | custom-call | bytes 1487872 | tf_op jit(solution)/shard_map/pallas_call | solution.py:510
  47.9 3.0 %collective-permute-done.9.other_ref = bf16[464,128]{1,0:T(8,128)(2,1)S(1)} collective-permute-done((bf16[464,128]{1,0:T(8,128)(2,1)S(1)}, bf16[464,128]{1,0:T(8,128)(2,1)S(1)}, u32[]{:S(2)}, u32[]{:S(2)}) %collective-permute-start.9) | collective-permute-done | bytes 118816 | tf_op jit(solution)/shard_map/ppermute | solution.py:730
  50.9 1.0 %collective-permute-start.10 = (bf16[464,128]{1,0:T(8,128)(2,1)S(1)}, bf16[464,128]{1,0:T(8,128)(2,1)S(1)}, u32[]{:S(2)}, u32[]{:S(2)}) collective-permute-start(bf16[464,128]{1,0:T(8,128)(2,1)S(1)} %shard_map.317.own_ref), channel_id=1, source_target_pairs={{0,8},{4,12},{8,0},{12,4},{1,9},{5,13},{9,1},{13,5},{2,10},{6,14},... | collective-permute-start | bytes 356360 | tf_op jit(solution)/shard_map/ppermute | solution.py:730
  51.9 7.7 %collective-permute-done.10.other_ref = bf16[464,128]{1,0:T(8,128)(2,1)S(1)} collective-permute-done((bf16[464,128]{1,0:T(8,128)(2,1)S(1)}, bf16[464,128]{1,0:T(8,128)(2,1)S(1)}, u32[]{:S(2)}, u32[]{:S(2)}) %collective-permute-start.10) | collective-permute-done | bytes 118816 | tf_op jit(solution)/shard_map/ppermute | solution.py:730
  59.6 0.6 collective-permute-start.11
  60.2 1.0 %collective-permute-done.11.other_ref = bf16[464,128]{1,0:T(8,128)(2,1)S(1)} collective-permute-done((bf16[464,128]{1,0:T(8,128)(2,1)S(1)}, bf16[464,128]{1,0:T(8,128)(2,1)S(1)}, u32[]{:S(2)}, u32[]{:S(2)}) %collective-permute-start.11) | collective-permute-done | bytes 118816 | tf_op jit(solution)/shard_map/ppermute | solution.py:734
  61.2 0.8 %shard_map.319 = (f32[384,128]{1,0:T(8,128)}, f32[128,128]{1,0:T(8,128)}, f32[256,128]{1,0:T(8,128)}, f32[128,128]{1,0:T(8,128)}, f32[1,128]{1,0:T(1,128)}, /*in...) custom-call(bf16[464,128]{1,0:T(8,128)(2,1)S(1)} %shard_map.318.own_, ...), custom_call_target="tpu_custom_call" | custom-call | bytes 237568 | tf_op jit(solution)/shard_map/pallas_call | solution.py:510
  (14 shorter events, 0.2 us)
Async XLA Ops:
  2.5 7.6 %collective-permute-start = (bf16[128,128]{1,0:T(8,128)(2,1)S(1)}, bf16[128,128]{1,0:T(8,128)(2,1)S(1)}, u32[]{:S(2)}, u32[]{:S(2)}) collective-permute-start(bf16[128,128]{1,0:T(8,128)(2,1)S(1)} %get-tuple-element.64), channel_id=1, source_target_pairs={{0,1},{4,5},{8,9},{12,13},{1,0},{5,4},{9,8},{13,12},{2,3},{6,7},{1... | collective-permute-start | bytes 98312 | tf_op jit(solution)/shard_map/ppermute | solution.py:528
  2.7 7.5 %collective-permute-start.1 = (bf16[128,128]{1,0:T(8,128)(2,1)S(1)}, bf16[128,128]{1,0:T(8,128)(2,1)S(1)}, u32[]{:S(2)}, u32[]{:S(2)}) collective-permute-start(bf16[128,128]{1,0:T(8,128)(2,1)S(1)} %get-tuple-element.65), channel_id=1, source_target_pairs={{1,4},{5,8},{9,12},{4,1},{8,5},{12,9},{3,6},{7,10},{11,14},{6,3},{... | collective-permute-start | bytes 98312 | tf_op jit(solution)/shard_map/ppermute | solution.py:527
  16.9 5.7 %collective-permute-start.2 = (bf16[128,128]{1,0:T(8,128)(2,1)S(1)}, bf16[128,128]{1,0:T(8,128)(2,1)S(1)}, u32[]{:S(2)}, u32[]{:S(2)}) collective-permute-start(bf16[128,128]{1,0:T(8,128)(2,1)S(1)} %get-tuple-element.69), channel_id=1, source_target_pairs={{0,1},{4,5},{8,9},{12,13},{1,0},{5,4},{9,8},{13,12},{2,3},{6,7},{1... | collective-permute-start | bytes 98312 | tf_op jit(solution)/shard_map/ppermute | solution.py:528
  16.9 5.7 %collective-permute-start.3 = (bf16[128,128]{1,0:T(8,128)(2,1)S(1)}, bf16[128,128]{1,0:T(8,128)(2,1)S(1)}, u32[]{:S(2)}, u32[]{:S(2)}) collective-permute-start(bf16[128,128]{1,0:T(8,128)(2,1)S(1)} %get-tuple-element.70), channel_id=1, source_target_pairs={{1,4},{5,8},{9,12},{4,1},{8,5},{12,9},{3,6},{7,10},{11,14},{6,3},{... | collective-permute-start | bytes 98312 | tf_op jit(solution)/shard_map/ppermute | solution.py:527
  24.4 5.5 %collective-permute-start.4 = (bf16[128,128]{1,0:T(8,128)(2,1)S(1)}, bf16[128,128]{1,0:T(8,128)(2,1)S(1)}, u32[]{:S(2)}, u32[]{:S(2)}) collective-permute-start(bf16[128,128]{1,0:T(8,128)(2,1)S(1)} %get-tuple-element.78), channel_id=1, source_target_pairs={{0,1},{4,5},{8,9},{12,13},{1,0},{5,4},{9,8},{13,12},{2,3},{6,7},{1... | collective-permute-start | bytes 98312 | tf_op jit(solution)/shard_map/ppermute | solution.py:528
  24.5 5.5 %collective-permute-start.5 = (bf16[128,128]{1,0:T(8,128)(2,1)S(1)}, bf16[128,128]{1,0:T(8,128)(2,1)S(1)}, u32[]{:S(2)}, u32[]{:S(2)}) collective-permute-start(bf16[128,128]{1,0:T(8,128)(2,1)S(1)} %get-tuple-element.79), channel_id=1, source_target_pairs={{1,4},{5,8},{9,12},{4,1},{8,5},{12,9},{3,6},{7,10},{11,14},{6,3},{... | collective-permute-start | bytes 98312 | tf_op jit(solution)/shard_map/ppermute | solution.py:527
  37.2 1.4 %collective-permute-start.6 = (bf16[592,128]{1,0:T(8,128)(2,1)S(1)}, bf16[592,128]{1,0:T(8,128)(2,1)S(1)}, u32[]{:S(2)}, u32[]{:S(2)}) collective-permute-start(bf16[592,128]{1,0:T(8,128)(2,1)S(1)} %get-tuple-element.84), channel_id=1, source_target_pairs={{0,1},{4,5},{8,9},{12,13},{1,0},{5,4},{9,8},{13,12},{2,3},{6,7},{1... | collective-permute-start | bytes 454664 | tf_op jit(solution)/shard_map/ppermute | solution.py:528
  38.7 6.9 %collective-permute-start.8 = (bf16[464,128]{1,0:T(8,128)(2,1)S(1)}, bf16[464,128]{1,0:T(8,128)(2,1)S(1)}, u32[]{:S(2)}, u32[]{:S(2)}) collective-permute-start(bf16[464,128]{1,0:T(8,128)(2,1)S(1)} %shard_map.315.own_ref), channel_id=1, source_target_pairs={{0,2},{2,0},{1,3},{3,1},{4,6},{6,4},{5,7},{7,5},{8,10},{10,8},{9,1... | collective-permute-start | bytes 356360 | tf_op jit(solution)/shard_map/ppermute | solution.py:730
  40.0 5.7 %collective-permute-start.7 = (bf16[128,128]{1,0:T(8,128)(2,1)S(1)}, bf16[128,128]{1,0:T(8,128)(2,1)S(1)}, u32[]{:S(2)}, u32[]{:S(2)}) collective-permute-start(bf16[128,128]{1,0:T(8,128)(2,1)S(1)} %get-tuple-element.85), channel_id=1, source_target_pairs={{1,4},{5,8},{9,12},{4,1},{8,5},{12,9},{3,6},{7,10},{11,14},{6,3},{... | collective-permute-start | bytes 98312 | tf_op jit(solution)/shard_map/ppermute | solution.py:527
  45.7 5.2 %collective-permute-start.9 = (bf16[464,128]{1,0:T(8,128)(2,1)S(1)}, bf16[464,128]{1,0:T(8,128)(2,1)S(1)}, u32[]{:S(2)}, u32[]{:S(2)}) collective-permute-start(bf16[464,128]{1,0:T(8,128)(2,1)S(1)} %shard_map.316.own_ref), channel_id=1, source_target_pairs={{0,4},{4,0},{8,12},{12,8},{1,5},{5,1},{9,13},{13,9},{2,6},{6,2},{1... | collective-permute-start | bytes 356360 | tf_op jit(solution)/shard_map/ppermute | solution.py:730
  50.9 8.7 %collective-permute-start.10 = (bf16[464,128]{1,0:T(8,128)(2,1)S(1)}, bf16[464,128]{1,0:T(8,128)(2,1)S(1)}, u32[]{:S(2)}, u32[]{:S(2)}) collective-permute-start(bf16[464,128]{1,0:T(8,128)(2,1)S(1)} %shard_map.317.own_ref), channel_id=1, source_target_pairs={{0,8},{4,12},{8,0},{12,4},{1,9},{5,13},{9,1},{13,5},{2,10},{6,14},... | collective-permute-start | bytes 356360 | tf_op jit(solution)/shard_map/ppermute | solution.py:730
  59.6 1.5 %collective-permute-start.11 = (bf16[464,128]{1,0:T(8,128)(2,1)S(1)}, bf16[464,128]{1,0:T(8,128)(2,1)S(1)}, u32[]{:S(2)}, u32[]{:S(2)}) collective-permute-start(bf16[464,128]{1,0:T(8,128)(2,1)S(1)} %shard_map.318.own_ref), channel_id=1, source_target_pairs={{0,1},{1,0},{2,3},{3,2},{4,5},{5,4},{6,7},{7,6},{8,9},{9,8},{10,11... | collective-permute-start | bytes 356360 | tf_op jit(solution)/shard_map/ppermute | solution.py:734

commit v5 on v4

--- a/solution.py
+++ b/solution.py
@@ -33,22 +33,26 @@
     return jnp.broadcast_to(row, (lane, lane)).T
 
 
-def hot_columns(ids, width):
-    targets = lax.broadcasted_iota(jnp.int32, ids.shape, 1)
+def hot_columns(low, *spans):
+    targets = lax.broadcasted_iota(jnp.int16, low.shape, 1)
+    one, zero = jnp.ones((), bf16), jnp.zeros((), bf16)
     parts = [
-        jnp.where(ids == targets + at, 1.0, 0.0).astype(bf16) for at in range(0, width, lane)
+        jnp.where(low == targets + jnp.int16(at), one, zero)
+        for start, stop in spans
+        for at in range(start, stop, lane)
     ]
     return jnp.concatenate(parts, axis=1)
 
 
 def hot_rows(row, height):
-    targets = lax.broadcasted_iota(jnp.int32, (height, lane), 0)
-    return jnp.where(row == targets, 1.0, 0.0).astype(bf16)
-
-
-def fold(ids, half):
-    upper = ids >= half
-    return upper, jnp.where(upper, ids - half, ids)
+    low = jnp.broadcast_to(row, (16, lane)).astype(jnp.int16)
+    targets = lax.broadcasted_iota(jnp.int16, (height, lane), 0).reshape(height // 16, 16, lane)
+    one, zero = jnp.ones((), bf16), jnp.zeros((), bf16)
+    return jnp.where(targets == low[None], one, zero).reshape(height, lane)
+
+
+def folded(ids, half):
+    return jnp.where((ids >= half) & (ids < 2 * half), ids - half, ids)
 
 
 def side_by_side(rows):
@@ -56,25 +60,23 @@
     return jnp.concatenate([rows[:half], rows[half:]], axis=1)
 
 
-def pick(ids, table):
-    half = table.shape[0]
-    upper, low = fold(ids, half)
-    both = dot(hot_columns(low, half), table)
-    return jnp.where(upper, both[:, lane:], both[:, :lane])
+def pick(ids, low, half, table, *halo):
+    both = dot(hot_columns(low, (0, half), *halo), table)
+    return jnp.where(ids >= half, both[:, lane:], both[:, :lane])
+
+
+def rows_of_ids(ids_ref, first, count, height, change):
+    parts = [hot_rows(change(ids_ref[pl.ds(first + k, 1), :]), height) for k in range(count)]
+    return jnp.concatenate(parts, axis=1)
 
 
 def spread(ids_ref, first, count, half, ids, values):
-    upper, unused = fold(ids, half)
+    upper = ids >= half
     paired = jnp.concatenate(
         [jnp.where(upper, 0.0, values).astype(bf16), jnp.where(upper, values, 0.0).astype(bf16)],
         axis=1,
     )
-    parts = []
-    for k in range(count):
-        row = ids_ref[pl.ds(first + k, 1), :]
-        unused, low = fold(row, half)
-        parts.append(hot_rows(low, half))
-    return dot(jnp.concatenate(parts, axis=1), paired)
+    return dot(rows_of_ids(ids_ref, first, count, half, lambda row: folded(row, half)), paired)
 
 
 def sigmoid(z):
@@ -93,24 +95,34 @@
     return jnp.concatenate([high, low], axis=1), b - jnp.mean(b, axis=1, keepdims=True)
 
 
-def normed_of(act, w_pair, b_centred):
+def mean_weights():
+    shape = (2 * lane, 2 * lane)
+    left = lax.broadcasted_iota(jnp.int32, shape, 0) < lane
+    right = lax.broadcasted_iota(jnp.int32, shape, 1) < lane
+    return jnp.where(left == right, 1.0 / lane, 0.0).astype(bf16)
+
+
+def normed_of(act, w_pair, b_centred, means):
     both = dot(act, w_pair)
     center = both[:, :lane] + both[:, lane:] + b_centred
-    scale_inv = lax.rsqrt(jnp.mean(center * center, axis=1, keepdims=True) + epsilon)
+    variance = dot((center * center).astype(bf16), means[:lane, :lane])
+    scale_inv = lax.rsqrt(variance + epsilon)
     return center * scale_inv, scale_inv
 
 
-def back_norm(upstream, normed, scale_inv, gain):
+def back_norm(upstream, normed, scale_inv, gain, means):
     d_normed = upstream * gain
-    return scale_inv * (
-        d_normed
-        - jnp.mean(d_normed, axis=1, keepdims=True)
-        - normed * jnp.mean(d_normed * normed, axis=1, keepdims=True)
-    )
+    pair = jnp.concatenate([d_normed.astype(bf16), (d_normed * normed).astype(bf16)], axis=1)
+    both = dot(pair, means)
+    return scale_inv * (d_normed - both[:, :lane] - normed * both[:, lane:])
 
 
 def column_sum(values):
     return jnp.sum(values, axis=0, keepdims=True)
+
+
+def eight_sums(values):
+    return jnp.sum(values.reshape(values.shape[0] // 8, 8, lane), axis=0)
 
 
 def parity_of_place():
@@ -155,7 +167,8 @@
     parity = parity_of_place()
     node = node_ref[...]
     for side, out_ref in ((1 - parity, near_ref), (parity, far_ref)):
-        hot = hot_columns(column_of(ids_ref[pl.ds(2 * chunks + side, 1), :]), node.shape[0])
+        column = column_of(ids_ref[pl.ds(2 * chunks + side, 1), :]).astype(jnp.int16)
+        hot = hot_columns(column, (0, node.shape[0]))
         out_ref[...] = dot(hot, node).astype(bf16)
     for copy in copies[2:]:
         copy.wait()
@@ -169,25 +182,32 @@
     edge_ref,
     snd_column,
     rcv_column,
+    snd_low,
+    rcv_low,
     z_ref,
     rcv_local,
     snd_table,
 ):
     chunks = snd_column.shape[0] // lane
+    half = snd_table.shape[0]
     for k in range(chunks):
         at = slice(k * lane, (k + 1) * lane)
-        snd_column[at, :] = column_of(ids_ref[k : k + 1, :])
-        rcv_column[at, :] = column_of(ids_ref[chunks + k : chunks + k + 1, :])
+        snd = column_of(ids_ref[k : k + 1, :])
+        rcv = column_of(ids_ref[chunks + k : chunks + k + 1, :])
+        snd_column[at, :] = snd
+        rcv_column[at, :] = rcv
+        snd_low[at, :] = folded(snd, half).astype(jnp.int16)
+        rcv_low[at, :] = folded(rcv, half).astype(jnp.int16)
     node = node_ref[...]
     snd_table[...] = side_by_side(dot(node, weights_ref[lane : 2 * lane]).astype(bf16))
-    rcv_local[...] = dot(node, weights_ref[2 * lane : 3 * lane]).astype(bf16)
+    rcv_local[...] = side_by_side(dot(node, weights_ref[2 * lane : 3 * lane]).astype(bf16))
     w1_edge = weights_ref[:lane]
     b1 = vector(vectors_ref, 0)
 
     def tile(i, carry):
         rows = pl.ds(pl.multiple_of(i * edge_tile, edge_tile), edge_tile)
         z = dot(edge_ref[rows, :], w1_edge) + b1
-        z_ref[rows, :] = z + pick(snd_column[rows, :], snd_table[...])
+        z_ref[rows, :] = z + pick(snd_column[rows, :], snd_low[rows, :], half, snd_table[...])
         return carry
 
     lax.fori_loop(0, edge_ref.shape[0] // edge_tile, tile, 0)
@@ -201,53 +221,56 @@
     weights_ref,
     vectors_ref,
     rcv_column,
+    rcv_low,
     z_sent,
     rcv_local,
     out_ref,
     z_ref,
+    normed_ref,
+    scale_ref,
     message_ref,
     agg_near_ref,
     agg_far_ref,
-    halo,
-    rcv_table,
+    table,
     w2_pair,
+    means,
     total,
 ):
-    nodes = rcv_local.shape[0]
+    half = rcv_local.shape[0]
+    nodes = 2 * half
     rim = near_ref.shape[0]
-    half = rcv_table.shape[0]
     parity = parity_of_place()
     near_at = pl.multiple_of((1 - parity) * rim, rim)
     far_at = pl.multiple_of(parity * rim, rim)
     w1_rcv = weights_ref[2 * lane : 3 * lane]
     gain, shift = vector(vectors_ref, 2), vector(vectors_ref, 3)
-    halo[pl.ds(near_at, rim), :] = dot(near_ref[...], w1_rcv).astype(bf16)
-    halo[pl.ds(far_at, rim), :] = dot(far_ref[...], w1_rcv).astype(bf16)
-    rcv_table[:, :lane] = rcv_local[:half, :]
-    rcv_table[: nodes - half, lane:] = rcv_local[half:, :]
-    rcv_table[nodes - half :, lane:] = halo[...]
+    table[:half, :] = rcv_local[...]
+    table[half:, :lane] = jnp.zeros((2 * rim, lane), bf16)
+    table[pl.ds(half + near_at, rim), lane:] = dot(near_ref[...], w1_rcv).astype(bf16)
+    table[pl.ds(half + far_at, rim), lane:] = dot(far_ref[...], w1_rcv).astype(bf16)
     pair, b2 = centred_second(weights_ref[3 * lane : 4 * lane], vector(vectors_ref, 1))
     w2_pair[...] = pair
+    means[...] = mean_weights()
     total[...] = jnp.zeros_like(total)
 
     def tile(i, carry):
         rows = pl.ds(pl.multiple_of(i * edge_tile, edge_tile), edge_tile)
         x = edge_ref[rows, :]
-        rcv = rcv_column[rows, :]
-        z = z_sent[rows, :] + pick(rcv, rcv_table[...])
+        slots = (nodes, nodes + 2 * rim)
+        z = z_sent[rows, :]
+        z = z + pick(rcv_column[rows, :], rcv_low[rows, :], half, table[...], slots)
         z_ref[rows, :] = z
         act = (z * sigmoid(z)).astype(bf16)
-        normed, unused = normed_of(act, w2_pair[...], b2)
+        normed, scale_inv = normed_of(act, w2_pair[...], b2, means[...])
+        normed_ref[rows, :] = normed
+        scale_ref[rows, :] = scale_inv
         update = normed * gain + shift
         out_ref[rows, :] = (x.astype(f32) + update).astype(bf16)
         message = update.astype(bf16)
         message_ref[rows, :] = message
         first = (rcv_column.shape[0] + i * edge_tile) // lane
-        parts = [
-            hot_rows(ids_ref[pl.ds(first + k, 1), :] - nodes, 2 * rim)
-            for k in range(edge_tile // lane)
-        ]
-        total[...] += dot(jnp.concatenate(parts, axis=1), message)
+        hot = rows_of_ids(ids_ref, first, edge_tile // lane, 2 * rim, lambda row: row - nodes)
+        total[...] += dot(hot, message)
         return carry
 
     lax.fori_loop(0, edge_ref.shape[0] // edge_tile, tile, 0)
@@ -255,7 +278,7 @@
     agg_far_ref[...] = total[pl.ds(far_at, rim), :].astype(bf16)
 
 
-def collect_kernel(ids_ref, rcv_column, message_ref, agg_ref, total):
+def collect_kernel(ids_ref, rcv_column, message_ref, edge_ref, agg_ref, turned_ref, total):
     half = total.shape[0]
     total[...] = jnp.zeros_like(total)
 
@@ -264,6 +287,7 @@
         first = (rcv_column.shape[0] + i * edge_tile) // lane
         message = message_ref[rows, :].astype(f32)
         total[...] += spread(ids_ref, first, edge_tile // lane, half, rcv_column[rows, :], message)
+        turned_ref[:, rows] = edge_ref[rows, :].T
         return carry
 
     lax.fori_loop(0, rcv_column.shape[0] // edge_tile, tile, 0)
@@ -306,11 +330,12 @@
     sig = sigmoid(z)
     act = (z * sig).astype(bf16)
     pair, b2 = centred_second(w2, vector(vectors_ref, 5))
-    normed, scale_inv = normed_of(act, pair, b2)
+    means = mean_weights()
+    normed, scale_inv = normed_of(act, pair, b2, means)
     gain = vector(vectors_ref, 6)
     out_ref[...] = (node.astype(f32) + normed * gain + vector(vectors_ref, 7)).astype(bf16)
     upstream = cot_ref[...].astype(f32)
-    dz2 = back_norm(upstream, normed, scale_inv, gain)
+    dz2 = back_norm(upstream, normed, scale_inv, gain, means)
     dz2b = dz2.astype(bf16)
     da = dot_back(dz2b, w2)
     dz1 = da * sig * (1.0 + z * (1.0 - sig))
@@ -322,7 +347,8 @@
     parity = parity_of_place()
     first = ids_ref.shape[0] - 2
     for side, rim_ref in ((1 - parity, rim_near_ref), (parity, rim_far_ref)):
-        picked = hot_columns(column_of(ids_ref[pl.ds(first + side, 1), :]), nodes)
+        column = column_of(ids_ref[pl.ds(first + side, 1), :]).astype(jnp.int16)
+        picked = hot_columns(column, (0, nodes))
         rim_ref[...] = dot(picked, dagg).astype(bf16)
     first = 2 * lane
     second = first + lane
@@ -333,21 +359,32 @@
     grads_ref[second:, :] = jnp.concatenate(sums, axis=0)
 
 
-def upstream_kernel(rcv_column, dagg_ref, cot_ref, up_ref, table):
+def upstream_kernel(
+    rcv_column, rcv_low, dagg_ref, cot_ref, z_ref, up_ref, slope_ref, act_ref, table
+):
+    half = table.shape[0]
     table[...] = side_by_side(dagg_ref[...])
 
     def tile(i, carry):
         rows = pl.ds(pl.multiple_of(i * edge_tile, edge_tile), edge_tile)
-        up_ref[rows, :] = cot_ref[rows, :].astype(f32) + pick(rcv_column[rows, :], table[...])
+        local = pick(rcv_column[rows, :], rcv_low[rows, :], half, table[...])
+        up_ref[rows, :] = cot_ref[rows, :].astype(f32) + local
+        z = z_ref[rows, :]
+        sig = sigmoid(z)
+        slope_ref[rows, :] = sig * (1.0 + z * (1.0 - sig))
+        act_ref[:, rows] = (z * sig).astype(bf16).T
         return carry
 
     lax.fori_loop(0, cot_ref.shape[0] // edge_tile, tile, 0)
 
 
 def edge_backward_kernel(
-    z_ref,
     up_ref,
-    edge_ref,
+    normed_ref,
+    scale_ref,
+    slope_ref,
+    act_ref,
+    turned_ref,
     ids_ref,
     node_ref,
     near_ref,
@@ -359,6 +396,7 @@
     node_grads_ref,
     snd_column,
     rcv_column,
+    rcv_low,
     dz_ref,
     snd_sum_ref,
     rcv_sum_ref,
@@ -368,16 +406,16 @@
     halo,
     grads_ref,
     table,
-    w2_pair,
+    means,
     snd_total,
     rcv_total,
+    halo_total,
     squares,
     sums,
 ):
     nodes = node_ref.shape[0]
     rim = near_ref.shape[0]
-    snd_half = snd_total.shape[0]
-    rcv_half = rcv_total.shape[0]
+    half = snd_total.shape[0]
     parity = parity_of_place()
     near_at = pl.multiple_of((1 - parity) * rim, rim)
     far_at = pl.multiple_of(parity * rim, rim)
@@ -387,61 +425,57 @@
     table[pl.ds(far_at, rim), :] = dagg_far_ref[...]
     halo[pl.ds(near_at, rim), :] = near_ref[...]
     halo[pl.ds(far_at, rim), :] = far_ref[...]
-    pair, b2 = centred_second(w2, vector(vectors_ref, 1))
-    w2_pair[...] = pair
-    snd_total[...] = jnp.zeros_like(snd_total)
-    rcv_total[...] = jnp.zeros_like(rcv_total)
-    squares[...] = jnp.zeros_like(squares)
-    sums[...] = jnp.zeros_like(sums)
+    means[...] = mean_weights()
+    for total in (snd_total, rcv_total, halo_total, squares, sums):
+        total[...] = jnp.zeros_like(total)
 
     def tile(i, carry):
         rows = pl.ds(pl.multiple_of(i * edge_tile, edge_tile), edge_tile)
         chunk = edge_tile // lane
-        rcv = rcv_column[rows, :]
-        snd = snd_column[rows, :]
-        x = edge_ref[rows, :]
-        z = z_ref[rows, :]
-        upstream = up_ref[rows, :] + dot(hot_columns(rcv - nodes, 2 * rim), table[...])
-        sig = sigmoid(z)
-        act = (z * sig).astype(bf16)
-        normed, scale_inv = normed_of(act, w2_pair[...], b2)
-        dz2 = back_norm(upstream, normed, scale_inv, gain)
+        hot = hot_columns(rcv_low[rows, :], (nodes, nodes + 2 * rim))
+        upstream = up_ref[rows, :] + dot(hot, table[...])
+        normed = normed_ref[rows, :]
+        dz2 = back_norm(upstream, normed, scale_ref[rows, :], gain, means[...])
         dz2b = dz2.astype(bf16)
-        da = dot_back(dz2b, w2)
-        dz1 = da * sig * (1.0 + z * (1.0 - sig))
+        dz1 = dot_back(dz2b, w2) * slope_ref[rows, :]
         dz1b = dz1.astype(bf16)
         dz_ref[rows, :] = dz1b
-        squares[:lane, :] += dot_rows(x, dz1b)
-        squares[lane:, :] += dot_rows(act, dz2b)
-        sums[0:1, :] += column_sum(dz1)
-        sums[1:2, :] += column_sum(dz2)
-        sums[2:3, :] += column_sum(upstream * normed)
-        sums[3:4, :] += column_sum(upstream)
+        squares[:lane, :] += dot(turned_ref[:, rows], dz1b)
+        squares[lane:, :] += dot(act_ref[:, rows], dz2b)
+        sums[0:8, :] += eight_sums(dz1)
+        sums[8:16, :] += eight_sums(dz2)
+        sums[16:24, :] += eight_sums(upstream * normed)
+        sums[24:32, :] += eight_sums(upstream)
         first = rcv_column.shape[0] // lane + i * chunk
-        snd_total[...] += spread(ids_ref, i * chunk, chunk, snd_half, snd, dz1)
-        rcv_total[...] += spread(ids_ref, first, chunk, rcv_half, rcv, dz1)
+        snd_total[...] += spread(ids_ref, i * chunk, chunk, half, snd_column[rows, :], dz1)
+        rcv_total[...] += spread(ids_ref, first, chunk, half, rcv_column[rows, :], dz1)
+        slots = rows_of_ids(ids_ref, first, chunk, 2 * rim, lambda row: row - nodes)
+        halo_total[...] += dot(slots, dz1b)
         return carry
 
-    lax.fori_loop(0, edge_ref.shape[0] // edge_tile, tile, 0)
+    lax.fori_loop(0, up_ref.shape[0] // edge_tile, tile, 0)
     snd_sum = jnp.concatenate([snd_total[:, :lane], snd_total[:, lane:]], axis=0).astype(bf16)
     rcv_sum = jnp.concatenate([rcv_total[:, :lane], rcv_total[:, lane:]], axis=0).astype(bf16)
+    halo_sum = halo_total[...].astype(bf16)
     snd_sum_ref[...] = snd_sum
-    rcv_sum_ref[...] = rcv_sum[:nodes]
+    rcv_sum_ref[...] = rcv_sum
     w1_rcv = weights_ref[2 * lane : 3 * lane]
     kept = kept_ref.shape[0]
     for at, back_ref in ((near_at, sent_ref.at[kept:]), (far_at, far_back_ref)):
-        returned = rcv_total[pl.ds(nodes - rcv_half + at, rim), lane:].astype(bf16)
+        returned = halo_total[pl.ds(at, rim), :].astype(bf16)
         back_ref[...] = dot_back(returned, w1_rcv).astype(bf16)
     extended = jnp.concatenate([node_ref[...], halo[...]], axis=0)
+    extended_sum = jnp.concatenate([rcv_sum, halo_sum], axis=0)
     grads_ref[:lane, :] = squares[:lane, :]
     grads_ref[lane : 2 * lane, :] = dot_rows(node_ref[...], snd_sum)
-    grads_ref[2 * lane : 3 * lane, :] = dot_rows(extended, rcv_sum)
+    grads_ref[2 * lane : 3 * lane, :] = dot_rows(extended, extended_sum)
     grads_ref[3 * lane : 4 * lane, :] = squares[lane:, :]
     node_rows = node_grads_ref.shape[0] - sum_rows
     last = 4 * lane + node_rows
     grads_ref[4 * lane : last, :] = node_grads_ref[:node_rows, :]
     grads_ref[last : last + sum_rows, :] = jnp.concatenate(
-        [sums[0:4, :], node_grads_ref[node_rows : node_rows + 4, :], jnp.zeros((8, lane), f32)],
+        [column_sum(sums[8 * k : 8 * k + 8, :]) for k in range(4)]
+        + [node_grads_ref[node_rows : node_rows + 4, :], jnp.zeros((8, lane), f32)],
         axis=0,
     )
     if last + sum_rows < grads_ref.shape[0]:
@@ -565,7 +599,6 @@
     rim = send_list.shape[2]
     rim_shape = ((rim, lane), bf16)
     snd_half = nodes // 2
-    rcv_half = (nodes + 2 * rim) // 2
     kept = -(-(7 * lane + sum_rows) // (2 * sum_rows)) * sum_rows
     row = lambda x: x.reshape(1, lane)
     small = [w_edge_first, w_edge_second, w_node_first, w_node_second]
@@ -600,13 +633,15 @@
         sems=len(sources),
     )
     near, far = swap(rim_near, rim_far)
-    snd_column, rcv_column, z_sent, rcv_local = call(
+    snd_column, rcv_column, snd_low, rcv_low, z_sent, rcv_local = call(
         prepare_kernel,
         [
             ((edges, lane), jnp.int32),
             ((edges, lane), jnp.int32),
+            ((edges, lane), jnp.int16),
+            ((edges, lane), jnp.int16),
             ((edges, lane), f32),
-            ((nodes, lane), bf16),
+            ((snd_half, 2 * lane), bf16),
         ],
         [((snd_half, 2 * lane), bf16)],
         ids,
@@ -615,13 +650,21 @@
         vectors,
         edge,
     )
-    edge_out, z, message, agg_near, agg_far = call(
+    edge_out, z, normed, scale, message, agg_near, agg_far = call(
         edge_forward_kernel,
-        [((edges, lane), bf16), ((edges, lane), f32), ((edges, lane), bf16), rim_shape, rim_shape],
         [
-            ((2 * rim, lane), bf16),
-            ((rcv_half, 2 * lane), bf16),
+            ((edges, lane), bf16),
+            ((edges, lane), f32),
+            ((edges, lane), f32),
+            ((edges, lane), f32),
+            ((edges, lane), bf16),
+            rim_shape,
+            rim_shape,
+        ],
+        [
+            ((snd_half + 2 * rim, 2 * lane), bf16),
             ((lane, 2 * lane), bf16),
+            ((2 * lane, 2 * lane), bf16),
             ((2 * rim, lane), f32),
         ],
         near,
@@ -631,17 +674,19 @@
         weights,
         vectors,
         rcv_column,
+        rcv_low,
         z_sent,
         rcv_local,
     )
     back_near, back_far = swap(agg_near, agg_far)
-    (agg,) = call(
+    agg, turned = call(
         collect_kernel,
-        [((nodes, lane), f32)],
+        [((nodes, lane), f32), ((lane, edges), bf16)],
         [((snd_half, 2 * lane), f32)],
         ids,
         rcv_column,
         message,
+        edge,
     )
     node_out, base, dagg, dagg_rim_near, dagg_rim_far, node_grads = call(
         node_kernel,
@@ -664,13 +709,15 @@
         node_cot,
     )
     dagg_near, dagg_far = swap(dagg_rim_near, dagg_rim_far)
-    (upstream,) = call(
+    upstream, slope, act = call(
         upstream_kernel,
-        [((edges, lane), f32)],
+        [((edges, lane), f32), ((edges, lane), f32), ((lane, edges), bf16)],
         [((snd_half, 2 * lane), bf16)],
         rcv_column,
+        rcv_low,
         dagg,
         edge_cot,
+        z,
     )
     dz, snd_sum, rcv_sum, grad_far, grads_kept, grads_sent = call(
         edge_backward_kernel,
@@ -686,15 +733,19 @@
             ((2 * rim, lane), bf16),
             ((2 * kept, lane), f32),
             ((2 * rim, lane), bf16),
-            ((lane, 2 * lane), bf16),
+            ((2 * lane, 2 * lane), bf16),
             ((snd_half, 2 * lane), f32),
-            ((rcv_half, 2 * lane), f32),
+            ((snd_half, 2 * lane), f32),
+            ((2 * rim, lane), f32),
             ((2 * lane, lane), f32),
-            ((8, lane), f32),
+            ((32, lane), f32),
         ],
-        z,
         upstream,
-        edge,
+        normed,
+        scale,
+        slope,
+        act,
+        turned,
         ids,
         node,
         near,
@@ -706,6 +757,7 @@
         node_grads,
         snd_column,
         rcv_column,
+        rcv_low,
     )
     returned_near, returned_far = swap(grads_sent, grad_far)
     (edge_grad,) = call(

time: 62.5 us -> 63 us (level)
    pallas_call x14, Pallas kernels: 28.7 us -> 29.3 us  [call(): pl.pallas_call(kernel, out_shape=[jax.ShapeDtypeStruct(shape, dtype) for...]
  transfers between devices with their start and end apart: 12 -> 12, of which waited for: 4 -> 4; matrix products, arithmetic and copies ran while one was open for 0% -> 0% of each run, Pallas kernels for 16% -> 17%
where the time goes in v5:
time: 63 us; the launch traced here: 62.5 us
  Pallas kernels  29.3 us (47%)
  starting transfers between devices  19.3 us (31%)
  waiting for transfers between devices  13 us (21%)
  between operations  0.78 us (1%)
    pallas_call x14, Pallas kernels, call(): pl.pallas_call(kernel, out_shape=[jax.ShapeDtypeStruct(shape, dtype) for...  29.3 us
    ppermute x4, starting transfers between devices, swap(): far = lax.ppermute(far, chain, outer)  15.2 us
    ppermute x3, waiting for transfers between devices, on_device(): other = lax.ppermute(grads, axis, pairs)  10.7 us
    ppermute x3, starting transfers between devices, on_device(): other = lax.ppermute(grads, axis, pairs)  3.31 us
    ppermute x4, waiting for transfers between devices, swap(): return (lax.ppermute(near, chain, inner), far)  1.37 us
  transfers between devices with their start and end apart: 12, of which 4 were waited for; matrix products, arithmetic and copies ran while one was open for 0% of the time, Pallas kernels for 17%

profile of v5, /device:TPU:1, one launch (start us, length us, event | category | flops | bytes accessed | tf_op | source)
XLA Modules:
  0.0 62.5 jit_solution(18277173911496898892)
XLA Ops:
  0.7 1.9 %shard_map.306 = (bf16[1024,128]{1,0:T(8,128)(2,1)S(1)}, s32[50,128]{1,0:T(8,128)S(1)}, bf16[3072,128]{1,0:T(8,128)(2,1)S(1)}, bf16[3072,128]{1,0:T(8,128)(2,1)S...) custom-call(bf16[1024,128]{1,0:T(8,128)(2,1)} %bitcast.31, ...), custom_call_target="tpu_custom_call" | custom-call | bytes 2356224 | tf_op jit(solution)/shard_map/pallas_call | solution.py:544
  2.5 0.1 collective-permute-start
  2.7 4.6 %collective-permute-start.1 = (bf16[128,128]{1,0:T(8,128)(2,1)S(1)}, bf16[128,128]{1,0:T(8,128)(2,1)S(1)}, u32[]{:S(2)}, u32[]{:S(2)}) collective-permute-start(bf16[128,128]{1,0:T(8,128)(2,1)S(1)} %get-tuple-element.73), channel_id=1, source_target_pairs={{1,4},{5,8},{9,12},{4,1},{8,5},{12,9},{3,6},{7,10},{11,14},{6,3},{... | collective-permute-start | bytes 98312 | tf_op jit(solution)/shard_map/ppermute | solution.py:561
  7.2 3.5 %shard_map.307 = (s32[3072,128]{1,0:T(8,128)S(1)}, s32[3072,128]{1,0:T(8,128)S(1)}, s16[3072,128]{1,0:T(8,128)(2,1)}, s16[3072,128]{1,0:T(8,128)(2,1)S(1)}, f32[...) custom-call(s32[50,128]{1,0:T(8,128)S(1)} %get-tuple-element.67.ids_ref, ...), custom_call_target="tpu_custom_call" | custom-call | bytes 1307648 | tf_op jit(solution)/shard_map/pallas_call | solution.py:544
  10.7 6.7 %shard_map.308 = (bf16[3072,128]{1,0:T(8,128)(2,1)}, f32[3072,128]{1,0:T(8,128)S(1)}, f32[3072,128]{1,0:T(8,128)S(1)}, f32[3072,128]{1,0:T(8,128)S(1)}, bf16[307...) custom-call(bf16[128,128]{1,0:T(8,128)(2,1)S(1)} %collective-permute-done.near_ref, ...), custom_call_target="tpu_custom_call" | custom-call | bytes 5305344 | tf_op jit(solution)/shard_map/pallas_call | solution.py:544
  17.4 3.6 %collective-permute-start.3 = (bf16[128,128]{1,0:T(8,128)(2,1)S(1)}, bf16[128,128]{1,0:T(8,128)(2,1)S(1)}, u32[]{:S(2)}, u32[]{:S(2)}) collective-permute-start(bf16[128,128]{1,0:T(8,128)(2,1)S(1)} %get-tuple-element.80), channel_id=1, source_target_pairs={{1,4},{5,8},{9,12},{4,1},{8,5},{12,9},{3,6},{7,10},{11,14},{6,3},{... | collective-permute-start | bytes 98312 | tf_op jit(solution)/shard_map/ppermute | solution.py:561
  21.0 2.1 %shard_map.309 = (f32[1024,128]{1,0:T(8,128)S(1)}, bf16[128,3072]{1,0:T(8,128)(2,1)S(1)}) custom-call(s32[50,128]{1,0:T(8,128)S(1)} %get-tuple-element.67.ids_ref, s32[3072,128]{1,0:T(8,128)S(1)} %get-tuple-element.71.rcv_column, bf16[3072,128]{1,0:T(8,128)(2,1)S(1)} %get-tuple-element.77.message_ref, bf16[3072,128]{1,0:T(8,128)(2,1)S(1)} %get-tuple-element.70.edge_ref), custom_call_target="tpu_custom_call" | custom-call | bytes 3171328 | tf_op jit(solution)/shard_map/pallas_call | solution.py:544
  23.1 2.0 %shard_map.310 = (bf16[1024,128]{1,0:T(8,128)(2,1)}, f32[1024,128]{1,0:T(8,128)S(1)}, bf16[1024,128]{1,0:T(8,128)(2,1)S(1)}, bf16[128,128]{1,0:T(8,128)(2,1)S(1)...) custom-call(bf16[1024,128]{1,0:T(8,128)(2,1)S(1)} %get-tuple-element.66.node_ref, ...), custom_call_target="tpu_custom_call" | custom-call | bytes 1373184 | tf_op jit(solution)/shard_map/pallas_call | solution.py:544
  25.1 0.1 collective-permute-start.4
  25.2 3.6 %collective-permute-start.5 = (bf16[128,128]{1,0:T(8,128)(2,1)S(1)}, bf16[128,128]{1,0:T(8,128)(2,1)S(1)}, u32[]{:S(2)}, u32[]{:S(2)}) collective-permute-start(bf16[128,128]{1,0:T(8,128)(2,1)S(1)} %get-tuple-element.95), channel_id=1, source_target_pairs={{1,4},{5,8},{9,12},{4,1},{8,5},{12,9},{3,6},{7,10},{11,14},{6,3},{... | collective-permute-start | bytes 98312 | tf_op jit(solution)/shard_map/ppermute | solution.py:561
  28.8 2.0 %shard_map.311 = (f32[3072,128]{1,0:T(8,128)S(1)}, f32[3072,128]{1,0:T(8,128)S(1)}, bf16[128,3072]{1,0:T(8,128)(2,1)S(1)}) custom-call(s32[3072,128]{1,0:T(8,128)S(1)} %get-tuple-element.71.rcv_column, s16[3072,128]{1,0:T(8,128)(2,1)S(1)} %get-tuple-element.74.rcv_low, bf16[1024,128]{1,0:T(8,128)(2,1)S(1)} %get-tuple-element.85.dagg_ref, ...), custom_call_target="tpu_custom_call" | custom-call | bytes 4980736 | tf_op jit(solution)/shard_map/pallas_call | solution.py:544
  30.8 7.1 %shard_map.312 = (bf16[3072,128]{1,0:T(8,128)(2,1)S(1)}, bf16[1024,128]{1,0:T(8,128)(2,1)S(1)}, bf16[1024,128]{1,0:T(8,128)(2,1)S(1)}, bf16[128,128]{1,0:T(8,128...) custom-call(f32[3072,128]{1,0:T(8,128)S(1)} %get-tuple-element.88.up_ref, ...), custom_call_target="tpu_custom_call" | custom-call | bytes 12653568 | tf_op jit(solution)/shard_map/pallas_call | solution.py:544
  37.9 1.4 %collective-permute-done.6.near_ref.other_ref = bf16[592,128]{1,0:T(8,128)(2,1)S(1)} collective-permute-done((bf16[592,128]{1,0:T(8,128)(2,1)S(1)}, bf16[592,128]{1,0:T(8,128)(2,1)S(1)}, u32[]{:S(2)}, u32[]{:S(2)}) %collective-permute-start.6) | collective-permute-done | bytes 151584 | tf_op jit(solution)/shard_map/ppermute | solution.py:562
  39.3 1.3 %collective-permute-start.8 = (bf16[464,128]{1,0:T(8,128)(2,1)S(1)}, bf16[464,128]{1,0:T(8,128)(2,1)S(1)}, u32[]{:S(2)}, u32[]{:S(2)}) collective-permute-start(bf16[464,128]{1,0:T(8,128)(2,1)S(1)} %shard_map.315.own_ref), channel_id=1, source_target_pairs={{0,2},{2,0},{1,3},{3,1},{4,6},{6,4},{5,7},{7,5},{8,10},{10,8},{9,1... | collective-permute-start | bytes 356360 | tf_op jit(solution)/shard_map/ppermute | solution.py:782
  40.6 3.5 %collective-permute-start.7 = (bf16[128,128]{1,0:T(8,128)(2,1)S(1)}, bf16[128,128]{1,0:T(8,128)(2,1)S(1)}, u32[]{:S(2)}, u32[]{:S(2)}) collective-permute-start(bf16[128,128]{1,0:T(8,128)(2,1)S(1)} %get-tuple-element.101), channel_id=1, source_target_pairs={{1,4},{5,8},{9,12},{4,1},{8,5},{12,9},{3,6},{7,10},{11,14},{6,3},{... | collective-permute-start | bytes 98312 | tf_op jit(solution)/shard_map/ppermute | solution.py:561
  44.1 2.0 %shard_map.314.refs_1_ = bf16[3072,128]{1,0:T(8,128)(2,1)} custom-call(bf16[3072,128]{1,0:T(8,128)(2,1)S(1)} %get-tuple-element.102.dz_ref, bf16[3072,128]{1,0:T(8,128)(2,1)S(1)} %get-tuple-element.86.cot_ref, bf16[896,128]{1,0:T(8,128)(2,1)S(1)} %get-tuple-element.68.weights_ref), custom_call_target="tpu_custom_call" | custom-call | bytes 1802240 | tf_op jit(solution)/shard_map/pallas_call | solution.py:544
  46.2 1.1 %collective-permute-start.9 = (bf16[464,128]{1,0:T(8,128)(2,1)S(1)}, bf16[464,128]{1,0:T(8,128)(2,1)S(1)}, u32[]{:S(2)}, u32[]{:S(2)}) collective-permute-start(bf16[464,128]{1,0:T(8,128)(2,1)S(1)} %shard_map.316.own_ref), channel_id=1, source_target_pairs={{0,4},{4,0},{8,12},{12,8},{1,5},{5,1},{9,13},{13,9},{2,6},{6,2},{1... | collective-permute-start | bytes 356360 | tf_op jit(solution)/shard_map/ppermute | solution.py:782
  47.3 1.1 %shard_map.313.refs_0_ = bf16[1024,128]{1,0:T(8,128)(2,1)} custom-call(f32[1024,128]{1,0:T(8,128)S(1)} %get-tuple-element.84.base_ref, bf16[1024,128]{1,0:T(8,128)(2,1)S(1)} %get-tuple-element.98.snd_sum_ref, bf16[1024,128]{1,0:T(8,128)(2,1)S(1)} %get-tuple-element.99.rcv_sum_ref, bf16[896,128]{1,0:T(8,128)(2,1)S(1)} %get-tuple-element.68.weights_ref, ...), custom_call_target="tpu_custom_call" | custom-call | bytes 1487872 | tf_op jit(solution)/shard_map/pallas_call | solution.py:544
  48.4 3.0 %collective-permute-done.9.other_ref = bf16[464,128]{1,0:T(8,128)(2,1)S(1)} collective-permute-done((bf16[464,128]{1,0:T(8,128)(2,1)S(1)}, bf16[464,128]{1,0:T(8,128)(2,1)S(1)}, u32[]{:S(2)}, u32[]{:S(2)}) %collective-permute-start.9) | collective-permute-done | bytes 118816 | tf_op jit(solution)/shard_map/ppermute | solution.py:782
  51.4 1.0 %collective-permute-start.10 = (bf16[464,128]{1,0:T(8,128)(2,1)S(1)}, bf16[464,128]{1,0:T(8,128)(2,1)S(1)}, u32[]{:S(2)}, u32[]{:S(2)}) collective-permute-start(bf16[464,128]{1,0:T(8,128)(2,1)S(1)} %shard_map.317.own_ref), channel_id=1, source_target_pairs={{0,8},{4,12},{8,0},{12,4},{1,9},{5,13},{9,1},{13,5},{2,10},{6,14},... | collective-permute-start | bytes 356360 | tf_op jit(solution)/shard_map/ppermute | solution.py:782
  52.4 7.7 %collective-permute-done.10.other_ref = bf16[464,128]{1,0:T(8,128)(2,1)S(1)} collective-permute-done((bf16[464,128]{1,0:T(8,128)(2,1)S(1)}, bf16[464,128]{1,0:T(8,128)(2,1)S(1)}, u32[]{:S(2)}, u32[]{:S(2)}) %collective-permute-start.10) | collective-permute-done | bytes 118816 | tf_op jit(solution)/shard_map/ppermute | solution.py:782
  60.1 0.6 collective-permute-start.11
  60.7 1.0 %collective-permute-done.11.other_ref = bf16[464,128]{1,0:T(8,128)(2,1)S(1)} collective-permute-done((bf16[464,128]{1,0:T(8,128)(2,1)S(1)}, bf16[464,128]{1,0:T(8,128)(2,1)S(1)}, u32[]{:S(2)}, u32[]{:S(2)}) %collective-permute-start.11) | collective-permute-done | bytes 118816 | tf_op jit(solution)/shard_map/ppermute | solution.py:786
  61.7 0.8 %shard_map.319 = (f32[384,128]{1,0:T(8,128)}, f32[128,128]{1,0:T(8,128)}, f32[256,128]{1,0:T(8,128)}, f32[128,128]{1,0:T(8,128)}, f32[1,128]{1,0:T(1,128)}, /*in...) custom-call(bf16[464,128]{1,0:T(8,128)(2,1)S(1)} %shard_map.318.own_, ...), custom_call_target="tpu_custom_call" | custom-call | bytes 237568 | tf_op jit(solution)/shard_map/pallas_call | solution.py:544
  (14 shorter events, 0.2 us)
Async XLA Ops:
  2.5 8.2 %collective-permute-start = (bf16[128,128]{1,0:T(8,128)(2,1)S(1)}, bf16[128,128]{1,0:T(8,128)(2,1)S(1)}, u32[]{:S(2)}, u32[]{:S(2)}) collective-permute-start(bf16[128,128]{1,0:T(8,128)(2,1)S(1)} %get-tuple-element.72), channel_id=1, source_target_pairs={{0,1},{4,5},{8,9},{12,13},{1,0},{5,4},{9,8},{13,12},{2,3},{6,7},{1... | collective-permute-start | bytes 98312 | tf_op jit(solution)/shard_map/ppermute | solution.py:562
  2.7 8.0 %collective-permute-start.1 = (bf16[128,128]{1,0:T(8,128)(2,1)S(1)}, bf16[128,128]{1,0:T(8,128)(2,1)S(1)}, u32[]{:S(2)}, u32[]{:S(2)}) collective-permute-start(bf16[128,128]{1,0:T(8,128)(2,1)S(1)} %get-tuple-element.73), channel_id=1, source_target_pairs={{1,4},{5,8},{9,12},{4,1},{8,5},{12,9},{3,6},{7,10},{11,14},{6,3},{... | collective-permute-start | bytes 98312 | tf_op jit(solution)/shard_map/ppermute | solution.py:561
  17.4 5.7 %collective-permute-start.2 = (bf16[128,128]{1,0:T(8,128)(2,1)S(1)}, bf16[128,128]{1,0:T(8,128)(2,1)S(1)}, u32[]{:S(2)}, u32[]{:S(2)}) collective-permute-start(bf16[128,128]{1,0:T(8,128)(2,1)S(1)} %get-tuple-element.79), channel_id=1, source_target_pairs={{0,1},{4,5},{8,9},{12,13},{1,0},{5,4},{9,8},{13,12},{2,3},{6,7},{1... | collective-permute-start | bytes 98312 | tf_op jit(solution)/shard_map/ppermute | solution.py:562
  17.4 5.7 %collective-permute-start.3 = (bf16[128,128]{1,0:T(8,128)(2,1)S(1)}, bf16[128,128]{1,0:T(8,128)(2,1)S(1)}, u32[]{:S(2)}, u32[]{:S(2)}) collective-permute-start(bf16[128,128]{1,0:T(8,128)(2,1)S(1)} %get-tuple-element.80), channel_id=1, source_target_pairs={{1,4},{5,8},{9,12},{4,1},{8,5},{12,9},{3,6},{7,10},{11,14},{6,3},{... | collective-permute-start | bytes 98312 | tf_op jit(solution)/shard_map/ppermute | solution.py:561
  25.1 5.6 %collective-permute-start.4 = (bf16[128,128]{1,0:T(8,128)(2,1)S(1)}, bf16[128,128]{1,0:T(8,128)(2,1)S(1)}, u32[]{:S(2)}, u32[]{:S(2)}) collective-permute-start(bf16[128,128]{1,0:T(8,128)(2,1)S(1)} %get-tuple-element.94), channel_id=1, source_target_pairs={{0,1},{4,5},{8,9},{12,13},{1,0},{5,4},{9,8},{13,12},{2,3},{6,7},{1... | collective-permute-start | bytes 98312 | tf_op jit(solution)/shard_map/ppermute | solution.py:562
  25.2 5.6 %collective-permute-start.5 = (bf16[128,128]{1,0:T(8,128)(2,1)S(1)}, bf16[128,128]{1,0:T(8,128)(2,1)S(1)}, u32[]{:S(2)}, u32[]{:S(2)}) collective-permute-start(bf16[128,128]{1,0:T(8,128)(2,1)S(1)} %get-tuple-element.95), channel_id=1, source_target_pairs={{1,4},{5,8},{9,12},{4,1},{8,5},{12,9},{3,6},{7,10},{11,14},{6,3},{... | collective-permute-start | bytes 98312 | tf_op jit(solution)/shard_map/ppermute | solution.py:561
  37.9 1.4 %collective-permute-start.6 = (bf16[592,128]{1,0:T(8,128)(2,1)S(1)}, bf16[592,128]{1,0:T(8,128)(2,1)S(1)}, u32[]{:S(2)}, u32[]{:S(2)}) collective-permute-start(bf16[592,128]{1,0:T(8,128)(2,1)S(1)} %get-tuple-element.100), channel_id=1, source_target_pairs={{0,1},{4,5},{8,9},{12,13},{1,0},{5,4},{9,8},{13,12},{2,3},{6,7},{1... | collective-permute-start | bytes 454664 | tf_op jit(solution)/shard_map/ppermute | solution.py:562
  39.3 6.8 %collective-permute-start.8 = (bf16[464,128]{1,0:T(8,128)(2,1)S(1)}, bf16[464,128]{1,0:T(8,128)(2,1)S(1)}, u32[]{:S(2)}, u32[]{:S(2)}) collective-permute-start(bf16[464,128]{1,0:T(8,128)(2,1)S(1)} %shard_map.315.own_ref), channel_id=1, source_target_pairs={{0,2},{2,0},{1,3},{3,1},{4,6},{6,4},{5,7},{7,5},{8,10},{10,8},{9,1... | collective-permute-start | bytes 356360 | tf_op jit(solution)/shard_map/ppermute | solution.py:782
  40.6 5.5 %collective-permute-start.7 = (bf16[128,128]{1,0:T(8,128)(2,1)S(1)}, bf16[128,128]{1,0:T(8,128)(2,1)S(1)}, u32[]{:S(2)}, u32[]{:S(2)}) collective-permute-start(bf16[128,128]{1,0:T(8,128)(2,1)S(1)} %get-tuple-element.101), channel_id=1, source_target_pairs={{1,4},{5,8},{9,12},{4,1},{8,5},{12,9},{3,6},{7,10},{11,14},{6,3},{... | collective-permute-start | bytes 98312 | tf_op jit(solution)/shard_map/ppermute | solution.py:561
  46.2 5.2 %collective-permute-start.9 = (bf16[464,128]{1,0:T(8,128)(2,1)S(1)}, bf16[464,128]{1,0:T(8,128)(2,1)S(1)}, u32[]{:S(2)}, u32[]{:S(2)}) collective-permute-start(bf16[464,128]{1,0:T(8,128)(2,1)S(1)} %shard_map.316.own_ref), channel_id=1, source_target_pairs={{0,4},{4,0},{8,12},{12,8},{1,5},{5,1},{9,13},{13,9},{2,6},{6,2},{1... | collective-permute-start | bytes 356360 | tf_op jit(solution)/shard_map/ppermute | solution.py:782
  51.4 8.7 %collective-permute-start.10 = (bf16[464,128]{1,0:T(8,128)(2,1)S(1)}, bf16[464,128]{1,0:T(8,128)(2,1)S(1)}, u32[]{:S(2)}, u32[]{:S(2)}) collective-permute-start(bf16[464,128]{1,0:T(8,128)(2,1)S(1)} %shard_map.317.own_ref), channel_id=1, source_target_pairs={{0,8},{4,12},{8,0},{12,4},{1,9},{5,13},{9,1},{13,5},{2,10},{6,14},... | collective-permute-start | bytes 356360 | tf_op jit(solution)/shard_map/ppermute | solution.py:782
  60.1 1.5 %collective-permute-start.11 = (bf16[464,128]{1,0:T(8,128)(2,1)S(1)}, bf16[464,128]{1,0:T(8,128)(2,1)S(1)}, u32[]{:S(2)}, u32[]{:S(2)}) collective-permute-start(bf16[464,128]{1,0:T(8,128)(2,1)S(1)} %shard_map.318.own_ref), channel_id=1, source_target_pairs={{0,1},{1,0},{2,3},{3,2},{4,5},{5,4},{6,7},{7,6},{8,9},{9,8},{10,11... | collective-permute-start | bytes 356360 | tf_op jit(solution)/shard_map/ppermute | solution.py:786

commit v6 on v5

--- a/solution.py
+++ b/solution.py
@@ -1,3 +1,5 @@
+import math
+
 import jax
 import jax.numpy as jnp
 from jax import lax
@@ -12,9 +14,22 @@
 bf16 = jnp.bfloat16
 lane = 128
 edge_tile = 512
+tile_group = 3
 vmem_limit = 32 * 1024 * 1024
 sum_rows = 16
 chain = ("dom", "sub")
+
+
+def each_tile(rows, tile):
+    count = rows // edge_tile
+    group = math.gcd(count, tile_group)
+
+    def several(i, carry):
+        for k in range(group):
+            tile(i * group + k)
+        return carry
+
+    lax.fori_loop(0, count // group, several, 0)
 
 
 def dot(left, right):
@@ -204,13 +219,12 @@
     w1_edge = weights_ref[:lane]
     b1 = vector(vectors_ref, 0)
 
-    def tile(i, carry):
+    def tile(i):
         rows = pl.ds(pl.multiple_of(i * edge_tile, edge_tile), edge_tile)
         z = dot(edge_ref[rows, :], w1_edge) + b1
         z_ref[rows, :] = z + pick(snd_column[rows, :], snd_low[rows, :], half, snd_table[...])
-        return carry
-
-    lax.fori_loop(0, edge_ref.shape[0] // edge_tile, tile, 0)
+
+    each_tile(edge_ref.shape[0], tile)
 
 
 def edge_forward_kernel(
@@ -253,7 +267,7 @@
     means[...] = mean_weights()
     total[...] = jnp.zeros_like(total)
 
-    def tile(i, carry):
+    def tile(i):
         rows = pl.ds(pl.multiple_of(i * edge_tile, edge_tile), edge_tile)
         x = edge_ref[rows, :]
         slots = (nodes, nodes + 2 * rim)
@@ -271,9 +285,8 @@
         first = (rcv_column.shape[0] + i * edge_tile) // lane
         hot = rows_of_ids(ids_ref, first, edge_tile // lane, 2 * rim, lambda row: row - nodes)
         total[...] += dot(hot, message)
-        return carry
-
-    lax.fori_loop(0, edge_ref.shape[0] // edge_tile, tile, 0)
+
+    each_tile(edge_ref.shape[0], tile)
     agg_near_ref[...] = total[pl.ds(near_at, rim), :].astype(bf16)
     agg_far_ref[...] = total[pl.ds(far_at, rim), :].astype(bf16)
 
@@ -282,15 +295,14 @@
     half = total.shape[0]
     total[...] = jnp.zeros_like(total)
 
-    def tile(i, carry):
+    def tile(i):
         rows = pl.ds(pl.multiple_of(i * edge_tile, edge_tile), edge_tile)
         first = (rcv_column.shape[0] + i * edge_tile) // lane
         message = message_ref[rows, :].astype(f32)
         total[...] += spread(ids_ref, first, edge_tile // lane, half, rcv_column[rows, :], message)
         turned_ref[:, rows] = edge_ref[rows, :].T
-        return carry
-
-    lax.fori_loop(0, rcv_column.shape[0] // edge_tile, tile, 0)
+
+    each_tile(rcv_column.shape[0], tile)
     agg_ref[:half, :] = total[:, :lane]
     agg_ref[half:, :] = total[:, lane:]
 
@@ -365,7 +377,7 @@
     half = table.shape[0]
     table[...] = side_by_side(dagg_ref[...])
 
-    def tile(i, carry):
+    def tile(i):
         rows = pl.ds(pl.multiple_of(i * edge_tile, edge_tile), edge_tile)
         local = pick(rcv_column[rows, :], rcv_low[rows, :], half, table[...])
         up_ref[rows, :] = cot_ref[rows, :].astype(f32) + local
@@ -373,9 +385,8 @@
         sig = sigmoid(z)
         slope_ref[rows, :] = sig * (1.0 + z * (1.0 - sig))
         act_ref[:, rows] = (z * sig).astype(bf16).T
-        return carry
-
-    lax.fori_loop(0, cot_ref.shape[0] // edge_tile, tile, 0)
+
+    each_tile(cot_ref.shape[0], tile)
 
 
 def edge_backward_kernel(
@@ -406,6 +417,7 @@
     halo,
     grads_ref,
     table,
+    w2_turned,
     means,
     snd_total,
     rcv_total,
@@ -419,7 +431,7 @@
     parity = parity_of_place()
     near_at = pl.multiple_of((1 - parity) * rim, rim)
     far_at = pl.multiple_of(parity * rim, rim)
-    w2 = weights_ref[3 * lane : 4 * lane]
+    w2_turned[...] = weights_ref[3 * lane : 4 * lane].T
     gain = vector(vectors_ref, 2)
     table[pl.ds(near_at, rim), :] = dagg_near_ref[...]
     table[pl.ds(far_at, rim), :] = dagg_far_ref[...]
@@ -429,7 +441,7 @@
     for total in (snd_total, rcv_total, halo_total, squares, sums):
         total[...] = jnp.zeros_like(total)
 
-    def tile(i, carry):
+    def tile(i):
         rows = pl.ds(pl.multiple_of(i * edge_tile, edge_tile), edge_tile)
         chunk = edge_tile // lane
         hot = hot_columns(rcv_low[rows, :], (nodes, nodes + 2 * rim))
@@ -437,7 +449,7 @@
         normed = normed_ref[rows, :]
         dz2 = back_norm(upstream, normed, scale_ref[rows, :], gain, means[...])
         dz2b = dz2.astype(bf16)
-        dz1 = dot_back(dz2b, w2) * slope_ref[rows, :]
+        dz1 = dot(dz2b, w2_turned[...]) * slope_ref[rows, :]
         dz1b = dz1.astype(bf16)
         dz_ref[rows, :] = dz1b
         squares[:lane, :] += dot(turned_ref[:, rows], dz1b)
@@ -451,9 +463,8 @@
         rcv_total[...] += spread(ids_ref, first, chunk, half, rcv_column[rows, :], dz1)
         slots = rows_of_ids(ids_ref, first, chunk, 2 * rim, lambda row: row - nodes)
         halo_total[...] += dot(slots, dz1b)
-        return carry
-
-    lax.fori_loop(0, up_ref.shape[0] // edge_tile, tile, 0)
+
+    each_tile(up_ref.shape[0], tile)
     snd_sum = jnp.concatenate([snd_total[:, :lane], snd_total[:, lane:]], axis=0).astype(bf16)
     rcv_sum = jnp.concatenate([rcv_total[:, :lane], rcv_total[:, lane:]], axis=0).astype(bf16)
     halo_sum = halo_total[...].astype(bf16)
@@ -488,16 +499,15 @@
     sent_ref[:kept, :] = grads_ref[pl.ds(other, kept), :].astype(bf16)
 
 
-def edge_grad_kernel(dz_ref, cot_ref, weights_ref, out_ref):
-    w1_edge = weights_ref[:lane]
-
-    def tile(i, carry):
+def edge_grad_kernel(dz_ref, cot_ref, weights_ref, out_ref, w1_turned):
+    w1_turned[...] = weights_ref[:lane].T
+
+    def tile(i):
         rows = pl.ds(pl.multiple_of(i * edge_tile, edge_tile), edge_tile)
         cot = cot_ref[rows, :].astype(f32)
-        out_ref[rows, :] = (cot + dot_back(dz_ref[rows, :], w1_edge)).astype(bf16)
-        return carry
-
-    lax.fori_loop(0, cot_ref.shape[0] // edge_tile, tile, 0)
+        out_ref[rows, :] = (cot + dot(dz_ref[rows, :], w1_turned[...])).astype(bf16)
+
+    each_tile(cot_ref.shape[0], tile)
 
 
 def node_grad_kernel(
@@ -733,6 +743,7 @@
             ((2 * rim, lane), bf16),
             ((2 * kept, lane), f32),
             ((2 * rim, lane), bf16),
+            ((lane, lane), bf16),
             ((2 * lane, 2 * lane), bf16),
             ((snd_half, 2 * lane), f32),
             ((snd_half, 2 * lane), f32),
@@ -761,7 +772,12 @@
     )
     returned_near, returned_far = swap(grads_sent, grad_far)
     (edge_grad,) = call(
-        edge_grad_kernel, [((edges, lane), bf16)], [], dz, edge_cot, weights
+        edge_grad_kernel,
+        [((edges, lane), bf16)],
+        [((lane, lane), bf16)],
+        dz,
+        edge_cot,
+        weights,
     )
     (node_grad,) = call(
         node_grad_kernel,

time: 63 us -> 58.5 us (0.929)
  Pallas kernels: 29.3 us -> 24.4 us
  starting transfers between devices: 19.3 us -> 22.5 us
  waiting for transfers between devices: 13 us -> 10.4 us
    pallas_call x14, Pallas kernels: 29.3 us -> 24.4 us  [call(): pl.pallas_call(kernel, out_shape=[jax.ShapeDtypeStruct(shape, dtype) for...]
    ppermute x3, waiting for transfers between devices: 10.7 us -> 7.7 us  [on_device(): other = lax.ppermute(grads, axis, pairs)]
    ppermute x3, starting transfers between devices: 3.31 us -> 5 us  [on_device(): other = lax.ppermute(grads, axis, pairs)]
    ppermute x1, starting transfers between devices: 0.55 us -> 1.46 us  [on_device(): others = lax.ppermute(grads, 'sub', [(0, 1), (1, 0)])]
  transfers between devices with their start and end apart: 12 -> 12, of which waited for: 4 -> 6; matrix products, arithmetic and copies ran while one was open for 0% -> 0% of each run, Pallas kernels for 17% -> 14%
where the time goes in v6:
time: 58.5 us; the launch traced here: 58 us
  Pallas kernels  24.4 us (42%)
  starting transfers between devices  22.5 us (38%)
  waiting for transfers between devices  10.4 us (18%)
  between operations  0.78 us (1%)
    pallas_call x14, Pallas kernels, call(): pl.pallas_call(kernel, out_shape=[jax.ShapeDtypeStruct(shape, dtype) for...  24.4 us
    ppermute x4, starting transfers between devices, swap(): far = lax.ppermute(far, chain, outer)  15.7 us
    ppermute x3, waiting for transfers between devices, on_device(): other = lax.ppermute(grads, axis, pairs)  7.7 us
    ppermute x3, starting transfers between devices, on_device(): other = lax.ppermute(grads, axis, pairs)  5 us
    ppermute x1, starting transfers between devices, on_device(): others = lax.ppermute(grads, 'sub', [(0, 1), (1, 0)])  1.46 us
    ppermute x4, waiting for transfers between devices, swap(): return (lax.ppermute(near, chain, inner), far)  1.37 us
  transfers between devices with their start and end apart: 12, of which 6 were waited for; matrix products, arithmetic and copies ran while one was open for 0% of the time, Pallas kernels for 14%

profile of v6, /device:TPU:1, one launch (start us, length us, event | category | flops | bytes accessed | tf_op | source)
XLA Modules:
  0.0 58.0 jit_solution(9729075119844896788)
XLA Ops:
  0.7 1.9 %shard_map.306 = (bf16[1024,128]{1,0:T(8,128)(2,1)S(1)}, s32[50,128]{1,0:T(8,128)S(1)}, bf16[3072,128]{1,0:T(8,128)(2,1)S(1)}, bf16[3072,128]{1,0:T(8,128)(2,1)S...) custom-call(bf16[1024,128]{1,0:T(8,128)(2,1)} %bitcast.31, ...), custom_call_target="tpu_custom_call" | custom-call | bytes 2356224 | tf_op jit(solution)/shard_map/pallas_call | solution.py:554
  2.5 0.1 collective-permute-start
  2.7 4.6 %collective-permute-start.1 = (bf16[128,128]{1,0:T(8,128)(2,1)S(1)}, bf16[128,128]{1,0:T(8,128)(2,1)S(1)}, u32[]{:S(2)}, u32[]{:S(2)}) collective-permute-start(bf16[128,128]{1,0:T(8,128)(2,1)S(1)} %get-tuple-element.73), channel_id=1, source_target_pairs={{1,4},{5,8},{9,12},{4,1},{8,5},{12,9},{3,6},{7,10},{11,14},{6,3},{... | collective-permute-start | bytes 98312 | tf_op jit(solution)/shard_map/ppermute | solution.py:571
  7.2 2.5 %shard_map.307 = (s32[3072,128]{1,0:T(8,128)S(1)}, s32[3072,128]{1,0:T(8,128)S(1)}, s16[3072,128]{1,0:T(8,128)(2,1)}, s16[3072,128]{1,0:T(8,128)(2,1)S(1)}, f32[...) custom-call(s32[50,128]{1,0:T(8,128)S(1)} %get-tuple-element.67.ids_ref, ...), custom_call_target="tpu_custom_call" | custom-call | bytes 1307648 | tf_op jit(solution)/shard_map/pallas_call | solution.py:554
  9.7 5.5 %shard_map.308 = (bf16[3072,128]{1,0:T(8,128)(2,1)}, f32[3072,128]{1,0:T(8,128)S(1)}, f32[3072,128]{1,0:T(8,128)S(1)}, f32[3072,128]{1,0:T(8,128)S(1)}, bf16[307...) custom-call(bf16[128,128]{1,0:T(8,128)(2,1)S(1)} %collective-permute-done.near_ref, ...), custom_call_target="tpu_custom_call" | custom-call | bytes 5305344 | tf_op jit(solution)/shard_map/pallas_call | solution.py:554
  15.2 3.6 %collective-permute-start.3 = (bf16[128,128]{1,0:T(8,128)(2,1)S(1)}, bf16[128,128]{1,0:T(8,128)(2,1)S(1)}, u32[]{:S(2)}, u32[]{:S(2)}) collective-permute-start(bf16[128,128]{1,0:T(8,128)(2,1)S(1)} %get-tuple-element.80), channel_id=1, source_target_pairs={{1,4},{5,8},{9,12},{4,1},{8,5},{12,9},{3,6},{7,10},{11,14},{6,3},{... | collective-permute-start | bytes 98312 | tf_op jit(solution)/shard_map/ppermute | solution.py:571
  18.8 1.4 %shard_map.309 = (f32[1024,128]{1,0:T(8,128)S(1)}, bf16[128,3072]{1,0:T(8,128)(2,1)S(1)}) custom-call(s32[50,128]{1,0:T(8,128)S(1)} %get-tuple-element.67.ids_ref, s32[3072,128]{1,0:T(8,128)S(1)} %get-tuple-element.71.rcv_column, bf16[3072,128]{1,0:T(8,128)(2,1)S(1)} %get-tuple-element.77.message_ref, bf16[3072,128]{1,0:T(8,128)(2,1)S(1)} %get-tuple-element.70.edge_ref), custom_call_target="tpu_custom_call" | custom-call | bytes 3171328 | tf_op jit(solution)/shard_map/pallas_call | solution.py:554
  20.2 0.3 collective-permute-done.3.far_ref
  20.5 2.0 %shard_map.310 = (bf16[1024,128]{1,0:T(8,128)(2,1)}, f32[1024,128]{1,0:T(8,128)S(1)}, bf16[1024,128]{1,0:T(8,128)(2,1)S(1)}, bf16[128,128]{1,0:T(8,128)(2,1)S(1)...) custom-call(bf16[1024,128]{1,0:T(8,128)(2,1)S(1)} %get-tuple-element.66.node_ref, ...), custom_call_target="tpu_custom_call" | custom-call | bytes 1373184 | tf_op jit(solution)/shard_map/pallas_call | solution.py:554
  22.5 3.7 %collective-permute-start.5 = (bf16[128,128]{1,0:T(8,128)(2,1)S(1)}, bf16[128,128]{1,0:T(8,128)(2,1)S(1)}, u32[]{:S(2)}, u32[]{:S(2)}) collective-permute-start(bf16[128,128]{1,0:T(8,128)(2,1)S(1)} %get-tuple-element.95), channel_id=1, source_target_pairs={{1,4},{5,8},{9,12},{4,1},{8,5},{12,9},{3,6},{7,10},{11,14},{6,3},{... | collective-permute-start | bytes 98312 | tf_op jit(solution)/shard_map/ppermute | solution.py:571
  26.2 1.6 %shard_map.311 = (f32[3072,128]{1,0:T(8,128)S(1)}, f32[3072,128]{1,0:T(8,128)S(1)}, bf16[128,3072]{1,0:T(8,128)(2,1)S(1)}) custom-call(s32[3072,128]{1,0:T(8,128)S(1)} %get-tuple-element.71.rcv_column, s16[3072,128]{1,0:T(8,128)(2,1)S(1)} %get-tuple-element.74.rcv_low, bf16[1024,128]{1,0:T(8,128)(2,1)S(1)} %get-tuple-element.85.dagg_ref, ...), custom_call_target="tpu_custom_call" | custom-call | bytes 4980736 | tf_op jit(solution)/shard_map/pallas_call | solution.py:554
  27.9 6.0 %shard_map.312 = (bf16[3072,128]{1,0:T(8,128)(2,1)S(1)}, bf16[1024,128]{1,0:T(8,128)(2,1)S(1)}, bf16[1024,128]{1,0:T(8,128)(2,1)S(1)}, bf16[128,128]{1,0:T(8,128...) custom-call(f32[3072,128]{1,0:T(8,128)S(1)} %get-tuple-element.88.up_ref, ...), custom_call_target="tpu_custom_call" | custom-call | bytes 12653568 | tf_op jit(solution)/shard_map/pallas_call | solution.py:554
  33.9 1.4 %collective-permute-done.6.near_ref.other_ref = bf16[592,128]{1,0:T(8,128)(2,1)S(1)} collective-permute-done((bf16[592,128]{1,0:T(8,128)(2,1)S(1)}, bf16[592,128]{1,0:T(8,128)(2,1)S(1)}, u32[]{:S(2)}, u32[]{:S(2)}) %collective-permute-start.6) | collective-permute-done | bytes 151584 | tf_op jit(solution)/shard_map/ppermute | solution.py:572
  35.3 1.3 %collective-permute-start.8 = (bf16[464,128]{1,0:T(8,128)(2,1)S(1)}, bf16[464,128]{1,0:T(8,128)(2,1)S(1)}, u32[]{:S(2)}, u32[]{:S(2)}) collective-permute-start(bf16[464,128]{1,0:T(8,128)(2,1)S(1)} %shard_map.315.own_ref), channel_id=1, source_target_pairs={{0,2},{2,0},{1,3},{3,1},{4,6},{6,4},{5,7},{7,5},{8,10},{10,8},{9,1... | collective-permute-start | bytes 356360 | tf_op jit(solution)/shard_map/ppermute | solution.py:798
  36.6 3.9 %collective-permute-start.7 = (bf16[128,128]{1,0:T(8,128)(2,1)S(1)}, bf16[128,128]{1,0:T(8,128)(2,1)S(1)}, u32[]{:S(2)}, u32[]{:S(2)}) collective-permute-start(bf16[128,128]{1,0:T(8,128)(2,1)S(1)} %get-tuple-element.101), channel_id=1, source_target_pairs={{1,4},{5,8},{9,12},{4,1},{8,5},{12,9},{3,6},{7,10},{11,14},{6,3},{... | collective-permute-start | bytes 98312 | tf_op jit(solution)/shard_map/ppermute | solution.py:571
  40.5 1.5 %shard_map.314.refs_1_ = bf16[3072,128]{1,0:T(8,128)(2,1)} custom-call(bf16[3072,128]{1,0:T(8,128)(2,1)S(1)} %get-tuple-element.102.dz_ref, bf16[3072,128]{1,0:T(8,128)(2,1)S(1)} %get-tuple-element.86.cot_ref, bf16[896,128]{1,0:T(8,128)(2,1)S(1)} %get-tuple-element.68.weights_ref), custom_call_target="tpu_custom_call" | custom-call | bytes 1802240 | tf_op jit(solution)/shard_map/pallas_call | solution.py:554
  42.1 1.5 %collective-permute-start.9 = (bf16[464,128]{1,0:T(8,128)(2,1)S(1)}, bf16[464,128]{1,0:T(8,128)(2,1)S(1)}, u32[]{:S(2)}, u32[]{:S(2)}) collective-permute-start(bf16[464,128]{1,0:T(8,128)(2,1)S(1)} %shard_map.316.own_ref), channel_id=1, source_target_pairs={{0,4},{4,0},{8,12},{12,8},{1,5},{5,1},{9,13},{13,9},{2,6},{6,2},{1... | collective-permute-start | bytes 356360 | tf_op jit(solution)/shard_map/ppermute | solution.py:798
  43.6 1.1 %shard_map.313.refs_0_ = bf16[1024,128]{1,0:T(8,128)(2,1)} custom-call(f32[1024,128]{1,0:T(8,128)S(1)} %get-tuple-element.84.base_ref, bf16[1024,128]{1,0:T(8,128)(2,1)S(1)} %get-tuple-element.98.snd_sum_ref, bf16[1024,128]{1,0:T(8,128)(2,1)S(1)} %get-tuple-element.99.rcv_sum_ref, bf16[896,128]{1,0:T(8,128)(2,1)S(1)} %get-tuple-element.68.weights_ref, ...), custom_call_target="tpu_custom_call" | custom-call | bytes 1487872 | tf_op jit(solution)/shard_map/pallas_call | solution.py:554
  44.8 2.1 %collective-permute-done.9.other_ref = bf16[464,128]{1,0:T(8,128)(2,1)S(1)} collective-permute-done((bf16[464,128]{1,0:T(8,128)(2,1)S(1)}, bf16[464,128]{1,0:T(8,128)(2,1)S(1)}, u32[]{:S(2)}, u32[]{:S(2)}) %collective-permute-start.9) | collective-permute-done | bytes 118816 | tf_op jit(solution)/shard_map/ppermute | solution.py:798
  46.9 2.2 %collective-permute-start.10 = (bf16[464,128]{1,0:T(8,128)(2,1)S(1)}, bf16[464,128]{1,0:T(8,128)(2,1)S(1)}, u32[]{:S(2)}, u32[]{:S(2)}) collective-permute-start(bf16[464,128]{1,0:T(8,128)(2,1)S(1)} %shard_map.317.own_ref), channel_id=1, source_target_pairs={{0,8},{4,12},{8,0},{12,4},{1,9},{5,13},{9,1},{13,5},{2,10},{6,14},... | collective-permute-start | bytes 356360 | tf_op jit(solution)/shard_map/ppermute | solution.py:798
  49.2 5.6 %collective-permute-done.10.other_ref = bf16[464,128]{1,0:T(8,128)(2,1)S(1)} collective-permute-done((bf16[464,128]{1,0:T(8,128)(2,1)S(1)}, bf16[464,128]{1,0:T(8,128)(2,1)S(1)}, u32[]{:S(2)}, u32[]{:S(2)}) %collective-permute-start.10) | collective-permute-done | bytes 118816 | tf_op jit(solution)/shard_map/ppermute | solution.py:798
  54.7 1.5 %collective-permute-start.11 = (bf16[464,128]{1,0:T(8,128)(2,1)S(1)}, bf16[464,128]{1,0:T(8,128)(2,1)S(1)}, u32[]{:S(2)}, u32[]{:S(2)}) collective-permute-start(bf16[464,128]{1,0:T(8,128)(2,1)S(1)} %shard_map.318.own_ref), channel_id=1, source_target_pairs={{0,1},{1,0},{2,3},{3,2},{4,5},{5,4},{6,7},{7,6},{8,9},{9,8},{10,11... | collective-permute-start | bytes 356360 | tf_op jit(solution)/shard_map/ppermute | solution.py:802
  56.2 1.0 %collective-permute-done.11.other_ref = bf16[464,128]{1,0:T(8,128)(2,1)S(1)} collective-permute-done((bf16[464,128]{1,0:T(8,128)(2,1)S(1)}, bf16[464,128]{1,0:T(8,128)(2,1)S(1)}, u32[]{:S(2)}, u32[]{:S(2)}) %collective-permute-start.11) | collective-permute-done | bytes 118816 | tf_op jit(solution)/shard_map/ppermute | solution.py:802
  57.2 0.8 %shard_map.319 = (f32[384,128]{1,0:T(8,128)}, f32[128,128]{1,0:T(8,128)}, f32[256,128]{1,0:T(8,128)}, f32[128,128]{1,0:T(8,128)}, f32[1,128]{1,0:T(1,128)}, /*in...) custom-call(bf16[464,128]{1,0:T(8,128)(2,1)S(1)} %shard_map.318.own_, ...), custom_call_target="tpu_custom_call" | custom-call | bytes 237568 | tf_op jit(solution)/shard_map/pallas_call | solution.py:554
  (14 shorter events, 0.4 us)
Async XLA Ops:
  2.5 7.2 %collective-permute-start = (bf16[128,128]{1,0:T(8,128)(2,1)S(1)}, bf16[128,128]{1,0:T(8,128)(2,1)S(1)}, u32[]{:S(2)}, u32[]{:S(2)}) collective-permute-start(bf16[128,128]{1,0:T(8,128)(2,1)S(1)} %get-tuple-element.72), channel_id=1, source_target_pairs={{0,1},{4,5},{8,9},{12,13},{1,0},{5,4},{9,8},{13,12},{2,3},{6,7},{1... | collective-permute-start | bytes 98312 | tf_op jit(solution)/shard_map/ppermute | solution.py:572
  2.7 7.1 %collective-permute-start.1 = (bf16[128,128]{1,0:T(8,128)(2,1)S(1)}, bf16[128,128]{1,0:T(8,128)(2,1)S(1)}, u32[]{:S(2)}, u32[]{:S(2)}) collective-permute-start(bf16[128,128]{1,0:T(8,128)(2,1)S(1)} %get-tuple-element.73), channel_id=1, source_target_pairs={{1,4},{5,8},{9,12},{4,1},{8,5},{12,9},{3,6},{7,10},{11,14},{6,3},{... | collective-permute-start | bytes 98312 | tf_op jit(solution)/shard_map/ppermute | solution.py:571
  15.2 5.0 %collective-permute-start.2 = (bf16[128,128]{1,0:T(8,128)(2,1)S(1)}, bf16[128,128]{1,0:T(8,128)(2,1)S(1)}, u32[]{:S(2)}, u32[]{:S(2)}) collective-permute-start(bf16[128,128]{1,0:T(8,128)(2,1)S(1)} %get-tuple-element.79), channel_id=1, source_target_pairs={{0,1},{4,5},{8,9},{12,13},{1,0},{5,4},{9,8},{13,12},{2,3},{6,7},{1... | collective-permute-start | bytes 98312 | tf_op jit(solution)/shard_map/ppermute | solution.py:572
  15.2 5.2 %collective-permute-start.3 = (bf16[128,128]{1,0:T(8,128)(2,1)S(1)}, bf16[128,128]{1,0:T(8,128)(2,1)S(1)}, u32[]{:S(2)}, u32[]{:S(2)}) collective-permute-start(bf16[128,128]{1,0:T(8,128)(2,1)S(1)} %get-tuple-element.80), channel_id=1, source_target_pairs={{1,4},{5,8},{9,12},{4,1},{8,5},{12,9},{3,6},{7,10},{11,14},{6,3},{... | collective-permute-start | bytes 98312 | tf_op jit(solution)/shard_map/ppermute | solution.py:571
  22.5 5.4 %collective-permute-start.4 = (bf16[128,128]{1,0:T(8,128)(2,1)S(1)}, bf16[128,128]{1,0:T(8,128)(2,1)S(1)}, u32[]{:S(2)}, u32[]{:S(2)}) collective-permute-start(bf16[128,128]{1,0:T(8,128)(2,1)S(1)} %get-tuple-element.94), channel_id=1, source_target_pairs={{0,1},{4,5},{8,9},{12,13},{1,0},{5,4},{9,8},{13,12},{2,3},{6,7},{1... | collective-permute-start | bytes 98312 | tf_op jit(solution)/shard_map/ppermute | solution.py:572
  22.5 5.3 %collective-permute-start.5 = (bf16[128,128]{1,0:T(8,128)(2,1)S(1)}, bf16[128,128]{1,0:T(8,128)(2,1)S(1)}, u32[]{:S(2)}, u32[]{:S(2)}) collective-permute-start(bf16[128,128]{1,0:T(8,128)(2,1)S(1)} %get-tuple-element.95), channel_id=1, source_target_pairs={{1,4},{5,8},{9,12},{4,1},{8,5},{12,9},{3,6},{7,10},{11,14},{6,3},{... | collective-permute-start | bytes 98312 | tf_op jit(solution)/shard_map/ppermute | solution.py:571
  33.8 1.4 %collective-permute-start.6 = (bf16[592,128]{1,0:T(8,128)(2,1)S(1)}, bf16[592,128]{1,0:T(8,128)(2,1)S(1)}, u32[]{:S(2)}, u32[]{:S(2)}) collective-permute-start(bf16[592,128]{1,0:T(8,128)(2,1)S(1)} %get-tuple-element.100), channel_id=1, source_target_pairs={{0,1},{4,5},{8,9},{12,13},{1,0},{5,4},{9,8},{13,12},{2,3},{6,7},{1... | collective-permute-start | bytes 454664 | tf_op jit(solution)/shard_map/ppermute | solution.py:572
  35.3 6.8 %collective-permute-start.8 = (bf16[464,128]{1,0:T(8,128)(2,1)S(1)}, bf16[464,128]{1,0:T(8,128)(2,1)S(1)}, u32[]{:S(2)}, u32[]{:S(2)}) collective-permute-start(bf16[464,128]{1,0:T(8,128)(2,1)S(1)} %shard_map.315.own_ref), channel_id=1, source_target_pairs={{0,2},{2,0},{1,3},{3,1},{4,6},{6,4},{5,7},{7,5},{8,10},{10,8},{9,1... | collective-permute-start | bytes 356360 | tf_op jit(solution)/shard_map/ppermute | solution.py:798
  36.6 5.5 %collective-permute-start.7 = (bf16[128,128]{1,0:T(8,128)(2,1)S(1)}, bf16[128,128]{1,0:T(8,128)(2,1)S(1)}, u32[]{:S(2)}, u32[]{:S(2)}) collective-permute-start(bf16[128,128]{1,0:T(8,128)(2,1)S(1)} %get-tuple-element.101), channel_id=1, source_target_pairs={{1,4},{5,8},{9,12},{4,1},{8,5},{12,9},{3,6},{7,10},{11,14},{6,3},{... | collective-permute-start | bytes 98312 | tf_op jit(solution)/shard_map/ppermute | solution.py:571
  42.1 4.8 %collective-permute-start.9 = (bf16[464,128]{1,0:T(8,128)(2,1)S(1)}, bf16[464,128]{1,0:T(8,128)(2,1)S(1)}, u32[]{:S(2)}, u32[]{:S(2)}) collective-permute-start(bf16[464,128]{1,0:T(8,128)(2,1)S(1)} %shard_map.316.own_ref), channel_id=1, source_target_pairs={{0,4},{4,0},{8,12},{12,8},{1,5},{5,1},{9,13},{13,9},{2,6},{6,2},{1... | collective-permute-start | bytes 356360 | tf_op jit(solution)/shard_map/ppermute | solution.py:798
  46.9 7.8 %collective-permute-start.10 = (bf16[464,128]{1,0:T(8,128)(2,1)S(1)}, bf16[464,128]{1,0:T(8,128)(2,1)S(1)}, u32[]{:S(2)}, u32[]{:S(2)}) collective-permute-start(bf16[464,128]{1,0:T(8,128)(2,1)S(1)} %shard_map.317.own_ref), channel_id=1, source_target_pairs={{0,8},{4,12},{8,0},{12,4},{1,9},{5,13},{9,1},{13,5},{2,10},{6,14},... | collective-permute-start | bytes 356360 | tf_op jit(solution)/shard_map/ppermute | solution.py:798
  54.7 2.4 %collective-permute-start.11 = (bf16[464,128]{1,0:T(8,128)(2,1)S(1)}, bf16[464,128]{1,0:T(8,128)(2,1)S(1)}, u32[]{:S(2)}, u32[]{:S(2)}) collective-permute-start(bf16[464,128]{1,0:T(8,128)(2,1)S(1)} %shard_map.318.own_ref), channel_id=1, source_target_pairs={{0,1},{1,0},{2,3},{3,2},{4,5},{5,4},{6,7},{7,6},{8,9},{9,8},{10,11... | collective-permute-start | bytes 356360 | tf_op jit(solution)/shard_map/ppermute | solution.py:802

commit v7 on v6

--- a/solution.py
+++ b/solution.py
@@ -1,3 +1,4 @@
+import functools
 import math
 
 import jax
@@ -197,10 +198,11 @@
     edge_ref,
     snd_column,
     rcv_column,
-    snd_low,
     rcv_low,
     z_ref,
     rcv_local,
+    turned_ref,
+    snd_low,
     snd_table,
 ):
     chunks = snd_column.shape[0] // lane
@@ -214,23 +216,25 @@
         snd_low[at, :] = folded(snd, half).astype(jnp.int16)
         rcv_low[at, :] = folded(rcv, half).astype(jnp.int16)
     node = node_ref[...]
-    snd_table[...] = side_by_side(dot(node, weights_ref[lane : 2 * lane]).astype(bf16))
+    snd_table[...] = side_by_side(node)
     rcv_local[...] = side_by_side(dot(node, weights_ref[2 * lane : 3 * lane]).astype(bf16))
-    w1_edge = weights_ref[:lane]
+    w1 = weights_ref[: 2 * lane]
     b1 = vector(vectors_ref, 0)
 
     def tile(i):
         rows = pl.ds(pl.multiple_of(i * edge_tile, edge_tile), edge_tile)
-        z = dot(edge_ref[rows, :], w1_edge) + b1
-        z_ref[rows, :] = z + pick(snd_column[rows, :], snd_low[rows, :], half, snd_table[...])
+        x = edge_ref[rows, :]
+        sent = pick(snd_column[rows, :], snd_low[rows, :], half, snd_table[...]).astype(bf16)
+        z_ref[rows, :] = dot(jnp.concatenate([x, sent], axis=1), w1) + b1
+        turned_ref[:lane, rows] = x.T
+        turned_ref[lane:, rows] = sent.T
 
     each_tile(edge_ref.shape[0], tile)
 
 
 def edge_forward_kernel(
+    far_ref,
     near_ref,
-    far_ref,
-    edge_ref,
     ids_ref,
     weights_ref,
     vectors_ref,
@@ -238,7 +242,6 @@
     rcv_low,
     z_sent,
     rcv_local,
-    out_ref,
     z_ref,
     normed_ref,
     scale_ref,
@@ -269,7 +272,6 @@
 
     def tile(i):
         rows = pl.ds(pl.multiple_of(i * edge_tile, edge_tile), edge_tile)
-        x = edge_ref[rows, :]
         slots = (nodes, nodes + 2 * rim)
         z = z_sent[rows, :]
         z = z + pick(rcv_column[rows, :], rcv_low[rows, :], half, table[...], slots)
@@ -278,21 +280,22 @@
         normed, scale_inv = normed_of(act, w2_pair[...], b2, means[...])
         normed_ref[rows, :] = normed
         scale_ref[rows, :] = scale_inv
-        update = normed * gain + shift
-        out_ref[rows, :] = (x.astype(f32) + update).astype(bf16)
-        message = update.astype(bf16)
+        message = (normed * gain + shift).astype(bf16)
         message_ref[rows, :] = message
         first = (rcv_column.shape[0] + i * edge_tile) // lane
         hot = rows_of_ids(ids_ref, first, edge_tile // lane, 2 * rim, lambda row: row - nodes)
         total[...] += dot(hot, message)
 
-    each_tile(edge_ref.shape[0], tile)
+    each_tile(rcv_column.shape[0], tile)
     agg_near_ref[...] = total[pl.ds(near_at, rim), :].astype(bf16)
     agg_far_ref[...] = total[pl.ds(far_at, rim), :].astype(bf16)
 
 
-def collect_kernel(ids_ref, rcv_column, message_ref, edge_ref, agg_ref, turned_ref, total):
+def collect_kernel(
+    ids_ref, rcv_column, message_ref, edge_ref, normed_ref, vectors_ref, agg_ref, out_ref, total
+):
     half = total.shape[0]
+    gain, shift = vector(vectors_ref, 2), vector(vectors_ref, 3)
     total[...] = jnp.zeros_like(total)
 
     def tile(i):
@@ -300,7 +303,8 @@
         first = (rcv_column.shape[0] + i * edge_tile) // lane
         message = message_ref[rows, :].astype(f32)
         total[...] += spread(ids_ref, first, edge_tile // lane, half, rcv_column[rows, :], message)
-        turned_ref[:, rows] = edge_ref[rows, :].T
+        update = normed_ref[rows, :] * gain + shift
+        out_ref[rows, :] = (edge_ref[rows, :].astype(f32) + update).astype(bf16)
 
     each_tile(rcv_column.shape[0], tile)
     agg_ref[:half, :] = total[:, :lane]
@@ -316,134 +320,168 @@
 
 
 def node_kernel(
+    far_ref,
+    near_ref,
     node_ref,
     agg_ref,
-    near_ref,
-    far_ref,
     ids_ref,
+    weights_ref,
+    vectors_ref,
+    cot_ref,
+    x_ref,
+    act_ref,
+    normed_ref,
+    dz1_ref,
+    dz2_ref,
+    sums_ref,
+    dagg_ref,
+    rim_near_ref,
+    rim_far_ref,
+):
+    nodes = node_ref.shape[0]
+    returned = jnp.concatenate([near_ref[...], far_ref[...]], axis=0)
+    agg = (agg_ref[...] + dot(hot_lists(ids_ref, nodes), returned)).astype(bf16)
+    x = jnp.concatenate([node_ref[...], agg], axis=1)
+    x_ref[...] = x
+    w1 = weights_ref[4 * lane : 6 * lane]
+    w2 = weights_ref[6 * lane :]
+    z = dot(x, w1) + vector(vectors_ref, 4)
+    sig = sigmoid(z)
+    act = (z * sig).astype(bf16)
+    act_ref[...] = act
+    pair, b2 = centred_second(w2, vector(vectors_ref, 5))
+    means = mean_weights()
+    normed, scale_inv = normed_of(act, pair, b2, means)
+    normed_ref[...] = normed
+    upstream = cot_ref[...].astype(f32)
+    dz2 = back_norm(upstream, normed, scale_inv, vector(vectors_ref, 6), means)
+    dz2b = dz2.astype(bf16)
+    dz2_ref[...] = dz2b
+    dz1 = dot(dz2b, w2.T) * (sig * (1.0 + z * (1.0 - sig)))
+    dz1b = dz1.astype(bf16)
+    dz1_ref[...] = dz1b
+    dagg = dot(dz1b, w1[lane:].T).astype(bf16)
+    dagg_ref[...] = dagg
+    parity = parity_of_place()
+    first = ids_ref.shape[0] - 2
+    for side, rim_ref in ((parity, rim_far_ref), (1 - parity, rim_near_ref)):
+        column = column_of(ids_ref[pl.ds(first + side, 1), :]).astype(jnp.int16)
+        picked = hot_columns(column, (0, nodes))
+        rim_ref[...] = dot(picked, dagg).astype(bf16)
+    sums_ref[0:8, :] = eight_sums(dz1)
+    sums_ref[8:16, :] = eight_sums(dz2)
+
+
+def node_rest_kernel(
+    x_ref,
+    act_ref,
+    normed_ref,
+    dz1_ref,
+    dz2_ref,
+    sums_ref,
     weights_ref,
     vectors_ref,
     cot_ref,
     out_ref,
     base_ref,
-    dagg_ref,
-    rim_near_ref,
-    rim_far_ref,
     grads_ref,
 ):
-    nodes = node_ref.shape[0]
-    node = node_ref[...]
-    returned = jnp.concatenate([near_ref[...], far_ref[...]], axis=0)
-    agg = (agg_ref[...] + dot(hot_lists(ids_ref, nodes), returned)).astype(bf16)
-    x = jnp.concatenate([node, agg], axis=1)
-    w1 = weights_ref[4 * lane : 6 * lane]
-    w2 = weights_ref[6 * lane :]
-    z = dot(x, w1) + vector(vectors_ref, 4)
-    sig = sigmoid(z)
-    act = (z * sig).astype(bf16)
-    pair, b2 = centred_second(w2, vector(vectors_ref, 5))
-    means = mean_weights()
-    normed, scale_inv = normed_of(act, pair, b2, means)
-    gain = vector(vectors_ref, 6)
-    out_ref[...] = (node.astype(f32) + normed * gain + vector(vectors_ref, 7)).astype(bf16)
+    x = x_ref[...]
+    normed = normed_ref[...]
+    dz1b = dz1_ref[...]
+    update = normed * vector(vectors_ref, 6) + vector(vectors_ref, 7)
+    out_ref[...] = (x[:, :lane].astype(f32) + update).astype(bf16)
     upstream = cot_ref[...].astype(f32)
-    dz2 = back_norm(upstream, normed, scale_inv, gain, means)
-    dz2b = dz2.astype(bf16)
-    da = dot_back(dz2b, w2)
-    dz1 = da * sig * (1.0 + z * (1.0 - sig))
-    dz1b = dz1.astype(bf16)
-    dx = dot_back(dz1b, w1)
-    base_ref[...] = upstream + dx[:, :lane]
-    dagg = dx[:, lane:].astype(bf16)
-    dagg_ref[...] = dagg
-    parity = parity_of_place()
-    first = ids_ref.shape[0] - 2
-    for side, rim_ref in ((1 - parity, rim_near_ref), (parity, rim_far_ref)):
-        column = column_of(ids_ref[pl.ds(first + side, 1), :]).astype(jnp.int16)
-        picked = hot_columns(column, (0, nodes))
-        rim_ref[...] = dot(picked, dagg).astype(bf16)
+    base_ref[...] = upstream + dot(dz1b, weights_ref[4 * lane : 5 * lane].T)
     first = 2 * lane
     second = first + lane
     grads_ref[:first, :] = dot_rows(x, dz1b)
-    grads_ref[first:second, :] = dot_rows(act, dz2b)
-    sums = [column_sum(dz1), column_sum(dz2), column_sum(upstream * normed), column_sum(upstream)]
+    grads_ref[first:second, :] = dot_rows(act_ref[...], dz2_ref[...])
+    sums = [column_sum(sums_ref[0:8, :]), column_sum(sums_ref[8:16, :])]
+    sums += [column_sum(eight_sums(upstream * normed)), column_sum(eight_sums(upstream))]
     sums.append(jnp.zeros((sum_rows - len(sums), lane), f32))
     grads_ref[second:, :] = jnp.concatenate(sums, axis=0)
 
 
 def upstream_kernel(
-    rcv_column, rcv_low, dagg_ref, cot_ref, z_ref, up_ref, slope_ref, act_ref, table
-):
-    half = table.shape[0]
-    table[...] = side_by_side(dagg_ref[...])
+    rcv_column,
+    rcv_low,
+    node_ref,
+    far_ref,
+    near_ref,
+    dagg_ref,
+    cot_ref,
+    z_ref,
+    up_ref,
+    slope_ref,
+    turned_ref,
+    table,
+):
+    rim = near_ref.shape[0]
+    half = table.shape[0] - 2 * rim
+    nodes = 2 * half
+    parity = parity_of_place()
+    near_at = pl.multiple_of((1 - parity) * rim, rim)
+    far_at = pl.multiple_of(parity * rim, rim)
+    table[:half, :] = jnp.concatenate(
+        [side_by_side(node_ref[...]), side_by_side(dagg_ref[...])], axis=1
+    )
+    table[half:, :] = jnp.zeros((2 * rim, 4 * lane), bf16)
+    table[pl.ds(half + near_at, rim), lane : 2 * lane] = near_ref[...]
+    table[pl.ds(half + far_at, rim), lane : 2 * lane] = far_ref[...]
 
     def tile(i):
         rows = pl.ds(pl.multiple_of(i * edge_tile, edge_tile), edge_tile)
-        local = pick(rcv_column[rows, :], rcv_low[rows, :], half, table[...])
+        hot = hot_columns(rcv_low[rows, :], (0, half), (nodes, nodes + 2 * rim))
+        four = dot(hot, table[...])
+        upper = rcv_column[rows, :] >= half
+        received = jnp.where(upper, four[:, lane : 2 * lane], four[:, :lane])
+        local = jnp.where(upper, four[:, 3 * lane :], four[:, 2 * lane : 3 * lane])
         up_ref[rows, :] = cot_ref[rows, :].astype(f32) + local
         z = z_ref[rows, :]
         sig = sigmoid(z)
         slope_ref[rows, :] = sig * (1.0 + z * (1.0 - sig))
-        act_ref[:, rows] = (z * sig).astype(bf16).T
+        turned_ref[:lane, rows] = received.astype(bf16).T
+        turned_ref[lane:, rows] = (z * sig).astype(bf16).T
 
     each_tile(cot_ref.shape[0], tile)
 
 
 def edge_backward_kernel(
+    nodes,
+    dagg_far_ref,
+    dagg_near_ref,
     up_ref,
     normed_ref,
     scale_ref,
     slope_ref,
-    act_ref,
-    turned_ref,
-    ids_ref,
-    node_ref,
-    near_ref,
-    far_ref,
-    dagg_near_ref,
-    dagg_far_ref,
+    first_turned,
+    second_turned,
     weights_ref,
     vectors_ref,
     node_grads_ref,
-    snd_column,
-    rcv_column,
     rcv_low,
     dz_ref,
-    snd_sum_ref,
-    rcv_sum_ref,
-    far_back_ref,
     kept_ref,
     sent_ref,
-    halo,
     grads_ref,
     table,
     w2_turned,
     means,
-    snd_total,
-    rcv_total,
-    halo_total,
-    squares,
     sums,
 ):
-    nodes = node_ref.shape[0]
-    rim = near_ref.shape[0]
-    half = snd_total.shape[0]
+    rim = dagg_near_ref.shape[0]
     parity = parity_of_place()
-    near_at = pl.multiple_of((1 - parity) * rim, rim)
-    far_at = pl.multiple_of(parity * rim, rim)
     w2_turned[...] = weights_ref[3 * lane : 4 * lane].T
     gain = vector(vectors_ref, 2)
-    table[pl.ds(near_at, rim), :] = dagg_near_ref[...]
-    table[pl.ds(far_at, rim), :] = dagg_far_ref[...]
-    halo[pl.ds(near_at, rim), :] = near_ref[...]
-    halo[pl.ds(far_at, rim), :] = far_ref[...]
+    table[pl.ds(pl.multiple_of((1 - parity) * rim, rim), rim), :] = dagg_near_ref[...]
+    table[pl.ds(pl.multiple_of(parity * rim, rim), rim), :] = dagg_far_ref[...]
     means[...] = mean_weights()
-    for total in (snd_total, rcv_total, halo_total, squares, sums):
-        total[...] = jnp.zeros_like(total)
+    grads_ref[: 4 * lane, :] = jnp.zeros((4 * lane, lane), f32)
+    sums[...] = jnp.zeros_like(sums)
 
     def tile(i):
         rows = pl.ds(pl.multiple_of(i * edge_tile, edge_tile), edge_tile)
-        chunk = edge_tile // lane
         hot = hot_columns(rcv_low[rows, :], (nodes, nodes + 2 * rim))
         upstream = up_ref[rows, :] + dot(hot, table[...])
         normed = normed_ref[rows, :]
@@ -452,35 +490,16 @@
         dz1 = dot(dz2b, w2_turned[...]) * slope_ref[rows, :]
         dz1b = dz1.astype(bf16)
         dz_ref[rows, :] = dz1b
-        squares[:lane, :] += dot(turned_ref[:, rows], dz1b)
-        squares[lane:, :] += dot(act_ref[:, rows], dz2b)
+        grads_ref[: 2 * lane, :] += dot(first_turned[:, rows], dz1b)
+        grads_ref[2 * lane : 3 * lane, :] += dot(second_turned[:lane, rows], dz1b)
+        grads_ref[3 * lane : 4 * lane, :] += dot(second_turned[lane:, rows], dz2b)
         sums[0:8, :] += eight_sums(dz1)
         sums[8:16, :] += eight_sums(dz2)
         sums[16:24, :] += eight_sums(upstream * normed)
         sums[24:32, :] += eight_sums(upstream)
-        first = rcv_column.shape[0] // lane + i * chunk
-        snd_total[...] += spread(ids_ref, i * chunk, chunk, half, snd_column[rows, :], dz1)
-        rcv_total[...] += spread(ids_ref, first, chunk, half, rcv_column[rows, :], dz1)
-        slots = rows_of_ids(ids_ref, first, chunk, 2 * rim, lambda row: row - nodes)
-        halo_total[...] += dot(slots, dz1b)
 
     each_tile(up_ref.shape[0], tile)
-    snd_sum = jnp.concatenate([snd_total[:, :lane], snd_total[:, lane:]], axis=0).astype(bf16)
-    rcv_sum = jnp.concatenate([rcv_total[:, :lane], rcv_total[:, lane:]], axis=0).astype(bf16)
-    halo_sum = halo_total[...].astype(bf16)
-    snd_sum_ref[...] = snd_sum
-    rcv_sum_ref[...] = rcv_sum
-    w1_rcv = weights_ref[2 * lane : 3 * lane]
     kept = kept_ref.shape[0]
-    for at, back_ref in ((near_at, sent_ref.at[kept:]), (far_at, far_back_ref)):
-        returned = halo_total[pl.ds(at, rim), :].astype(bf16)
-        back_ref[...] = dot_back(returned, w1_rcv).astype(bf16)
-    extended = jnp.concatenate([node_ref[...], halo[...]], axis=0)
-    extended_sum = jnp.concatenate([rcv_sum, halo_sum], axis=0)
-    grads_ref[:lane, :] = squares[:lane, :]
-    grads_ref[lane : 2 * lane, :] = dot_rows(node_ref[...], snd_sum)
-    grads_ref[2 * lane : 3 * lane, :] = dot_rows(extended, extended_sum)
-    grads_ref[3 * lane : 4 * lane, :] = squares[lane:, :]
     node_rows = node_grads_ref.shape[0] - sum_rows
     last = 4 * lane + node_rows
     grads_ref[4 * lane : last, :] = node_grads_ref[:node_rows, :]
@@ -496,7 +515,49 @@
     own = lax.axis_index("sub")
     kept_ref[...] = grads_ref[pl.ds(pl.multiple_of(own * kept, sum_rows), kept), :]
     other = pl.multiple_of((1 - own) * kept, sum_rows)
-    sent_ref[:kept, :] = grads_ref[pl.ds(other, kept), :].astype(bf16)
+    sent_ref[...] = grads_ref[pl.ds(other, kept), :].astype(bf16)
+
+
+def scatter_kernel(
+    ids_ref,
+    dz_ref,
+    snd_column,
+    rcv_column,
+    weights_ref,
+    snd_sum_ref,
+    rcv_sum_ref,
+    far_back_ref,
+    near_back_ref,
+    snd_total,
+    rcv_total,
+    halo_total,
+):
+    half = snd_total.shape[0]
+    nodes = 2 * half
+    rim = near_back_ref.shape[0]
+    parity = parity_of_place()
+    for total in (snd_total, rcv_total, halo_total):
+        total[...] = jnp.zeros_like(total)
+
+    def tile(i):
+        rows = pl.ds(pl.multiple_of(i * edge_tile, edge_tile), edge_tile)
+        chunk = edge_tile // lane
+        dz1b = dz_ref[rows, :]
+        dz1 = dz1b.astype(f32)
+        first = rcv_column.shape[0] // lane + i * chunk
+        snd_total[...] += spread(ids_ref, i * chunk, chunk, half, snd_column[rows, :], dz1)
+        rcv_total[...] += spread(ids_ref, first, chunk, half, rcv_column[rows, :], dz1)
+        slots = rows_of_ids(ids_ref, first, chunk, 2 * rim, lambda row: row - nodes)
+        halo_total[...] += dot(slots, dz1b)
+
+    each_tile(dz_ref.shape[0], tile)
+    for total, out_ref in ((snd_total, snd_sum_ref), (rcv_total, rcv_sum_ref)):
+        out_ref[:half, :] = total[:, :lane].astype(bf16)
+        out_ref[half:, :] = total[:, lane:].astype(bf16)
+    w1_turned = weights_ref[2 * lane : 3 * lane].T
+    for side, back_ref in ((parity, far_back_ref), (1 - parity, near_back_ref)):
+        returned = halo_total[pl.ds(pl.multiple_of(side * rim, rim), rim), :].astype(bf16)
+        back_ref[...] = dot(returned, w1_turned).astype(bf16)
 
 
 def edge_grad_kernel(dz_ref, cot_ref, weights_ref, out_ref, w1_turned):
@@ -511,19 +572,20 @@
 
 
 def node_grad_kernel(
-    base_ref, snd_sum_ref, rcv_sum_ref, weights_ref, near_ref, far_ref, ids_ref, out_ref
-):
-    rim = far_ref.shape[0]
-    returned = jnp.concatenate([near_ref[near_ref.shape[0] - rim :, :], far_ref[...]], axis=0)
-    total = base_ref[...] + dot_back(snd_sum_ref[...], weights_ref[lane : 2 * lane])
-    total = total + dot_back(rcv_sum_ref[...], weights_ref[2 * lane : 3 * lane])
+    far_ref, near_ref, base_ref, snd_sum_ref, rcv_sum_ref, weights_ref, ids_ref, out_ref
+):
+    returned = jnp.concatenate([near_ref[...], far_ref[...]], axis=0)
+    total = base_ref[...] + dot(snd_sum_ref[...], weights_ref[lane : 2 * lane].T)
+    total = total + dot(rcv_sum_ref[...], weights_ref[2 * lane : 3 * lane].T)
     hot = hot_lists(ids_ref, base_ref.shape[0])
     out_ref[...] = (total + dot(hot, returned)).astype(bf16)
 
 
-def add_kernel(own_ref, other_ref, *refs):
-    own = own_ref[...].astype(f32)
-    refs[-1][...] = (own + other_ref[: own.shape[0], :].astype(f32)).astype(bf16)
+def add_kernel(passed, own_ref, other_ref, *refs):
+    out_refs = refs[len(refs) - passed - 1 :]
+    out_refs[0][...] = (own_ref[...].astype(f32) + other_ref[...].astype(f32)).astype(bf16)
+    for source, target in zip(refs[:passed], out_refs[1:]):
+        target[...] = source[...]
 
 
 def finish_kernel(own_ref, other_ref, *refs):
@@ -643,43 +705,38 @@
         sems=len(sources),
     )
     near, far = swap(rim_near, rim_far)
-    snd_column, rcv_column, snd_low, rcv_low, z_sent, rcv_local = call(
+    edge_shape = ((edges, lane), bf16)
+    wide_shape = ((edges, lane), f32)
+    turned_shape = ((2 * lane, edges), bf16)
+    node_shape = ((nodes, lane), bf16)
+    snd_column, rcv_column, rcv_low, z_sent, rcv_local, first_turned = call(
         prepare_kernel,
         [
             ((edges, lane), jnp.int32),
             ((edges, lane), jnp.int32),
             ((edges, lane), jnp.int16),
-            ((edges, lane), jnp.int16),
-            ((edges, lane), f32),
+            wide_shape,
             ((snd_half, 2 * lane), bf16),
+            turned_shape,
         ],
-        [((snd_half, 2 * lane), bf16)],
+        [((edges, lane), jnp.int16), ((snd_half, 2 * lane), bf16)],
         ids,
         node,
         weights,
         vectors,
         edge,
     )
-    edge_out, z, normed, scale, message, agg_near, agg_far = call(
+    z, normed, scale, message, agg_near, agg_far = call(
         edge_forward_kernel,
-        [
-            ((edges, lane), bf16),
-            ((edges, lane), f32),
-            ((edges, lane), f32),
-            ((edges, lane), f32),
-            ((edges, lane), bf16),
-            rim_shape,
-            rim_shape,
-        ],
+        [wide_shape, wide_shape, wide_shape, edge_shape, rim_shape, rim_shape],
         [
             ((snd_half + 2 * rim, 2 * lane), bf16),
             ((lane, 2 * lane), bf16),
             ((2 * lane, 2 * lane), bf16),
             ((2 * rim, lane), f32),
         ],
+        far,
         near,
-        far,
-        edge,
         ids,
         weights,
         vectors,
@@ -689,117 +746,152 @@
         rcv_local,
     )
     back_near, back_far = swap(agg_near, agg_far)
-    agg, turned = call(
+    agg, edge_out = call(
         collect_kernel,
-        [((nodes, lane), f32), ((lane, edges), bf16)],
+        [((nodes, lane), f32), edge_shape],
         [((snd_half, 2 * lane), f32)],
         ids,
         rcv_column,
         message,
         edge,
-    )
-    node_out, base, dagg, dagg_rim_near, dagg_rim_far, node_grads = call(
+        normed,
+        vectors,
+    )
+    node_x, node_act, node_normed, node_dz1, node_dz2, node_sums, dagg, rim_near, rim_far = call(
         node_kernel,
         [
-            ((nodes, lane), bf16),
+            ((nodes, 2 * lane), bf16),
+            node_shape,
             ((nodes, lane), f32),
-            ((nodes, lane), bf16),
+            node_shape,
+            node_shape,
+            ((16, lane), f32),
+            node_shape,
             rim_shape,
             rim_shape,
-            ((3 * lane + sum_rows, lane), f32),
         ],
         [],
+        back_far,
+        back_near,
         node,
         agg,
-        back_near,
-        back_far,
         ids,
         weights,
         vectors,
         node_cot,
     )
-    dagg_near, dagg_far = swap(dagg_rim_near, dagg_rim_far)
-    upstream, slope, act = call(
+    dagg_near, dagg_far = swap(rim_near, rim_far)
+    upstream, slope, second_turned = call(
         upstream_kernel,
-        [((edges, lane), f32), ((edges, lane), f32), ((lane, edges), bf16)],
-        [((snd_half, 2 * lane), bf16)],
+        [wide_shape, wide_shape, turned_shape],
+        [((snd_half + 2 * rim, 4 * lane), bf16)],
         rcv_column,
         rcv_low,
+        node,
+        far,
+        near,
         dagg,
         edge_cot,
         z,
     )
-    dz, snd_sum, rcv_sum, grad_far, grads_kept, grads_sent = call(
-        edge_backward_kernel,
+    node_out, base, node_grads = call(
+        node_rest_kernel,
+        [node_shape, ((nodes, lane), f32), ((3 * lane + sum_rows, lane), f32)],
+        [],
+        node_x,
+        node_act,
+        node_normed,
+        node_dz1,
+        node_dz2,
+        node_sums,
+        weights,
+        vectors,
+        node_cot,
+    )
+    half_shape = ((kept, lane), bf16)
+    dz, grads_kept, grads_sent = call(
+        functools.partial(edge_backward_kernel, nodes),
+        [edge_shape, ((kept, lane), f32), half_shape],
         [
-            ((edges, lane), bf16),
-            ((nodes, lane), bf16),
-            ((nodes, lane), bf16),
-            rim_shape,
-            ((kept, lane), f32),
-            ((kept + rim, lane), bf16),
-        ],
-        [
-            ((2 * rim, lane), bf16),
             ((2 * kept, lane), f32),
             ((2 * rim, lane), bf16),
             ((lane, lane), bf16),
             ((2 * lane, 2 * lane), bf16),
-            ((snd_half, 2 * lane), f32),
-            ((snd_half, 2 * lane), f32),
-            ((2 * rim, lane), f32),
-            ((2 * lane, lane), f32),
             ((32, lane), f32),
         ],
+        dagg_far,
+        dagg_near,
         upstream,
         normed,
         scale,
         slope,
-        act,
-        turned,
-        ids,
-        node,
-        near,
-        far,
-        dagg_near,
-        dagg_far,
+        first_turned,
+        second_turned,
         weights,
         vectors,
         node_grads,
+        rcv_low,
+    )
+    core_pairs = [(0, 1), (1, 0)]
+    other = lax.ppermute(grads_sent, "sub", core_pairs)
+    (grads,) = call(functools.partial(add_kernel, 0), [half_shape], [], grads_kept, other)
+    snd_sum, rcv_sum, back_far, back_near = call(
+        scatter_kernel,
+        [node_shape, node_shape, rim_shape, rim_shape],
+        [
+            ((snd_half, 2 * lane), f32),
+            ((snd_half, 2 * lane), f32),
+            ((2 * rim, lane), f32),
+        ],
+        ids,
+        dz,
         snd_column,
         rcv_column,
-        rcv_low,
-    )
-    returned_near, returned_far = swap(grads_sent, grad_far)
+        weights,
+    )
     (edge_grad,) = call(
         edge_grad_kernel,
-        [((edges, lane), bf16)],
+        [edge_shape],
         [((lane, lane), bf16)],
         dz,
         edge_cot,
         weights,
     )
-    (node_grad,) = call(
-        node_grad_kernel,
-        [((nodes, lane), bf16)],
-        [],
-        base,
-        snd_sum,
-        rcv_sum,
-        weights,
-        returned_near,
-        returned_far,
-        ids,
-    )
-    half_shape = ((kept, lane), bf16)
-    (grads,) = call(add_kernel, [half_shape], [], grads_kept, returned_near)
-    between = [[returned_far, edge_grad], [node_grad]]
+    node_grad = None
     for number, (axis, pairs) in enumerate(sum_rounds()):
         other = lax.ppermute(grads, axis, pairs)
-        early = between[number] if number < len(between) else []
-        written = 1 if early else 0
-        (grads,) = call(add_kernel, [half_shape], [], grads, other, *early, anywhere=written)
-    others = lax.ppermute(grads, "sub", [(0, 1), (1, 0)])
+        passed, written = [], []
+        if number == 0:
+            passed, written = [back_near, back_far], [edge_grad]
+        elif number == 1:
+            passed = list(swap(back_near, back_far))
+        elif number == 2:
+            (node_grad,) = call(
+                node_grad_kernel,
+                [node_shape],
+                [],
+                back_far,
+                back_near,
+                base,
+                snd_sum,
+                rcv_sum,
+                weights,
+                ids,
+            )
+            written = [node_grad]
+        grads, *passed = call(
+            functools.partial(add_kernel, len(passed)),
+            [half_shape] + [rim_shape] * len(passed),
+            [],
+            grads,
+            other,
+            *passed,
+            *written,
+            anywhere=len(written),
+        )
+        if passed:
+            back_near, back_far = passed
+    others = lax.ppermute(grads, "sub", core_pairs)
     matrices = [3 * lane, lane, 2 * lane, lane]
     totals = call(
         finish_kernel,

time: 58.5 us -> 59.6 us (1.019)
  Pallas kernels: 24.4 us -> 28.5 us
  starting transfers between devices: 22.5 us -> 19.3 us
    pallas_call x14 -> x16, Pallas kernels: 24.4 us -> 28.5 us  [call(): pl.pallas_call(kernel, out_shape=[jax.ShapeDtypeStruct(shape, dtype) for...]
    ppermute x4, waiting for transfers between devices: 0.37 us -> 2.84 us  [swap(): far = lax.ppermute(far, chain, outer)]
    ppermute x3, waiting for transfers between devices: 7.7 us -> 5.42 us  [on_device(): other = lax.ppermute(grads, axis, pairs)]
    ppermute x3, starting transfers between devices: 5 us -> 3.22 us  [on_device(): other = lax.ppermute(grads, axis, pairs)]
    ppermute x4, starting transfers between devices: 15.7 us -> 14.3 us  [swap(): far = lax.ppermute(far, chain, outer)]
    ppermute x4, waiting for transfers between devices: 1.37 us -> 0.01 us  [swap(): return (lax.ppermute(near, chain, inner), far)]
    ppermute x1 -> x2, waiting for transfers between devices: 0.97 us -> 2.29 us  [the longest x1 1.32 us: on_device(): others = lax.ppermute(grads, 'sub', core_pairs)]
    ppermute x4, starting transfers between devices: 0.27 us -> 1.13 us  [swap(): return (lax.ppermute(near, chain, inner), far)]
  transfers between devices with their start and end apart: 12 -> 13, of which waited for: 6 -> 4; matrix products, arithmetic and copies ran while one was open for 0% -> 0% of each run, Pallas kernels for 14% -> 26%
where the time goes in v7:
time: 59.6 us; the launch traced here: 59.3 us
  Pallas kernels  28.5 us (48%)
  starting transfers between devices  19.3 us (32%)
  waiting for transfers between devices  10.6 us (18%)
  between operations  0.99 us (2%)
    pallas_call x16, Pallas kernels, call(): pl.pallas_call(kernel, out_shape=[jax.ShapeDtypeStruct(shape, dtype) for...  28.5 us
    ppermute x4, starting transfers between devices, swap(): far = lax.ppermute(far, chain, outer)  14.3 us
    ppermute x3, waiting for transfers between devices, on_device(): other = lax.ppermute(grads, axis, pairs)  5.42 us
    ppermute x3, starting transfers between devices, on_device(): other = lax.ppermute(grads, axis, pairs)  3.22 us
    ppermute x4, waiting for transfers between devices, swap(): far = lax.ppermute(far, chain, outer)  2.84 us
    ppermute x1, waiting for transfers between devices, on_device(): others = lax.ppermute(grads, 'sub', core_pairs)  1.32 us
  transfers between devices with their start and end apart: 13, of which 4 were waited for; matrix products, arithmetic and copies ran while one was open for 0% of the time, Pallas kernels for 26%

profile of v7, /device:TPU:1, one launch (start us, length us, event | category | flops | bytes accessed | tf_op | source)
XLA Modules:
  0.0 59.3 jit_solution(17363187120987477941)
XLA Ops:
  0.7 1.9 %shard_map.306 = (bf16[1024,128]{1,0:T(8,128)(2,1)S(1)}, s32[50,128]{1,0:T(8,128)S(1)}, bf16[3072,128]{1,0:T(8,128)(2,1)S(1)}, bf16[3072,128]{1,0:T(8,128)(2,1)S...) custom-call(bf16[1024,128]{1,0:T(8,128)(2,1)} %bitcast.31, ...), custom_call_target="tpu_custom_call" | custom-call | bytes 2356224 | tf_op jit(solution)/shard_map/pallas_call | solution.py:616
  2.5 4.6 %collective-permute-start = (bf16[128,128]{1,0:T(8,128)(2,1)S(1)}, bf16[128,128]{1,0:T(8,128)(2,1)S(1)}, u32[]{:S(2)}, u32[]{:S(2)}) collective-permute-start(bf16[128,128]{1,0:T(8,128)(2,1)S(1)} %get-tuple-element.79), channel_id=1, source_target_pairs={{1,4},{5,8},{9,12},{4,1},{8,5},{12,9},{3,6},{7,10},{11,14},{6,3},{... | collective-permute-start | bytes 98312 | tf_op jit(solution)/shard_map/ppermute | solution.py:633
  7.2 3.5 %shard_map.307 = (s32[3072,128]{1,0:T(8,128)S(1)}, s32[3072,128]{1,0:T(8,128)S(1)}, s16[3072,128]{1,0:T(8,128)(2,1)S(1)}, f32[3072,128]{1,0:T(8,128)S(1)}, bf16[...) custom-call(s32[50,128]{1,0:T(8,128)S(1)} %get-tuple-element.81.ids_ref, ...), custom_call_target="tpu_custom_call" | custom-call | bytes 1307648 | tf_op jit(solution)/shard_map/pallas_call | solution.py:616
  10.7 4.8 %shard_map.308 = (f32[3072,128]{1,0:T(8,128)S(1)}, f32[3072,128]{1,0:T(8,128)S(1)}, f32[3072,128]{1,0:T(8,128)S(1)}, bf16[3072,128]{1,0:T(8,128)(2,1)S(1)}, bf16...) custom-call(bf16[128,128]{1,0:T(8,128)(2,1)S(1)} %collective-permute-done.far_ref, ...), custom_call_target="tpu_custom_call" | custom-call | bytes 4518912 | tf_op jit(solution)/shard_map/pallas_call | solution.py:616
  15.5 3.6 %collective-permute-start.2 = (bf16[128,128]{1,0:T(8,128)(2,1)S(1)}, bf16[128,128]{1,0:T(8,128)(2,1)S(1)}, u32[]{:S(2)}, u32[]{:S(2)}) collective-permute-start(bf16[128,128]{1,0:T(8,128)(2,1)S(1)} %get-tuple-element.90), channel_id=1, source_target_pairs={{1,4},{5,8},{9,12},{4,1},{8,5},{12,9},{3,6},{7,10},{11,14},{6,3},{... | collective-permute-start | bytes 98312 | tf_op jit(solution)/shard_map/ppermute | solution.py:633
  19.2 2.0 %shard_map.309 = (f32[1024,128]{1,0:T(8,128)S(1)}, bf16[3072,128]{1,0:T(8,128)(2,1)}) custom-call(s32[50,128]{1,0:T(8,128)S(1)} %get-tuple-element.81.ids_ref, s32[3072,128]{1,0:T(8,128)S(1)} %get-tuple-element.86.rcv_column, bf16[3072,128]{1,0:T(8,128)(2,1)S(1)} %get-tuple-element.92.message_ref, bf16[3072,128]{1,0:T(8,128)(2,1)S(1)} %get-tuple-element.85.edge_ref, ...), custom_call_target="tpu_custom_call" | custom-call | bytes 4748288 | tf_op jit(solution)/shard_map/pallas_call | solution.py:616
  21.2 1.6 %shard_map.310 = (bf16[1024,256]{1,0:T(8,128)(2,1)S(1)}, bf16[1024,128]{1,0:T(8,128)(2,1)S(1)}, f32[1024,128]{1,0:T(8,128)S(1)}, bf16[1024,128]{1,0:T(8,128)(2,1...) custom-call(bf16[128,128]{1,0:T(8,128)(2,1)S(1)} %collective-permute, ...), custom_call_target="tpu_custom_call" | custom-call | bytes 1373184 | tf_op jit(solution)/shard_map/pallas_call | solution.py:616
  22.8 3.8 %collective-permute-start.4 = (bf16[128,128]{1,0:T(8,128)(2,1)S(1)}, bf16[128,128]{1,0:T(8,128)(2,1)S(1)}, u32[]{:S(2)}, u32[]{:S(2)}) collective-permute-start(bf16[128,128]{1,0:T(8,128)(2,1)S(1)} %get-tuple-element.104), channel_id=1, source_target_pairs={{1,4},{5,8},{9,12},{4,1},{8,5},{12,9},{3,6},{7,10},{11,14},{6,3},{... | collective-permute-start | bytes 98312 | tf_op jit(solution)/shard_map/ppermute | solution.py:633
  26.6 1.0 %shard_map.311 = (bf16[1024,128]{1,0:T(8,128)(2,1)}, f32[1024,128]{1,0:T(8,128)S(1)}, f32[400,128]{1,0:T(8,128)S(1)}) custom-call(bf16[1024,256]{1,0:T(8,128)(2,1)S(1)} %get-tuple-element.96.x_ref, bf16[1024,128]{1,0:T(8,128)(2,1)S(1)} %get-tuple-element.97.act_ref, f32[1024,128]{1,0:T(8,128)S(1)} %get-tuple-element.98.normed_ref, ...), custom_call_target="tpu_custom_call" | custom-call | bytes 2338816 | tf_op jit(solution)/shard_map/pallas_call | solution.py:616
  27.6 3.2 %shard_map.312 = (f32[3072,128]{1,0:T(8,128)S(1)}, f32[3072,128]{1,0:T(8,128)S(1)}, bf16[256,3072]{1,0:T(8,128)(2,1)S(1)}) custom-call(s32[3072,128]{1,0:T(8,128)S(1)} %get-tuple-element.86.rcv_column, s16[3072,128]{1,0:T(8,128)(2,1)S(1)} %get-tuple-element.87.rcv_low, bf16[1024,128]{1,0:T(8,128)(2,1)S(1)} %get-tuple-element.84.node_ref, ...), custom_call_target="tpu_custom_call" | custom-call | bytes 5308416 | tf_op jit(solution)/shard_map/pallas_call | solution.py:616
  30.8 4.1 %shard_map.313 = (bf16[3072,128]{1,0:T(8,128)(2,1)S(1)}, f32[464,128]{1,0:T(8,128)S(1)}, bf16[464,128]{1,0:T(8,128)(2,1)S(1)}) custom-call(bf16[128,128]{1,0:T(8,128)(2,1)S(1)} %collective-permute-done.4.dagg_far_ref, bf16[128,128]{1,0:T(8,128)(2,1)S(1)} %collective-permute-done.5.dagg_near_ref, f32[3072,128]{1,0:T(8,128)S(1)} %get-tuple-element.109.up_ref, ...), custom_call_target="tpu_custom_call" | custom-call | bytes 10727424 | tf_op jit(solution)/shard_map/pallas_call | solution.py:616
  35.4 1.0 %collective-permute-done.6.other_ref = bf16[464,128]{1,0:T(8,128)(2,1)S(1)} collective-permute-done((bf16[464,128]{1,0:T(8,128)(2,1)S(1)}, bf16[464,128]{1,0:T(8,128)(2,1)S(1)}, u32[]{:S(2)}, u32[]{:S(2)}) %collective-permute-start.6) | collective-permute-done | bytes 118816 | tf_op jit(solution)/shard_map/ppermute | solution.py:836
  36.4 1.3 %collective-permute-start.7 = (bf16[464,128]{1,0:T(8,128)(2,1)S(1)}, bf16[464,128]{1,0:T(8,128)(2,1)S(1)}, u32[]{:S(2)}, u32[]{:S(2)}) collective-permute-start(bf16[464,128]{1,0:T(8,128)(2,1)S(1)} %shard_map.314.own_ref), channel_id=1, source_target_pairs={{0,2},{2,0},{1,3},{3,1},{4,6},{6,4},{5,7},{7,5},{8,10},{10,8},{9,1... | collective-permute-start | bytes 356360 | tf_op jit(solution)/shard_map/ppermute | solution.py:862
  37.7 1.5 %shard_map.316.refs_2_ = bf16[3072,128]{1,0:T(8,128)(2,1)} custom-call(bf16[3072,128]{1,0:T(8,128)(2,1)S(1)} %get-tuple-element.117.dz_ref, bf16[3072,128]{1,0:T(8,128)(2,1)S(1)} %get-tuple-element.107.cot_ref, bf16[896,128]{1,0:T(8,128)(2,1)S(1)} %get-tuple-element.82.weights_ref), custom_call_target="tpu_custom_call" | custom-call | bytes 1802240 | tf_op jit(solution)/shard_map/pallas_call | solution.py:616
  39.2 3.0 %shard_map.315 = (bf16[1024,128]{1,0:T(8,128)(2,1)S(1)}, bf16[1024,128]{1,0:T(8,128)(2,1)S(1)}, bf16[128,128]{1,0:T(8,128)(2,1)S(1)}, bf16[128,128]{1,0:T(8,128)(2,1)S(1)}) custom-call(s32[50,128]{1,0:T(8,128)S(1)} %get-tuple-element.81.ids_ref, bf16[3072,128]{1,0:T(8,128)(2,1)S(1)} %get-tuple-element.117.dz_ref, ...), custom_call_target="tpu_custom_call" | custom-call | bytes 4187136 | tf_op jit(solution)/shard_map/pallas_call | solution.py:616
  42.2 0.9 %collective-permute-start.8 = (bf16[464,128]{1,0:T(8,128)(2,1)S(1)}, bf16[464,128]{1,0:T(8,128)(2,1)S(1)}, u32[]{:S(2)}, u32[]{:S(2)}) collective-permute-start(bf16[464,128]{1,0:T(8,128)(2,1)S(1)} %get-tuple-element.121.own_ref), channel_id=1, source_target_pairs={{0,4},{4,0},{8,12},{12,8},{1,5},{5,1},{9,13},{13,9},{2,6},{6,2},{1... | collective-permute-start | bytes 356360 | tf_op jit(solution)/shard_map/ppermute | solution.py:862
  43.2 0.9 %collective-permute-start.9 = (bf16[128,128]{1,0:T(8,128)(2,1)S(1)}, bf16[128,128]{1,0:T(8,128)(2,1)S(1)}, u32[]{:S(2)}, u32[]{:S(2)}) collective-permute-start(bf16[128,128]{1,0:T(8,128)(2,1)S(1)} %get-tuple-element.122), channel_id=1, source_target_pairs={{0,1},{4,5},{8,9},{12,13},{1,0},{5,4},{9,8},{13,12},{2,3},{6,7},{1... | collective-permute-start | bytes 98312 | tf_op jit(solution)/shard_map/ppermute | solution.py:634
  44.1 2.4 %collective-permute-start.10 = (bf16[128,128]{1,0:T(8,128)(2,1)S(1)}, bf16[128,128]{1,0:T(8,128)(2,1)S(1)}, u32[]{:S(2)}, u32[]{:S(2)}) collective-permute-start(bf16[128,128]{1,0:T(8,128)(2,1)S(1)} %get-tuple-element.123), channel_id=1, source_target_pairs={{1,4},{5,8},{9,12},{4,1},{8,5},{12,9},{3,6},{7,10},{11,14},{6,3},{... | collective-permute-start | bytes 98312 | tf_op jit(solution)/shard_map/ppermute | solution.py:633
  46.5 2.8 %collective-permute-done.10.refs_1_ = bf16[128,128]{1,0:T(8,128)(2,1)S(1)} collective-permute-done((bf16[128,128]{1,0:T(8,128)(2,1)S(1)}, bf16[128,128]{1,0:T(8,128)(2,1)S(1)}, u32[]{:S(2)}, u32[]{:S(2)}) %collective-permute-start.10) | collective-permute-done | bytes 32800 | tf_op jit(solution)/shard_map/ppermute | solution.py:633
  49.3 1.0 %collective-permute-start.11 = (bf16[464,128]{1,0:T(8,128)(2,1)S(1)}, bf16[464,128]{1,0:T(8,128)(2,1)S(1)}, u32[]{:S(2)}, u32[]{:S(2)}) collective-permute-start(bf16[464,128]{1,0:T(8,128)(2,1)S(1)} %get-tuple-element.129.own_ref), channel_id=1, source_target_pairs={{0,8},{4,12},{8,0},{12,4},{1,9},{5,13},{9,1},{13,5},{2,10},{6,14},... | collective-permute-start | bytes 356360 | tf_op jit(solution)/shard_map/ppermute | solution.py:862
  50.3 1.1 %shard_map.319.refs_0_ = bf16[1024,128]{1,0:T(8,128)(2,1)} custom-call(bf16[128,128]{1,0:T(8,128)(2,1)S(1)} %get-tuple-element.124.far_ref, bf16[128,128]{1,0:T(8,128)(2,1)S(1)} %get-tuple-element.125.near_ref, f32[1024,128]{1,0:T(8,128)S(1)} %get-tuple-element.126.base_ref, bf16[1024,128]{1,0:T(8,128)(2,1)S(1)} %get-tuple-element.127.snd_sum_ref, ...), custom_call_target="tpu_custom_call" | custom-call | bytes 1369088 | tf_op jit(solution)/shard_map/pallas_call | solution.py:616
  51.5 5.4 %collective-permute-done.11.other_ref = bf16[464,128]{1,0:T(8,128)(2,1)S(1)} collective-permute-done((bf16[464,128]{1,0:T(8,128)(2,1)S(1)}, bf16[464,128]{1,0:T(8,128)(2,1)S(1)}, u32[]{:S(2)}, u32[]{:S(2)}) %collective-permute-start.11) | collective-permute-done | bytes 118816 | tf_op jit(solution)/shard_map/ppermute | solution.py:862
  57.0 1.3 %collective-permute-done.12.other_ref = bf16[464,128]{1,0:T(8,128)(2,1)S(1)} collective-permute-done((bf16[464,128]{1,0:T(8,128)(2,1)S(1)}, bf16[464,128]{1,0:T(8,128)(2,1)S(1)}, u32[]{:S(2)}, u32[]{:S(2)}) %collective-permute-start.12) | collective-permute-done | bytes 118816 | tf_op jit(solution)/shard_map/ppermute | solution.py:894
  58.3 0.8 %shard_map.321 = (f32[384,128]{1,0:T(8,128)}, f32[128,128]{1,0:T(8,128)}, f32[256,128]{1,0:T(8,128)}, f32[128,128]{1,0:T(8,128)}, f32[1,128]{1,0:T(1,128)}, /*in...) custom-call(bf16[464,128]{1,0:T(8,128)(2,1)S(1)} %shard_map.320.own_, ...), custom_call_target="tpu_custom_call" | custom-call | bytes 237568 | tf_op jit(solution)/shard_map/pallas_call | solution.py:616
  (18 shorter events, 1.0 us)
Async XLA Ops:
  2.5 8.1 %collective-permute-start = (bf16[128,128]{1,0:T(8,128)(2,1)S(1)}, bf16[128,128]{1,0:T(8,128)(2,1)S(1)}, u32[]{:S(2)}, u32[]{:S(2)}) collective-permute-start(bf16[128,128]{1,0:T(8,128)(2,1)S(1)} %get-tuple-element.79), channel_id=1, source_target_pairs={{1,4},{5,8},{9,12},{4,1},{8,5},{12,9},{3,6},{7,10},{11,14},{6,3},{... | collective-permute-start | bytes 98312 | tf_op jit(solution)/shard_map/ppermute | solution.py:633
  7.1 3.5 %collective-permute-start.1 = (bf16[128,128]{1,0:T(8,128)(2,1)S(1)}, bf16[128,128]{1,0:T(8,128)(2,1)S(1)}, u32[]{:S(2)}, u32[]{:S(2)}) collective-permute-start(bf16[128,128]{1,0:T(8,128)(2,1)S(1)} %get-tuple-element.80), channel_id=1, source_target_pairs={{0,1},{4,5},{8,9},{12,13},{1,0},{5,4},{9,8},{13,12},{2,3},{6,7},{1... | collective-permute-start | bytes 98312 | tf_op jit(solution)/shard_map/ppermute | solution.py:634
  15.5 5.6 %collective-permute-start.2 = (bf16[128,128]{1,0:T(8,128)(2,1)S(1)}, bf16[128,128]{1,0:T(8,128)(2,1)S(1)}, u32[]{:S(2)}, u32[]{:S(2)}) collective-permute-start(bf16[128,128]{1,0:T(8,128)(2,1)S(1)} %get-tuple-element.90), channel_id=1, source_target_pairs={{1,4},{5,8},{9,12},{4,1},{8,5},{12,9},{3,6},{7,10},{11,14},{6,3},{... | collective-permute-start | bytes 98312 | tf_op jit(solution)/shard_map/ppermute | solution.py:633
  19.1 2.0 %collective-permute-start.3 = (bf16[128,128]{1,0:T(8,128)(2,1)S(1)}, bf16[128,128]{1,0:T(8,128)(2,1)S(1)}, u32[]{:S(2)}, u32[]{:S(2)}) collective-permute-start(bf16[128,128]{1,0:T(8,128)(2,1)S(1)} %get-tuple-element.91), channel_id=1, source_target_pairs={{0,1},{4,5},{8,9},{12,13},{1,0},{5,4},{9,8},{13,12},{2,3},{6,7},{1... | collective-permute-start | bytes 98312 | tf_op jit(solution)/shard_map/ppermute | solution.py:634
  22.8 8.0 %collective-permute-start.4 = (bf16[128,128]{1,0:T(8,128)(2,1)S(1)}, bf16[128,128]{1,0:T(8,128)(2,1)S(1)}, u32[]{:S(2)}, u32[]{:S(2)}) collective-permute-start(bf16[128,128]{1,0:T(8,128)(2,1)S(1)} %get-tuple-element.104), channel_id=1, source_target_pairs={{1,4},{5,8},{9,12},{4,1},{8,5},{12,9},{3,6},{7,10},{11,14},{6,3},{... | collective-permute-start | bytes 98312 | tf_op jit(solution)/shard_map/ppermute | solution.py:633
  26.5 4.3 %collective-permute-start.5 = (bf16[128,128]{1,0:T(8,128)(2,1)S(1)}, bf16[128,128]{1,0:T(8,128)(2,1)S(1)}, u32[]{:S(2)}, u32[]{:S(2)}) collective-permute-start(bf16[128,128]{1,0:T(8,128)(2,1)S(1)} %get-tuple-element.105), channel_id=1, source_target_pairs={{0,1},{4,5},{8,9},{12,13},{1,0},{5,4},{9,8},{13,12},{2,3},{6,7},{1... | collective-permute-start | bytes 98312 | tf_op jit(solution)/shard_map/ppermute | solution.py:634
  34.9 1.6 %collective-permute-start.6 = (bf16[464,128]{1,0:T(8,128)(2,1)S(1)}, bf16[464,128]{1,0:T(8,128)(2,1)S(1)}, u32[]{:S(2)}, u32[]{:S(2)}) collective-permute-start(bf16[464,128]{1,0:T(8,128)(2,1)S(1)} %get-tuple-element.116), channel_id=1, source_target_pairs={{0,1},{1,0},{2,3},{3,2},{4,5},{5,4},{6,7},{7,6},{8,9},{9,8},{10,11... | collective-permute-start | bytes 356360 | tf_op jit(solution)/shard_map/ppermute | solution.py:836
  36.4 5.7 %collective-permute-start.7 = (bf16[464,128]{1,0:T(8,128)(2,1)S(1)}, bf16[464,128]{1,0:T(8,128)(2,1)S(1)}, u32[]{:S(2)}, u32[]{:S(2)}) collective-permute-start(bf16[464,128]{1,0:T(8,128)(2,1)S(1)} %shard_map.314.own_ref), channel_id=1, source_target_pairs={{0,2},{2,0},{1,3},{3,1},{4,6},{6,4},{5,7},{7,5},{8,10},{10,8},{9,1... | collective-permute-start | bytes 356360 | tf_op jit(solution)/shard_map/ppermute | solution.py:862
  42.2 7.1 %collective-permute-start.8 = (bf16[464,128]{1,0:T(8,128)(2,1)S(1)}, bf16[464,128]{1,0:T(8,128)(2,1)S(1)}, u32[]{:S(2)}, u32[]{:S(2)}) collective-permute-start(bf16[464,128]{1,0:T(8,128)(2,1)S(1)} %get-tuple-element.121.own_ref), channel_id=1, source_target_pairs={{0,4},{4,0},{8,12},{12,8},{1,5},{5,1},{9,13},{13,9},{2,6},{6,2},{1... | collective-permute-start | bytes 356360 | tf_op jit(solution)/shard_map/ppermute | solution.py:862
  43.2 3.3 %collective-permute-start.9 = (bf16[128,128]{1,0:T(8,128)(2,1)S(1)}, bf16[128,128]{1,0:T(8,128)(2,1)S(1)}, u32[]{:S(2)}, u32[]{:S(2)}) collective-permute-start(bf16[128,128]{1,0:T(8,128)(2,1)S(1)} %get-tuple-element.122), channel_id=1, source_target_pairs={{0,1},{4,5},{8,9},{12,13},{1,0},{5,4},{9,8},{13,12},{2,3},{6,7},{1... | collective-permute-start | bytes 98312 | tf_op jit(solution)/shard_map/ppermute | solution.py:634
  44.1 5.2 %collective-permute-start.10 = (bf16[128,128]{1,0:T(8,128)(2,1)S(1)}, bf16[128,128]{1,0:T(8,128)(2,1)S(1)}, u32[]{:S(2)}, u32[]{:S(2)}) collective-permute-start(bf16[128,128]{1,0:T(8,128)(2,1)S(1)} %get-tuple-element.123), channel_id=1, source_target_pairs={{1,4},{5,8},{9,12},{4,1},{8,5},{12,9},{3,6},{7,10},{11,14},{6,3},{... | collective-permute-start | bytes 98312 | tf_op jit(solution)/shard_map/ppermute | solution.py:633
  49.3 7.6 %collective-permute-start.11 = (bf16[464,128]{1,0:T(8,128)(2,1)S(1)}, bf16[464,128]{1,0:T(8,128)(2,1)S(1)}, u32[]{:S(2)}, u32[]{:S(2)}) collective-permute-start(bf16[464,128]{1,0:T(8,128)(2,1)S(1)} %get-tuple-element.129.own_ref), channel_id=1, source_target_pairs={{0,8},{4,12},{8,0},{12,4},{1,9},{5,13},{9,1},{13,5},{2,10},{6,14},... | collective-permute-start | bytes 356360 | tf_op jit(solution)/shard_map/ppermute | solution.py:862
  56.9 1.4 %collective-permute-start.12 = (bf16[464,128]{1,0:T(8,128)(2,1)S(1)}, bf16[464,128]{1,0:T(8,128)(2,1)S(1)}, u32[]{:S(2)}, u32[]{:S(2)}) collective-permute-start(bf16[464,128]{1,0:T(8,128)(2,1)S(1)} %shard_map.320.own_ref), channel_id=1, source_target_pairs={{0,1},{1,0},{2,3},{3,2},{4,5},{5,4},{6,7},{7,6},{8,9},{9,8},{10,11... | collective-permute-start | bytes 356360 | tf_op jit(solution)/shard_map/ppermute | solution.py:894

commit v8 on v7

--- a/solution.py
+++ b/solution.py
@@ -226,15 +226,14 @@
         x = edge_ref[rows, :]
         sent = pick(snd_column[rows, :], snd_low[rows, :], half, snd_table[...]).astype(bf16)
         z_ref[rows, :] = dot(jnp.concatenate([x, sent], axis=1), w1) + b1
-        turned_ref[:lane, rows] = x.T
-        turned_ref[lane:, rows] = sent.T
+        turned_ref[:, rows] = sent.T
 
     each_tile(edge_ref.shape[0], tile)
 
 
 def edge_forward_kernel(
+    near_ref,
     far_ref,
-    near_ref,
     ids_ref,
     weights_ref,
     vectors_ref,
@@ -292,19 +291,38 @@
 
 
 def collect_kernel(
-    ids_ref, rcv_column, message_ref, edge_ref, normed_ref, vectors_ref, agg_ref, out_ref, total
-):
+    ids_ref,
+    rcv_column,
+    rcv_low,
+    message_ref,
+    node_ref,
+    near_ref,
+    far_ref,
+    agg_ref,
+    turned_ref,
+    table,
+    total,
+):
+    rim = near_ref.shape[0]
     half = total.shape[0]
-    gain, shift = vector(vectors_ref, 2), vector(vectors_ref, 3)
+    nodes = 2 * half
+    parity = parity_of_place()
+    near_at = pl.multiple_of((1 - parity) * rim, rim)
+    far_at = pl.multiple_of(parity * rim, rim)
+    table[:half, :] = side_by_side(node_ref[...])
+    table[half:, :lane] = jnp.zeros((2 * rim, lane), bf16)
+    table[pl.ds(half + near_at, rim), lane:] = near_ref[...]
+    table[pl.ds(half + far_at, rim), lane:] = far_ref[...]
     total[...] = jnp.zeros_like(total)
 
     def tile(i):
         rows = pl.ds(pl.multiple_of(i * edge_tile, edge_tile), edge_tile)
         first = (rcv_column.shape[0] + i * edge_tile) // lane
+        rcv = rcv_column[rows, :]
         message = message_ref[rows, :].astype(f32)
-        total[...] += spread(ids_ref, first, edge_tile // lane, half, rcv_column[rows, :], message)
-        update = normed_ref[rows, :] * gain + shift
-        out_ref[rows, :] = (edge_ref[rows, :].astype(f32) + update).astype(bf16)
+        total[...] += spread(ids_ref, first, edge_tile // lane, half, rcv, message)
+        slots = (nodes, nodes + 2 * rim)
+        turned_ref[:, rows] = pick(rcv, rcv_low[rows, :], half, table[...], slots).astype(bf16).T
 
     each_tile(rcv_column.shape[0], tile)
     agg_ref[:half, :] = total[:, :lane]
@@ -320,8 +338,8 @@
 
 
 def node_kernel(
+    near_ref,
     far_ref,
-    near_ref,
     node_ref,
     agg_ref,
     ids_ref,
@@ -404,44 +422,19 @@
 
 
 def upstream_kernel(
-    rcv_column,
-    rcv_low,
-    node_ref,
-    far_ref,
-    near_ref,
-    dagg_ref,
-    cot_ref,
-    z_ref,
-    up_ref,
-    slope_ref,
-    turned_ref,
-    table,
-):
-    rim = near_ref.shape[0]
-    half = table.shape[0] - 2 * rim
-    nodes = 2 * half
-    parity = parity_of_place()
-    near_at = pl.multiple_of((1 - parity) * rim, rim)
-    far_at = pl.multiple_of(parity * rim, rim)
-    table[:half, :] = jnp.concatenate(
-        [side_by_side(node_ref[...]), side_by_side(dagg_ref[...])], axis=1
-    )
-    table[half:, :] = jnp.zeros((2 * rim, 4 * lane), bf16)
-    table[pl.ds(half + near_at, rim), lane : 2 * lane] = near_ref[...]
-    table[pl.ds(half + far_at, rim), lane : 2 * lane] = far_ref[...]
+    rcv_column, rcv_low, dagg_ref, cot_ref, z_ref, edge_ref, up_ref, slope_ref, turned_ref, table
+):
+    half = table.shape[0]
+    table[...] = side_by_side(dagg_ref[...])
 
     def tile(i):
         rows = pl.ds(pl.multiple_of(i * edge_tile, edge_tile), edge_tile)
-        hot = hot_columns(rcv_low[rows, :], (0, half), (nodes, nodes + 2 * rim))
-        four = dot(hot, table[...])
-        upper = rcv_column[rows, :] >= half
-        received = jnp.where(upper, four[:, lane : 2 * lane], four[:, :lane])
-        local = jnp.where(upper, four[:, 3 * lane :], four[:, 2 * lane : 3 * lane])
+        local = pick(rcv_column[rows, :], rcv_low[rows, :], half, table[...])
         up_ref[rows, :] = cot_ref[rows, :].astype(f32) + local
         z = z_ref[rows, :]
         sig = sigmoid(z)
         slope_ref[rows, :] = sig * (1.0 + z * (1.0 - sig))
-        turned_ref[:lane, rows] = received.astype(bf16).T
+        turned_ref[:lane, rows] = edge_ref[rows, :].T
         turned_ref[lane:, rows] = (z * sig).astype(bf16).T
 
     each_tile(cot_ref.shape[0], tile)
@@ -449,14 +442,15 @@
 
 def edge_backward_kernel(
     nodes,
+    dagg_near_ref,
     dagg_far_ref,
-    dagg_near_ref,
     up_ref,
     normed_ref,
     scale_ref,
     slope_ref,
-    first_turned,
-    second_turned,
+    sent_turned,
+    received_turned,
+    turned,
     weights_ref,
     vectors_ref,
     node_grads_ref,
@@ -490,9 +484,10 @@
         dz1 = dot(dz2b, w2_turned[...]) * slope_ref[rows, :]
         dz1b = dz1.astype(bf16)
         dz_ref[rows, :] = dz1b
-        grads_ref[: 2 * lane, :] += dot(first_turned[:, rows], dz1b)
-        grads_ref[2 * lane : 3 * lane, :] += dot(second_turned[:lane, rows], dz1b)
-        grads_ref[3 * lane : 4 * lane, :] += dot(second_turned[lane:, rows], dz2b)
+        grads_ref[:lane, :] += dot(turned[:lane, rows], dz1b)
+        grads_ref[lane : 2 * lane, :] += dot(sent_turned[:, rows], dz1b)
+        grads_ref[2 * lane : 3 * lane, :] += dot(received_turned[:, rows], dz1b)
+        grads_ref[3 * lane : 4 * lane, :] += dot(turned[lane:, rows], dz2b)
         sums[0:8, :] += eight_sums(dz1)
         sums[8:16, :] += eight_sums(dz2)
         sums[16:24, :] += eight_sums(upstream * normed)
@@ -560,19 +555,24 @@
         back_ref[...] = dot(returned, w1_turned).astype(bf16)
 
 
-def edge_grad_kernel(dz_ref, cot_ref, weights_ref, out_ref, w1_turned):
-    w1_turned[...] = weights_ref[:lane].T
+def edge_outputs_kernel(
+    dz_ref, cot_ref, edge_ref, normed_ref, vectors_ref, w1_ref, out_ref, grad_ref, w1_turned
+):
+    w1_turned[...] = w1_ref[...].T
+    gain, shift = vector(vectors_ref, 2), vector(vectors_ref, 3)
 
     def tile(i):
         rows = pl.ds(pl.multiple_of(i * edge_tile, edge_tile), edge_tile)
         cot = cot_ref[rows, :].astype(f32)
-        out_ref[rows, :] = (cot + dot(dz_ref[rows, :], w1_turned[...])).astype(bf16)
+        grad_ref[rows, :] = (cot + dot(dz_ref[rows, :], w1_turned[...])).astype(bf16)
+        update = normed_ref[rows, :] * gain + shift
+        out_ref[rows, :] = (edge_ref[rows, :].astype(f32) + update).astype(bf16)
 
     each_tile(cot_ref.shape[0], tile)
 
 
 def node_grad_kernel(
-    far_ref, near_ref, base_ref, snd_sum_ref, rcv_sum_ref, weights_ref, ids_ref, out_ref
+    near_ref, far_ref, base_ref, snd_sum_ref, rcv_sum_ref, weights_ref, ids_ref, out_ref
 ):
     returned = jnp.concatenate([near_ref[...], far_ref[...]], axis=0)
     total = base_ref[...] + dot(snd_sum_ref[...], weights_ref[lane : 2 * lane].T)
@@ -637,10 +637,10 @@
 def sum_rounds():
     for axis in ("sample", "dom"):
         count = lax.axis_size(axis)
-        step = 1
-        while step < count:
+        step = count // 2
+        while step > 0:
             yield axis, [(i, i ^ step) for i in range(count)]
-            step *= 2
+            step //= 2
 
 
 def on_device(
@@ -707,9 +707,8 @@
     near, far = swap(rim_near, rim_far)
     edge_shape = ((edges, lane), bf16)
     wide_shape = ((edges, lane), f32)
-    turned_shape = ((2 * lane, edges), bf16)
     node_shape = ((nodes, lane), bf16)
-    snd_column, rcv_column, rcv_low, z_sent, rcv_local, first_turned = call(
+    snd_column, rcv_column, rcv_low, z_sent, rcv_local, sent_turned = call(
         prepare_kernel,
         [
             ((edges, lane), jnp.int32),
@@ -717,7 +716,7 @@
             ((edges, lane), jnp.int16),
             wide_shape,
             ((snd_half, 2 * lane), bf16),
-            turned_shape,
+            ((lane, edges), bf16),
         ],
         [((edges, lane), jnp.int16), ((snd_half, 2 * lane), bf16)],
         ids,
@@ -735,8 +734,8 @@
             ((2 * lane, 2 * lane), bf16),
             ((2 * rim, lane), f32),
         ],
+        near,
         far,
-        near,
         ids,
         weights,
         vectors,
@@ -746,16 +745,17 @@
         rcv_local,
     )
     back_near, back_far = swap(agg_near, agg_far)
-    agg, edge_out = call(
+    agg, received_turned = call(
         collect_kernel,
-        [((nodes, lane), f32), edge_shape],
-        [((snd_half, 2 * lane), f32)],
+        [((nodes, lane), f32), ((lane, edges), bf16)],
+        [((snd_half + 2 * rim, 2 * lane), bf16), ((snd_half, 2 * lane), f32)],
         ids,
         rcv_column,
+        rcv_low,
         message,
-        edge,
-        normed,
-        vectors,
+        node,
+        near,
+        far,
     )
     node_x, node_act, node_normed, node_dz1, node_dz2, node_sums, dagg, rim_near, rim_far = call(
         node_kernel,
@@ -771,8 +771,8 @@
             rim_shape,
         ],
         [],
+        back_near,
         back_far,
-        back_near,
         node,
         agg,
         ids,
@@ -781,18 +781,16 @@
         node_cot,
     )
     dagg_near, dagg_far = swap(rim_near, rim_far)
-    upstream, slope, second_turned = call(
+    upstream, slope, turned = call(
         upstream_kernel,
-        [wide_shape, wide_shape, turned_shape],
-        [((snd_half + 2 * rim, 4 * lane), bf16)],
+        [wide_shape, wide_shape, ((2 * lane, edges), bf16)],
+        [((snd_half, 2 * lane), bf16)],
         rcv_column,
         rcv_low,
-        node,
-        far,
-        near,
         dagg,
         edge_cot,
         z,
+        edge,
     )
     node_out, base, node_grads = call(
         node_rest_kernel,
@@ -819,14 +817,15 @@
             ((2 * lane, 2 * lane), bf16),
             ((32, lane), f32),
         ],
+        dagg_near,
         dagg_far,
-        dagg_near,
         upstream,
         normed,
         scale,
         slope,
-        first_turned,
-        second_turned,
+        sent_turned,
+        received_turned,
+        turned,
         weights,
         vectors,
         node_grads,
@@ -849,39 +848,43 @@
         rcv_column,
         weights,
     )
-    (edge_grad,) = call(
-        edge_grad_kernel,
-        [edge_shape],
-        [((lane, lane), bf16)],
-        dz,
-        edge_cot,
-        weights,
-    )
-    node_grad = None
+    w1_edge = weights[:lane]
+    edge_out = edge_grad = node_grad = None
     for number, (axis, pairs) in enumerate(sum_rounds()):
         other = lax.ppermute(grads, axis, pairs)
         passed, written = [], []
         if number == 0:
-            passed, written = [back_near, back_far], [edge_grad]
+            passed = [back_near, back_far]
         elif number == 1:
-            passed = list(swap(back_near, back_far))
+            passed = [*swap(back_near, back_far), vectors, w1_edge]
         elif number == 2:
             (node_grad,) = call(
                 node_grad_kernel,
                 [node_shape],
                 [],
+                back_near,
                 back_far,
-                back_near,
                 base,
                 snd_sum,
                 rcv_sum,
                 weights,
                 ids,
             )
-            written = [node_grad]
+            edge_out, edge_grad = call(
+                edge_outputs_kernel,
+                [edge_shape, edge_shape],
+                [((lane, lane), bf16)],
+                dz,
+                edge_cot,
+                edge,
+                normed,
+                vectors,
+                w1_edge,
+            )
+            written = [node_grad, edge_out, edge_grad]
         grads, *passed = call(
             functools.partial(add_kernel, len(passed)),
-            [half_shape] + [rim_shape] * len(passed),
+            [half_shape] + [(x.shape, x.dtype) for x in passed],
             [],
             grads,
             other,
@@ -889,8 +892,10 @@
             *written,
             anywhere=len(written),
         )
-        if passed:
+        if number == 0:
             back_near, back_far = passed
+        elif number == 1:
+            back_near, back_far, vectors, w1_edge = passed
     others = lax.ppermute(grads, "sub", core_pairs)
     matrices = [3 * lane, lane, 2 * lane, lane]
     totals = call(

time: 59.6 us -> 57.1 us (0.958)
  waiting for transfers between devices: 10.6 us -> 7.9 us
    ppermute x3, waiting for transfers between devices: 5.42 us -> 1.62 us  [on_device(): other = lax.ppermute(grads, axis, pairs)]
    ppermute x1, starting transfers between devices: 0.07 us -> 1.34 us  [on_device(): others = lax.ppermute(grads, 'sub', core_pairs)]
    ppermute x4, waiting for transfers between devices: 2.84 us -> 3.99 us  [swap(): far = lax.ppermute(far, chain, outer)]
    ppermute x3, starting transfers between devices: 3.22 us -> 2.31 us  [on_device(): other = lax.ppermute(grads, axis, pairs)]
    ppermute x4, starting transfers between devices: 1.13 us -> 1.73 us  [swap(): return (lax.ppermute(near, chain, inner), far)]
  transfers between devices with their start and end apart: 13 -> 13, of which waited for: 4 -> 5; matrix products, arithmetic and copies ran while one was open for 0% -> 0% of each run, Pallas kernels for 26% -> 26%
where the time goes in v8:
time: 57.1 us; the launch traced here: 56.6 us
  Pallas kernels  28 us (49%)
  starting transfers between devices  19.7 us (35%)
  waiting for transfers between devices  7.9 us (14%)
  between operations  0.99 us (2%)
    pallas_call x16, Pallas kernels, call(): pl.pallas_call(kernel, out_shape=[jax.ShapeDtypeStruct(shape, dtype) for...  28 us
    ppermute x4, starting transfers between devices, swap(): far = lax.ppermute(far, chain, outer)  14.3 us
    ppermute x4, waiting for transfers between devices, swap(): far = lax.ppermute(far, chain, outer)  3.99 us
    ppermute x3, starting transfers between devices, on_device(): other = lax.ppermute(grads, axis, pairs)  2.31 us
    ppermute x4, starting transfers between devices, swap(): return (lax.ppermute(near, chain, inner), far)  1.73 us
    ppermute x3, waiting for transfers between devices, on_device(): other = lax.ppermute(grads, axis, pairs)  1.62 us
    ppermute x1, starting transfers between devices, on_device(): others = lax.ppermute(grads, 'sub', core_pairs)  1.34 us
    ppermute x1, waiting for transfers between devices, on_device(): other = lax.ppermute(grads_sent, 'sub', core_pairs)  1.32 us
  transfers between devices with their start and end apart: 13, of which 5 were waited for; matrix products, arithmetic and copies ran while one was open for 0% of the time, Pallas kernels for 26%

profile of v8, /device:TPU:1, one launch (start us, length us, event | category | flops | bytes accessed | tf_op | source)
XLA Modules:
  0.0 56.6 jit_solution(9717167817247169912)
XLA Ops:
  0.7 1.9 %shard_map.306 = (bf16[1024,128]{1,0:T(8,128)(2,1)S(1)}, s32[50,128]{1,0:T(8,128)S(1)}, bf16[3072,128]{1,0:T(8,128)(2,1)S(1)}, bf16[3072,128]{1,0:T(8,128)(2,1)S...) custom-call(bf16[1024,128]{1,0:T(8,128)(2,1)} %bitcast.32, ...), custom_call_target="tpu_custom_call" | custom-call | bytes 2356224 | tf_op jit(solution)/shard_map/pallas_call | solution.py:616
  2.7 4.6 %collective-permute-start.1 = (bf16[128,128]{1,0:T(8,128)(2,1)S(1)}, bf16[128,128]{1,0:T(8,128)(2,1)S(1)}, u32[]{:S(2)}, u32[]{:S(2)}) collective-permute-start(bf16[128,128]{1,0:T(8,128)(2,1)S(1)} %get-tuple-element.84), channel_id=1, source_target_pairs={{1,4},{5,8},{9,12},{4,1},{8,5},{12,9},{3,6},{7,10},{11,14},{6,3},{... | collective-permute-start | bytes 98312 | tf_op jit(solution)/shard_map/ppermute | solution.py:633
  7.2 3.4 %shard_map.307 = (s32[3072,128]{1,0:T(8,128)S(1)}, s32[3072,128]{1,0:T(8,128)S(1)}, s16[3072,128]{1,0:T(8,128)(2,1)S(1)}, f32[3072,128]{1,0:T(8,128)S(1)}, bf16[...) custom-call(s32[50,128]{1,0:T(8,128)S(1)} %get-tuple-element.85.ids_ref, ...), custom_call_target="tpu_custom_call" | custom-call | bytes 1307648 | tf_op jit(solution)/shard_map/pallas_call | solution.py:616
  10.7 4.8 %shard_map.308 = (f32[3072,128]{1,0:T(8,128)S(1)}, f32[3072,128]{1,0:T(8,128)S(1)}, f32[3072,128]{1,0:T(8,128)S(1)}, bf16[3072,128]{1,0:T(8,128)(2,1)S(1)}, bf16...) custom-call(bf16[128,128]{1,0:T(8,128)(2,1)S(1)} %collective-permute-done.near_ref, ...), custom_call_target="tpu_custom_call" | custom-call | bytes 4518912 | tf_op jit(solution)/shard_map/pallas_call | solution.py:616
  15.6 3.6 %collective-permute-start.3 = (bf16[128,128]{1,0:T(8,128)(2,1)S(1)}, bf16[128,128]{1,0:T(8,128)(2,1)S(1)}, u32[]{:S(2)}, u32[]{:S(2)}) collective-permute-start(bf16[128,128]{1,0:T(8,128)(2,1)S(1)} %get-tuple-element.95), channel_id=1, source_target_pairs={{1,4},{5,8},{9,12},{4,1},{8,5},{12,9},{3,6},{7,10},{11,14},{6,3},{... | collective-permute-start | bytes 98312 | tf_op jit(solution)/shard_map/ppermute | solution.py:633
  19.2 2.7 %shard_map.309 = (f32[1024,128]{1,0:T(8,128)S(1)}, bf16[128,3072]{1,0:T(8,128)(2,1)S(1)}) custom-call(s32[50,128]{1,0:T(8,128)S(1)} %get-tuple-element.85.ids_ref, s32[3072,128]{1,0:T(8,128)S(1)} %get-tuple-element.90.rcv_column, s16[3072,128]{1,0:T(8,128)(2,1)S(1)} %get-tuple-element.91.rcv_low, bf16[3072,128]{1,0:T(8,128)(2,1)S(1)} %get-tuple-element.96.message_ref, ...), custom_call_target="tpu_custom_call" | custom-call | bytes 3499008 | tf_op jit(solution)/shard_map/pallas_call | solution.py:616
  22.0 1.6 %shard_map.310 = (bf16[1024,256]{1,0:T(8,128)(2,1)S(1)}, bf16[1024,128]{1,0:T(8,128)(2,1)S(1)}, f32[1024,128]{1,0:T(8,128)S(1)}, bf16[1024,128]{1,0:T(8,128)(2,1...) custom-call(bf16[128,128]{1,0:T(8,128)(2,1)S(1)} %collective-permute, ...), custom_call_target="tpu_custom_call" | custom-call | bytes 1373184 | tf_op jit(solution)/shard_map/pallas_call | solution.py:616
  23.6 3.8 %collective-permute-start.5 = (bf16[128,128]{1,0:T(8,128)(2,1)S(1)}, bf16[128,128]{1,0:T(8,128)(2,1)S(1)}, u32[]{:S(2)}, u32[]{:S(2)}) collective-permute-start(bf16[128,128]{1,0:T(8,128)(2,1)S(1)} %get-tuple-element.107), channel_id=1, source_target_pairs={{1,4},{5,8},{9,12},{4,1},{8,5},{12,9},{3,6},{7,10},{11,14},{6,3},{... | collective-permute-start | bytes 98312 | tf_op jit(solution)/shard_map/ppermute | solution.py:633
  27.4 1.7 %shard_map.312 = (f32[3072,128]{1,0:T(8,128)S(1)}, f32[3072,128]{1,0:T(8,128)S(1)}, bf16[256,3072]{1,0:T(8,128)(2,1)S(1)}) custom-call(s32[3072,128]{1,0:T(8,128)S(1)} %get-tuple-element.90.rcv_column, s16[3072,128]{1,0:T(8,128)(2,1)S(1)} %get-tuple-element.91.rcv_low, bf16[1024,128]{1,0:T(8,128)(2,1)S(1)} %get-tuple-element.108.dagg_ref, ...), custom_call_target="tpu_custom_call" | custom-call | bytes 5767168 | tf_op jit(solution)/shard_map/pallas_call | solution.py:616
  29.1 1.0 %shard_map.311 = (bf16[1024,128]{1,0:T(8,128)(2,1)}, f32[1024,128]{1,0:T(8,128)S(1)}, f32[400,128]{1,0:T(8,128)S(1)}) custom-call(bf16[1024,256]{1,0:T(8,128)(2,1)S(1)} %get-tuple-element.99.x_ref, bf16[1024,128]{1,0:T(8,128)(2,1)S(1)} %get-tuple-element.100.act_ref, f32[1024,128]{1,0:T(8,128)S(1)} %get-tuple-element.101.normed_ref, ...), custom_call_target="tpu_custom_call" | custom-call | bytes 2338816 | tf_op jit(solution)/shard_map/pallas_call | solution.py:616
  30.0 4.0 %shard_map.313 = (bf16[3072,128]{1,0:T(8,128)(2,1)S(1)}, f32[464,128]{1,0:T(8,128)S(1)}, bf16[464,128]{1,0:T(8,128)(2,1)S(1)}) custom-call(bf16[128,128]{1,0:T(8,128)(2,1)S(1)} %collective-permute-done.4.dagg_near_ref, bf16[128,128]{1,0:T(8,128)(2,1)S(1)} %collective-permute-done.5.dagg_far_ref, f32[3072,128]{1,0:T(8,128)S(1)} %get-tuple-element.111.up_ref, ...), custom_call_target="tpu_custom_call" | custom-call | bytes 10727424 | tf_op jit(solution)/shard_map/pallas_call | solution.py:616
  34.1 1.3 %collective-permute-done.6.other_ref = bf16[464,128]{1,0:T(8,128)(2,1)S(1)} collective-permute-done((bf16[464,128]{1,0:T(8,128)(2,1)S(1)}, bf16[464,128]{1,0:T(8,128)(2,1)S(1)}, u32[]{:S(2)}, u32[]{:S(2)}) %collective-permute-start.6) | collective-permute-done | bytes 118816 | tf_op jit(solution)/shard_map/ppermute | solution.py:835
  35.4 1.3 %collective-permute-start.7 = (bf16[464,128]{1,0:T(8,128)(2,1)S(1)}, bf16[464,128]{1,0:T(8,128)(2,1)S(1)}, u32[]{:S(2)}, u32[]{:S(2)}) collective-permute-start(bf16[464,128]{1,0:T(8,128)(2,1)S(1)} %shard_map.314.own_ref), channel_id=1, source_target_pairs={{0,2},{2,0},{1,3},{3,1},{4,6},{6,4},{5,7},{7,5},{8,10},{10,8},{9,1... | collective-permute-start | bytes 356360 | tf_op jit(solution)/shard_map/ppermute | solution.py:854
  36.7 3.0 %shard_map.315 = (bf16[1024,128]{1,0:T(8,128)(2,1)S(1)}, bf16[1024,128]{1,0:T(8,128)(2,1)S(1)}, bf16[128,128]{1,0:T(8,128)(2,1)S(1)}, bf16[128,128]{1,0:T(8,128)(2,1)S(1)}) custom-call(s32[50,128]{1,0:T(8,128)S(1)} %get-tuple-element.85.ids_ref, bf16[3072,128]{1,0:T(8,128)(2,1)S(1)} %get-tuple-element.119.dz_ref, ...), custom_call_target="tpu_custom_call" | custom-call | bytes 4187136 | tf_op jit(solution)/shard_map/pallas_call | solution.py:616
  40.2 0.7 %collective-permute-start.8 = (bf16[464,128]{1,0:T(8,128)(2,1)S(1)}, bf16[464,128]{1,0:T(8,128)(2,1)S(1)}, u32[]{:S(2)}, u32[]{:S(2)}) collective-permute-start(bf16[464,128]{1,0:T(8,128)(2,1)S(1)} %get-tuple-element.125.own_ref), channel_id=1, source_target_pairs={{0,8},{4,12},{8,0},{12,4},{1,9},{5,13},{9,1},{13,5},{2,10},{6,14},... | collective-permute-start | bytes 356360 | tf_op jit(solution)/shard_map/ppermute | solution.py:854
  40.9 1.5 %collective-permute-start.9 = (bf16[128,128]{1,0:T(8,128)(2,1)S(1)}, bf16[128,128]{1,0:T(8,128)(2,1)S(1)}, u32[]{:S(2)}, u32[]{:S(2)}) collective-permute-start(bf16[128,128]{1,0:T(8,128)(2,1)S(1)} %get-tuple-element.126), channel_id=1, source_target_pairs={{0,1},{4,5},{8,9},{12,13},{1,0},{5,4},{9,8},{13,12},{2,3},{6,7},{1... | collective-permute-start | bytes 98312 | tf_op jit(solution)/shard_map/ppermute | solution.py:634
  42.4 2.4 %collective-permute-start.10 = (bf16[128,128]{1,0:T(8,128)(2,1)S(1)}, bf16[128,128]{1,0:T(8,128)(2,1)S(1)}, u32[]{:S(2)}, u32[]{:S(2)}) collective-permute-start(bf16[128,128]{1,0:T(8,128)(2,1)S(1)} %get-tuple-element.127), channel_id=1, source_target_pairs={{1,4},{5,8},{9,12},{4,1},{8,5},{12,9},{3,6},{7,10},{11,14},{6,3},{... | collective-permute-start | bytes 98312 | tf_op jit(solution)/shard_map/ppermute | solution.py:633
  44.8 4.0 %collective-permute-done.10.refs_1_ = bf16[128,128]{1,0:T(8,128)(2,1)S(1)} collective-permute-done((bf16[128,128]{1,0:T(8,128)(2,1)S(1)}, bf16[128,128]{1,0:T(8,128)(2,1)S(1)}, u32[]{:S(2)}, u32[]{:S(2)}) %collective-permute-start.10) | collective-permute-done | bytes 32800 | tf_op jit(solution)/shard_map/ppermute | solution.py:633
  49.2 1.8 %shard_map.318 = (bf16[3072,128]{1,0:T(8,128)(2,1)}, bf16[3072,128]{1,0:T(8,128)(2,1)}) custom-call(bf16[3072,128]{1,0:T(8,128)(2,1)S(1)} %get-tuple-element.119.dz_ref, bf16[3072,128]{1,0:T(8,128)(2,1)S(1)} %get-tuple-element.109.cot_ref, bf16[3072,128]{1,0:T(8,128)(2,1)S(1)} %get-tuple-element.89.edge_ref, f32[3072,128]{1,0:T(8,128)S(1)} %get-tuple-element.112.normed_ref, ...), custom_call_target="tpu_custom_call" | custom-call | bytes 3969024 | tf_op jit(solution)/shard_map/pallas_call | solution.py:616
  51.0 1.1 %shard_map.319.refs_0_ = bf16[1024,128]{1,0:T(8,128)(2,1)} custom-call(bf16[128,128]{1,0:T(8,128)(2,1)S(1)} %get-tuple-element.131.near_ref, bf16[128,128]{1,0:T(8,128)(2,1)S(1)} %get-tuple-element.132.far_ref, f32[1024,128]{1,0:T(8,128)S(1)} %get-tuple-element.133.base_ref, bf16[1024,128]{1,0:T(8,128)(2,1)S(1)} %get-tuple-element.134.snd_sum_ref, ...), custom_call_target="tpu_custom_call" | custom-call | bytes 1369088 | tf_op jit(solution)/shard_map/pallas_call | solution.py:616
  52.2 1.1 %collective-permute-done.11.other_ref = bf16[464,128]{1,0:T(8,128)(2,1)S(1)} collective-permute-done((bf16[464,128]{1,0:T(8,128)(2,1)S(1)}, bf16[464,128]{1,0:T(8,128)(2,1)S(1)}, u32[]{:S(2)}, u32[]{:S(2)}) %collective-permute-start.11) | collective-permute-done | bytes 118816 | tf_op jit(solution)/shard_map/ppermute | solution.py:854
  53.3 1.3 %collective-permute-start.12 = (bf16[464,128]{1,0:T(8,128)(2,1)S(1)}, bf16[464,128]{1,0:T(8,128)(2,1)S(1)}, u32[]{:S(2)}, u32[]{:S(2)}) collective-permute-start(bf16[464,128]{1,0:T(8,128)(2,1)S(1)} %shard_map.320.own_ref), channel_id=1, source_target_pairs={{0,1},{1,0},{2,3},{3,2},{4,5},{5,4},{6,7},{7,6},{8,9},{9,8},{10,11... | collective-permute-start | bytes 356360 | tf_op jit(solution)/shard_map/ppermute | solution.py:899
  54.6 1.0 %collective-permute-done.12.other_ref = bf16[464,128]{1,0:T(8,128)(2,1)S(1)} collective-permute-done((bf16[464,128]{1,0:T(8,128)(2,1)S(1)}, bf16[464,128]{1,0:T(8,128)(2,1)S(1)}, u32[]{:S(2)}, u32[]{:S(2)}) %collective-permute-start.12) | collective-permute-done | bytes 118816 | tf_op jit(solution)/shard_map/ppermute | solution.py:899
  55.6 0.8 %shard_map.321 = (f32[384,128]{1,0:T(8,128)}, f32[128,128]{1,0:T(8,128)}, f32[256,128]{1,0:T(8,128)}, f32[128,128]{1,0:T(8,128)}, f32[1,128]{1,0:T(1,128)}, /*in...) custom-call(bf16[464,128]{1,0:T(8,128)(2,1)S(1)} %shard_map.320.own_, ...), custom_call_target="tpu_custom_call" | custom-call | bytes 237568 | tf_op jit(solution)/shard_map/pallas_call | solution.py:616
  (19 shorter events, 1.3 us)
Async XLA Ops:
  2.5 8.1 %collective-permute-start = (bf16[128,128]{1,0:T(8,128)(2,1)S(1)}, bf16[128,128]{1,0:T(8,128)(2,1)S(1)}, u32[]{:S(2)}, u32[]{:S(2)}) collective-permute-start(bf16[128,128]{1,0:T(8,128)(2,1)S(1)} %get-tuple-element.83), channel_id=1, source_target_pairs={{0,1},{4,5},{8,9},{12,13},{1,0},{5,4},{9,8},{13,12},{2,3},{6,7},{1... | collective-permute-start | bytes 98312 | tf_op jit(solution)/shard_map/ppermute | solution.py:634
  2.7 8.0 %collective-permute-start.1 = (bf16[128,128]{1,0:T(8,128)(2,1)S(1)}, bf16[128,128]{1,0:T(8,128)(2,1)S(1)}, u32[]{:S(2)}, u32[]{:S(2)}) collective-permute-start(bf16[128,128]{1,0:T(8,128)(2,1)S(1)} %get-tuple-element.84), channel_id=1, source_target_pairs={{1,4},{5,8},{9,12},{4,1},{8,5},{12,9},{3,6},{7,10},{11,14},{6,3},{... | collective-permute-start | bytes 98312 | tf_op jit(solution)/shard_map/ppermute | solution.py:633
  15.5 6.4 %collective-permute-start.2 = (bf16[128,128]{1,0:T(8,128)(2,1)S(1)}, bf16[128,128]{1,0:T(8,128)(2,1)S(1)}, u32[]{:S(2)}, u32[]{:S(2)}) collective-permute-start(bf16[128,128]{1,0:T(8,128)(2,1)S(1)} %get-tuple-element.94), channel_id=1, source_target_pairs={{0,1},{4,5},{8,9},{12,13},{1,0},{5,4},{9,8},{13,12},{2,3},{6,7},{1... | collective-permute-start | bytes 98312 | tf_op jit(solution)/shard_map/ppermute | solution.py:634
  15.6 6.4 %collective-permute-start.3 = (bf16[128,128]{1,0:T(8,128)(2,1)S(1)}, bf16[128,128]{1,0:T(8,128)(2,1)S(1)}, u32[]{:S(2)}, u32[]{:S(2)}) collective-permute-start(bf16[128,128]{1,0:T(8,128)(2,1)S(1)} %get-tuple-element.95), channel_id=1, source_target_pairs={{1,4},{5,8},{9,12},{4,1},{8,5},{12,9},{3,6},{7,10},{11,14},{6,3},{... | collective-permute-start | bytes 98312 | tf_op jit(solution)/shard_map/ppermute | solution.py:633
  23.5 6.5 %collective-permute-start.4 = (bf16[128,128]{1,0:T(8,128)(2,1)S(1)}, bf16[128,128]{1,0:T(8,128)(2,1)S(1)}, u32[]{:S(2)}, u32[]{:S(2)}) collective-permute-start(bf16[128,128]{1,0:T(8,128)(2,1)S(1)} %get-tuple-element.106), channel_id=1, source_target_pairs={{0,1},{4,5},{8,9},{12,13},{1,0},{5,4},{9,8},{13,12},{2,3},{6,7},{1... | collective-permute-start | bytes 98312 | tf_op jit(solution)/shard_map/ppermute | solution.py:634
  23.6 6.4 %collective-permute-start.5 = (bf16[128,128]{1,0:T(8,128)(2,1)S(1)}, bf16[128,128]{1,0:T(8,128)(2,1)S(1)}, u32[]{:S(2)}, u32[]{:S(2)}) collective-permute-start(bf16[128,128]{1,0:T(8,128)(2,1)S(1)} %get-tuple-element.107), channel_id=1, source_target_pairs={{1,4},{5,8},{9,12},{4,1},{8,5},{12,9},{3,6},{7,10},{11,14},{6,3},{... | collective-permute-start | bytes 98312 | tf_op jit(solution)/shard_map/ppermute | solution.py:633
  34.0 1.4 %collective-permute-start.6 = (bf16[464,128]{1,0:T(8,128)(2,1)S(1)}, bf16[464,128]{1,0:T(8,128)(2,1)S(1)}, u32[]{:S(2)}, u32[]{:S(2)}) collective-permute-start(bf16[464,128]{1,0:T(8,128)(2,1)S(1)} %get-tuple-element.121), channel_id=1, source_target_pairs={{0,1},{1,0},{2,3},{3,2},{4,5},{5,4},{6,7},{7,6},{8,9},{9,8},{10,11... | collective-permute-start | bytes 356360 | tf_op jit(solution)/shard_map/ppermute | solution.py:835
  35.4 4.7 %collective-permute-start.7 = (bf16[464,128]{1,0:T(8,128)(2,1)S(1)}, bf16[464,128]{1,0:T(8,128)(2,1)S(1)}, u32[]{:S(2)}, u32[]{:S(2)}) collective-permute-start(bf16[464,128]{1,0:T(8,128)(2,1)S(1)} %shard_map.314.own_ref), channel_id=1, source_target_pairs={{0,2},{2,0},{1,3},{3,1},{4,6},{6,4},{5,7},{7,5},{8,10},{10,8},{9,1... | collective-permute-start | bytes 356360 | tf_op jit(solution)/shard_map/ppermute | solution.py:854
  40.2 8.6 %collective-permute-start.8 = (bf16[464,128]{1,0:T(8,128)(2,1)S(1)}, bf16[464,128]{1,0:T(8,128)(2,1)S(1)}, u32[]{:S(2)}, u32[]{:S(2)}) collective-permute-start(bf16[464,128]{1,0:T(8,128)(2,1)S(1)} %get-tuple-element.125.own_ref), channel_id=1, source_target_pairs={{0,8},{4,12},{8,0},{12,4},{1,9},{5,13},{9,1},{13,5},{2,10},{6,14},... | collective-permute-start | bytes 356360 | tf_op jit(solution)/shard_map/ppermute | solution.py:854
  40.9 3.9 %collective-permute-start.9 = (bf16[128,128]{1,0:T(8,128)(2,1)S(1)}, bf16[128,128]{1,0:T(8,128)(2,1)S(1)}, u32[]{:S(2)}, u32[]{:S(2)}) collective-permute-start(bf16[128,128]{1,0:T(8,128)(2,1)S(1)} %get-tuple-element.126), channel_id=1, source_target_pairs={{0,1},{4,5},{8,9},{12,13},{1,0},{5,4},{9,8},{13,12},{2,3},{6,7},{1... | collective-permute-start | bytes 98312 | tf_op jit(solution)/shard_map/ppermute | solution.py:634
  42.4 6.4 %collective-permute-start.10 = (bf16[128,128]{1,0:T(8,128)(2,1)S(1)}, bf16[128,128]{1,0:T(8,128)(2,1)S(1)}, u32[]{:S(2)}, u32[]{:S(2)}) collective-permute-start(bf16[128,128]{1,0:T(8,128)(2,1)S(1)} %get-tuple-element.127), channel_id=1, source_target_pairs={{1,4},{5,8},{9,12},{4,1},{8,5},{12,9},{3,6},{7,10},{11,14},{6,3},{... | collective-permute-start | bytes 98312 | tf_op jit(solution)/shard_map/ppermute | solution.py:633
  48.8 4.4 %collective-permute-start.11 = (bf16[464,128]{1,0:T(8,128)(2,1)S(1)}, bf16[464,128]{1,0:T(8,128)(2,1)S(1)}, u32[]{:S(2)}, u32[]{:S(2)}) collective-permute-start(bf16[464,128]{1,0:T(8,128)(2,1)S(1)} %get-tuple-element.137.own_ref), channel_id=1, source_target_pairs={{0,4},{4,0},{8,12},{12,8},{1,5},{5,1},{9,13},{13,9},{2,6},{6,2},{1... | collective-permute-start | bytes 356360 | tf_op jit(solution)/shard_map/ppermute | solution.py:854
  53.3 2.3 %collective-permute-start.12 = (bf16[464,128]{1,0:T(8,128)(2,1)S(1)}, bf16[464,128]{1,0:T(8,128)(2,1)S(1)}, u32[]{:S(2)}, u32[]{:S(2)}) collective-permute-start(bf16[464,128]{1,0:T(8,128)(2,1)S(1)} %shard_map.320.own_ref), channel_id=1, source_target_pairs={{0,1},{1,0},{2,3},{3,2},{4,5},{5,4},{6,7},{7,6},{8,9},{9,8},{10,11... | collective-permute-start | bytes 356360 | tf_op jit(solution)/shard_map/ppermute | solution.py:899

commit v9 on v8

--- a/solution.py
+++ b/solution.py
@@ -15,7 +15,7 @@
 bf16 = jnp.bfloat16
 lane = 128
 edge_tile = 512
-tile_group = 3
+tile_group = 6
 vmem_limit = 32 * 1024 * 1024
 sum_rows = 16
 chain = ("dom", "sub")
@@ -145,8 +145,31 @@
     return lax.axis_index(chain) % 2
 
 
-def first_kernel(
-    node_hbm,
+def started(moves, sems):
+    copies = [
+        pltpu.make_async_copy(source, target, sems.at[k])
+        for k, (source, target) in enumerate(moves)
+    ]
+    for copy in copies:
+        copy.start()
+    return copies
+
+
+def first_kernel(node_hbm, list_hbm, node_ref, message_ref, list_ref, sems):
+    for copy in started([(node_hbm, node_ref), (list_hbm, list_ref)], sems):
+        copy.wait()
+    parity = parity_of_place()
+    node = node_ref[...]
+    rim = message_ref.shape[0] // 2
+    for k, side in enumerate((1 - parity, parity)):
+        column = column_of(list_ref[pl.ds(side, 1), :]).astype(jnp.int16)
+        hot = hot_columns(column, (0, node.shape[0]))
+        message_ref[k * rim : (k + 1) * rim, :] = dot(hot, node).astype(bf16)
+
+
+def prepare_kernel(
+    node_ref,
+    unused_ref,
     snd_hbm,
     rcv_hbm,
     list_hbm,
@@ -156,14 +179,14 @@
     *refs,
 ):
     small = refs[:12]
-    node_ref, ids_ref, edge_ref, edge_cot_ref, node_cot_ref, weights_ref, vectors_ref = refs[12:19]
-    near_ref, far_ref, sems = refs[19:]
+    ids_ref, edge_ref, edge_cot_ref, node_cot_ref, weights_ref, vectors_ref = refs[12:18]
+    snd_column, rcv_column, rcv_low, z_ref, rcv_local, turned_ref = refs[18:24]
+    snd_low, snd_table, sems = refs[24:]
     chunks = snd_hbm.shape[0]
     moves = [
-        (node_hbm, node_ref),
-        (list_hbm, ids_ref.at[2 * chunks : 2 * chunks + 2]),
         (snd_hbm, ids_ref.at[:chunks]),
         (rcv_hbm, ids_ref.at[chunks : 2 * chunks]),
+        (list_hbm, ids_ref.at[2 * chunks : 2 * chunks + 2]),
     ]
     at = 0
     for source in small[:4]:
@@ -172,41 +195,12 @@
     for k, source in enumerate(small[4:]):
         moves.append((source, vectors_ref.at[k : k + 1]))
     moves += [(edge_hbm, edge_ref), (edge_cot_hbm, edge_cot_ref), (node_cot_hbm, node_cot_ref)]
-    copies = [
-        pltpu.make_async_copy(source, target, sems.at[k])
-        for k, (source, target) in enumerate(moves)
-    ]
-    for copy in copies:
-        copy.start()
+    copies = started(moves, sems)
+    half = snd_table.shape[0]
+    node = node_ref[...]
+    snd_table[...] = side_by_side(node)
     for copy in copies[:2]:
         copy.wait()
-    parity = parity_of_place()
-    node = node_ref[...]
-    for side, out_ref in ((1 - parity, near_ref), (parity, far_ref)):
-        column = column_of(ids_ref[pl.ds(2 * chunks + side, 1), :]).astype(jnp.int16)
-        hot = hot_columns(column, (0, node.shape[0]))
-        out_ref[...] = dot(hot, node).astype(bf16)
-    for copy in copies[2:]:
-        copy.wait()
-
-
-def prepare_kernel(
-    ids_ref,
-    node_ref,
-    weights_ref,
-    vectors_ref,
-    edge_ref,
-    snd_column,
-    rcv_column,
-    rcv_low,
-    z_ref,
-    rcv_local,
-    turned_ref,
-    snd_low,
-    snd_table,
-):
-    chunks = snd_column.shape[0] // lane
-    half = snd_table.shape[0]
     for k in range(chunks):
         at = slice(k * lane, (k + 1) * lane)
         snd = column_of(ids_ref[k : k + 1, :])
@@ -215,8 +209,8 @@
         rcv_column[at, :] = rcv
         snd_low[at, :] = folded(snd, half).astype(jnp.int16)
         rcv_low[at, :] = folded(rcv, half).astype(jnp.int16)
-    node = node_ref[...]
-    snd_table[...] = side_by_side(node)
+    for copy in copies[2:]:
+        copy.wait()
     rcv_local[...] = side_by_side(dot(node, weights_ref[2 * lane : 3 * lane]).astype(bf16))
     w1 = weights_ref[: 2 * lane]
     b1 = vector(vectors_ref, 0)
@@ -229,6 +223,12 @@
         turned_ref[:, rows] = sent.T
 
     each_tile(edge_ref.shape[0], tile)
+
+
+def split_kernel(message_ref, near_ref, onward_ref):
+    rim = near_ref.shape[0]
+    near_ref[...] = message_ref[:rim, :]
+    onward_ref[...] = message_ref[rim:, :]
 
 
 def edge_forward_kernel(
@@ -245,8 +245,7 @@
     normed_ref,
     scale_ref,
     message_ref,
-    agg_near_ref,
-    agg_far_ref,
+    rims_ref,
     table,
     w2_pair,
     means,
@@ -286,8 +285,8 @@
         total[...] += dot(hot, message)
 
     each_tile(rcv_column.shape[0], tile)
-    agg_near_ref[...] = total[pl.ds(near_at, rim), :].astype(bf16)
-    agg_far_ref[...] = total[pl.ds(far_at, rim), :].astype(bf16)
+    rims_ref[:rim, :] = total[pl.ds(near_at, rim), :].astype(bf16)
+    rims_ref[rim:, :] = total[pl.ds(far_at, rim), :].astype(bf16)
 
 
 def collect_kernel(
@@ -298,6 +297,7 @@
     node_ref,
     near_ref,
     far_ref,
+    unused_ref,
     agg_ref,
     turned_ref,
     table,
@@ -353,8 +353,7 @@
     dz2_ref,
     sums_ref,
     dagg_ref,
-    rim_near_ref,
-    rim_far_ref,
+    rims_ref,
 ):
     nodes = node_ref.shape[0]
     returned = jnp.concatenate([near_ref[...], far_ref[...]], axis=0)
@@ -382,10 +381,11 @@
     dagg_ref[...] = dagg
     parity = parity_of_place()
     first = ids_ref.shape[0] - 2
-    for side, rim_ref in ((parity, rim_far_ref), (1 - parity, rim_near_ref)):
+    rim = rims_ref.shape[0] // 2
+    for k, side in enumerate((1 - parity, parity)):
         column = column_of(ids_ref[pl.ds(first + side, 1), :]).astype(jnp.int16)
         picked = hot_columns(column, (0, nodes))
-        rim_ref[...] = dot(picked, dagg).astype(bf16)
+        rims_ref[k * rim : (k + 1) * rim, :] = dot(picked, dagg).astype(bf16)
     sums_ref[0:8, :] = eight_sums(dz1)
     sums_ref[8:16, :] = eight_sums(dz2)
 
@@ -400,6 +400,7 @@
     weights_ref,
     vectors_ref,
     cot_ref,
+    unused_ref,
     out_ref,
     base_ref,
     grads_ref,
@@ -422,7 +423,17 @@
 
 
 def upstream_kernel(
-    rcv_column, rcv_low, dagg_ref, cot_ref, z_ref, edge_ref, up_ref, slope_ref, turned_ref, table
+    rcv_column,
+    rcv_low,
+    dagg_ref,
+    cot_ref,
+    z_ref,
+    edge_ref,
+    unused_ref,
+    up_ref,
+    slope_ref,
+    turned_ref,
+    table,
 ):
     half = table.shape[0]
     table[...] = side_by_side(dagg_ref[...])
@@ -521,15 +532,14 @@
     weights_ref,
     snd_sum_ref,
     rcv_sum_ref,
-    far_back_ref,
-    near_back_ref,
+    rims_ref,
     snd_total,
     rcv_total,
     halo_total,
 ):
     half = snd_total.shape[0]
     nodes = 2 * half
-    rim = near_back_ref.shape[0]
+    rim = rims_ref.shape[0] // 2
     parity = parity_of_place()
     for total in (snd_total, rcv_total, halo_total):
         total[...] = jnp.zeros_like(total)
@@ -550,9 +560,9 @@
         out_ref[:half, :] = total[:, :lane].astype(bf16)
         out_ref[half:, :] = total[:, lane:].astype(bf16)
     w1_turned = weights_ref[2 * lane : 3 * lane].T
-    for side, back_ref in ((parity, far_back_ref), (1 - parity, near_back_ref)):
+    for k, side in enumerate((1 - parity, parity)):
         returned = halo_total[pl.ds(pl.multiple_of(side * rim, rim), rim), :].astype(bf16)
-        back_ref[...] = dot(returned, w1_turned).astype(bf16)
+        rims_ref[k * rim : (k + 1) * rim, :] = dot(returned, w1_turned).astype(bf16)
 
 
 def edge_outputs_kernel(
@@ -624,14 +634,18 @@
     )(*operands)
 
 
-def swap(near, far):
-    count = lax.axis_size("dom") * lax.axis_size("sub")
-    outer = [(i, i + 1) for i in range(1, count - 1, 2)]
-    inner = [(i, i + 1) for i in range(0, count - 1, 2)]
-    outer += [(target, source) for source, target in outer]
-    inner += [(target, source) for source, target in inner]
-    far = lax.ppermute(far, chain, outer)
-    return lax.ppermute(near, chain, inner), far
+def exchange(message):
+    chips = lax.axis_size("dom")
+    inner, outer = [], []
+    for chip in range(chips):
+        inner += [(2 * chip, 2 * chip + 1), (2 * chip + 1, 2 * chip)]
+        if chip + 1 < chips:
+            outer += [(2 * chip, 2 * chip + 2), (2 * chip + 3, 2 * chip + 1)]
+    rim_shape = ((message.shape[0] // 2, lane), bf16)
+    near, onward = call(
+        split_kernel, [rim_shape, rim_shape], [], lax.ppermute(message, chain, inner)
+    )
+    return near, lax.ppermute(onward, chain, outer), onward
 
 
 def sum_rounds():
@@ -669,7 +683,6 @@
     nodes = node.shape[0]
     edges = edge.shape[0]
     rim = send_list.shape[2]
-    rim_shape = ((rim, lane), bf16)
     snd_half = nodes // 2
     kept = -(-(7 * lane + sum_rows) // (2 * sum_rows)) * sum_rows
     row = lambda x: x.reshape(1, lane)
@@ -678,7 +691,6 @@
     small += [row(b_node_first), row(b_node_second), row(node_gain), row(node_shift)]
     chunks = edges // lane
     sources = [
-        node,
         senders.reshape(chunks, lane),
         receivers.reshape(chunks, lane),
         send_list[0],
@@ -686,31 +698,29 @@
         edge_cotangent[0],
         node_cotangent[0],
     ] + small
-    node, ids, edge, edge_cot, node_cot, weights, vectors, rim_near, rim_far = call(
+    rims_shape = ((2 * rim, lane), bf16)
+    node, rims = call(
         first_kernel,
-        [
-            ((nodes, lane), bf16),
-            ((2 * chunks + 2, lane), jnp.int32),
-            ((edges, lane), bf16),
-            ((edges, lane), bf16),
-            ((nodes, lane), bf16),
-            ((7 * lane, lane), bf16),
-            ((8, lane), f32),
-            rim_shape,
-            rim_shape,
-        ],
-        [],
-        *sources,
-        anywhere=len(sources),
-        sems=len(sources),
-    )
-    near, far = swap(rim_near, rim_far)
+        [((nodes, lane), bf16), rims_shape],
+        [((2, rim), jnp.int32)],
+        node,
+        send_list[0],
+        anywhere=2,
+        sems=2,
+    )
+    near, far, onward = exchange(rims)
     edge_shape = ((edges, lane), bf16)
     wide_shape = ((edges, lane), f32)
     node_shape = ((nodes, lane), bf16)
-    snd_column, rcv_column, rcv_low, z_sent, rcv_local, sent_turned = call(
+    prepared = call(
         prepare_kernel,
         [
+            ((2 * chunks + 2, lane), jnp.int32),
+            edge_shape,
+            edge_shape,
+            node_shape,
+            ((7 * lane, lane), bf16),
+            ((8, lane), f32),
             ((edges, lane), jnp.int32),
             ((edges, lane), jnp.int32),
             ((edges, lane), jnp.int16),
@@ -719,15 +729,17 @@
             ((lane, edges), bf16),
         ],
         [((edges, lane), jnp.int16), ((snd_half, 2 * lane), bf16)],
-        ids,
         node,
-        weights,
-        vectors,
-        edge,
-    )
-    z, normed, scale, message, agg_near, agg_far = call(
+        onward,
+        *sources,
+        anywhere=len(sources),
+        sems=len(sources),
+    )
+    ids, edge, edge_cot, node_cot, weights, vectors = prepared[:6]
+    snd_column, rcv_column, rcv_low, z_sent, rcv_local, sent_turned = prepared[6:]
+    z, normed, scale, message, rims = call(
         edge_forward_kernel,
-        [wide_shape, wide_shape, wide_shape, edge_shape, rim_shape, rim_shape],
+        [wide_shape, wide_shape, wide_shape, edge_shape, rims_shape],
         [
             ((snd_half + 2 * rim, 2 * lane), bf16),
             ((lane, 2 * lane), bf16),
@@ -744,7 +756,7 @@
         z_sent,
         rcv_local,
     )
-    back_near, back_far = swap(agg_near, agg_far)
+    back_near, back_far, onward = exchange(rims)
     agg, received_turned = call(
         collect_kernel,
         [((nodes, lane), f32), ((lane, edges), bf16)],
@@ -756,8 +768,9 @@
         node,
         near,
         far,
-    )
-    node_x, node_act, node_normed, node_dz1, node_dz2, node_sums, dagg, rim_near, rim_far = call(
+        onward,
+    )
+    node_x, node_act, node_normed, node_dz1, node_dz2, node_sums, dagg, rims = call(
         node_kernel,
         [
             ((nodes, 2 * lane), bf16),
@@ -767,8 +780,7 @@
             node_shape,
             ((16, lane), f32),
             node_shape,
-            rim_shape,
-            rim_shape,
+            rims_shape,
         ],
         [],
         back_near,
@@ -780,7 +792,7 @@
         vectors,
         node_cot,
     )
-    dagg_near, dagg_far = swap(rim_near, rim_far)
+    dagg_near, dagg_far, onward = exchange(rims)
     upstream, slope, turned = call(
         upstream_kernel,
         [wide_shape, wide_shape, ((2 * lane, edges), bf16)],
@@ -791,6 +803,7 @@
         edge_cot,
         z,
         edge,
+        onward,
     )
     node_out, base, node_grads = call(
         node_rest_kernel,
@@ -805,6 +818,7 @@
         weights,
         vectors,
         node_cot,
+        onward,
     )
     half_shape = ((kept, lane), bf16)
     dz, grads_kept, grads_sent = call(
@@ -834,9 +848,9 @@
     core_pairs = [(0, 1), (1, 0)]
     other = lax.ppermute(grads_sent, "sub", core_pairs)
     (grads,) = call(functools.partial(add_kernel, 0), [half_shape], [], grads_kept, other)
-    snd_sum, rcv_sum, back_far, back_near = call(
+    snd_sum, rcv_sum, rims = call(
         scatter_kernel,
-        [node_shape, node_shape, rim_shape, rim_shape],
+        [node_shape, node_shape, rims_shape],
         [
             ((snd_half, 2 * lane), f32),
             ((snd_half, 2 * lane), f32),
@@ -854,9 +868,10 @@
         other = lax.ppermute(grads, axis, pairs)
         passed, written = [], []
         if number == 0:
-            passed = [back_near, back_far]
+            passed = [rims]
         elif number == 1:
-            passed = [*swap(back_near, back_far), vectors, w1_edge]
+            back_near, back_far, unused = exchange(rims)
+            passed = [back_near, back_far, vectors, w1_edge]
         elif number == 2:
             (node_grad,) = call(
                 node_grad_kernel,
@@ -893,7 +908,7 @@
             anywhere=len(written),
         )
         if number == 0:
-            back_near, back_far = passed
+            (rims,) = passed
         elif number == 1:
             back_near, back_far, vectors, w1_edge = passed
     others = lax.ppermute(grads, "sub", core_pairs)

time: 57.1 us -> 60.7 us (1.063)
  waiting for transfers between devices: 7.9 us -> 13.2 us
  starting transfers between devices: 19.7 us -> 18.8 us
  Pallas kernels: 28 us -> 27.3 us
    ppermute x8, waiting for transfers between devices: 4 us -> 8.94 us  [the longest x4 5.04 us: exchange(): return (near, lax.ppermute(onward, chain, outer), onward)]
    ppermute x8, starting transfers between devices: 16 us -> 12.2 us  [the longest x4 6.94 us: exchange(): lax.ppermute(message, chain, inner)]
    ppermute x1, starting transfers between devices: 0.07 us -> 1.96 us  [on_device(): other = lax.ppermute(grads_sent, 'sub', core_pairs)]
    ppermute x3, starting transfers between devices: 2.31 us -> 3.58 us  [on_device(): other = lax.ppermute(grads, axis, pairs)]
    pallas_call x16 -> x20, Pallas kernels: 28 us -> 27.3 us  [call(): pl.pallas_call(kernel, out_shape=[jax.ShapeDtypeStruct(shape, dtype) for...]
    ppermute x3, waiting for transfers between devices: 1.62 us -> 2.27 us  [on_device(): other = lax.ppermute(grads, axis, pairs)]
  transfers between devices with their start and end apart: 13 -> 13, of which waited for: 5 -> 11; matrix products, arithmetic and copies ran while one was open for 0% -> 0% of each run, Pallas kernels for 26% -> 24%
where the time goes in v9:
time: 60.7 us; the launch traced here: 60.1 us
  Pallas kernels  27.3 us (45%)
  starting transfers between devices  18.8 us (31%)
  waiting for transfers between devices  13.2 us (22%)
  between operations  0.92 us (2%)
    pallas_call x20, Pallas kernels, call(): pl.pallas_call(kernel, out_shape=[jax.ShapeDtypeStruct(shape, dtype) for...  27.3 us
    ppermute x4, starting transfers between devices, exchange(): lax.ppermute(message, chain, inner)  6.94 us
    ppermute x4, starting transfers between devices, exchange(): return (near, lax.ppermute(onward, chain, outer), onward)  5.3 us
    ppermute x4, waiting for transfers between devices, exchange(): return (near, lax.ppermute(onward, chain, outer), onward)  5.04 us
    ppermute x4, waiting for transfers between devices, exchange(): lax.ppermute(message, chain, inner)  3.9 us
    ppermute x3, starting transfers between devices, on_device(): other = lax.ppermute(grads, axis, pairs)  3.58 us
    ppermute x3, waiting for transfers between devices, on_device(): other = lax.ppermute(grads, axis, pairs)  2.27 us
    ppermute x1, starting transfers between devices, on_device(): other = lax.ppermute(grads_sent, 'sub', core_pairs)  1.96 us
  transfers between devices with their start and end apart: 13, of which 11 were waited for; matrix products, arithmetic and copies ran while one was open for 0% of the time, Pallas kernels for 24%

profile of v9, /device:TPU:1, one launch (start us, length us, event | category | flops | bytes accessed | tf_op | source)
XLA Modules:
  0.0 60.1 jit_solution(13906117400987201460)
XLA Ops:
  0.6 1.3 %shard_map.306 = (bf16[1024,128]{1,0:T(8,128)(2,1)S(1)}, bf16[256,128]{1,0:T(8,128)(2,1)S(1)}) custom-call(bf16[1024,128]{1,0:T(8,128)(2,1)} %bitcast.33, s32[2,128]{1,0:T(2,128)} %bitcast.36), custom_call_target="tpu_custom_call" | custom-call | bytes 263168 | tf_op jit(solution)/shard_map/pallas_call | solution.py:626
  2.1 1.2 %collective-permute-done.message_ref = bf16[256,128]{1,0:T(8,128)(2,1)S(1)} collective-permute-done((bf16[256,128]{1,0:T(8,128)(2,1)S(1)}, bf16[256,128]{1,0:T(8,128)(2,1)S(1)}, u32[]{:S(2)}, u32[]{:S(2)}) %collective-permute-start) | collective-permute-done | bytes 65568 | tf_op jit(solution)/shard_map/ppermute | solution.py:646
  3.3 1.3 %collective-permute-start.1 = (bf16[128,128]{1,0:T(8,128)(2,1)S(1)}, bf16[128,128]{1,0:T(8,128)(2,1)S(1)}, u32[]{:S(2)}, u32[]{:S(2)}) collective-permute-start(bf16[128,128]{1,0:T(8,128)(2,1)S(1)} %get-tuple-element.88.unused_ref), channel_id=1, source_target_pairs={{0,4},{5,1},{4,8},{9,5},{8,12},{13,9},{2,6},{7,3},{6,10},{11,7},{1... | collective-permute-start | bytes 98312 | tf_op jit(solution)/shard_map/ppermute | solution.py:648
  4.6 4.5 %shard_map.308 = (s32[50,128]{1,0:T(8,128)S(1)}, bf16[3072,128]{1,0:T(8,128)(2,1)S(1)}, bf16[3072,128]{1,0:T(8,128)(2,1)S(1)}, bf16[1024,128]{1,0:T(8,128)(2,1)S...) custom-call(bf16[1024,128]{1,0:T(8,128)(2,1)S(1)} %get-tuple-element, ...), custom_call_target="tpu_custom_call" | custom-call | bytes 2388992 | tf_op jit(solution)/shard_map/pallas_call | solution.py:626
  9.1 5.0 %shard_map.309 = (f32[3072,128]{1,0:T(8,128)S(1)}, f32[3072,128]{1,0:T(8,128)S(1)}, f32[3072,128]{1,0:T(8,128)S(1)}, bf16[3072,128]{1,0:T(8,128)(2,1)S(1)}, bf16[256,128]{1,0:T(8,128)(2,1)S(1)}) custom-call(bf16[128,128]{1,0:T(8,128)(2,1)S(1)} %get-tuple-element.87.near_ref, bf16[128,128]{1,0:T(8,128)(2,1)S(1)} %collective-permute-done.1.far_ref, ...), custom_call_target="tpu_custom_call" | custom-call | bytes 4518912 | tf_op jit(solution)/shard_map/pallas_call | solution.py:626
  14.1 3.8 %collective-permute-start.2 = (bf16[256,128]{1,0:T(8,128)(2,1)S(1)}, bf16[256,128]{1,0:T(8,128)(2,1)S(1)}, u32[]{:S(2)}, u32[]{:S(2)}) collective-permute-start(bf16[256,128]{1,0:T(8,128)(2,1)S(1)} %get-tuple-element.97), channel_id=1, source_target_pairs={{0,1},{1,0},{4,5},{5,4},{8,9},{9,8},{12,13},{13,12},{2,3},{3,2},{6... | collective-permute-start | bytes 196616 | tf_op jit(solution)/shard_map/ppermute | solution.py:646
  18.7 1.3 %collective-permute-start.3 = (bf16[128,128]{1,0:T(8,128)(2,1)S(1)}, bf16[128,128]{1,0:T(8,128)(2,1)S(1)}, u32[]{:S(2)}, u32[]{:S(2)}) collective-permute-start(bf16[128,128]{1,0:T(8,128)(2,1)S(1)} %get-tuple-element.99.unused_ref), channel_id=1, source_target_pairs={{0,4},{5,1},{4,8},{9,5},{8,12},{13,9},{2,6},{7,3},{6,10},{11,7},{1... | collective-permute-start | bytes 98312 | tf_op jit(solution)/shard_map/ppermute | solution.py:648
  20.0 2.3 %shard_map.311 = (f32[1024,128]{1,0:T(8,128)S(1)}, bf16[128,3072]{1,0:T(8,128)(2,1)S(1)}) custom-call(s32[50,128]{1,0:T(8,128)S(1)} %get-tuple-element.90.ids_ref, s32[3072,128]{1,0:T(8,128)S(1)} %get-tuple-element.93.rcv_column, s16[3072,128]{1,0:T(8,128)(2,1)S(1)} %get-tuple-element.94.rcv_low, bf16[3072,128]{1,0:T(8,128)(2,1)S(1)} %get-tuple-element.100.message_ref, ...), custom_call_target="tpu_custom_call" | custom-call | bytes 3531776 | tf_op jit(solution)/shard_map/pallas_call | solution.py:626
  22.3 1.0 %collective-permute-done.3.far_ref = bf16[128,128]{1,0:T(8,128)(2,1)S(1)} collective-permute-done((bf16[128,128]{1,0:T(8,128)(2,1)S(1)}, bf16[128,128]{1,0:T(8,128)(2,1)S(1)}, u32[]{:S(2)}, u32[]{:S(2)}) %collective-permute-start.3) | collective-permute-done | bytes 32800 | tf_op jit(solution)/shard_map/ppermute | solution.py:648
  23.4 1.6 %shard_map.312 = (bf16[1024,256]{1,0:T(8,128)(2,1)S(1)}, bf16[1024,128]{1,0:T(8,128)(2,1)S(1)}, f32[1024,128]{1,0:T(8,128)S(1)}, bf16[1024,128]{1,0:T(8,128)(2,1...) custom-call(bf16[128,128]{1,0:T(8,128)(2,1)S(1)} %get-tuple-element., ...), custom_call_target="tpu_custom_call" | custom-call | bytes 1373184 | tf_op jit(solution)/shard_map/pallas_call | solution.py:626
  25.0 1.6 %collective-permute-start.4 = (bf16[256,128]{1,0:T(8,128)(2,1)S(1)}, bf16[256,128]{1,0:T(8,128)(2,1)S(1)}, u32[]{:S(2)}, u32[]{:S(2)}) collective-permute-start(bf16[256,128]{1,0:T(8,128)(2,1)S(1)} %get-tuple-element.109), channel_id=1, source_target_pairs={{0,1},{1,0},{4,5},{5,4},{8,9},{9,8},{12,13},{13,12},{2,3},{3,2},{6... | collective-permute-start | bytes 196616 | tf_op jit(solution)/shard_map/ppermute | solution.py:646
  27.5 1.5 %collective-permute-start.5 = (bf16[128,128]{1,0:T(8,128)(2,1)S(1)}, bf16[128,128]{1,0:T(8,128)(2,1)S(1)}, u32[]{:S(2)}, u32[]{:S(2)}) collective-permute-start(bf16[128,128]{1,0:T(8,128)(2,1)S(1)} %get-tuple-element.110.unused_ref), channel_id=1, source_target_pairs={{0,4},{5,1},{4,8},{9,5},{8,12},{13,9},{2,6},{7,3},{6,10},{11,7},{1... | collective-permute-start | bytes 98312 | tf_op jit(solution)/shard_map/ppermute | solution.py:648
  28.9 1.6 %shard_map.315 = (f32[3072,128]{1,0:T(8,128)S(1)}, f32[3072,128]{1,0:T(8,128)S(1)}, bf16[256,3072]{1,0:T(8,128)(2,1)S(1)}) custom-call(s32[3072,128]{1,0:T(8,128)S(1)} %get-tuple-element.93.rcv_column, s16[3072,128]{1,0:T(8,128)(2,1)S(1)} %get-tuple-element.94.rcv_low, bf16[1024,128]{1,0:T(8,128)(2,1)S(1)} %get-tuple-element.113.dagg_ref, ...), custom_call_target="tpu_custom_call" | custom-call | bytes 5799936 | tf_op jit(solution)/shard_map/pallas_call | solution.py:626
  32.1 3.7 %shard_map.316 = (bf16[3072,128]{1,0:T(8,128)(2,1)S(1)}, f32[464,128]{1,0:T(8,128)S(1)}, bf16[464,128]{1,0:T(8,128)(2,1)S(1)}) custom-call(bf16[128,128]{1,0:T(8,128)(2,1)S(1)} %get-tuple-element.112.dagg_near_ref, bf16[128,128]{1,0:T(8,128)(2,1)S(1)} %collective-permute-done.5.dagg_far_ref, f32[3072,128]{1,0:T(8,128)S(1)} %get-tuple-element.117.up_ref, ...), custom_call_target="tpu_custom_call" | custom-call | bytes 10727424 | tf_op jit(solution)/shard_map/pallas_call | solution.py:626
  35.8 2.0 %collective-permute-start.6 = (bf16[464,128]{1,0:T(8,128)(2,1)S(1)}, bf16[464,128]{1,0:T(8,128)(2,1)S(1)}, u32[]{:S(2)}, u32[]{:S(2)}) collective-permute-start(bf16[464,128]{1,0:T(8,128)(2,1)S(1)} %get-tuple-element.127), channel_id=1, source_target_pairs={{0,1},{1,0},{2,3},{3,2},{4,5},{5,4},{6,7},{7,6},{8,9},{9,8},{10,11... | collective-permute-start | bytes 356360 | tf_op jit(solution)/shard_map/ppermute | solution.py:849
  38.8 1.3 %collective-permute-start.7 = (bf16[464,128]{1,0:T(8,128)(2,1)S(1)}, bf16[464,128]{1,0:T(8,128)(2,1)S(1)}, u32[]{:S(2)}, u32[]{:S(2)}) collective-permute-start(bf16[464,128]{1,0:T(8,128)(2,1)S(1)} %shard_map.317.own_ref), channel_id=1, source_target_pairs={{0,2},{2,0},{1,3},{3,1},{4,6},{6,4},{5,7},{7,5},{8,10},{10,8},{9,1... | collective-permute-start | bytes 356360 | tf_op jit(solution)/shard_map/ppermute | solution.py:868
  40.1 2.6 %shard_map.318 = (bf16[1024,128]{1,0:T(8,128)(2,1)S(1)}, bf16[1024,128]{1,0:T(8,128)(2,1)S(1)}, bf16[256,128]{1,0:T(8,128)(2,1)S(1)}) custom-call(s32[50,128]{1,0:T(8,128)S(1)} %get-tuple-element.90.ids_ref, bf16[3072,128]{1,0:T(8,128)(2,1)S(1)} %get-tuple-element.125.dz_ref, s32[3072,128]{1,0:T(8,128)S(1)} %get-tuple-element.128.snd_column, ...), custom_call_target="tpu_custom_call" | custom-call | bytes 4187136 | tf_op jit(solution)/shard_map/pallas_call | solution.py:626
  43.3 2.0 %collective-permute-start.8 = (bf16[464,128]{1,0:T(8,128)(2,1)S(1)}, bf16[464,128]{1,0:T(8,128)(2,1)S(1)}, u32[]{:S(2)}, u32[]{:S(2)}) collective-permute-start(bf16[464,128]{1,0:T(8,128)(2,1)S(1)} %get-tuple-element.130.own_ref), channel_id=1, source_target_pairs={{0,8},{4,12},{8,0},{12,4},{1,9},{5,13},{9,1},{13,5},{2,10},{6,14},... | collective-permute-start | bytes 356360 | tf_op jit(solution)/shard_map/ppermute | solution.py:868
  45.3 1.5 %collective-permute-start.9 = (bf16[256,128]{1,0:T(8,128)(2,1)S(1)}, bf16[256,128]{1,0:T(8,128)(2,1)S(1)}, u32[]{:S(2)}, u32[]{:S(2)}) collective-permute-start(bf16[256,128]{1,0:T(8,128)(2,1)S(1)} %get-tuple-element.131), channel_id=1, source_target_pairs={{0,1},{1,0},{4,5},{5,4},{8,9},{9,8},{12,13},{13,12},{2,3},{3,2},{6... | collective-permute-start | bytes 196616 | tf_op jit(solution)/shard_map/ppermute | solution.py:646
  47.7 1.3 %collective-permute-start.10 = (bf16[128,128]{1,0:T(8,128)(2,1)S(1)}, bf16[128,128]{1,0:T(8,128)(2,1)S(1)}, u32[]{:S(2)}, u32[]{:S(2)}) collective-permute-start(bf16[128,128]{1,0:T(8,128)(2,1)S(1)} %get-tuple-element.133), channel_id=1, source_target_pairs={{0,4},{5,1},{4,8},{9,5},{8,12},{13,9},{2,6},{7,3},{6,10},{11,7},{1... | collective-permute-start | bytes 98312 | tf_op jit(solution)/shard_map/ppermute | solution.py:648
  49.0 3.3 %collective-permute-done.10.refs_1_ = bf16[128,128]{1,0:T(8,128)(2,1)S(1)} collective-permute-done((bf16[128,128]{1,0:T(8,128)(2,1)S(1)}, bf16[128,128]{1,0:T(8,128)(2,1)S(1)}, u32[]{:S(2)}, u32[]{:S(2)}) %collective-permute-start.10) | collective-permute-done | bytes 32800 | tf_op jit(solution)/shard_map/ppermute | solution.py:648
  52.7 1.6 %shard_map.322 = (bf16[3072,128]{1,0:T(8,128)(2,1)}, bf16[3072,128]{1,0:T(8,128)(2,1)}) custom-call(bf16[3072,128]{1,0:T(8,128)(2,1)S(1)} %get-tuple-element.125.dz_ref, bf16[3072,128]{1,0:T(8,128)(2,1)S(1)} %get-tuple-element.114.cot_ref, bf16[3072,128]{1,0:T(8,128)(2,1)S(1)} %get-tuple-element.116.edge_ref, f32[3072,128]{1,0:T(8,128)S(1)} %get-tuple-element.118.normed_ref, ...), custom_call_target="tpu_custom_call" | custom-call | bytes 3969024 | tf_op jit(solution)/shard_map/pallas_call | solution.py:626
  54.3 1.1 %shard_map.323.refs_0_ = bf16[1024,128]{1,0:T(8,128)(2,1)} custom-call(bf16[128,128]{1,0:T(8,128)(2,1)S(1)} %get-tuple-element.137.near_ref, bf16[128,128]{1,0:T(8,128)(2,1)S(1)} %get-tuple-element.138.far_ref, f32[1024,128]{1,0:T(8,128)S(1)} %get-tuple-element.139.base_ref, bf16[1024,128]{1,0:T(8,128)(2,1)S(1)} %get-tuple-element.140.snd_sum_ref, ...), custom_call_target="tpu_custom_call" | custom-call | bytes 1369088 | tf_op jit(solution)/shard_map/pallas_call | solution.py:626
  55.5 1.7 %collective-permute-done.11.other_ref = bf16[464,128]{1,0:T(8,128)(2,1)S(1)} collective-permute-done((bf16[464,128]{1,0:T(8,128)(2,1)S(1)}, bf16[464,128]{1,0:T(8,128)(2,1)S(1)}, u32[]{:S(2)}, u32[]{:S(2)}) %collective-permute-start.11) | collective-permute-done | bytes 118816 | tf_op jit(solution)/shard_map/ppermute | solution.py:868
  (23 shorter events, 9.4 us)
Async XLA Ops:
  2.0 1.3 %collective-permute-start = (bf16[256,128]{1,0:T(8,128)(2,1)S(1)}, bf16[256,128]{1,0:T(8,128)(2,1)S(1)}, u32[]{:S(2)}, u32[]{:S(2)}) collective-permute-start(bf16[256,128]{1,0:T(8,128)(2,1)S(1)} %get-tuple-element.86), channel_id=1, source_target_pairs={{0,1},{1,0},{4,5},{5,4},{8,9},{9,8},{12,13},{13,12},{2,3},{3,2},{6... | collective-permute-start | bytes 196616 | tf_op jit(solution)/shard_map/ppermute | solution.py:646
  3.3 5.8 %collective-permute-start.1 = (bf16[128,128]{1,0:T(8,128)(2,1)S(1)}, bf16[128,128]{1,0:T(8,128)(2,1)S(1)}, u32[]{:S(2)}, u32[]{:S(2)}) collective-permute-start(bf16[128,128]{1,0:T(8,128)(2,1)S(1)} %get-tuple-element.88.unused_ref), channel_id=1, source_target_pairs={{0,4},{5,1},{4,8},{9,5},{8,12},{13,9},{2,6},{7,3},{6,10},{11,7},{1... | collective-permute-start | bytes 98312 | tf_op jit(solution)/shard_map/ppermute | solution.py:648
  14.1 4.7 %collective-permute-start.2 = (bf16[256,128]{1,0:T(8,128)(2,1)S(1)}, bf16[256,128]{1,0:T(8,128)(2,1)S(1)}, u32[]{:S(2)}, u32[]{:S(2)}) collective-permute-start(bf16[256,128]{1,0:T(8,128)(2,1)S(1)} %get-tuple-element.97), channel_id=1, source_target_pairs={{0,1},{1,0},{4,5},{5,4},{8,9},{9,8},{12,13},{13,12},{2,3},{3,2},{6... | collective-permute-start | bytes 196616 | tf_op jit(solution)/shard_map/ppermute | solution.py:646
  18.7 4.6 %collective-permute-start.3 = (bf16[128,128]{1,0:T(8,128)(2,1)S(1)}, bf16[128,128]{1,0:T(8,128)(2,1)S(1)}, u32[]{:S(2)}, u32[]{:S(2)}) collective-permute-start(bf16[128,128]{1,0:T(8,128)(2,1)S(1)} %get-tuple-element.99.unused_ref), channel_id=1, source_target_pairs={{0,4},{5,1},{4,8},{9,5},{8,12},{13,9},{2,6},{7,3},{6,10},{11,7},{1... | collective-permute-start | bytes 98312 | tf_op jit(solution)/shard_map/ppermute | solution.py:648
  25.0 2.5 %collective-permute-start.4 = (bf16[256,128]{1,0:T(8,128)(2,1)S(1)}, bf16[256,128]{1,0:T(8,128)(2,1)S(1)}, u32[]{:S(2)}, u32[]{:S(2)}) collective-permute-start(bf16[256,128]{1,0:T(8,128)(2,1)S(1)} %get-tuple-element.109), channel_id=1, source_target_pairs={{0,1},{1,0},{4,5},{5,4},{8,9},{9,8},{12,13},{13,12},{2,3},{3,2},{6... | collective-permute-start | bytes 196616 | tf_op jit(solution)/shard_map/ppermute | solution.py:646
  27.5 4.6 %collective-permute-start.5 = (bf16[128,128]{1,0:T(8,128)(2,1)S(1)}, bf16[128,128]{1,0:T(8,128)(2,1)S(1)}, u32[]{:S(2)}, u32[]{:S(2)}) collective-permute-start(bf16[128,128]{1,0:T(8,128)(2,1)S(1)} %get-tuple-element.110.unused_ref), channel_id=1, source_target_pairs={{0,4},{5,1},{4,8},{9,5},{8,12},{13,9},{2,6},{7,3},{6,10},{11,7},{1... | collective-permute-start | bytes 98312 | tf_op jit(solution)/shard_map/ppermute | solution.py:648
  35.8 2.9 %collective-permute-start.6 = (bf16[464,128]{1,0:T(8,128)(2,1)S(1)}, bf16[464,128]{1,0:T(8,128)(2,1)S(1)}, u32[]{:S(2)}, u32[]{:S(2)}) collective-permute-start(bf16[464,128]{1,0:T(8,128)(2,1)S(1)} %get-tuple-element.127), channel_id=1, source_target_pairs={{0,1},{1,0},{2,3},{3,2},{4,5},{5,4},{6,7},{7,6},{8,9},{9,8},{10,11... | collective-permute-start | bytes 356360 | tf_op jit(solution)/shard_map/ppermute | solution.py:849
  38.8 4.5 %collective-permute-start.7 = (bf16[464,128]{1,0:T(8,128)(2,1)S(1)}, bf16[464,128]{1,0:T(8,128)(2,1)S(1)}, u32[]{:S(2)}, u32[]{:S(2)}) collective-permute-start(bf16[464,128]{1,0:T(8,128)(2,1)S(1)} %shard_map.317.own_ref), channel_id=1, source_target_pairs={{0,2},{2,0},{1,3},{3,1},{4,6},{6,4},{5,7},{7,5},{8,10},{10,8},{9,1... | collective-permute-start | bytes 356360 | tf_op jit(solution)/shard_map/ppermute | solution.py:868
  43.3 9.0 %collective-permute-start.8 = (bf16[464,128]{1,0:T(8,128)(2,1)S(1)}, bf16[464,128]{1,0:T(8,128)(2,1)S(1)}, u32[]{:S(2)}, u32[]{:S(2)}) collective-permute-start(bf16[464,128]{1,0:T(8,128)(2,1)S(1)} %get-tuple-element.130.own_ref), channel_id=1, source_target_pairs={{0,8},{4,12},{8,0},{12,4},{1,9},{5,13},{9,1},{13,5},{2,10},{6,14},... | collective-permute-start | bytes 356360 | tf_op jit(solution)/shard_map/ppermute | solution.py:868
  45.3 2.4 %collective-permute-start.9 = (bf16[256,128]{1,0:T(8,128)(2,1)S(1)}, bf16[256,128]{1,0:T(8,128)(2,1)S(1)}, u32[]{:S(2)}, u32[]{:S(2)}) collective-permute-start(bf16[256,128]{1,0:T(8,128)(2,1)S(1)} %get-tuple-element.131), channel_id=1, source_target_pairs={{0,1},{1,0},{4,5},{5,4},{8,9},{9,8},{12,13},{13,12},{2,3},{3,2},{6... | collective-permute-start | bytes 196616 | tf_op jit(solution)/shard_map/ppermute | solution.py:646
  47.7 4.6 %collective-permute-start.10 = (bf16[128,128]{1,0:T(8,128)(2,1)S(1)}, bf16[128,128]{1,0:T(8,128)(2,1)S(1)}, u32[]{:S(2)}, u32[]{:S(2)}) collective-permute-start(bf16[128,128]{1,0:T(8,128)(2,1)S(1)} %get-tuple-element.133), channel_id=1, source_target_pairs={{0,4},{5,1},{4,8},{9,5},{8,12},{13,9},{2,6},{7,3},{6,10},{11,7},{1... | collective-permute-start | bytes 98312 | tf_op jit(solution)/shard_map/ppermute | solution.py:648
  52.4 4.7 %collective-permute-start.11 = (bf16[464,128]{1,0:T(8,128)(2,1)S(1)}, bf16[464,128]{1,0:T(8,128)(2,1)S(1)}, u32[]{:S(2)}, u32[]{:S(2)}) collective-permute-start(bf16[464,128]{1,0:T(8,128)(2,1)S(1)} %get-tuple-element.143.own_ref), channel_id=1, source_target_pairs={{0,4},{4,0},{8,12},{12,8},{1,5},{5,1},{9,13},{13,9},{2,6},{6,2},{1... | collective-permute-start | bytes 356360 | tf_op jit(solution)/shard_map/ppermute | solution.py:868
  57.2 2.0 %collective-permute-start.12 = (bf16[464,128]{1,0:T(8,128)(2,1)S(1)}, bf16[464,128]{1,0:T(8,128)(2,1)S(1)}, u32[]{:S(2)}, u32[]{:S(2)}) collective-permute-start(bf16[464,128]{1,0:T(8,128)(2,1)S(1)} %shard_map.324.own_ref), channel_id=1, source_target_pairs={{0,1},{1,0},{2,3},{3,2},{4,5},{5,4},{6,7},{7,6},{8,9},{9,8},{10,11... | collective-permute-start | bytes 356360 | tf_op jit(solution)/shard_map/ppermute | solution.py:914

commit v10 on v9

--- a/solution.py
+++ b/solution.py
@@ -15,13 +15,12 @@
 bf16 = jnp.bfloat16
 lane = 128
 edge_tile = 512
-tile_group = 6
 vmem_limit = 32 * 1024 * 1024
 sum_rows = 16
 chain = ("dom", "sub")
 
 
-def each_tile(rows, tile):
+def each_tile(rows, tile, tile_group=6):
     count = rows // edge_tile
     group = math.gcd(count, tile_group)
 
@@ -155,38 +154,15 @@
     return copies
 
 
-def first_kernel(node_hbm, list_hbm, node_ref, message_ref, list_ref, sems):
-    for copy in started([(node_hbm, node_ref), (list_hbm, list_ref)], sems):
-        copy.wait()
-    parity = parity_of_place()
-    node = node_ref[...]
-    rim = message_ref.shape[0] // 2
-    for k, side in enumerate((1 - parity, parity)):
-        column = column_of(list_ref[pl.ds(side, 1), :]).astype(jnp.int16)
-        hot = hot_columns(column, (0, node.shape[0]))
-        message_ref[k * rim : (k + 1) * rim, :] = dot(hot, node).astype(bf16)
-
-
-def prepare_kernel(
-    node_ref,
-    unused_ref,
-    snd_hbm,
-    rcv_hbm,
-    list_hbm,
-    edge_hbm,
-    edge_cot_hbm,
-    node_cot_hbm,
-    *refs,
-):
+def first_kernel(node_hbm, list_hbm, snd_hbm, rcv_hbm, edge_hbm, *refs):
     small = refs[:12]
-    ids_ref, edge_ref, edge_cot_ref, node_cot_ref, weights_ref, vectors_ref = refs[12:18]
-    snd_column, rcv_column, rcv_low, z_ref, rcv_local, turned_ref = refs[18:24]
-    snd_low, snd_table, sems = refs[24:]
+    node_ref, message_ref, ids_ref, edge_ref, weights_ref, vectors_ref, sems = refs[12:]
     chunks = snd_hbm.shape[0]
     moves = [
+        (node_hbm, node_ref),
+        (list_hbm, ids_ref.at[2 * chunks : 2 * chunks + 2]),
         (snd_hbm, ids_ref.at[:chunks]),
         (rcv_hbm, ids_ref.at[chunks : 2 * chunks]),
-        (list_hbm, ids_ref.at[2 * chunks : 2 * chunks + 2]),
     ]
     at = 0
     for source in small[:4]:
@@ -194,13 +170,45 @@
         at += source.shape[0]
     for k, source in enumerate(small[4:]):
         moves.append((source, vectors_ref.at[k : k + 1]))
-    moves += [(edge_hbm, edge_ref), (edge_cot_hbm, edge_cot_ref), (node_cot_hbm, node_cot_ref)]
+    moves.append((edge_hbm, edge_ref))
     copies = started(moves, sems)
-    half = snd_table.shape[0]
-    node = node_ref[...]
-    snd_table[...] = side_by_side(node)
     for copy in copies[:2]:
         copy.wait()
+    parity = parity_of_place()
+    node = node_ref[...]
+    rim = message_ref.shape[0] // 2
+    for k, side in enumerate((1 - parity, parity)):
+        column = column_of(ids_ref[pl.ds(2 * chunks + side, 1), :]).astype(jnp.int16)
+        hot = hot_columns(column, (0, node.shape[0]))
+        message_ref[k * rim : (k + 1) * rim, :] = dot(hot, node).astype(bf16)
+    for copy in copies[2:]:
+        copy.wait()
+
+
+def prepare_kernel(
+    ids_ref,
+    node_ref,
+    weights_ref,
+    vectors_ref,
+    edge_ref,
+    unused_ref,
+    edge_cot_hbm,
+    node_cot_hbm,
+    edge_cot_ref,
+    node_cot_ref,
+    snd_column,
+    rcv_column,
+    rcv_low,
+    z_ref,
+    rcv_local,
+    turned_ref,
+    snd_low,
+    snd_table,
+    sems,
+):
+    copies = started([(edge_cot_hbm, edge_cot_ref), (node_cot_hbm, node_cot_ref)], sems)
+    chunks = snd_column.shape[0] // lane
+    half = snd_table.shape[0]
     for k in range(chunks):
         at = slice(k * lane, (k + 1) * lane)
         snd = column_of(ids_ref[k : k + 1, :])
@@ -209,8 +217,8 @@
         rcv_column[at, :] = rcv
         snd_low[at, :] = folded(snd, half).astype(jnp.int16)
         rcv_low[at, :] = folded(rcv, half).astype(jnp.int16)
-    for copy in copies[2:]:
-        copy.wait()
+    node = node_ref[...]
+    snd_table[...] = side_by_side(node)
     rcv_local[...] = side_by_side(dot(node, weights_ref[2 * lane : 3 * lane]).astype(bf16))
     w1 = weights_ref[: 2 * lane]
     b1 = vector(vectors_ref, 0)
@@ -223,12 +231,14 @@
         turned_ref[:, rows] = sent.T
 
     each_tile(edge_ref.shape[0], tile)
-
-
-def split_kernel(message_ref, near_ref, onward_ref):
+    for copy in copies:
+        copy.wait()
+
+
+def split_kernel(message_ref, near_ref, far_ref):
     rim = near_ref.shape[0]
     near_ref[...] = message_ref[:rim, :]
-    onward_ref[...] = message_ref[rim:, :]
+    far_ref[...] = message_ref[rim:, :]
 
 
 def edge_forward_kernel(
@@ -284,7 +294,7 @@
         hot = rows_of_ids(ids_ref, first, edge_tile // lane, 2 * rim, lambda row: row - nodes)
         total[...] += dot(hot, message)
 
-    each_tile(rcv_column.shape[0], tile)
+    each_tile(rcv_column.shape[0], tile, 3)
     rims_ref[:rim, :] = total[pl.ds(near_at, rim), :].astype(bf16)
     rims_ref[rim:, :] = total[pl.ds(far_at, rim), :].astype(bf16)
 
@@ -635,17 +645,12 @@
 
 
 def exchange(message):
-    chips = lax.axis_size("dom")
-    inner, outer = [], []
-    for chip in range(chips):
-        inner += [(2 * chip, 2 * chip + 1), (2 * chip + 1, 2 * chip)]
-        if chip + 1 < chips:
-            outer += [(2 * chip, 2 * chip + 2), (2 * chip + 3, 2 * chip + 1)]
+    count = lax.axis_size("dom") * lax.axis_size("sub")
+    inner = [(i, i ^ 1) for i in range(count)]
+    outer = [(i, (((i - 1) % count ^ 1) + 1) % count) for i in range(count)]
     rim_shape = ((message.shape[0] // 2, lane), bf16)
-    near, onward = call(
-        split_kernel, [rim_shape, rim_shape], [], lax.ppermute(message, chain, inner)
-    )
-    return near, lax.ppermute(onward, chain, outer), onward
+    near, far = call(split_kernel, [rim_shape, rim_shape], [], message)
+    return lax.ppermute(near, chain, inner), lax.ppermute(far, chain, outer), far
 
 
 def sum_rounds():
@@ -691,36 +696,37 @@
     small += [row(b_node_first), row(b_node_second), row(node_gain), row(node_shift)]
     chunks = edges // lane
     sources = [
+        node,
+        send_list[0],
         senders.reshape(chunks, lane),
         receivers.reshape(chunks, lane),
-        send_list[0],
         edge,
-        edge_cotangent[0],
-        node_cotangent[0],
     ] + small
     rims_shape = ((2 * rim, lane), bf16)
-    node, rims = call(
-        first_kernel,
-        [((nodes, lane), bf16), rims_shape],
-        [((2, rim), jnp.int32)],
-        node,
-        send_list[0],
-        anywhere=2,
-        sems=2,
-    )
-    near, far, onward = exchange(rims)
     edge_shape = ((edges, lane), bf16)
     wide_shape = ((edges, lane), f32)
     node_shape = ((nodes, lane), bf16)
+    node, rims, ids, edge, weights, vectors = call(
+        first_kernel,
+        [
+            node_shape,
+            rims_shape,
+            ((2 * chunks + 2, lane), jnp.int32),
+            edge_shape,
+            ((7 * lane, lane), bf16),
+            ((8, lane), f32),
+        ],
+        [],
+        *sources,
+        anywhere=len(sources),
+        sems=len(sources),
+    )
+    near, far, onward = exchange(rims)
     prepared = call(
         prepare_kernel,
         [
-            ((2 * chunks + 2, lane), jnp.int32),
-            edge_shape,
             edge_shape,
             node_shape,
-            ((7 * lane, lane), bf16),
-            ((8, lane), f32),
             ((edges, lane), jnp.int32),
             ((edges, lane), jnp.int32),
             ((edges, lane), jnp.int16),
@@ -729,14 +735,18 @@
             ((lane, edges), bf16),
         ],
         [((edges, lane), jnp.int16), ((snd_half, 2 * lane), bf16)],
+        ids,
         node,
+        weights,
+        vectors,
+        edge,
         onward,
-        *sources,
-        anywhere=len(sources),
-        sems=len(sources),
-    )
-    ids, edge, edge_cot, node_cot, weights, vectors = prepared[:6]
-    snd_column, rcv_column, rcv_low, z_sent, rcv_local, sent_turned = prepared[6:]
+        edge_cotangent[0],
+        node_cotangent[0],
+        anywhere=2,
+        sems=2,
+    )
+    edge_cot, node_cot, snd_column, rcv_column, rcv_low, z_sent, rcv_local, sent_turned = prepared
     z, normed, scale, message, rims = call(
         edge_forward_kernel,
         [wide_shape, wide_shape, wide_shape, edge_shape, rims_shape],

time: 60.7 us -> 53.8 us (0.89)
  waiting for transfers between devices: 13.2 us -> 9.56 us
  starting transfers between devices: 18.8 us -> 17.1 us
  Pallas kernels: 27.3 us -> 25.7 us
    ppermute x8, waiting for transfers between devices: 8.94 us -> 3.71 us  [the longest x4 3.7 us: exchange(): lax.ppermute(far, chain, outer)]
    ppermute x3, waiting for transfers between devices: 2.27 us -> 3.9 us  [on_device(): other = lax.ppermute(grads, axis, pairs)]
    pallas_call x20, Pallas kernels: 27.3 us -> 25.7 us  [call(): pl.pallas_call(kernel, out_shape=[jax.ShapeDtypeStruct(shape, dtype) for...]
    ppermute x8, starting transfers between devices: 12.2 us -> 10.8 us  [the longest x4 5.83 us: exchange(): lax.ppermute(near, chain, inner)]
    ppermute x3, starting transfers between devices: 3.58 us -> 2.7 us  [on_device(): other = lax.ppermute(grads, axis, pairs)]
    ppermute x1, starting transfers between devices: 1.03 us -> 1.69 us  [on_device(): others = lax.ppermute(grads, 'sub', core_pairs)]
  transfers between devices with their start and end apart: 13 -> 13, of which waited for: 11 -> 8; matrix products, arithmetic and copies ran while one was open for 0% -> 0% of each run, Pallas kernels for 24% -> 24%
where the time goes in v10:
time: 53.8 us; the launch traced here: 53.4 us
  Pallas kernels  25.7 us (48%)
  starting transfers between devices  17.1 us (32%)
  waiting for transfers between devices  9.56 us (18%)
  between operations  0.93 us (2%)
    pallas_call x20, Pallas kernels, call(): pl.pallas_call(kernel, out_shape=[jax.ShapeDtypeStruct(shape, dtype) for...  25.7 us
    ppermute x4, starting transfers between devices, exchange(): lax.ppermute(near, chain, inner)  5.83 us
    ppermute x4, starting transfers between devices, exchange(): lax.ppermute(far, chain, outer)  4.95 us
    ppermute x3, waiting for transfers between devices, on_device(): other = lax.ppermute(grads, axis, pairs)  3.9 us
    ppermute x4, waiting for transfers between devices, exchange(): lax.ppermute(far, chain, outer)  3.7 us
    ppermute x3, starting transfers between devices, on_device(): other = lax.ppermute(grads, axis, pairs)  2.7 us
    ppermute x1, starting transfers between devices, on_device(): other = lax.ppermute(grads_sent, 'sub', core_pairs)  1.95 us
    ppermute x1, starting transfers between devices, on_device(): others = lax.ppermute(grads, 'sub', core_pairs)  1.69 us
  transfers between devices with their start and end apart: 13, of which 8 were waited for; matrix products, arithmetic and copies ran while one was open for 0% of the time, Pallas kernels for 24%

profile of v10, /device:TPU:1, one launch (start us, length us, event | category | flops | bytes accessed | tf_op | source)
XLA Modules:
  0.0 53.4 jit_solution(4986777030222591417)
XLA Ops:
  0.7 1.6 %shard_map.306 = (bf16[1024,128]{1,0:T(8,128)(2,1)S(1)}, bf16[256,128]{1,0:T(8,128)(2,1)S(1)}, s32[50,128]{1,0:T(8,128)S(1)}, bf16[3072,128]{1,0:T(8,128)(2,1)S(...) custom-call(bf16[1024,128]{1,0:T(8,128)(2,1)} %bitcast.33, s32[2,128]{1,0:T(2,128)} %bitcast.36, ...), custom_call_target="tpu_custom_call" | custom-call | bytes 1307648 | tf_op jit(solution)/shard_map/pallas_call | solution.py:636
  2.4 2.7 %collective-permute-start.1 = (bf16[128,128]{1,0:T(8,128)(2,1)S(1)}, bf16[128,128]{1,0:T(8,128)(2,1)S(1)}, u32[]{:S(2)}, u32[]{:S(2)}) collective-permute-start(bf16[128,128]{1,0:T(8,128)(2,1)S(1)} %get-tuple-element.88.unused_ref), channel_id=1, source_target_pairs={{0,13},{1,4},{4,1},{5,8},{8,5},{9,12},{12,9},{13,0},{2,15},{3,6},{... | collective-permute-start | bytes 98312 | tf_op jit(solution)/shard_map/ppermute | solution.py:653
  5.1 2.7 %shard_map.308 = (bf16[3072,128]{1,0:T(8,128)(2,1)S(1)}, bf16[1024,128]{1,0:T(8,128)(2,1)S(1)}, s32[3072,128]{1,0:T(8,128)S(1)}, s32[3072,128]{1,0:T(8,128)S(1)}...) custom-call(s32[50,128]{1,0:T(8,128)S(1)} %get-tuple-element.89.ids_, ...), custom_call_target="tpu_custom_call" | custom-call | bytes 2388992 | tf_op jit(solution)/shard_map/pallas_call | solution.py:636
  7.8 5.0 %shard_map.309 = (f32[3072,128]{1,0:T(8,128)S(1)}, f32[3072,128]{1,0:T(8,128)S(1)}, f32[3072,128]{1,0:T(8,128)S(1)}, bf16[3072,128]{1,0:T(8,128)(2,1)S(1)}, bf16[256,128]{1,0:T(8,128)(2,1)S(1)}) custom-call(bf16[128,128]{1,0:T(8,128)(2,1)S(1)} %collective-permute-done.near_ref, bf16[128,128]{1,0:T(8,128)(2,1)S(1)} %collective-permute-done.1.far_ref, ...), custom_call_target="tpu_custom_call" | custom-call | bytes 4518912 | tf_op jit(solution)/shard_map/pallas_call | solution.py:636
  12.8 2.5 %collective-permute-start.2 = (bf16[128,128]{1,0:T(8,128)(2,1)S(1)}, bf16[128,128]{1,0:T(8,128)(2,1)S(1)}, u32[]{:S(2)}, u32[]{:S(2)}) collective-permute-start(bf16[128,128]{1,0:T(8,128)(2,1)S(1)} %get-tuple-element.99), channel_id=1, source_target_pairs={{0,1},{1,0},{4,5},{5,4},{8,9},{9,8},{12,13},{13,12},{2,3},{3,2},{6... | collective-permute-start | bytes 98312 | tf_op jit(solution)/shard_map/ppermute | solution.py:653
  15.3 2.3 %shard_map.311 = (f32[1024,128]{1,0:T(8,128)S(1)}, bf16[128,3072]{1,0:T(8,128)(2,1)S(1)}) custom-call(s32[50,128]{1,0:T(8,128)S(1)} %get-tuple-element.89.ids_ref, s32[3072,128]{1,0:T(8,128)S(1)} %get-tuple-element.94.rcv_column, s16[3072,128]{1,0:T(8,128)(2,1)S(1)} %get-tuple-element.95.rcv_low, bf16[3072,128]{1,0:T(8,128)(2,1)S(1)} %get-tuple-element.101.message_ref, ...), custom_call_target="tpu_custom_call" | custom-call | bytes 3531776 | tf_op jit(solution)/shard_map/pallas_call | solution.py:636
  17.7 1.0 %collective-permute-done.3.far_ref = bf16[128,128]{1,0:T(8,128)(2,1)S(1)} collective-permute-done((bf16[128,128]{1,0:T(8,128)(2,1)S(1)}, bf16[128,128]{1,0:T(8,128)(2,1)S(1)}, u32[]{:S(2)}, u32[]{:S(2)}) %collective-permute-start.3) | collective-permute-done | bytes 32800 | tf_op jit(solution)/shard_map/ppermute | solution.py:653
  18.7 1.6 %shard_map.312 = (bf16[1024,256]{1,0:T(8,128)(2,1)S(1)}, bf16[1024,128]{1,0:T(8,128)(2,1)S(1)}, f32[1024,128]{1,0:T(8,128)S(1)}, bf16[1024,128]{1,0:T(8,128)(2,1...) custom-call(bf16[128,128]{1,0:T(8,128)(2,1)S(1)} %collective-permute, ...), custom_call_target="tpu_custom_call" | custom-call | bytes 1373184 | tf_op jit(solution)/shard_map/pallas_call | solution.py:636
  20.3 1.9 %collective-permute-start.4 = (bf16[128,128]{1,0:T(8,128)(2,1)S(1)}, bf16[128,128]{1,0:T(8,128)(2,1)S(1)}, u32[]{:S(2)}, u32[]{:S(2)}) collective-permute-start(bf16[128,128]{1,0:T(8,128)(2,1)S(1)} %get-tuple-element.113), channel_id=1, source_target_pairs={{0,1},{1,0},{4,5},{5,4},{8,9},{9,8},{12,13},{13,12},{2,3},{3,2},{6... | collective-permute-start | bytes 98312 | tf_op jit(solution)/shard_map/ppermute | solution.py:653
  22.2 1.6 %shard_map.315 = (f32[3072,128]{1,0:T(8,128)S(1)}, f32[3072,128]{1,0:T(8,128)S(1)}, bf16[256,3072]{1,0:T(8,128)(2,1)S(1)}) custom-call(s32[3072,128]{1,0:T(8,128)S(1)} %get-tuple-element.94.rcv_column, s16[3072,128]{1,0:T(8,128)(2,1)S(1)} %get-tuple-element.95.rcv_low, bf16[1024,128]{1,0:T(8,128)(2,1)S(1)} %get-tuple-element.114.dagg_ref, ...), custom_call_target="tpu_custom_call" | custom-call | bytes 5799936 | tf_op jit(solution)/shard_map/pallas_call | solution.py:636
  23.8 1.0 %shard_map.314 = (bf16[1024,128]{1,0:T(8,128)(2,1)}, f32[1024,128]{1,0:T(8,128)S(1)}, f32[400,128]{1,0:T(8,128)S(1)}) custom-call(bf16[1024,256]{1,0:T(8,128)(2,1)S(1)} %get-tuple-element.104.x_ref, bf16[1024,128]{1,0:T(8,128)(2,1)S(1)} %get-tuple-element.105.act_ref, f32[1024,128]{1,0:T(8,128)S(1)} %get-tuple-element.106.normed_ref, ...), custom_call_target="tpu_custom_call" | custom-call | bytes 2371584 | tf_op jit(solution)/shard_map/pallas_call | solution.py:636
  25.6 3.7 %shard_map.316 = (bf16[3072,128]{1,0:T(8,128)(2,1)S(1)}, f32[464,128]{1,0:T(8,128)S(1)}, bf16[464,128]{1,0:T(8,128)(2,1)S(1)}) custom-call(bf16[128,128]{1,0:T(8,128)(2,1)S(1)} %collective-permute-done.4.dagg_near_ref, bf16[128,128]{1,0:T(8,128)(2,1)S(1)} %collective-permute-done.5.dagg_far_ref, f32[3072,128]{1,0:T(8,128)S(1)} %get-tuple-element.117.up_ref, ...), custom_call_target="tpu_custom_call" | custom-call | bytes 10727424 | tf_op jit(solution)/shard_map/pallas_call | solution.py:636
  29.3 1.9 %collective-permute-start.6 = (bf16[464,128]{1,0:T(8,128)(2,1)S(1)}, bf16[464,128]{1,0:T(8,128)(2,1)S(1)}, u32[]{:S(2)}, u32[]{:S(2)}) collective-permute-start(bf16[464,128]{1,0:T(8,128)(2,1)S(1)} %get-tuple-element.127), channel_id=1, source_target_pairs={{0,1},{1,0},{2,3},{3,2},{4,5},{5,4},{6,7},{7,6},{8,9},{9,8},{10,11... | collective-permute-start | bytes 356360 | tf_op jit(solution)/shard_map/ppermute | solution.py:859
  31.2 1.0 %collective-permute-done.6.other_ref = bf16[464,128]{1,0:T(8,128)(2,1)S(1)} collective-permute-done((bf16[464,128]{1,0:T(8,128)(2,1)S(1)}, bf16[464,128]{1,0:T(8,128)(2,1)S(1)}, u32[]{:S(2)}, u32[]{:S(2)}) %collective-permute-start.6) | collective-permute-done | bytes 118816 | tf_op jit(solution)/shard_map/ppermute | solution.py:859
  32.2 1.3 %collective-permute-start.7 = (bf16[464,128]{1,0:T(8,128)(2,1)S(1)}, bf16[464,128]{1,0:T(8,128)(2,1)S(1)}, u32[]{:S(2)}, u32[]{:S(2)}) collective-permute-start(bf16[464,128]{1,0:T(8,128)(2,1)S(1)} %shard_map.317.own_ref), channel_id=1, source_target_pairs={{0,2},{2,0},{1,3},{3,1},{4,6},{6,4},{5,7},{7,5},{8,10},{10,8},{9,1... | collective-permute-start | bytes 356360 | tf_op jit(solution)/shard_map/ppermute | solution.py:878
  33.5 2.6 %shard_map.318 = (bf16[1024,128]{1,0:T(8,128)(2,1)S(1)}, bf16[1024,128]{1,0:T(8,128)(2,1)S(1)}, bf16[256,128]{1,0:T(8,128)(2,1)S(1)}) custom-call(s32[50,128]{1,0:T(8,128)S(1)} %get-tuple-element.89.ids_ref, bf16[3072,128]{1,0:T(8,128)(2,1)S(1)} %get-tuple-element.125.dz_ref, s32[3072,128]{1,0:T(8,128)S(1)} %get-tuple-element.128.snd_column, ...), custom_call_target="tpu_custom_call" | custom-call | bytes 4187136 | tf_op jit(solution)/shard_map/pallas_call | solution.py:636
  37.4 1.2 %collective-permute-start.9 = (bf16[128,128]{1,0:T(8,128)(2,1)S(1)}, bf16[128,128]{1,0:T(8,128)(2,1)S(1)}, u32[]{:S(2)}, u32[]{:S(2)}) collective-permute-start(bf16[128,128]{1,0:T(8,128)(2,1)S(1)} %get-tuple-element.132), channel_id=1, source_target_pairs={{0,1},{1,0},{4,5},{5,4},{8,9},{9,8},{12,13},{13,12},{2,3},{3,2},{6... | collective-permute-start | bytes 98312 | tf_op jit(solution)/shard_map/ppermute | solution.py:653
  38.7 2.2 %collective-permute-start.10 = (bf16[128,128]{1,0:T(8,128)(2,1)S(1)}, bf16[128,128]{1,0:T(8,128)(2,1)S(1)}, u32[]{:S(2)}, u32[]{:S(2)}) collective-permute-start(bf16[128,128]{1,0:T(8,128)(2,1)S(1)} %get-tuple-element.133), channel_id=1, source_target_pairs={{0,13},{1,4},{4,1},{5,8},{8,5},{9,12},{12,9},{13,0},{2,15},{3,6},{... | collective-permute-start | bytes 98312 | tf_op jit(solution)/shard_map/ppermute | solution.py:653
  40.9 1.9 %collective-permute-done.10.refs_1_ = bf16[128,128]{1,0:T(8,128)(2,1)S(1)} collective-permute-done((bf16[128,128]{1,0:T(8,128)(2,1)S(1)}, bf16[128,128]{1,0:T(8,128)(2,1)S(1)}, u32[]{:S(2)}, u32[]{:S(2)}) %collective-permute-start.10) | collective-permute-done | bytes 32800 | tf_op jit(solution)/shard_map/ppermute | solution.py:653
  42.8 2.7 %collective-permute-done.8.other_ref = bf16[464,128]{1,0:T(8,128)(2,1)S(1)} collective-permute-done((bf16[464,128]{1,0:T(8,128)(2,1)S(1)}, bf16[464,128]{1,0:T(8,128)(2,1)S(1)}, u32[]{:S(2)}, u32[]{:S(2)}) %collective-permute-start.8) | collective-permute-done | bytes 118816 | tf_op jit(solution)/shard_map/ppermute | solution.py:878
  46.3 1.6 %shard_map.322 = (bf16[3072,128]{1,0:T(8,128)(2,1)}, bf16[3072,128]{1,0:T(8,128)(2,1)}) custom-call(bf16[3072,128]{1,0:T(8,128)(2,1)S(1)} %get-tuple-element.125.dz_ref, bf16[3072,128]{1,0:T(8,128)(2,1)S(1)} %get-tuple-element.115.cot_ref, bf16[3072,128]{1,0:T(8,128)(2,1)S(1)} %get-tuple-element.93.edge_ref, f32[3072,128]{1,0:T(8,128)S(1)} %get-tuple-element.118.normed_ref, ...), custom_call_target="tpu_custom_call" | custom-call | bytes 3969024 | tf_op jit(solution)/shard_map/pallas_call | solution.py:636
  47.9 1.1 %shard_map.323.refs_0_ = bf16[1024,128]{1,0:T(8,128)(2,1)} custom-call(bf16[128,128]{1,0:T(8,128)(2,1)S(1)} %get-tuple-element.137.near_ref, bf16[128,128]{1,0:T(8,128)(2,1)S(1)} %get-tuple-element.138.far_ref, f32[1024,128]{1,0:T(8,128)S(1)} %get-tuple-element.139.base_ref, bf16[1024,128]{1,0:T(8,128)(2,1)S(1)} %get-tuple-element.140.snd_sum_ref, ...), custom_call_target="tpu_custom_call" | custom-call | bytes 1369088 | tf_op jit(solution)/shard_map/pallas_call | solution.py:636
  49.7 1.7 %collective-permute-start.12 = (bf16[464,128]{1,0:T(8,128)(2,1)S(1)}, bf16[464,128]{1,0:T(8,128)(2,1)S(1)}, u32[]{:S(2)}, u32[]{:S(2)}) collective-permute-start(bf16[464,128]{1,0:T(8,128)(2,1)S(1)} %shard_map.324.own_ref), channel_id=1, source_target_pairs={{0,1},{1,0},{2,3},{3,2},{4,5},{5,4},{6,7},{7,6},{8,9},{9,8},{10,11... | collective-permute-start | bytes 356360 | tf_op jit(solution)/shard_map/ppermute | solution.py:924
  51.4 1.0 %collective-permute-done.12.other_ref = bf16[464,128]{1,0:T(8,128)(2,1)S(1)} collective-permute-done((bf16[464,128]{1,0:T(8,128)(2,1)S(1)}, bf16[464,128]{1,0:T(8,128)(2,1)S(1)}, u32[]{:S(2)}, u32[]{:S(2)}) %collective-permute-start.12) | collective-permute-done | bytes 118816 | tf_op jit(solution)/shard_map/ppermute | solution.py:924
  (23 shorter events, 4.6 us)
Async XLA Ops:
  2.3 5.5 %collective-permute-start = (bf16[128,128]{1,0:T(8,128)(2,1)S(1)}, bf16[128,128]{1,0:T(8,128)(2,1)S(1)}, u32[]{:S(2)}, u32[]{:S(2)}) collective-permute-start(bf16[128,128]{1,0:T(8,128)(2,1)S(1)} %get-tuple-element.87), channel_id=1, source_target_pairs={{0,1},{1,0},{4,5},{5,4},{8,9},{9,8},{12,13},{13,12},{2,3},{3,2},{6... | collective-permute-start | bytes 98312 | tf_op jit(solution)/shard_map/ppermute | solution.py:653
  2.4 5.4 %collective-permute-start.1 = (bf16[128,128]{1,0:T(8,128)(2,1)S(1)}, bf16[128,128]{1,0:T(8,128)(2,1)S(1)}, u32[]{:S(2)}, u32[]{:S(2)}) collective-permute-start(bf16[128,128]{1,0:T(8,128)(2,1)S(1)} %get-tuple-element.88.unused_ref), channel_id=1, source_target_pairs={{0,13},{1,4},{4,1},{5,8},{8,5},{9,12},{12,9},{13,0},{2,15},{3,6},{... | collective-permute-start | bytes 98312 | tf_op jit(solution)/shard_map/ppermute | solution.py:653
  12.8 4.8 %collective-permute-start.2 = (bf16[128,128]{1,0:T(8,128)(2,1)S(1)}, bf16[128,128]{1,0:T(8,128)(2,1)S(1)}, u32[]{:S(2)}, u32[]{:S(2)}) collective-permute-start(bf16[128,128]{1,0:T(8,128)(2,1)S(1)} %get-tuple-element.99), channel_id=1, source_target_pairs={{0,1},{1,0},{4,5},{5,4},{8,9},{9,8},{12,13},{13,12},{2,3},{3,2},{6... | collective-permute-start | bytes 98312 | tf_op jit(solution)/shard_map/ppermute | solution.py:653
  15.3 3.3 %collective-permute-start.3 = (bf16[128,128]{1,0:T(8,128)(2,1)S(1)}, bf16[128,128]{1,0:T(8,128)(2,1)S(1)}, u32[]{:S(2)}, u32[]{:S(2)}) collective-permute-start(bf16[128,128]{1,0:T(8,128)(2,1)S(1)} %get-tuple-element.100.unused_ref), channel_id=1, source_target_pairs={{0,13},{1,4},{4,1},{5,8},{8,5},{9,12},{12,9},{13,0},{2,15},{3,6},{... | collective-permute-start | bytes 98312 | tf_op jit(solution)/shard_map/ppermute | solution.py:653
  20.3 4.5 %collective-permute-start.4 = (bf16[128,128]{1,0:T(8,128)(2,1)S(1)}, bf16[128,128]{1,0:T(8,128)(2,1)S(1)}, u32[]{:S(2)}, u32[]{:S(2)}) collective-permute-start(bf16[128,128]{1,0:T(8,128)(2,1)S(1)} %get-tuple-element.113), channel_id=1, source_target_pairs={{0,1},{1,0},{4,5},{5,4},{8,9},{9,8},{12,13},{13,12},{2,3},{3,2},{6... | collective-permute-start | bytes 98312 | tf_op jit(solution)/shard_map/ppermute | solution.py:653
  22.2 3.3 %collective-permute-start.5 = (bf16[128,128]{1,0:T(8,128)(2,1)S(1)}, bf16[128,128]{1,0:T(8,128)(2,1)S(1)}, u32[]{:S(2)}, u32[]{:S(2)}) collective-permute-start(bf16[128,128]{1,0:T(8,128)(2,1)S(1)} %get-tuple-element.111.unused_ref), channel_id=1, source_target_pairs={{0,13},{1,4},{4,1},{5,8},{8,5},{9,12},{12,9},{13,0},{2,15},{3,6},{... | collective-permute-start | bytes 98312 | tf_op jit(solution)/shard_map/ppermute | solution.py:653
  29.3 2.9 %collective-permute-start.6 = (bf16[464,128]{1,0:T(8,128)(2,1)S(1)}, bf16[464,128]{1,0:T(8,128)(2,1)S(1)}, u32[]{:S(2)}, u32[]{:S(2)}) collective-permute-start(bf16[464,128]{1,0:T(8,128)(2,1)S(1)} %get-tuple-element.127), channel_id=1, source_target_pairs={{0,1},{1,0},{2,3},{3,2},{4,5},{5,4},{6,7},{7,6},{8,9},{9,8},{10,11... | collective-permute-start | bytes 356360 | tf_op jit(solution)/shard_map/ppermute | solution.py:859
  32.2 4.5 %collective-permute-start.7 = (bf16[464,128]{1,0:T(8,128)(2,1)S(1)}, bf16[464,128]{1,0:T(8,128)(2,1)S(1)}, u32[]{:S(2)}, u32[]{:S(2)}) collective-permute-start(bf16[464,128]{1,0:T(8,128)(2,1)S(1)} %shard_map.317.own_ref), channel_id=1, source_target_pairs={{0,2},{2,0},{1,3},{3,1},{4,6},{6,4},{5,7},{7,5},{8,10},{10,8},{9,1... | collective-permute-start | bytes 356360 | tf_op jit(solution)/shard_map/ppermute | solution.py:878
  36.8 8.8 %collective-permute-start.8 = (bf16[464,128]{1,0:T(8,128)(2,1)S(1)}, bf16[464,128]{1,0:T(8,128)(2,1)S(1)}, u32[]{:S(2)}, u32[]{:S(2)}) collective-permute-start(bf16[464,128]{1,0:T(8,128)(2,1)S(1)} %get-tuple-element.130.own_ref), channel_id=1, source_target_pairs={{0,8},{4,12},{8,0},{12,4},{1,9},{5,13},{9,1},{13,5},{2,10},{6,14},... | collective-permute-start | bytes 356360 | tf_op jit(solution)/shard_map/ppermute | solution.py:878
  37.4 3.5 %collective-permute-start.9 = (bf16[128,128]{1,0:T(8,128)(2,1)S(1)}, bf16[128,128]{1,0:T(8,128)(2,1)S(1)}, u32[]{:S(2)}, u32[]{:S(2)}) collective-permute-start(bf16[128,128]{1,0:T(8,128)(2,1)S(1)} %get-tuple-element.132), channel_id=1, source_target_pairs={{0,1},{1,0},{4,5},{5,4},{8,9},{9,8},{12,13},{13,12},{2,3},{3,2},{6... | collective-permute-start | bytes 98312 | tf_op jit(solution)/shard_map/ppermute | solution.py:653
  38.7 4.1 %collective-permute-start.10 = (bf16[128,128]{1,0:T(8,128)(2,1)S(1)}, bf16[128,128]{1,0:T(8,128)(2,1)S(1)}, u32[]{:S(2)}, u32[]{:S(2)}) collective-permute-start(bf16[128,128]{1,0:T(8,128)(2,1)S(1)} %get-tuple-element.133), channel_id=1, source_target_pairs={{0,13},{1,4},{4,1},{5,8},{8,5},{9,12},{12,9},{13,0},{2,15},{3,6},{... | collective-permute-start | bytes 98312 | tf_op jit(solution)/shard_map/ppermute | solution.py:653
  45.6 4.1 %collective-permute-start.11 = (bf16[464,128]{1,0:T(8,128)(2,1)S(1)}, bf16[464,128]{1,0:T(8,128)(2,1)S(1)}, u32[]{:S(2)}, u32[]{:S(2)}) collective-permute-start(bf16[464,128]{1,0:T(8,128)(2,1)S(1)} %get-tuple-element.143.own_ref), channel_id=1, source_target_pairs={{0,4},{4,0},{8,12},{12,8},{1,5},{5,1},{9,13},{13,9},{2,6},{6,2},{1... | collective-permute-start | bytes 356360 | tf_op jit(solution)/shard_map/ppermute | solution.py:878
  49.7 2.7 %collective-permute-start.12 = (bf16[464,128]{1,0:T(8,128)(2,1)S(1)}, bf16[464,128]{1,0:T(8,128)(2,1)S(1)}, u32[]{:S(2)}, u32[]{:S(2)}) collective-permute-start(bf16[464,128]{1,0:T(8,128)(2,1)S(1)} %shard_map.324.own_ref), channel_id=1, source_target_pairs={{0,1},{1,0},{2,3},{3,2},{4,5},{5,4},{6,7},{7,6},{8,9},{9,8},{10,11... | collective-permute-start | bytes 356360 | tf_op jit(solution)/shard_map/ppermute | solution.py:924

commit v11 on v10

--- a/solution.py
+++ b/solution.py
@@ -102,12 +102,16 @@
     return vectors_ref[k : k + 1, :]
 
 
-def centred_second(w, b):
+def centred_pair(w):
     w = w.astype(f32)
     w = w - jnp.mean(w, axis=1, keepdims=True)
     high = w.astype(bf16)
     low = (w - high.astype(f32)).astype(bf16)
-    return jnp.concatenate([high, low], axis=1), b - jnp.mean(b, axis=1, keepdims=True)
+    return jnp.concatenate([high, low], axis=1)
+
+
+def centred(b):
+    return b - jnp.mean(b, axis=1, keepdims=True)
 
 
 def mean_weights():
@@ -202,11 +206,21 @@
     z_ref,
     rcv_local,
     turned_ref,
+    pairs_ref,
+    means_ref,
+    turned_weights,
     snd_low,
     snd_table,
     sems,
 ):
     copies = started([(edge_cot_hbm, edge_cot_ref), (node_cot_hbm, node_cot_ref)], sems)
+    means_ref[...] = mean_weights()
+    for k, at in enumerate((3 * lane, 6 * lane)):
+        w = weights_ref[at : at + lane]
+        pairs_ref[k * lane : (k + 1) * lane, :] = centred_pair(w)
+    for k in range(7):
+        at = slice(k * lane, (k + 1) * lane)
+        turned_weights[at, :] = weights_ref[at, :].T
     chunks = snd_column.shape[0] // lane
     half = snd_table.shape[0]
     for k in range(chunks):
@@ -251,14 +265,14 @@
     rcv_low,
     z_sent,
     rcv_local,
+    pairs_ref,
+    means,
     z_ref,
     normed_ref,
     scale_ref,
     message_ref,
     rims_ref,
     table,
-    w2_pair,
-    means,
     total,
 ):
     half = rcv_local.shape[0]
@@ -273,9 +287,7 @@
     table[half:, :lane] = jnp.zeros((2 * rim, lane), bf16)
     table[pl.ds(half + near_at, rim), lane:] = dot(near_ref[...], w1_rcv).astype(bf16)
     table[pl.ds(half + far_at, rim), lane:] = dot(far_ref[...], w1_rcv).astype(bf16)
-    pair, b2 = centred_second(weights_ref[3 * lane : 4 * lane], vector(vectors_ref, 1))
-    w2_pair[...] = pair
-    means[...] = mean_weights()
+    b2 = centred(vector(vectors_ref, 1))
     total[...] = jnp.zeros_like(total)
 
     def tile(i):
@@ -285,7 +297,7 @@
         z = z + pick(rcv_column[rows, :], rcv_low[rows, :], half, table[...], slots)
         z_ref[rows, :] = z
         act = (z * sigmoid(z)).astype(bf16)
-        normed, scale_inv = normed_of(act, w2_pair[...], b2, means[...])
+        normed, scale_inv = normed_of(act, pairs_ref[:lane, :], b2, means[...])
         normed_ref[rows, :] = normed
         scale_ref[rows, :] = scale_inv
         message = (normed * gain + shift).astype(bf16)
@@ -356,6 +368,9 @@
     weights_ref,
     vectors_ref,
     cot_ref,
+    pairs_ref,
+    means,
+    turned_weights,
     x_ref,
     act_ref,
     normed_ref,
@@ -371,23 +386,21 @@
     x = jnp.concatenate([node_ref[...], agg], axis=1)
     x_ref[...] = x
     w1 = weights_ref[4 * lane : 6 * lane]
-    w2 = weights_ref[6 * lane :]
     z = dot(x, w1) + vector(vectors_ref, 4)
     sig = sigmoid(z)
     act = (z * sig).astype(bf16)
     act_ref[...] = act
-    pair, b2 = centred_second(w2, vector(vectors_ref, 5))
-    means = mean_weights()
-    normed, scale_inv = normed_of(act, pair, b2, means)
+    b2 = centred(vector(vectors_ref, 5))
+    normed, scale_inv = normed_of(act, pairs_ref[lane:, :], b2, means[...])
     normed_ref[...] = normed
     upstream = cot_ref[...].astype(f32)
-    dz2 = back_norm(upstream, normed, scale_inv, vector(vectors_ref, 6), means)
+    dz2 = back_norm(upstream, normed, scale_inv, vector(vectors_ref, 6), means[...])
     dz2b = dz2.astype(bf16)
     dz2_ref[...] = dz2b
-    dz1 = dot(dz2b, w2.T) * (sig * (1.0 + z * (1.0 - sig)))
+    dz1 = dot(dz2b, turned_weights[6 * lane :]) * (sig * (1.0 + z * (1.0 - sig)))
     dz1b = dz1.astype(bf16)
     dz1_ref[...] = dz1b
-    dagg = dot(dz1b, w1[lane:].T).astype(bf16)
+    dagg = dot(dz1b, turned_weights[5 * lane : 6 * lane]).astype(bf16)
     dagg_ref[...] = dagg
     parity = parity_of_place()
     first = ids_ref.shape[0] - 2
@@ -407,7 +420,7 @@
     dz1_ref,
     dz2_ref,
     sums_ref,
-    weights_ref,
+    turned_weights,
     vectors_ref,
     cot_ref,
     unused_ref,
@@ -421,7 +434,7 @@
     update = normed * vector(vectors_ref, 6) + vector(vectors_ref, 7)
     out_ref[...] = (x[:, :lane].astype(f32) + update).astype(bf16)
     upstream = cot_ref[...].astype(f32)
-    base_ref[...] = upstream + dot(dz1b, weights_ref[4 * lane : 5 * lane].T)
+    base_ref[...] = upstream + dot(dz1b, turned_weights[4 * lane : 5 * lane])
     first = 2 * lane
     second = first + lane
     grads_ref[:first, :] = dot_rows(x, dz1b)
@@ -472,7 +485,8 @@
     sent_turned,
     received_turned,
     turned,
-    weights_ref,
+    turned_weights,
+    means,
     vectors_ref,
     node_grads_ref,
     rcv_low,
@@ -481,17 +495,14 @@
     sent_ref,
     grads_ref,
     table,
-    w2_turned,
-    means,
     sums,
 ):
     rim = dagg_near_ref.shape[0]
     parity = parity_of_place()
-    w2_turned[...] = weights_ref[3 * lane : 4 * lane].T
+    w2_turned = turned_weights[3 * lane : 4 * lane]
     gain = vector(vectors_ref, 2)
     table[pl.ds(pl.multiple_of((1 - parity) * rim, rim), rim), :] = dagg_near_ref[...]
     table[pl.ds(pl.multiple_of(parity * rim, rim), rim), :] = dagg_far_ref[...]
-    means[...] = mean_weights()
     grads_ref[: 4 * lane, :] = jnp.zeros((4 * lane, lane), f32)
     sums[...] = jnp.zeros_like(sums)
 
@@ -502,7 +513,7 @@
         normed = normed_ref[rows, :]
         dz2 = back_norm(upstream, normed, scale_ref[rows, :], gain, means[...])
         dz2b = dz2.astype(bf16)
-        dz1 = dot(dz2b, w2_turned[...]) * slope_ref[rows, :]
+        dz1 = dot(dz2b, w2_turned) * slope_ref[rows, :]
         dz1b = dz1.astype(bf16)
         dz_ref[rows, :] = dz1b
         grads_ref[:lane, :] += dot(turned[:lane, rows], dz1b)
@@ -539,7 +550,7 @@
     dz_ref,
     snd_column,
     rcv_column,
-    weights_ref,
+    turned_weights,
     snd_sum_ref,
     rcv_sum_ref,
     rims_ref,
@@ -569,22 +580,22 @@
     for total, out_ref in ((snd_total, snd_sum_ref), (rcv_total, rcv_sum_ref)):
         out_ref[:half, :] = total[:, :lane].astype(bf16)
         out_ref[half:, :] = total[:, lane:].astype(bf16)
-    w1_turned = weights_ref[2 * lane : 3 * lane].T
+    w1_turned = turned_weights[2 * lane : 3 * lane]
     for k, side in enumerate((1 - parity, parity)):
         returned = halo_total[pl.ds(pl.multiple_of(side * rim, rim), rim), :].astype(bf16)
         rims_ref[k * rim : (k + 1) * rim, :] = dot(returned, w1_turned).astype(bf16)
 
 
 def edge_outputs_kernel(
-    dz_ref, cot_ref, edge_ref, normed_ref, vectors_ref, w1_ref, out_ref, grad_ref, w1_turned
-):
-    w1_turned[...] = w1_ref[...].T
+    dz_ref, cot_ref, edge_ref, normed_ref, vectors_ref, turned_weights, out_ref, grad_ref
+):
+    w1_turned = turned_weights[:lane]
     gain, shift = vector(vectors_ref, 2), vector(vectors_ref, 3)
 
     def tile(i):
         rows = pl.ds(pl.multiple_of(i * edge_tile, edge_tile), edge_tile)
         cot = cot_ref[rows, :].astype(f32)
-        grad_ref[rows, :] = (cot + dot(dz_ref[rows, :], w1_turned[...])).astype(bf16)
+        grad_ref[rows, :] = (cot + dot(dz_ref[rows, :], w1_turned)).astype(bf16)
         update = normed_ref[rows, :] * gain + shift
         out_ref[rows, :] = (edge_ref[rows, :].astype(f32) + update).astype(bf16)
 
@@ -592,11 +603,11 @@
 
 
 def node_grad_kernel(
-    near_ref, far_ref, base_ref, snd_sum_ref, rcv_sum_ref, weights_ref, ids_ref, out_ref
+    near_ref, far_ref, base_ref, snd_sum_ref, rcv_sum_ref, turned_weights, ids_ref, out_ref
 ):
     returned = jnp.concatenate([near_ref[...], far_ref[...]], axis=0)
-    total = base_ref[...] + dot(snd_sum_ref[...], weights_ref[lane : 2 * lane].T)
-    total = total + dot(rcv_sum_ref[...], weights_ref[2 * lane : 3 * lane].T)
+    total = base_ref[...] + dot(snd_sum_ref[...], turned_weights[lane : 2 * lane])
+    total = total + dot(rcv_sum_ref[...], turned_weights[2 * lane : 3 * lane])
     hot = hot_lists(ids_ref, base_ref.shape[0])
     out_ref[...] = (total + dot(hot, returned)).astype(bf16)
 
@@ -645,12 +656,20 @@
 
 
 def exchange(message):
-    count = lax.axis_size("dom") * lax.axis_size("sub")
-    inner = [(i, i ^ 1) for i in range(count)]
-    outer = [(i, (((i - 1) % count ^ 1) + 1) % count) for i in range(count)]
+    chips, samples = lax.axis_size("dom"), lax.axis_size("sample")
+    place = lambda chip, sample, core: (chip * samples + sample) * 2 + core
+    inner = [(i, i ^ 1) for i in range(2 * chips)]
+    outer = []
+    for sample in range(samples):
+        for chip in range(chips - 1):
+            ends = place(chip, sample, 1), place(chip + 1, sample, 0)
+            outer += [ends, ends[::-1]]
+        for chip, core in ((0, 0), (chips - 1, 1)):
+            outer.append((place(chip, sample, core), place(chip, sample ^ 1, core)))
     rim_shape = ((message.shape[0] // 2, lane), bf16)
     near, far = call(split_kernel, [rim_shape, rim_shape], [], message)
-    return lax.ppermute(near, chain, inner), lax.ppermute(far, chain, outer), far
+    near = lax.ppermute(near, chain, inner)
+    return near, lax.ppermute(far, ("dom", "sample", "sub"), outer), far
 
 
 def sum_rounds():
@@ -733,6 +752,9 @@
             wide_shape,
             ((snd_half, 2 * lane), bf16),
             ((lane, edges), bf16),
+            ((2 * lane, 2 * lane), bf16),
+            ((2 * lane, 2 * lane), bf16),
+            ((7 * lane, lane), bf16),
         ],
         [((edges, lane), jnp.int16), ((snd_half, 2 * lane), bf16)],
         ids,
@@ -746,14 +768,13 @@
         anywhere=2,
         sems=2,
     )
-    edge_cot, node_cot, snd_column, rcv_column, rcv_low, z_sent, rcv_local, sent_turned = prepared
+    edge_cot, node_cot, snd_column, rcv_column, rcv_low = prepared[:5]
+    z_sent, rcv_local, sent_turned, pairs, means, turned_weights = prepared[5:]
     z, normed, scale, message, rims = call(
         edge_forward_kernel,
         [wide_shape, wide_shape, wide_shape, edge_shape, rims_shape],
         [
             ((snd_half + 2 * rim, 2 * lane), bf16),
-            ((lane, 2 * lane), bf16),
-            ((2 * lane, 2 * lane), bf16),
             ((2 * rim, lane), f32),
         ],
         near,
@@ -765,6 +786,8 @@
         rcv_low,
         z_sent,
         rcv_local,
+        pairs,
+        means,
     )
     back_near, back_far, onward = exchange(rims)
     agg, received_turned = call(
@@ -801,6 +824,9 @@
         weights,
         vectors,
         node_cot,
+        pairs,
+        means,
+        turned_weights,
     )
     dagg_near, dagg_far, onward = exchange(rims)
     upstream, slope, turned = call(
@@ -825,7 +851,7 @@
         node_dz1,
         node_dz2,
         node_sums,
-        weights,
+        turned_weights,
         vectors,
         node_cot,
         onward,
@@ -837,8 +863,6 @@
         [
             ((2 * kept, lane), f32),
             ((2 * rim, lane), bf16),
-            ((lane, lane), bf16),
-            ((2 * lane, 2 * lane), bf16),
             ((32, lane), f32),
         ],
         dagg_near,
@@ -850,7 +874,8 @@
         sent_turned,
         received_turned,
         turned,
-        weights,
+        turned_weights,
+        means,
         vectors,
         node_grads,
         rcv_low,
@@ -870,43 +895,30 @@
         dz,
         snd_column,
         rcv_column,
-        weights,
-    )
-    w1_edge = weights[:lane]
-    edge_out = edge_grad = node_grad = None
-    for number, (axis, pairs) in enumerate(sum_rounds()):
-        other = lax.ppermute(grads, axis, pairs)
+        turned_weights,
+    )
+    node_grad = edge_out = edge_grad = None
+    early_vectors = vectors
+    for number, (axis, partners) in enumerate(sum_rounds()):
+        other = lax.ppermute(grads, axis, partners)
         passed, written = [], []
         if number == 0:
-            passed = [rims]
+            passed = [rims, vectors]
         elif number == 1:
-            back_near, back_far, unused = exchange(rims)
-            passed = [back_near, back_far, vectors, w1_edge]
-        elif number == 2:
-            (node_grad,) = call(
-                node_grad_kernel,
-                [node_shape],
-                [],
-                back_near,
-                back_far,
-                base,
-                snd_sum,
-                rcv_sum,
-                weights,
-                ids,
-            )
             edge_out, edge_grad = call(
                 edge_outputs_kernel,
                 [edge_shape, edge_shape],
-                [((lane, lane), bf16)],
+                [],
                 dz,
                 edge_cot,
                 edge,
                 normed,
-                vectors,
-                w1_edge,
+                early_vectors,
+                turned_weights,
             )
-            written = [node_grad, edge_out, edge_grad]
+            passed, written = [rims], [edge_out, edge_grad]
+        elif number == 2:
+            passed = exchange(rims)[:2]
         grads, *passed = call(
             functools.partial(add_kernel, len(passed)),
             [half_shape] + [(x.shape, x.dtype) for x in passed],
@@ -918,10 +930,24 @@
             anywhere=len(written),
         )
         if number == 0:
+            rims, early_vectors = passed
+        elif number == 1:
             (rims,) = passed
-        elif number == 1:
-            back_near, back_far, vectors, w1_edge = passed
+        elif number == 2:
+            back_near, back_far = passed
     others = lax.ppermute(grads, "sub", core_pairs)
+    (node_grad,) = call(
+        node_grad_kernel,
+        [node_shape],
+        [],
+        back_near,
+        back_far,
+        base,
+        snd_sum,
+        rcv_sum,
+        turned_weights,
+        ids,
+    )
     matrices = [3 * lane, lane, 2 * lane, lane]
     totals = call(
         finish_kernel,

time: 53.8 us -> 49.6 us (0.922)
  waiting for transfers between devices: 9.56 us -> 7.04 us
  starting transfers between devices: 17.1 us -> 15.2 us
    ppermute x11, waiting for transfers between devices: 7.61 us -> 6.03 us  [the longest x3 3.22 us: on_device(): other = lax.ppermute(grads, axis, partners)]
    ppermute x1, starting transfers between devices: 1.95 us -> 0.38 us  [on_device(): other = lax.ppermute(grads_sent, 'sub', core_pairs)]
    ppermute x1, starting transfers between devices: 1.69 us -> 0.4 us  [on_device(): others = lax.ppermute(grads, 'sub', core_pairs)]
    ppermute x1, waiting for transfers between devices: 0.97 us -> 0.01 us  [on_device(): others = lax.ppermute(grads, 'sub', core_pairs)]
    ppermute x11, starting transfers between devices: 13.5 us -> 14.4 us  [the longest x4 7.01 us: exchange(): return (near, lax.ppermute(far, ('dom', 'sample', 'sub'), outer), far)]
  transfers between devices with their start and end apart: 13 -> 13, of which waited for: 8 -> 4; matrix products, arithmetic and copies ran while one was open for 0% -> 0% of each run, Pallas kernels for 24% -> 27%
where the time goes in v11:
time: 49.6 us; the launch traced here: 49.3 us
  Pallas kernels  26.1 us (53%)
  starting transfers between devices  15.2 us (31%)
  waiting for transfers between devices  7.04 us (14%)
  between operations  0.94 us (2%)
    pallas_call x20, Pallas kernels, call(): pl.pallas_call(kernel, out_shape=[jax.ShapeDtypeStruct(shape, dtype) for...  26.1 us
    ppermute x4, starting transfers between devices, exchange(): return (near, lax.ppermute(far, ('dom', 'sample', 'sub'), outer), far)  7.01 us
    ppermute x3, starting transfers between devices, on_device(): other = lax.ppermute(grads, axis, partners)  3.92 us
    ppermute x4, starting transfers between devices, exchange(): near = lax.ppermute(near, chain, inner)  3.51 us
    ppermute x3, waiting for transfers between devices, on_device(): other = lax.ppermute(grads, axis, partners)  3.22 us
    ppermute x4, waiting for transfers between devices, exchange(): return (near, lax.ppermute(far, ('dom', 'sample', 'sub'), outer), far)  2.79 us
    ppermute x1, waiting for transfers between devices, on_device(): other = lax.ppermute(grads_sent, 'sub', core_pairs)  1.01 us
  transfers between devices with their start and end apart: 13, of which 4 were waited for; matrix products, arithmetic and copies ran while one was open for 0% of the time, Pallas kernels for 27%

profile of v11, /device:TPU:1, one launch (start us, length us, event | category | flops | bytes accessed | tf_op | source)
XLA Modules:
  0.0 49.3 jit_solution(5896520543824641622)
XLA Ops:
  0.7 1.6 %shard_map.306 = (bf16[1024,128]{1,0:T(8,128)(2,1)S(1)}, bf16[256,128]{1,0:T(8,128)(2,1)S(1)}, s32[50,128]{1,0:T(8,128)S(1)}, bf16[3072,128]{1,0:T(8,128)(2,1)S(...) custom-call(bf16[1024,128]{1,0:T(8,128)(2,1)} %bitcast.33, s32[2,128]{1,0:T(2,128)} %bitcast.36, ...), custom_call_target="tpu_custom_call" | custom-call | bytes 1307648 | tf_op jit(solution)/shard_map/pallas_call | solution.py:647
  2.4 2.7 %collective-permute-start.1 = (bf16[128,128]{1,0:T(8,128)(2,1)S(1)}, bf16[128,128]{1,0:T(8,128)(2,1)S(1)}, u32[]{:S(2)}, u32[]{:S(2)}) collective-permute-start(bf16[128,128]{1,0:T(8,128)(2,1)S(1)} %get-tuple-element.92.unused_ref), channel_id=1, source_target_pairs={{1,4},{4,1},{5,8},{8,5},{9,12},{12,9},{0,2},{13,15},{3,6},{6,3},{7... | collective-permute-start | bytes 98312 | tf_op jit(solution)/shard_map/ppermute | solution.py:672
  5.1 3.1 %shard_map.308 = (bf16[3072,128]{1,0:T(8,128)(2,1)S(1)}, bf16[1024,128]{1,0:T(8,128)(2,1)S(1)}, s32[3072,128]{1,0:T(8,128)S(1)}, s32[3072,128]{1,0:T(8,128)S(1)}...) custom-call(s32[50,128]{1,0:T(8,128)S(1)} %get-tuple-element.93.ids_, ...), custom_call_target="tpu_custom_call" | custom-call | bytes 2388992 | tf_op jit(solution)/shard_map/pallas_call | solution.py:647
  8.2 5.0 %shard_map.309 = (f32[3072,128]{1,0:T(8,128)S(1)}, f32[3072,128]{1,0:T(8,128)S(1)}, f32[3072,128]{1,0:T(8,128)S(1)}, bf16[3072,128]{1,0:T(8,128)(2,1)S(1)}, bf16[256,128]{1,0:T(8,128)(2,1)S(1)}) custom-call(bf16[128,128]{1,0:T(8,128)(2,1)S(1)} %collective-permute-done.near_ref, bf16[128,128]{1,0:T(8,128)(2,1)S(1)} %collective-permute-done.1.far_ref, ...), custom_call_target="tpu_custom_call" | custom-call | bytes 4781056 | tf_op jit(solution)/shard_map/pallas_call | solution.py:647
  13.6 1.4 %collective-permute-start.3 = (bf16[128,128]{1,0:T(8,128)(2,1)S(1)}, bf16[128,128]{1,0:T(8,128)(2,1)S(1)}, u32[]{:S(2)}, u32[]{:S(2)}) collective-permute-start(bf16[128,128]{1,0:T(8,128)(2,1)S(1)} %get-tuple-element.106.unused_ref), channel_id=1, source_target_pairs={{1,4},{4,1},{5,8},{8,5},{9,12},{12,9},{0,2},{13,15},{3,6},{6,3},{7... | collective-permute-start | bytes 98312 | tf_op jit(solution)/shard_map/ppermute | solution.py:672
  15.0 2.3 %shard_map.311 = (f32[1024,128]{1,0:T(8,128)S(1)}, bf16[128,3072]{1,0:T(8,128)(2,1)S(1)}) custom-call(s32[50,128]{1,0:T(8,128)S(1)} %get-tuple-element.93.ids_ref, s32[3072,128]{1,0:T(8,128)S(1)} %get-tuple-element.98.rcv_column, s16[3072,128]{1,0:T(8,128)(2,1)S(1)} %get-tuple-element.99.rcv_low, bf16[3072,128]{1,0:T(8,128)(2,1)S(1)} %get-tuple-element.107.message_ref, ...), custom_call_target="tpu_custom_call" | custom-call | bytes 3531776 | tf_op jit(solution)/shard_map/pallas_call | solution.py:647
  17.3 1.6 %shard_map.312 = (bf16[1024,256]{1,0:T(8,128)(2,1)S(1)}, bf16[1024,128]{1,0:T(8,128)(2,1)S(1)}, f32[1024,128]{1,0:T(8,128)S(1)}, bf16[1024,128]{1,0:T(8,128)(2,1...) custom-call(bf16[128,128]{1,0:T(8,128)(2,1)S(1)} %collective-permute, ...), custom_call_target="tpu_custom_call" | custom-call | bytes 1864704 | tf_op jit(solution)/shard_map/pallas_call | solution.py:647
  19.4 1.3 %collective-permute-start.5 = (bf16[128,128]{1,0:T(8,128)(2,1)S(1)}, bf16[128,128]{1,0:T(8,128)(2,1)S(1)}, u32[]{:S(2)}, u32[]{:S(2)}) collective-permute-start(bf16[128,128]{1,0:T(8,128)(2,1)S(1)} %get-tuple-element.118.unused_ref), channel_id=1, source_target_pairs={{1,4},{4,1},{5,8},{8,5},{9,12},{12,9},{0,2},{13,15},{3,6},{6,3},{7... | collective-permute-start | bytes 98312 | tf_op jit(solution)/shard_map/ppermute | solution.py:672
  20.7 1.6 %shard_map.315 = (f32[3072,128]{1,0:T(8,128)S(1)}, f32[3072,128]{1,0:T(8,128)S(1)}, bf16[256,3072]{1,0:T(8,128)(2,1)S(1)}) custom-call(s32[3072,128]{1,0:T(8,128)S(1)} %get-tuple-element.98.rcv_column, s16[3072,128]{1,0:T(8,128)(2,1)S(1)} %get-tuple-element.99.rcv_low, bf16[1024,128]{1,0:T(8,128)(2,1)S(1)} %get-tuple-element.121.dagg_ref, ...), custom_call_target="tpu_custom_call" | custom-call | bytes 5799936 | tf_op jit(solution)/shard_map/pallas_call | solution.py:647
  22.3 1.0 %shard_map.314 = (bf16[1024,128]{1,0:T(8,128)(2,1)}, f32[1024,128]{1,0:T(8,128)S(1)}, f32[400,128]{1,0:T(8,128)S(1)}) custom-call(bf16[1024,256]{1,0:T(8,128)(2,1)S(1)} %get-tuple-element.111.x_ref, bf16[1024,128]{1,0:T(8,128)(2,1)S(1)} %get-tuple-element.112.act_ref, f32[1024,128]{1,0:T(8,128)S(1)} %get-tuple-element.113.normed_ref, ...), custom_call_target="tpu_custom_call" | custom-call | bytes 2371584 | tf_op jit(solution)/shard_map/pallas_call | solution.py:647
  23.3 3.7 %shard_map.316 = (bf16[3072,128]{1,0:T(8,128)(2,1)S(1)}, f32[464,128]{1,0:T(8,128)S(1)}, bf16[464,128]{1,0:T(8,128)(2,1)S(1)}) custom-call(bf16[128,128]{1,0:T(8,128)(2,1)S(1)} %collective-permute-done.4.dagg_near_ref, bf16[128,128]{1,0:T(8,128)(2,1)S(1)} %collective-permute-done.5.dagg_far_ref, f32[3072,128]{1,0:T(8,128)S(1)} %get-tuple-element.124.up_ref, ...), custom_call_target="tpu_custom_call" | custom-call | bytes 10858496 | tf_op jit(solution)/shard_map/pallas_call | solution.py:647
  27.4 1.0 %collective-permute-done.6.other_ref = bf16[464,128]{1,0:T(8,128)(2,1)S(1)} collective-permute-done((bf16[464,128]{1,0:T(8,128)(2,1)S(1)}, bf16[464,128]{1,0:T(8,128)(2,1)S(1)}, u32[]{:S(2)}, u32[]{:S(2)}) %collective-permute-start.6) | collective-permute-done | bytes 118816 | tf_op jit(solution)/shard_map/ppermute | solution.py:884
  28.4 1.3 %collective-permute-start.7 = (bf16[464,128]{1,0:T(8,128)(2,1)S(1)}, bf16[464,128]{1,0:T(8,128)(2,1)S(1)}, u32[]{:S(2)}, u32[]{:S(2)}) collective-permute-start(bf16[464,128]{1,0:T(8,128)(2,1)S(1)} %shard_map.317.own_ref), channel_id=1, source_target_pairs={{0,2},{2,0},{1,3},{3,1},{4,6},{6,4},{5,7},{7,5},{8,10},{10,8},{9,1... | collective-permute-start | bytes 356360 | tf_op jit(solution)/shard_map/ppermute | solution.py:903
  29.7 2.6 %shard_map.318 = (bf16[1024,128]{1,0:T(8,128)(2,1)S(1)}, bf16[1024,128]{1,0:T(8,128)(2,1)S(1)}, bf16[256,128]{1,0:T(8,128)(2,1)S(1)}) custom-call(s32[50,128]{1,0:T(8,128)S(1)} %get-tuple-element.93.ids_ref, bf16[3072,128]{1,0:T(8,128)(2,1)S(1)} %get-tuple-element.132.dz_ref, s32[3072,128]{1,0:T(8,128)S(1)} %get-tuple-element.135.snd_column, ...), custom_call_target="tpu_custom_call" | custom-call | bytes 4187136 | tf_op jit(solution)/shard_map/pallas_call | solution.py:647
  32.3 0.7 %collective-permute-done.7.other_ref = bf16[464,128]{1,0:T(8,128)(2,1)S(1)} collective-permute-done((bf16[464,128]{1,0:T(8,128)(2,1)S(1)}, bf16[464,128]{1,0:T(8,128)(2,1)S(1)}, u32[]{:S(2)}, u32[]{:S(2)}) %collective-permute-start.7) | collective-permute-done | bytes 118816 | tf_op jit(solution)/shard_map/ppermute | solution.py:903
  33.0 1.8 %collective-permute-start.8 = (bf16[464,128]{1,0:T(8,128)(2,1)S(1)}, bf16[464,128]{1,0:T(8,128)(2,1)S(1)}, u32[]{:S(2)}, u32[]{:S(2)}) collective-permute-start(bf16[464,128]{1,0:T(8,128)(2,1)S(1)} %get-tuple-element.139.own_ref), channel_id=1, source_target_pairs={{0,8},{4,12},{8,0},{12,4},{1,9},{5,13},{9,1},{13,5},{2,10},{6,14},... | collective-permute-start | bytes 356360 | tf_op jit(solution)/shard_map/ppermute | solution.py:903
  34.8 1.5 %shard_map.320 = (bf16[3072,128]{1,0:T(8,128)(2,1)}, bf16[3072,128]{1,0:T(8,128)(2,1)}) custom-call(bf16[3072,128]{1,0:T(8,128)(2,1)S(1)} %get-tuple-element.132.dz_ref, bf16[3072,128]{1,0:T(8,128)(2,1)S(1)} %get-tuple-element.122.cot_ref, bf16[3072,128]{1,0:T(8,128)(2,1)S(1)} %get-tuple-element.97.edge_ref, f32[3072,128]{1,0:T(8,128)S(1)} %get-tuple-element.125.normed_ref, ...), custom_call_target="tpu_custom_call" | custom-call | bytes 4165632 | tf_op jit(solution)/shard_map/pallas_call | solution.py:647
  36.4 2.6 %collective-permute-done.8.other_ref = bf16[464,128]{1,0:T(8,128)(2,1)S(1)} collective-permute-done((bf16[464,128]{1,0:T(8,128)(2,1)S(1)}, bf16[464,128]{1,0:T(8,128)(2,1)S(1)}, u32[]{:S(2)}, u32[]{:S(2)}) %collective-permute-start.8) | collective-permute-done | bytes 118816 | tf_op jit(solution)/shard_map/ppermute | solution.py:903
  39.0 0.8 %collective-permute-start.9 = (bf16[464,128]{1,0:T(8,128)(2,1)S(1)}, bf16[464,128]{1,0:T(8,128)(2,1)S(1)}, u32[]{:S(2)}, u32[]{:S(2)}) collective-permute-start(bf16[464,128]{1,0:T(8,128)(2,1)S(1)} %get-tuple-element.142.own_ref), channel_id=1, source_target_pairs={{0,4},{4,0},{8,12},{12,8},{1,5},{5,1},{9,13},{13,9},{2,6},{6,2},{1... | collective-permute-start | bytes 356360 | tf_op jit(solution)/shard_map/ppermute | solution.py:903
  39.8 2.6 %collective-permute-start.10 = (bf16[128,128]{1,0:T(8,128)(2,1)S(1)}, bf16[128,128]{1,0:T(8,128)(2,1)S(1)}, u32[]{:S(2)}, u32[]{:S(2)}) collective-permute-start(bf16[128,128]{1,0:T(8,128)(2,1)S(1)} %get-tuple-element.144), channel_id=1, source_target_pairs={{0,1},{1,0},{4,5},{5,4},{8,9},{9,8},{12,13},{13,12},{2,3},{3,2},{6... | collective-permute-start | bytes 98312 | tf_op jit(solution)/shard_map/ppermute | solution.py:671
  42.4 1.6 %collective-permute-start.11 = (bf16[128,128]{1,0:T(8,128)(2,1)S(1)}, bf16[128,128]{1,0:T(8,128)(2,1)S(1)}, u32[]{:S(2)}, u32[]{:S(2)}) collective-permute-start(bf16[128,128]{1,0:T(8,128)(2,1)S(1)} %get-tuple-element.145), channel_id=1, source_target_pairs={{1,4},{4,1},{5,8},{8,5},{9,12},{12,9},{0,2},{13,15},{3,6},{6,3},{7... | collective-permute-start | bytes 98312 | tf_op jit(solution)/shard_map/ppermute | solution.py:672
  44.0 2.8 %collective-permute-done.11.refs_1_ = bf16[128,128]{1,0:T(8,128)(2,1)S(1)} collective-permute-done((bf16[128,128]{1,0:T(8,128)(2,1)S(1)}, bf16[128,128]{1,0:T(8,128)(2,1)S(1)}, u32[]{:S(2)}, u32[]{:S(2)}) %collective-permute-start.11) | collective-permute-done | bytes 32800 | tf_op jit(solution)/shard_map/ppermute | solution.py:672
  47.2 1.1 %shard_map.324 = bf16[1024,128]{1,0:T(8,128)(2,1)} custom-call(bf16[128,128]{1,0:T(8,128)(2,1)S(1)} %get-tuple-element.146.near_ref, bf16[128,128]{1,0:T(8,128)(2,1)S(1)} %get-tuple-element.147.far_ref, f32[1024,128]{1,0:T(8,128)S(1)} %get-tuple-element.148.base_ref, bf16[1024,128]{1,0:T(8,128)(2,1)S(1)} %get-tuple-element.149.snd_sum_ref, ...), custom_call_target="tpu_custom_call" | custom-call | bytes 1369088 | tf_op jit(solution)/shard_map/pallas_call | solution.py:647
  48.3 0.8 %shard_map.325 = (f32[384,128]{1,0:T(8,128)}, f32[128,128]{1,0:T(8,128)}, f32[256,128]{1,0:T(8,128)}, f32[128,128]{1,0:T(8,128)}, f32[1,128]{1,0:T(1,128)}, /*in...) custom-call(bf16[464,128]{1,0:T(8,128)(2,1)S(1)} %get-tuple-element., ...), custom_call_target="tpu_custom_call" | custom-call | bytes 237568 | tf_op jit(solution)/shard_map/pallas_call | solution.py:647
  (22 shorter events, 1.9 us)
Async XLA Ops:
  2.3 6.0 %collective-permute-start = (bf16[128,128]{1,0:T(8,128)(2,1)S(1)}, bf16[128,128]{1,0:T(8,128)(2,1)S(1)}, u32[]{:S(2)}, u32[]{:S(2)}) collective-permute-start(bf16[128,128]{1,0:T(8,128)(2,1)S(1)} %get-tuple-element.91), channel_id=1, source_target_pairs={{0,1},{1,0},{4,5},{5,4},{8,9},{9,8},{12,13},{13,12},{2,3},{3,2},{6... | collective-permute-start | bytes 98312 | tf_op jit(solution)/shard_map/ppermute | solution.py:671
  2.4 5.8 %collective-permute-start.1 = (bf16[128,128]{1,0:T(8,128)(2,1)S(1)}, bf16[128,128]{1,0:T(8,128)(2,1)S(1)}, u32[]{:S(2)}, u32[]{:S(2)}) collective-permute-start(bf16[128,128]{1,0:T(8,128)(2,1)S(1)} %get-tuple-element.92.unused_ref), channel_id=1, source_target_pairs={{1,4},{4,1},{5,8},{8,5},{9,12},{12,9},{0,2},{13,15},{3,6},{6,3},{7... | collective-permute-start | bytes 98312 | tf_op jit(solution)/shard_map/ppermute | solution.py:672
  13.2 4.1 %collective-permute-start.2 = (bf16[128,128]{1,0:T(8,128)(2,1)S(1)}, bf16[128,128]{1,0:T(8,128)(2,1)S(1)}, u32[]{:S(2)}, u32[]{:S(2)}) collective-permute-start(bf16[128,128]{1,0:T(8,128)(2,1)S(1)} %get-tuple-element.105), channel_id=1, source_target_pairs={{0,1},{1,0},{4,5},{5,4},{8,9},{9,8},{12,13},{13,12},{2,3},{3,2},{6... | collective-permute-start | bytes 98312 | tf_op jit(solution)/shard_map/ppermute | solution.py:671
  13.6 3.7 %collective-permute-start.3 = (bf16[128,128]{1,0:T(8,128)(2,1)S(1)}, bf16[128,128]{1,0:T(8,128)(2,1)S(1)}, u32[]{:S(2)}, u32[]{:S(2)}) collective-permute-start(bf16[128,128]{1,0:T(8,128)(2,1)S(1)} %get-tuple-element.106.unused_ref), channel_id=1, source_target_pairs={{1,4},{4,1},{5,8},{8,5},{9,12},{12,9},{0,2},{13,15},{3,6},{6,3},{7... | collective-permute-start | bytes 98312 | tf_op jit(solution)/shard_map/ppermute | solution.py:672
  19.0 4.3 %collective-permute-start.4 = (bf16[128,128]{1,0:T(8,128)(2,1)S(1)}, bf16[128,128]{1,0:T(8,128)(2,1)S(1)}, u32[]{:S(2)}, u32[]{:S(2)}) collective-permute-start(bf16[128,128]{1,0:T(8,128)(2,1)S(1)} %get-tuple-element.120), channel_id=1, source_target_pairs={{0,1},{1,0},{4,5},{5,4},{8,9},{9,8},{12,13},{13,12},{2,3},{3,2},{6... | collective-permute-start | bytes 98312 | tf_op jit(solution)/shard_map/ppermute | solution.py:671
  19.4 3.9 %collective-permute-start.5 = (bf16[128,128]{1,0:T(8,128)(2,1)S(1)}, bf16[128,128]{1,0:T(8,128)(2,1)S(1)}, u32[]{:S(2)}, u32[]{:S(2)}) collective-permute-start(bf16[128,128]{1,0:T(8,128)(2,1)S(1)} %get-tuple-element.118.unused_ref), channel_id=1, source_target_pairs={{1,4},{4,1},{5,8},{8,5},{9,12},{12,9},{0,2},{13,15},{3,6},{6,3},{7... | collective-permute-start | bytes 98312 | tf_op jit(solution)/shard_map/ppermute | solution.py:672
  27.0 1.4 %collective-permute-start.6 = (bf16[464,128]{1,0:T(8,128)(2,1)S(1)}, bf16[464,128]{1,0:T(8,128)(2,1)S(1)}, u32[]{:S(2)}, u32[]{:S(2)}) collective-permute-start(bf16[464,128]{1,0:T(8,128)(2,1)S(1)} %get-tuple-element.134), channel_id=1, source_target_pairs={{0,1},{1,0},{2,3},{3,2},{4,5},{5,4},{6,7},{7,6},{8,9},{9,8},{10,11... | collective-permute-start | bytes 356360 | tf_op jit(solution)/shard_map/ppermute | solution.py:884
  28.4 4.6 %collective-permute-start.7 = (bf16[464,128]{1,0:T(8,128)(2,1)S(1)}, bf16[464,128]{1,0:T(8,128)(2,1)S(1)}, u32[]{:S(2)}, u32[]{:S(2)}) collective-permute-start(bf16[464,128]{1,0:T(8,128)(2,1)S(1)} %shard_map.317.own_ref), channel_id=1, source_target_pairs={{0,2},{2,0},{1,3},{3,1},{4,6},{6,4},{5,7},{7,5},{8,10},{10,8},{9,1... | collective-permute-start | bytes 356360 | tf_op jit(solution)/shard_map/ppermute | solution.py:903
  33.0 5.9 %collective-permute-start.8 = (bf16[464,128]{1,0:T(8,128)(2,1)S(1)}, bf16[464,128]{1,0:T(8,128)(2,1)S(1)}, u32[]{:S(2)}, u32[]{:S(2)}) collective-permute-start(bf16[464,128]{1,0:T(8,128)(2,1)S(1)} %get-tuple-element.139.own_ref), channel_id=1, source_target_pairs={{0,8},{4,12},{8,0},{12,4},{1,9},{5,13},{9,1},{13,5},{2,10},{6,14},... | collective-permute-start | bytes 356360 | tf_op jit(solution)/shard_map/ppermute | solution.py:903
  39.0 7.8 %collective-permute-start.9 = (bf16[464,128]{1,0:T(8,128)(2,1)S(1)}, bf16[464,128]{1,0:T(8,128)(2,1)S(1)}, u32[]{:S(2)}, u32[]{:S(2)}) collective-permute-start(bf16[464,128]{1,0:T(8,128)(2,1)S(1)} %get-tuple-element.142.own_ref), channel_id=1, source_target_pairs={{0,4},{4,0},{8,12},{12,8},{1,5},{5,1},{9,13},{13,9},{2,6},{6,2},{1... | collective-permute-start | bytes 356360 | tf_op jit(solution)/shard_map/ppermute | solution.py:903
  39.8 4.2 %collective-permute-start.10 = (bf16[128,128]{1,0:T(8,128)(2,1)S(1)}, bf16[128,128]{1,0:T(8,128)(2,1)S(1)}, u32[]{:S(2)}, u32[]{:S(2)}) collective-permute-start(bf16[128,128]{1,0:T(8,128)(2,1)S(1)} %get-tuple-element.144), channel_id=1, source_target_pairs={{0,1},{1,0},{4,5},{5,4},{8,9},{9,8},{12,13},{13,12},{2,3},{3,2},{6... | collective-permute-start | bytes 98312 | tf_op jit(solution)/shard_map/ppermute | solution.py:671
  42.4 4.4 %collective-permute-start.11 = (bf16[128,128]{1,0:T(8,128)(2,1)S(1)}, bf16[128,128]{1,0:T(8,128)(2,1)S(1)}, u32[]{:S(2)}, u32[]{:S(2)}) collective-permute-start(bf16[128,128]{1,0:T(8,128)(2,1)S(1)} %get-tuple-element.145), channel_id=1, source_target_pairs={{1,4},{4,1},{5,8},{8,5},{9,12},{12,9},{0,2},{13,15},{3,6},{6,3},{7... | collective-permute-start | bytes 98312 | tf_op jit(solution)/shard_map/ppermute | solution.py:672
  46.8 1.5 %collective-permute-start.12 = (bf16[464,128]{1,0:T(8,128)(2,1)S(1)}, bf16[464,128]{1,0:T(8,128)(2,1)S(1)}, u32[]{:S(2)}, u32[]{:S(2)}) collective-permute-start(bf16[464,128]{1,0:T(8,128)(2,1)S(1)} %get-tuple-element.151.own_ref), channel_id=1, source_target_pairs={{0,1},{1,0},{2,3},{3,2},{4,5},{5,4},{6,7},{7,6},{8,9},{9,8},{10,11... | collective-permute-start | bytes 356360 | tf_op jit(solution)/shard_map/ppermute | solution.py:938

commit v12 on v11

--- a/solution.py
+++ b/solution.py
@@ -296,6 +296,10 @@
         z = z_sent[rows, :]
         z = z + pick(rcv_column[rows, :], rcv_low[rows, :], half, table[...], slots)
         z_ref[rows, :] = z
+
+    def rest(i):
+        rows = pl.ds(pl.multiple_of(i * edge_tile, edge_tile), edge_tile)
+        z = z_ref[rows, :]
         act = (z * sigmoid(z)).astype(bf16)
         normed, scale_inv = normed_of(act, pairs_ref[:lane, :], b2, means[...])
         normed_ref[rows, :] = normed
@@ -306,7 +310,8 @@
         hot = rows_of_ids(ids_ref, first, edge_tile // lane, 2 * rim, lambda row: row - nodes)
         total[...] += dot(hot, message)
 
-    each_tile(rcv_column.shape[0], tile, 3)
+    each_tile(rcv_column.shape[0], tile)
+    each_tile(rcv_column.shape[0], rest)
     rims_ref[:rim, :] = total[pl.ds(near_at, rim), :].astype(bf16)
     rims_ref[rim:, :] = total[pl.ds(far_at, rim), :].astype(bf16)
 
@@ -545,45 +550,52 @@
     sent_ref[...] = grads_ref[pl.ds(other, kept), :].astype(bf16)
 
 
+def halo_kernel(nodes, ids_ref, dz_ref, turned_weights, rims_ref, total):
+    rim = rims_ref.shape[0] // 2
+    edges = dz_ref.shape[0]
+    parity = parity_of_place()
+    total[...] = jnp.zeros_like(total)
+
+    def tile(i):
+        rows = pl.ds(pl.multiple_of(i * edge_tile, edge_tile), edge_tile)
+        first = (edges + i * edge_tile) // lane
+        slots = rows_of_ids(ids_ref, first, edge_tile // lane, 2 * rim, lambda row: row - nodes)
+        total[...] += dot(slots, dz_ref[rows, :])
+
+    each_tile(edges, tile)
+    w1_turned = turned_weights[2 * lane : 3 * lane]
+    for k, side in enumerate((1 - parity, parity)):
+        returned = total[pl.ds(pl.multiple_of(side * rim, rim), rim), :].astype(bf16)
+        rims_ref[k * rim : (k + 1) * rim, :] = dot(returned, w1_turned).astype(bf16)
+
+
 def scatter_kernel(
     ids_ref,
     dz_ref,
     snd_column,
     rcv_column,
-    turned_weights,
+    unused_ref,
     snd_sum_ref,
     rcv_sum_ref,
-    rims_ref,
     snd_total,
     rcv_total,
-    halo_total,
 ):
     half = snd_total.shape[0]
-    nodes = 2 * half
-    rim = rims_ref.shape[0] // 2
-    parity = parity_of_place()
-    for total in (snd_total, rcv_total, halo_total):
+    for total in (snd_total, rcv_total):
         total[...] = jnp.zeros_like(total)
 
     def tile(i):
         rows = pl.ds(pl.multiple_of(i * edge_tile, edge_tile), edge_tile)
         chunk = edge_tile // lane
-        dz1b = dz_ref[rows, :]
-        dz1 = dz1b.astype(f32)
+        dz1 = dz_ref[rows, :].astype(f32)
         first = rcv_column.shape[0] // lane + i * chunk
         snd_total[...] += spread(ids_ref, i * chunk, chunk, half, snd_column[rows, :], dz1)
         rcv_total[...] += spread(ids_ref, first, chunk, half, rcv_column[rows, :], dz1)
-        slots = rows_of_ids(ids_ref, first, chunk, 2 * rim, lambda row: row - nodes)
-        halo_total[...] += dot(slots, dz1b)
 
     each_tile(dz_ref.shape[0], tile)
     for total, out_ref in ((snd_total, snd_sum_ref), (rcv_total, rcv_sum_ref)):
         out_ref[:half, :] = total[:, :lane].astype(bf16)
         out_ref[half:, :] = total[:, lane:].astype(bf16)
-    w1_turned = turned_weights[2 * lane : 3 * lane]
-    for k, side in enumerate((1 - parity, parity)):
-        returned = halo_total[pl.ds(pl.multiple_of(side * rim, rim), rim), :].astype(bf16)
-        rims_ref[k * rim : (k + 1) * rim, :] = dot(returned, w1_turned).astype(bf16)
 
 
 def edge_outputs_kernel(
@@ -883,27 +895,32 @@
     core_pairs = [(0, 1), (1, 0)]
     other = lax.ppermute(grads_sent, "sub", core_pairs)
     (grads,) = call(functools.partial(add_kernel, 0), [half_shape], [], grads_kept, other)
-    snd_sum, rcv_sum, rims = call(
+    (rims,) = call(
+        functools.partial(halo_kernel, nodes),
+        [rims_shape],
+        [((2 * rim, lane), f32)],
+        ids,
+        dz,
+        turned_weights,
+    )
+    back_near, back_far, onward = exchange(rims)
+    snd_sum, rcv_sum = call(
         scatter_kernel,
-        [node_shape, node_shape, rims_shape],
-        [
-            ((snd_half, 2 * lane), f32),
-            ((snd_half, 2 * lane), f32),
-            ((2 * rim, lane), f32),
-        ],
+        [node_shape, node_shape],
+        [((snd_half, 2 * lane), f32), ((snd_half, 2 * lane), f32)],
         ids,
         dz,
         snd_column,
         rcv_column,
-        turned_weights,
+        onward,
     )
     node_grad = edge_out = edge_grad = None
-    early_vectors = vectors
+    early_vectors, early_ids = vectors, ids
     for number, (axis, partners) in enumerate(sum_rounds()):
         other = lax.ppermute(grads, axis, partners)
-        passed, written = [], []
+        passed, before, written = [], [], []
         if number == 0:
-            passed = [rims, vectors]
+            passed, before = [vectors], [back_near, back_far, snd_sum, rcv_sum]
         elif number == 1:
             edge_out, edge_grad = call(
                 edge_outputs_kernel,
@@ -916,9 +933,21 @@
                 early_vectors,
                 turned_weights,
             )
-            passed, written = [rims], [edge_out, edge_grad]
+            passed, written = [ids], [edge_out, edge_grad]
         elif number == 2:
-            passed = exchange(rims)[:2]
+            (node_grad,) = call(
+                node_grad_kernel,
+                [node_shape],
+                [],
+                back_near,
+                back_far,
+                base,
+                snd_sum,
+                rcv_sum,
+                turned_weights,
+                early_ids,
+            )
+            written = [node_grad]
         grads, *passed = call(
             functools.partial(add_kernel, len(passed)),
             [half_shape] + [(x.shape, x.dtype) for x in passed],
@@ -926,28 +955,15 @@
             grads,
             other,
             *passed,
+            *before,
             *written,
             anywhere=len(written),
         )
         if number == 0:
-            rims, early_vectors = passed
+            (early_vectors,) = passed
         elif number == 1:
-            (rims,) = passed
-        elif number == 2:
-            back_near, back_far = passed
+            (early_ids,) = passed
     others = lax.ppermute(grads, "sub", core_pairs)
-    (node_grad,) = call(
-        node_grad_kernel,
-        [node_shape],
-        [],
-        back_near,
-        back_far,
-        base,
-        snd_sum,
-        rcv_sum,
-        turned_weights,
-        ids,
-    )
     matrices = [3 * lane, lane, 2 * lane, lane]
     totals = call(
         finish_kernel,

time: 49.6 us -> 50.2 us (1.012)
  waiting for transfers between devices: 7.04 us -> 11.8 us
  starting transfers between devices: 15.2 us -> 11.9 us
  Pallas kernels: 26.1 us -> 25.1 us
    ppermute x3, waiting for transfers between devices: 3.22 us -> 8.92 us  [on_device(): other = lax.ppermute(grads, axis, partners)]
    ppermute x4, starting transfers between devices: 3.51 us -> 1.47 us  [exchange(): near = lax.ppermute(near, chain, inner)]
    ppermute x4, waiting for transfers between devices: 2.79 us -> 0.87 us  [exchange(): return (near, lax.ppermute(far, ('dom', 'sample', 'sub'), outer), far)]
    ppermute x3, starting transfers between devices: 3.92 us -> 2.35 us  [on_device(): other = lax.ppermute(grads, axis, partners)]
    ppermute x1, starting transfers between devices: 0.4 us -> 1.61 us  [on_device(): others = lax.ppermute(grads, 'sub', core_pairs)]
    pallas_call x20 -> x21, Pallas kernels: 26.1 us -> 25.1 us  [call(): pl.pallas_call(kernel, out_shape=[jax.ShapeDtypeStruct(shape, dtype) for...]
    ppermute x1, waiting for transfers between devices: 0.01 us -> 0.97 us  [on_device(): others = lax.ppermute(grads, 'sub', core_pairs)]
    ppermute x4, starting transfers between devices: 7.01 us -> 6.06 us  [exchange(): return (near, lax.ppermute(far, ('dom', 'sample', 'sub'), outer), far)]
  transfers between devices with their start and end apart: 13 -> 13, of which waited for: 4 -> 5; matrix products, arithmetic and copies ran while one was open for 0% -> 0% of each run, Pallas kernels for 27% -> 27%
where the time goes in v12:
time: 50.2 us; the launch traced here: 49.8 us
  Pallas kernels  25.1 us (50%)
  starting transfers between devices  11.9 us (24%)
  waiting for transfers between devices  11.8 us (24%)
  between operations  0.96 us (2%)
    pallas_call x21, Pallas kernels, call(): pl.pallas_call(kernel, out_shape=[jax.ShapeDtypeStruct(shape, dtype) for...  25.1 us
    ppermute x3, waiting for transfers between devices, on_device(): other = lax.ppermute(grads, axis, partners)  8.92 us
    ppermute x4, starting transfers between devices, exchange(): return (near, lax.ppermute(far, ('dom', 'sample', 'sub'), outer), far)  6.06 us
    ppermute x3, starting transfers between devices, on_device(): other = lax.ppermute(grads, axis, partners)  2.35 us
    ppermute x1, starting transfers between devices, on_device(): others = lax.ppermute(grads, 'sub', core_pairs)  1.61 us
    ppermute x4, starting transfers between devices, exchange(): near = lax.ppermute(near, chain, inner)  1.47 us
    ppermute x1, waiting for transfers between devices, on_device(): other = lax.ppermute(grads_sent, 'sub', core_pairs)  1.01 us
  transfers between devices with their start and end apart: 13, of which 5 were waited for; matrix products, arithmetic and copies ran while one was open for 0% of the time, Pallas kernels for 27%

profile of v12, /device:TPU:1, one launch (start us, length us, event | category | flops | bytes accessed | tf_op | source)
XLA Modules:
  0.0 49.8 jit_solution(463940130242160569)
XLA Ops:
  0.7 1.6 %shard_map.306 = (bf16[1024,128]{1,0:T(8,128)(2,1)S(1)}, bf16[256,128]{1,0:T(8,128)(2,1)S(1)}, s32[50,128]{1,0:T(8,128)S(1)}, bf16[3072,128]{1,0:T(8,128)(2,1)S(...) custom-call(bf16[1024,128]{1,0:T(8,128)(2,1)} %bitcast.33, s32[2,128]{1,0:T(2,128)} %bitcast.36, ...), custom_call_target="tpu_custom_call" | custom-call | bytes 1307648 | tf_op jit(solution)/shard_map/pallas_call | solution.py:659
  2.4 2.7 %collective-permute-start.1 = (bf16[128,128]{1,0:T(8,128)(2,1)S(1)}, bf16[128,128]{1,0:T(8,128)(2,1)S(1)}, u32[]{:S(2)}, u32[]{:S(2)}) collective-permute-start(bf16[128,128]{1,0:T(8,128)(2,1)S(1)} %get-tuple-element.87.unused_ref), channel_id=1, source_target_pairs={{1,4},{4,1},{5,8},{8,5},{9,12},{12,9},{0,2},{13,15},{3,6},{6,3},{7... | collective-permute-start | bytes 98312 | tf_op jit(solution)/shard_map/ppermute | solution.py:684
  5.1 3.1 %shard_map.308 = (bf16[3072,128]{1,0:T(8,128)(2,1)S(1)}, bf16[1024,128]{1,0:T(8,128)(2,1)S(1)}, s32[3072,128]{1,0:T(8,128)S(1)}, s32[3072,128]{1,0:T(8,128)S(1)}...) custom-call(s32[50,128]{1,0:T(8,128)S(1)} %get-tuple-element.88.ids_, ...), custom_call_target="tpu_custom_call" | custom-call | bytes 2388992 | tf_op jit(solution)/shard_map/pallas_call | solution.py:659
  8.2 3.9 %shard_map.309 = (f32[3072,128]{1,0:T(8,128)S(1)}, f32[3072,128]{1,0:T(8,128)S(1)}, f32[3072,128]{1,0:T(8,128)S(1)}, bf16[3072,128]{1,0:T(8,128)(2,1)S(1)}, bf16[256,128]{1,0:T(8,128)(2,1)S(1)}) custom-call(bf16[128,128]{1,0:T(8,128)(2,1)S(1)} %collective-permute-done.near_ref, bf16[128,128]{1,0:T(8,128)(2,1)S(1)} %collective-permute-done.1.far_ref, ...), custom_call_target="tpu_custom_call" | custom-call | bytes 4781056 | tf_op jit(solution)/shard_map/pallas_call | solution.py:659
  12.5 1.4 %collective-permute-start.3 = (bf16[128,128]{1,0:T(8,128)(2,1)S(1)}, bf16[128,128]{1,0:T(8,128)(2,1)S(1)}, u32[]{:S(2)}, u32[]{:S(2)}) collective-permute-start(bf16[128,128]{1,0:T(8,128)(2,1)S(1)} %get-tuple-element.101.unused_ref), channel_id=1, source_target_pairs={{1,4},{4,1},{5,8},{8,5},{9,12},{12,9},{0,2},{13,15},{3,6},{6,3},{7... | collective-permute-start | bytes 98312 | tf_op jit(solution)/shard_map/ppermute | solution.py:684
  13.9 2.3 %shard_map.311 = (f32[1024,128]{1,0:T(8,128)S(1)}, bf16[128,3072]{1,0:T(8,128)(2,1)S(1)}) custom-call(s32[50,128]{1,0:T(8,128)S(1)} %get-tuple-element.88.ids_ref.refs_0_, s32[3072,128]{1,0:T(8,128)S(1)} %get-tuple-element.93.rcv_column, s16[3072,128]{1,0:T(8,128)(2,1)S(1)} %get-tuple-element.94.rcv_low, ...), custom_call_target="tpu_custom_call" | custom-call | bytes 3531776 | tf_op jit(solution)/shard_map/pallas_call | solution.py:659
  16.2 1.6 %shard_map.312 = (bf16[1024,256]{1,0:T(8,128)(2,1)S(1)}, bf16[1024,128]{1,0:T(8,128)(2,1)S(1)}, f32[1024,128]{1,0:T(8,128)S(1)}, bf16[1024,128]{1,0:T(8,128)(2,1...) custom-call(bf16[128,128]{1,0:T(8,128)(2,1)S(1)} %collective-permute, ...), custom_call_target="tpu_custom_call" | custom-call | bytes 1864704 | tf_op jit(solution)/shard_map/pallas_call | solution.py:659
  18.3 1.3 %collective-permute-start.5 = (bf16[128,128]{1,0:T(8,128)(2,1)S(1)}, bf16[128,128]{1,0:T(8,128)(2,1)S(1)}, u32[]{:S(2)}, u32[]{:S(2)}) collective-permute-start(bf16[128,128]{1,0:T(8,128)(2,1)S(1)} %get-tuple-element.113.unused_ref), channel_id=1, source_target_pairs={{1,4},{4,1},{5,8},{8,5},{9,12},{12,9},{0,2},{13,15},{3,6},{6,3},{7... | collective-permute-start | bytes 98312 | tf_op jit(solution)/shard_map/ppermute | solution.py:684
  19.6 1.6 %shard_map.315 = (f32[3072,128]{1,0:T(8,128)S(1)}, f32[3072,128]{1,0:T(8,128)S(1)}, bf16[256,3072]{1,0:T(8,128)(2,1)S(1)}) custom-call(s32[3072,128]{1,0:T(8,128)S(1)} %get-tuple-element.93.rcv_column, s16[3072,128]{1,0:T(8,128)(2,1)S(1)} %get-tuple-element.94.rcv_low, bf16[1024,128]{1,0:T(8,128)(2,1)S(1)} %get-tuple-element.116.dagg_ref, ...), custom_call_target="tpu_custom_call" | custom-call | bytes 5799936 | tf_op jit(solution)/shard_map/pallas_call | solution.py:659
  21.2 1.0 %shard_map.314 = (bf16[1024,128]{1,0:T(8,128)(2,1)}, f32[1024,128]{1,0:T(8,128)S(1)}, f32[400,128]{1,0:T(8,128)S(1)}) custom-call(bf16[1024,256]{1,0:T(8,128)(2,1)S(1)} %get-tuple-element.106.x_ref, bf16[1024,128]{1,0:T(8,128)(2,1)S(1)} %get-tuple-element.107.act_ref, f32[1024,128]{1,0:T(8,128)S(1)} %get-tuple-element.108.normed_ref, ...), custom_call_target="tpu_custom_call" | custom-call | bytes 2371584 | tf_op jit(solution)/shard_map/pallas_call | solution.py:659
  22.2 3.7 %shard_map.316 = (bf16[3072,128]{1,0:T(8,128)(2,1)S(1)}, f32[464,128]{1,0:T(8,128)S(1)}, bf16[464,128]{1,0:T(8,128)(2,1)S(1)}) custom-call(bf16[128,128]{1,0:T(8,128)(2,1)S(1)} %collective-permute-done.4.dagg_near_ref, bf16[128,128]{1,0:T(8,128)(2,1)S(1)} %collective-permute-done.5.dagg_far_ref, f32[3072,128]{1,0:T(8,128)S(1)} %get-tuple-element.119.up_ref, ...), custom_call_target="tpu_custom_call" | custom-call | bytes 10858496 | tf_op jit(solution)/shard_map/pallas_call | solution.py:659
  26.3 1.0 %collective-permute-done.6.other_ref = bf16[464,128]{1,0:T(8,128)(2,1)S(1)} collective-permute-done((bf16[464,128]{1,0:T(8,128)(2,1)S(1)}, bf16[464,128]{1,0:T(8,128)(2,1)S(1)}, u32[]{:S(2)}, u32[]{:S(2)}) %collective-permute-start.6) | collective-permute-done | bytes 118816 | tf_op jit(solution)/shard_map/ppermute | solution.py:896
  27.3 1.3 %collective-permute-start.7 = (bf16[464,128]{1,0:T(8,128)(2,1)S(1)}, bf16[464,128]{1,0:T(8,128)(2,1)S(1)}, u32[]{:S(2)}, u32[]{:S(2)}) collective-permute-start(bf16[464,128]{1,0:T(8,128)(2,1)S(1)} %shard_map.317.own_ref), channel_id=1, source_target_pairs={{0,2},{2,0},{1,3},{3,1},{4,6},{6,4},{5,7},{7,5},{8,10},{10,8},{9,1... | collective-permute-start | bytes 356360 | tf_op jit(solution)/shard_map/ppermute | solution.py:920
  28.6 0.7 %shard_map.318.message_ref = bf16[256,128]{1,0:T(8,128)(2,1)S(1)} custom-call(s32[50,128]{1,0:T(8,128)S(1)} %get-tuple-element.88.ids_ref.refs_0_, bf16[3072,128]{1,0:T(8,128)(2,1)S(1)} %get-tuple-element.127.dz_ref, bf16[896,128]{1,0:T(8,128)(2,1)S(1)} %get-tuple-element.105.turned_weights), custom_call_target="tpu_custom_call" | custom-call | bytes 1041408 | tf_op jit(solution)/shard_map/pallas_call | solution.py:659
  30.5 2.0 %shard_map.320 = (bf16[1024,128]{1,0:T(8,128)(2,1)S(1)}, bf16[1024,128]{1,0:T(8,128)(2,1)S(1)}) custom-call(s32[50,128]{1,0:T(8,128)S(1)} %get-tuple-element.88.ids_ref.refs_0_, bf16[3072,128]{1,0:T(8,128)(2,1)S(1)} %get-tuple-element.127.dz_ref, s32[3072,128]{1,0:T(8,128)S(1)} %get-tuple-element.132.snd_column, ...), custom_call_target="tpu_custom_call" | custom-call | bytes 3990528 | tf_op jit(solution)/shard_map/pallas_call | solution.py:659
  32.5 0.9 %collective-permute-done.9.refs_2_.far_ref = bf16[128,128]{1,0:T(8,128)(2,1)S(1)} collective-permute-done((bf16[128,128]{1,0:T(8,128)(2,1)S(1)}, bf16[128,128]{1,0:T(8,128)(2,1)S(1)}, u32[]{:S(2)}, u32[]{:S(2)}) %collective-permute-start.9) | collective-permute-done | bytes 32800 | tf_op jit(solution)/shard_map/ppermute | solution.py:684
  33.5 1.0 %collective-permute-start.10 = (bf16[464,128]{1,0:T(8,128)(2,1)S(1)}, bf16[464,128]{1,0:T(8,128)(2,1)S(1)}, u32[]{:S(2)}, u32[]{:S(2)}) collective-permute-start(bf16[464,128]{1,0:T(8,128)(2,1)S(1)} %get-tuple-element.138.own_ref), channel_id=1, source_target_pairs={{0,8},{4,12},{8,0},{12,4},{1,9},{5,13},{9,1},{13,5},{2,10},{6,14},... | collective-permute-start | bytes 356360 | tf_op jit(solution)/shard_map/ppermute | solution.py:920
  34.5 1.5 %shard_map.322 = (bf16[3072,128]{1,0:T(8,128)(2,1)}, bf16[3072,128]{1,0:T(8,128)(2,1)}) custom-call(bf16[3072,128]{1,0:T(8,128)(2,1)S(1)} %get-tuple-element.127.dz_ref, bf16[3072,128]{1,0:T(8,128)(2,1)S(1)} %get-tuple-element.117.cot_ref, bf16[3072,128]{1,0:T(8,128)(2,1)S(1)} %get-tuple-element.92.edge_ref, f32[3072,128]{1,0:T(8,128)S(1)} %get-tuple-element.120.normed_ref, ...), custom_call_target="tpu_custom_call" | custom-call | bytes 4165632 | tf_op jit(solution)/shard_map/pallas_call | solution.py:659
  36.0 5.9 %collective-permute-done.10.other_ref = bf16[464,128]{1,0:T(8,128)(2,1)S(1)} collective-permute-done((bf16[464,128]{1,0:T(8,128)(2,1)S(1)}, bf16[464,128]{1,0:T(8,128)(2,1)S(1)}, u32[]{:S(2)}, u32[]{:S(2)}) %collective-permute-start.10) | collective-permute-done | bytes 118816 | tf_op jit(solution)/shard_map/ppermute | solution.py:920
  42.1 1.1 %shard_map.324.refs_0_ = bf16[1024,128]{1,0:T(8,128)(2,1)} custom-call(bf16[128,128]{1,0:T(8,128)(2,1)S(1)} %collective-permute-done.8.refs_1_.near_ref, bf16[128,128]{1,0:T(8,128)(2,1)S(1)} %collective-permute-done.9.refs_2_.far_ref, f32[1024,128]{1,0:T(8,128)S(1)} %get-tuple-element.137.base_ref, ...), custom_call_target="tpu_custom_call" | custom-call | bytes 1369088 | tf_op jit(solution)/shard_map/pallas_call | solution.py:659
  43.2 3.0 %collective-permute-done.11.other_ref = bf16[464,128]{1,0:T(8,128)(2,1)S(1)} collective-permute-done((bf16[464,128]{1,0:T(8,128)(2,1)S(1)}, bf16[464,128]{1,0:T(8,128)(2,1)S(1)}, u32[]{:S(2)}, u32[]{:S(2)}) %collective-permute-start.11) | collective-permute-done | bytes 118816 | tf_op jit(solution)/shard_map/ppermute | solution.py:920
  46.2 1.6 %collective-permute-start.12 = (bf16[464,128]{1,0:T(8,128)(2,1)S(1)}, bf16[464,128]{1,0:T(8,128)(2,1)S(1)}, u32[]{:S(2)}, u32[]{:S(2)}) collective-permute-start(bf16[464,128]{1,0:T(8,128)(2,1)S(1)} %shard_map.325.own_ref), channel_id=1, source_target_pairs={{0,1},{1,0},{2,3},{3,2},{4,5},{5,4},{6,7},{7,6},{8,9},{9,8},{10,11... | collective-permute-start | bytes 356360 | tf_op jit(solution)/shard_map/ppermute | solution.py:966
  47.8 1.0 %collective-permute-done.12.other_ref = bf16[464,128]{1,0:T(8,128)(2,1)S(1)} collective-permute-done((bf16[464,128]{1,0:T(8,128)(2,1)S(1)}, bf16[464,128]{1,0:T(8,128)(2,1)S(1)}, u32[]{:S(2)}, u32[]{:S(2)}) %collective-permute-start.12) | collective-permute-done | bytes 118816 | tf_op jit(solution)/shard_map/ppermute | solution.py:966
  48.8 0.8 %shard_map.326 = (f32[384,128]{1,0:T(8,128)}, f32[128,128]{1,0:T(8,128)}, f32[256,128]{1,0:T(8,128)}, f32[128,128]{1,0:T(8,128)}, f32[1,128]{1,0:T(1,128)}, /*in...) custom-call(bf16[464,128]{1,0:T(8,128)(2,1)S(1)} %shard_map.325.own_, ...), custom_call_target="tpu_custom_call" | custom-call | bytes 237568 | tf_op jit(solution)/shard_map/pallas_call | solution.py:659
  (23 shorter events, 2.8 us)
Async XLA Ops:
  2.3 6.0 %collective-permute-start = (bf16[128,128]{1,0:T(8,128)(2,1)S(1)}, bf16[128,128]{1,0:T(8,128)(2,1)S(1)}, u32[]{:S(2)}, u32[]{:S(2)}) collective-permute-start(bf16[128,128]{1,0:T(8,128)(2,1)S(1)} %get-tuple-element.86), channel_id=1, source_target_pairs={{0,1},{1,0},{4,5},{5,4},{8,9},{9,8},{12,13},{13,12},{2,3},{3,2},{6... | collective-permute-start | bytes 98312 | tf_op jit(solution)/shard_map/ppermute | solution.py:683
  2.4 5.8 %collective-permute-start.1 = (bf16[128,128]{1,0:T(8,128)(2,1)S(1)}, bf16[128,128]{1,0:T(8,128)(2,1)S(1)}, u32[]{:S(2)}, u32[]{:S(2)}) collective-permute-start(bf16[128,128]{1,0:T(8,128)(2,1)S(1)} %get-tuple-element.87.unused_ref), channel_id=1, source_target_pairs={{1,4},{4,1},{5,8},{8,5},{9,12},{12,9},{0,2},{13,15},{3,6},{6,3},{7... | collective-permute-start | bytes 98312 | tf_op jit(solution)/shard_map/ppermute | solution.py:684
  12.2 4.1 %collective-permute-start.2 = (bf16[128,128]{1,0:T(8,128)(2,1)S(1)}, bf16[128,128]{1,0:T(8,128)(2,1)S(1)}, u32[]{:S(2)}, u32[]{:S(2)}) collective-permute-start(bf16[128,128]{1,0:T(8,128)(2,1)S(1)} %get-tuple-element.100), channel_id=1, source_target_pairs={{0,1},{1,0},{4,5},{5,4},{8,9},{9,8},{12,13},{13,12},{2,3},{3,2},{6... | collective-permute-start | bytes 98312 | tf_op jit(solution)/shard_map/ppermute | solution.py:683
  12.5 3.7 %collective-permute-start.3 = (bf16[128,128]{1,0:T(8,128)(2,1)S(1)}, bf16[128,128]{1,0:T(8,128)(2,1)S(1)}, u32[]{:S(2)}, u32[]{:S(2)}) collective-permute-start(bf16[128,128]{1,0:T(8,128)(2,1)S(1)} %get-tuple-element.101.unused_ref), channel_id=1, source_target_pairs={{1,4},{4,1},{5,8},{8,5},{9,12},{12,9},{0,2},{13,15},{3,6},{6,3},{7... | collective-permute-start | bytes 98312 | tf_op jit(solution)/shard_map/ppermute | solution.py:684
  17.9 4.3 %collective-permute-start.4 = (bf16[128,128]{1,0:T(8,128)(2,1)S(1)}, bf16[128,128]{1,0:T(8,128)(2,1)S(1)}, u32[]{:S(2)}, u32[]{:S(2)}) collective-permute-start(bf16[128,128]{1,0:T(8,128)(2,1)S(1)} %get-tuple-element.115), channel_id=1, source_target_pairs={{0,1},{1,0},{4,5},{5,4},{8,9},{9,8},{12,13},{13,12},{2,3},{3,2},{6... | collective-permute-start | bytes 98312 | tf_op jit(solution)/shard_map/ppermute | solution.py:683
  18.3 3.9 %collective-permute-start.5 = (bf16[128,128]{1,0:T(8,128)(2,1)S(1)}, bf16[128,128]{1,0:T(8,128)(2,1)S(1)}, u32[]{:S(2)}, u32[]{:S(2)}) collective-permute-start(bf16[128,128]{1,0:T(8,128)(2,1)S(1)} %get-tuple-element.113.unused_ref), channel_id=1, source_target_pairs={{1,4},{4,1},{5,8},{8,5},{9,12},{12,9},{0,2},{13,15},{3,6},{6,3},{7... | collective-permute-start | bytes 98312 | tf_op jit(solution)/shard_map/ppermute | solution.py:684
  25.9 1.4 %collective-permute-start.6 = (bf16[464,128]{1,0:T(8,128)(2,1)S(1)}, bf16[464,128]{1,0:T(8,128)(2,1)S(1)}, u32[]{:S(2)}, u32[]{:S(2)}) collective-permute-start(bf16[464,128]{1,0:T(8,128)(2,1)S(1)} %get-tuple-element.129), channel_id=1, source_target_pairs={{0,1},{1,0},{2,3},{3,2},{4,5},{5,4},{6,7},{7,6},{8,9},{9,8},{10,11... | collective-permute-start | bytes 356360 | tf_op jit(solution)/shard_map/ppermute | solution.py:896
  27.3 6.1 %collective-permute-start.7 = (bf16[464,128]{1,0:T(8,128)(2,1)S(1)}, bf16[464,128]{1,0:T(8,128)(2,1)S(1)}, u32[]{:S(2)}, u32[]{:S(2)}) collective-permute-start(bf16[464,128]{1,0:T(8,128)(2,1)S(1)} %shard_map.317.own_ref), channel_id=1, source_target_pairs={{0,2},{2,0},{1,3},{3,1},{4,6},{6,4},{5,7},{7,5},{8,10},{10,8},{9,1... | collective-permute-start | bytes 356360 | tf_op jit(solution)/shard_map/ppermute | solution.py:920
  29.3 3.2 %collective-permute-start.8 = (bf16[128,128]{1,0:T(8,128)(2,1)S(1)}, bf16[128,128]{1,0:T(8,128)(2,1)S(1)}, u32[]{:S(2)}, u32[]{:S(2)}) collective-permute-start(bf16[128,128]{1,0:T(8,128)(2,1)S(1)} %get-tuple-element.130), channel_id=1, source_target_pairs={{0,1},{1,0},{4,5},{5,4},{8,9},{9,8},{12,13},{13,12},{2,3},{3,2},{6... | collective-permute-start | bytes 98312 | tf_op jit(solution)/shard_map/ppermute | solution.py:683
  29.8 3.6 %collective-permute-start.9 = (bf16[128,128]{1,0:T(8,128)(2,1)S(1)}, bf16[128,128]{1,0:T(8,128)(2,1)S(1)}, u32[]{:S(2)}, u32[]{:S(2)}) collective-permute-start(bf16[128,128]{1,0:T(8,128)(2,1)S(1)} %get-tuple-element.131.unused_ref), channel_id=1, source_target_pairs={{1,4},{4,1},{5,8},{8,5},{9,12},{12,9},{0,2},{13,15},{3,6},{6,3},{7... | collective-permute-start | bytes 98312 | tf_op jit(solution)/shard_map/ppermute | solution.py:684
  33.5 8.5 %collective-permute-start.10 = (bf16[464,128]{1,0:T(8,128)(2,1)S(1)}, bf16[464,128]{1,0:T(8,128)(2,1)S(1)}, u32[]{:S(2)}, u32[]{:S(2)}) collective-permute-start(bf16[464,128]{1,0:T(8,128)(2,1)S(1)} %get-tuple-element.138.own_ref), channel_id=1, source_target_pairs={{0,8},{4,12},{8,0},{12,4},{1,9},{5,13},{9,1},{13,5},{2,10},{6,14},... | collective-permute-start | bytes 356360 | tf_op jit(solution)/shard_map/ppermute | solution.py:920
  42.0 4.2 %collective-permute-start.11 = (bf16[464,128]{1,0:T(8,128)(2,1)S(1)}, bf16[464,128]{1,0:T(8,128)(2,1)S(1)}, u32[]{:S(2)}, u32[]{:S(2)}) collective-permute-start(bf16[464,128]{1,0:T(8,128)(2,1)S(1)} %get-tuple-element.141.own_ref), channel_id=1, source_target_pairs={{0,4},{4,0},{8,12},{12,8},{1,5},{5,1},{9,13},{13,9},{2,6},{6,2},{1... | collective-permute-start | bytes 356360 | tf_op jit(solution)/shard_map/ppermute | solution.py:920
  46.2 2.6 %collective-permute-start.12 = (bf16[464,128]{1,0:T(8,128)(2,1)S(1)}, bf16[464,128]{1,0:T(8,128)(2,1)S(1)}, u32[]{:S(2)}, u32[]{:S(2)}) collective-permute-start(bf16[464,128]{1,0:T(8,128)(2,1)S(1)} %shard_map.325.own_ref), channel_id=1, source_target_pairs={{0,1},{1,0},{2,3},{3,2},{4,5},{5,4},{6,7},{7,6},{8,9},{9,8},{10,11... | collective-permute-start | bytes 356360 | tf_op jit(solution)/shard_map/ppermute | solution.py:966

commit v13 on v12

--- a/solution.py
+++ b/solution.py
@@ -348,10 +348,15 @@
         rcv = rcv_column[rows, :]
         message = message_ref[rows, :].astype(f32)
         total[...] += spread(ids_ref, first, edge_tile // lane, half, rcv, message)
+
+    def receivers(i):
+        rows = pl.ds(pl.multiple_of(i * edge_tile, edge_tile), edge_tile)
+        rcv = rcv_column[rows, :]
         slots = (nodes, nodes + 2 * rim)
         turned_ref[:, rows] = pick(rcv, rcv_low[rows, :], half, table[...], slots).astype(bf16).T
 
     each_tile(rcv_column.shape[0], tile)
+    each_tile(rcv_column.shape[0], receivers)
     agg_ref[:half, :] = total[:, :lane]
     agg_ref[half:, :] = total[:, lane:]
 
@@ -501,6 +506,8 @@
     grads_ref,
     table,
     sums,
+    upstream_ref,
+    dz2_ref,
 ):
     rim = dagg_near_ref.shape[0]
     parity = parity_of_place()
@@ -508,29 +515,35 @@
     gain = vector(vectors_ref, 2)
     table[pl.ds(pl.multiple_of((1 - parity) * rim, rim), rim), :] = dagg_near_ref[...]
     table[pl.ds(pl.multiple_of(parity * rim, rim), rim), :] = dagg_far_ref[...]
-    grads_ref[: 4 * lane, :] = jnp.zeros((4 * lane, lane), f32)
     sums[...] = jnp.zeros_like(sums)
 
     def tile(i):
         rows = pl.ds(pl.multiple_of(i * edge_tile, edge_tile), edge_tile)
         hot = hot_columns(rcv_low[rows, :], (nodes, nodes + 2 * rim))
-        upstream = up_ref[rows, :] + dot(hot, table[...])
+        upstream_ref[rows, :] = up_ref[rows, :] + dot(hot, table[...])
+
+    def chain_of(i):
+        rows = pl.ds(pl.multiple_of(i * edge_tile, edge_tile), edge_tile)
+        upstream = upstream_ref[rows, :]
         normed = normed_ref[rows, :]
         dz2 = back_norm(upstream, normed, scale_ref[rows, :], gain, means[...])
         dz2b = dz2.astype(bf16)
         dz1 = dot(dz2b, w2_turned) * slope_ref[rows, :]
         dz1b = dz1.astype(bf16)
         dz_ref[rows, :] = dz1b
-        grads_ref[:lane, :] += dot(turned[:lane, rows], dz1b)
-        grads_ref[lane : 2 * lane, :] += dot(sent_turned[:, rows], dz1b)
-        grads_ref[2 * lane : 3 * lane, :] += dot(received_turned[:, rows], dz1b)
-        grads_ref[3 * lane : 4 * lane, :] += dot(turned[lane:, rows], dz2b)
+        dz2_ref[rows, :] = dz2b
         sums[0:8, :] += eight_sums(dz1)
         sums[8:16, :] += eight_sums(dz2)
         sums[16:24, :] += eight_sums(upstream * normed)
         sums[24:32, :] += eight_sums(upstream)
 
     each_tile(up_ref.shape[0], tile)
+    each_tile(up_ref.shape[0], chain_of)
+    dz1_all = dz_ref[...]
+    grads_ref[:lane, :] = dot(turned[:lane, :], dz1_all)
+    grads_ref[lane : 2 * lane, :] = dot(sent_turned[...], dz1_all)
+    grads_ref[2 * lane : 3 * lane, :] = dot(received_turned[...], dz1_all)
+    grads_ref[3 * lane : 4 * lane, :] = dot(turned[lane:, :], dz2_ref[...])
     kept = kept_ref.shape[0]
     node_rows = node_grads_ref.shape[0] - sum_rows
     last = 4 * lane + node_rows
@@ -876,6 +889,8 @@
             ((2 * kept, lane), f32),
             ((2 * rim, lane), bf16),
             ((32, lane), f32),
+            wide_shape,
+            edge_shape,
         ],
         dagg_near,
         dagg_far,
@@ -903,25 +918,25 @@
         dz,
         turned_weights,
     )
-    back_near, back_far, onward = exchange(rims)
-    snd_sum, rcv_sum = call(
-        scatter_kernel,
-        [node_shape, node_shape],
-        [((snd_half, 2 * lane), f32), ((snd_half, 2 * lane), f32)],
-        ids,
-        dz,
-        snd_column,
-        rcv_column,
-        onward,
-    )
+    back_near, back_far, unused = exchange(rims)
     node_grad = edge_out = edge_grad = None
     early_vectors, early_ids = vectors, ids
     for number, (axis, partners) in enumerate(sum_rounds()):
         other = lax.ppermute(grads, axis, partners)
         passed, before, written = [], [], []
         if number == 0:
-            passed, before = [vectors], [back_near, back_far, snd_sum, rcv_sum]
+            passed, before = [vectors], [back_near, back_far]
         elif number == 1:
+            snd_sum, rcv_sum = call(
+                scatter_kernel,
+                [node_shape, node_shape],
+                [((snd_half, 2 * lane), f32), ((snd_half, 2 * lane), f32)],
+                ids,
+                dz,
+                snd_column,
+                rcv_column,
+                early_vectors,
+            )
             edge_out, edge_grad = call(
                 edge_outputs_kernel,
                 [edge_shape, edge_shape],
@@ -933,7 +948,7 @@
                 early_vectors,
                 turned_weights,
             )
-            passed, written = [ids], [edge_out, edge_grad]
+            passed, before, written = [ids], [snd_sum, rcv_sum], [edge_out, edge_grad]
         elif number == 2:
             (node_grad,) = call(
                 node_grad_kernel,

time: 50.2 us -> 49.8 us (level)
    ppermute x3, waiting for transfers between devices: 8.92 us -> 6.87 us  [on_device(): other = lax.ppermute(grads, axis, partners)]
    ppermute x4, waiting for transfers between devices: 0.87 us -> 2.75 us  [exchange(): return (near, lax.ppermute(far, ('dom', 'sample', 'sub'), outer), far)]
  transfers between devices with their start and end apart: 13 -> 13, of which waited for: 5 -> 6; matrix products, arithmetic and copies ran while one was open for 0% -> 0% of each run, Pallas kernels for 27% -> 27%
where the time goes in v13:
time: 49.8 us; the launch traced here: 49.3 us
  Pallas kernels  24.7 us (50%)
  starting transfers between devices  11.9 us (24%)
  waiting for transfers between devices  11.8 us (24%)
  between operations  0.96 us (2%)
    pallas_call x21, Pallas kernels, call(): pl.pallas_call(kernel, out_shape=[jax.ShapeDtypeStruct(shape, dtype) for...  24.7 us
    ppermute x3, waiting for transfers between devices, on_device(): other = lax.ppermute(grads, axis, partners)  6.87 us
    ppermute x4, starting transfers between devices, exchange(): return (near, lax.ppermute(far, ('dom', 'sample', 'sub'), outer), far)  6.08 us
    ppermute x4, waiting for transfers between devices, exchange(): return (near, lax.ppermute(far, ('dom', 'sample', 'sub'), outer), far)  2.75 us
    ppermute x3, starting transfers between devices, on_device(): other = lax.ppermute(grads, axis, partners)  2.34 us
    ppermute x1, starting transfers between devices, on_device(): others = lax.ppermute(grads, 'sub', core_pairs)  1.62 us
    ppermute x4, starting transfers between devices, exchange(): near = lax.ppermute(near, chain, inner)  1.46 us
    ppermute x1, waiting for transfers between devices, on_device(): other = lax.ppermute(grads_sent, 'sub', core_pairs)  1 us
  transfers between devices with their start and end apart: 13, of which 6 were waited for; matrix products, arithmetic and copies ran while one was open for 0% of the time, Pallas kernels for 27%

profile of v13, /device:TPU:1, one launch (start us, length us, event | category | flops | bytes accessed | tf_op | source)
XLA Modules:
  0.0 49.3 jit_solution(9119476743592270377)
XLA Ops:
  0.7 1.6 %shard_map.306 = (bf16[1024,128]{1,0:T(8,128)(2,1)S(1)}, bf16[256,128]{1,0:T(8,128)(2,1)S(1)}, s32[50,128]{1,0:T(8,128)S(1)}, bf16[3072,128]{1,0:T(8,128)(2,1)S(...) custom-call(bf16[1024,128]{1,0:T(8,128)(2,1)} %bitcast.33, s32[2,128]{1,0:T(2,128)} %bitcast.36, ...), custom_call_target="tpu_custom_call" | custom-call | bytes 1307648 | tf_op jit(solution)/shard_map/pallas_call | solution.py:672
  2.4 2.7 %collective-permute-start.1 = (bf16[128,128]{1,0:T(8,128)(2,1)S(1)}, bf16[128,128]{1,0:T(8,128)(2,1)S(1)}, u32[]{:S(2)}, u32[]{:S(2)}) collective-permute-start(bf16[128,128]{1,0:T(8,128)(2,1)S(1)} %get-tuple-element.87.unused_ref), channel_id=1, source_target_pairs={{1,4},{4,1},{5,8},{8,5},{9,12},{12,9},{0,2},{13,15},{3,6},{6,3},{7... | collective-permute-start | bytes 98312 | tf_op jit(solution)/shard_map/ppermute | solution.py:697
  5.1 3.1 %shard_map.308 = (bf16[3072,128]{1,0:T(8,128)(2,1)S(1)}, bf16[1024,128]{1,0:T(8,128)(2,1)S(1)}, s32[3072,128]{1,0:T(8,128)S(1)}, s32[3072,128]{1,0:T(8,128)S(1)}...) custom-call(s32[50,128]{1,0:T(8,128)S(1)} %get-tuple-element.88.ids_, ...), custom_call_target="tpu_custom_call" | custom-call | bytes 2388992 | tf_op jit(solution)/shard_map/pallas_call | solution.py:672
  8.2 3.9 %shard_map.309 = (f32[3072,128]{1,0:T(8,128)S(1)}, f32[3072,128]{1,0:T(8,128)S(1)}, f32[3072,128]{1,0:T(8,128)S(1)}, bf16[3072,128]{1,0:T(8,128)(2,1)S(1)}, bf16[256,128]{1,0:T(8,128)(2,1)S(1)}) custom-call(bf16[128,128]{1,0:T(8,128)(2,1)S(1)} %collective-permute-done.near_ref, bf16[128,128]{1,0:T(8,128)(2,1)S(1)} %collective-permute-done.1.far_ref, ...), custom_call_target="tpu_custom_call" | custom-call | bytes 4781056 | tf_op jit(solution)/shard_map/pallas_call | solution.py:672
  12.5 1.4 %collective-permute-start.3 = (bf16[128,128]{1,0:T(8,128)(2,1)S(1)}, bf16[128,128]{1,0:T(8,128)(2,1)S(1)}, u32[]{:S(2)}, u32[]{:S(2)}) collective-permute-start(bf16[128,128]{1,0:T(8,128)(2,1)S(1)} %get-tuple-element.101.unused_ref), channel_id=1, source_target_pairs={{1,4},{4,1},{5,8},{8,5},{9,12},{12,9},{0,2},{13,15},{3,6},{6,3},{7... | collective-permute-start | bytes 98312 | tf_op jit(solution)/shard_map/ppermute | solution.py:697
  13.9 2.3 %shard_map.311 = (f32[1024,128]{1,0:T(8,128)S(1)}, bf16[128,3072]{1,0:T(8,128)(2,1)S(1)}) custom-call(s32[50,128]{1,0:T(8,128)S(1)} %get-tuple-element.88.ids_ref.refs_0_, s32[3072,128]{1,0:T(8,128)S(1)} %get-tuple-element.93.rcv_column, s16[3072,128]{1,0:T(8,128)(2,1)S(1)} %get-tuple-element.94.rcv_low, ...), custom_call_target="tpu_custom_call" | custom-call | bytes 3531776 | tf_op jit(solution)/shard_map/pallas_call | solution.py:672
  16.3 1.6 %shard_map.312 = (bf16[1024,256]{1,0:T(8,128)(2,1)S(1)}, bf16[1024,128]{1,0:T(8,128)(2,1)S(1)}, f32[1024,128]{1,0:T(8,128)S(1)}, bf16[1024,128]{1,0:T(8,128)(2,1...) custom-call(bf16[128,128]{1,0:T(8,128)(2,1)S(1)} %collective-permute, ...), custom_call_target="tpu_custom_call" | custom-call | bytes 1864704 | tf_op jit(solution)/shard_map/pallas_call | solution.py:672
  18.3 1.3 %collective-permute-start.5 = (bf16[128,128]{1,0:T(8,128)(2,1)S(1)}, bf16[128,128]{1,0:T(8,128)(2,1)S(1)}, u32[]{:S(2)}, u32[]{:S(2)}) collective-permute-start(bf16[128,128]{1,0:T(8,128)(2,1)S(1)} %get-tuple-element.113.unused_ref), channel_id=1, source_target_pairs={{1,4},{4,1},{5,8},{8,5},{9,12},{12,9},{0,2},{13,15},{3,6},{6,3},{7... | collective-permute-start | bytes 98312 | tf_op jit(solution)/shard_map/ppermute | solution.py:697
  19.6 1.6 %shard_map.315 = (f32[3072,128]{1,0:T(8,128)S(1)}, f32[3072,128]{1,0:T(8,128)S(1)}, bf16[256,3072]{1,0:T(8,128)(2,1)S(1)}) custom-call(s32[3072,128]{1,0:T(8,128)S(1)} %get-tuple-element.93.rcv_column, s16[3072,128]{1,0:T(8,128)(2,1)S(1)} %get-tuple-element.94.rcv_low, bf16[1024,128]{1,0:T(8,128)(2,1)S(1)} %get-tuple-element.116.dagg_ref, ...), custom_call_target="tpu_custom_call" | custom-call | bytes 5799936 | tf_op jit(solution)/shard_map/pallas_call | solution.py:672
  21.2 1.0 %shard_map.314 = (bf16[1024,128]{1,0:T(8,128)(2,1)}, f32[1024,128]{1,0:T(8,128)S(1)}, f32[400,128]{1,0:T(8,128)S(1)}) custom-call(bf16[1024,256]{1,0:T(8,128)(2,1)S(1)} %get-tuple-element.106.x_ref, bf16[1024,128]{1,0:T(8,128)(2,1)S(1)} %get-tuple-element.107.act_ref, f32[1024,128]{1,0:T(8,128)S(1)} %get-tuple-element.108.normed_ref, ...), custom_call_target="tpu_custom_call" | custom-call | bytes 2371584 | tf_op jit(solution)/shard_map/pallas_call | solution.py:672
  22.2 3.2 %shard_map.316 = (bf16[3072,128]{1,0:T(8,128)(2,1)S(1)}, f32[464,128]{1,0:T(8,128)S(1)}, bf16[464,128]{1,0:T(8,128)(2,1)S(1)}) custom-call(bf16[128,128]{1,0:T(8,128)(2,1)S(1)} %collective-permute-done.4.dagg_near_ref, bf16[128,128]{1,0:T(8,128)(2,1)S(1)} %collective-permute-done.5.dagg_far_ref, f32[3072,128]{1,0:T(8,128)S(1)} %get-tuple-element.119.up_ref, ...), custom_call_target="tpu_custom_call" | custom-call | bytes 10858496 | tf_op jit(solution)/shard_map/pallas_call | solution.py:672
  25.8 1.0 %collective-permute-done.6.other_ref = bf16[464,128]{1,0:T(8,128)(2,1)S(1)} collective-permute-done((bf16[464,128]{1,0:T(8,128)(2,1)S(1)}, bf16[464,128]{1,0:T(8,128)(2,1)S(1)}, u32[]{:S(2)}, u32[]{:S(2)}) %collective-permute-start.6) | collective-permute-done | bytes 118816 | tf_op jit(solution)/shard_map/ppermute | solution.py:911
  26.8 1.3 %collective-permute-start.7 = (bf16[464,128]{1,0:T(8,128)(2,1)S(1)}, bf16[464,128]{1,0:T(8,128)(2,1)S(1)}, u32[]{:S(2)}, u32[]{:S(2)}) collective-permute-start(bf16[464,128]{1,0:T(8,128)(2,1)S(1)} %shard_map.317.own_ref), channel_id=1, source_target_pairs={{0,2},{2,0},{1,3},{3,1},{4,6},{6,4},{5,7},{7,5},{8,10},{10,8},{9,1... | collective-permute-start | bytes 356360 | tf_op jit(solution)/shard_map/ppermute | solution.py:925
  28.1 0.7 %shard_map.318.message_ref = bf16[256,128]{1,0:T(8,128)(2,1)S(1)} custom-call(s32[50,128]{1,0:T(8,128)S(1)} %get-tuple-element.88.ids_ref.refs_0_, bf16[3072,128]{1,0:T(8,128)(2,1)S(1)} %get-tuple-element.127.dz_ref, bf16[896,128]{1,0:T(8,128)(2,1)S(1)} %get-tuple-element.105.turned_weights), custom_call_target="tpu_custom_call" | custom-call | bytes 1041408 | tf_op jit(solution)/shard_map/pallas_call | solution.py:672
  30.2 2.7 %collective-permute-done.9.refs_2_.far_ref = bf16[128,128]{1,0:T(8,128)(2,1)S(1)} collective-permute-done((bf16[128,128]{1,0:T(8,128)(2,1)S(1)}, bf16[128,128]{1,0:T(8,128)(2,1)S(1)}, u32[]{:S(2)}, u32[]{:S(2)}) %collective-permute-start.9) | collective-permute-done | bytes 32800 | tf_op jit(solution)/shard_map/ppermute | solution.py:697
  33.0 1.0 %collective-permute-start.10 = (bf16[464,128]{1,0:T(8,128)(2,1)S(1)}, bf16[464,128]{1,0:T(8,128)(2,1)S(1)}, u32[]{:S(2)}, u32[]{:S(2)}) collective-permute-start(bf16[464,128]{1,0:T(8,128)(2,1)S(1)} %get-tuple-element.138.own_ref), channel_id=1, source_target_pairs={{0,8},{4,12},{8,0},{12,4},{1,9},{5,13},{9,1},{13,5},{2,10},{6,14},... | collective-permute-start | bytes 356360 | tf_op jit(solution)/shard_map/ppermute | solution.py:925
  34.0 1.5 %shard_map.321 = (bf16[3072,128]{1,0:T(8,128)(2,1)}, bf16[3072,128]{1,0:T(8,128)(2,1)}) custom-call(bf16[3072,128]{1,0:T(8,128)(2,1)S(1)} %get-tuple-element.127.dz_ref, bf16[3072,128]{1,0:T(8,128)(2,1)S(1)} %get-tuple-element.117.cot_ref, bf16[3072,128]{1,0:T(8,128)(2,1)S(1)} %get-tuple-element.92.edge_ref, f32[3072,128]{1,0:T(8,128)S(1)} %get-tuple-element.120.normed_ref, ...), custom_call_target="tpu_custom_call" | custom-call | bytes 4165632 | tf_op jit(solution)/shard_map/pallas_call | solution.py:672
  35.5 2.0 %shard_map.322 = (bf16[1024,128]{1,0:T(8,128)(2,1)S(1)}, bf16[1024,128]{1,0:T(8,128)(2,1)S(1)}) custom-call(s32[50,128]{1,0:T(8,128)S(1)} %get-tuple-element.88.ids_ref.refs_0_, bf16[3072,128]{1,0:T(8,128)(2,1)S(1)} %get-tuple-element.127.dz_ref, s32[3072,128]{1,0:T(8,128)S(1)} %get-tuple-element.135.snd_column, ...), custom_call_target="tpu_custom_call" | custom-call | bytes 3961856 | tf_op jit(solution)/shard_map/pallas_call | solution.py:672
  37.6 3.9 %collective-permute-done.10.other_ref = bf16[464,128]{1,0:T(8,128)(2,1)S(1)} collective-permute-done((bf16[464,128]{1,0:T(8,128)(2,1)S(1)}, bf16[464,128]{1,0:T(8,128)(2,1)S(1)}, u32[]{:S(2)}, u32[]{:S(2)}) %collective-permute-start.10) | collective-permute-done | bytes 118816 | tf_op jit(solution)/shard_map/ppermute | solution.py:925
  41.6 1.1 %shard_map.324.refs_0_ = bf16[1024,128]{1,0:T(8,128)(2,1)} custom-call(bf16[128,128]{1,0:T(8,128)(2,1)S(1)} %collective-permute-done.8.refs_1_.near_ref, bf16[128,128]{1,0:T(8,128)(2,1)S(1)} %collective-permute-done.9.refs_2_.far_ref, f32[1024,128]{1,0:T(8,128)S(1)} %get-tuple-element.134.base_ref, ...), custom_call_target="tpu_custom_call" | custom-call | bytes 1369088 | tf_op jit(solution)/shard_map/pallas_call | solution.py:672
  42.7 3.0 %collective-permute-done.11.other_ref = bf16[464,128]{1,0:T(8,128)(2,1)S(1)} collective-permute-done((bf16[464,128]{1,0:T(8,128)(2,1)S(1)}, bf16[464,128]{1,0:T(8,128)(2,1)S(1)}, u32[]{:S(2)}, u32[]{:S(2)}) %collective-permute-start.11) | collective-permute-done | bytes 118816 | tf_op jit(solution)/shard_map/ppermute | solution.py:925
  45.7 1.6 %collective-permute-start.12 = (bf16[464,128]{1,0:T(8,128)(2,1)S(1)}, bf16[464,128]{1,0:T(8,128)(2,1)S(1)}, u32[]{:S(2)}, u32[]{:S(2)}) collective-permute-start(bf16[464,128]{1,0:T(8,128)(2,1)S(1)} %shard_map.325.own_ref), channel_id=1, source_target_pairs={{0,1},{1,0},{2,3},{3,2},{4,5},{5,4},{6,7},{7,6},{8,9},{9,8},{10,11... | collective-permute-start | bytes 356360 | tf_op jit(solution)/shard_map/ppermute | solution.py:981
  47.3 1.0 %collective-permute-done.12.other_ref = bf16[464,128]{1,0:T(8,128)(2,1)S(1)} collective-permute-done((bf16[464,128]{1,0:T(8,128)(2,1)S(1)}, bf16[464,128]{1,0:T(8,128)(2,1)S(1)}, u32[]{:S(2)}, u32[]{:S(2)}) %collective-permute-start.12) | collective-permute-done | bytes 118816 | tf_op jit(solution)/shard_map/ppermute | solution.py:981
  48.3 0.8 %shard_map.326 = (f32[384,128]{1,0:T(8,128)}, f32[128,128]{1,0:T(8,128)}, f32[256,128]{1,0:T(8,128)}, f32[128,128]{1,0:T(8,128)}, f32[1,128]{1,0:T(1,128)}, /*in...) custom-call(bf16[464,128]{1,0:T(8,128)(2,1)S(1)} %shard_map.325.own_, ...), custom_call_target="tpu_custom_call" | custom-call | bytes 237568 | tf_op jit(solution)/shard_map/pallas_call | solution.py:672
  (23 shorter events, 3.0 us)
Async XLA Ops:
  2.3 6.0 %collective-permute-start = (bf16[128,128]{1,0:T(8,128)(2,1)S(1)}, bf16[128,128]{1,0:T(8,128)(2,1)S(1)}, u32[]{:S(2)}, u32[]{:S(2)}) collective-permute-start(bf16[128,128]{1,0:T(8,128)(2,1)S(1)} %get-tuple-element.86), channel_id=1, source_target_pairs={{0,1},{1,0},{4,5},{5,4},{8,9},{9,8},{12,13},{13,12},{2,3},{3,2},{6... | collective-permute-start | bytes 98312 | tf_op jit(solution)/shard_map/ppermute | solution.py:696
  2.4 5.8 %collective-permute-start.1 = (bf16[128,128]{1,0:T(8,128)(2,1)S(1)}, bf16[128,128]{1,0:T(8,128)(2,1)S(1)}, u32[]{:S(2)}, u32[]{:S(2)}) collective-permute-start(bf16[128,128]{1,0:T(8,128)(2,1)S(1)} %get-tuple-element.87.unused_ref), channel_id=1, source_target_pairs={{1,4},{4,1},{5,8},{8,5},{9,12},{12,9},{0,2},{13,15},{3,6},{6,3},{7... | collective-permute-start | bytes 98312 | tf_op jit(solution)/shard_map/ppermute | solution.py:697
  12.2 4.1 %collective-permute-start.2 = (bf16[128,128]{1,0:T(8,128)(2,1)S(1)}, bf16[128,128]{1,0:T(8,128)(2,1)S(1)}, u32[]{:S(2)}, u32[]{:S(2)}) collective-permute-start(bf16[128,128]{1,0:T(8,128)(2,1)S(1)} %get-tuple-element.100), channel_id=1, source_target_pairs={{0,1},{1,0},{4,5},{5,4},{8,9},{9,8},{12,13},{13,12},{2,3},{3,2},{6... | collective-permute-start | bytes 98312 | tf_op jit(solution)/shard_map/ppermute | solution.py:696
  12.5 3.7 %collective-permute-start.3 = (bf16[128,128]{1,0:T(8,128)(2,1)S(1)}, bf16[128,128]{1,0:T(8,128)(2,1)S(1)}, u32[]{:S(2)}, u32[]{:S(2)}) collective-permute-start(bf16[128,128]{1,0:T(8,128)(2,1)S(1)} %get-tuple-element.101.unused_ref), channel_id=1, source_target_pairs={{1,4},{4,1},{5,8},{8,5},{9,12},{12,9},{0,2},{13,15},{3,6},{6,3},{7... | collective-permute-start | bytes 98312 | tf_op jit(solution)/shard_map/ppermute | solution.py:697
  17.9 4.3 %collective-permute-start.4 = (bf16[128,128]{1,0:T(8,128)(2,1)S(1)}, bf16[128,128]{1,0:T(8,128)(2,1)S(1)}, u32[]{:S(2)}, u32[]{:S(2)}) collective-permute-start(bf16[128,128]{1,0:T(8,128)(2,1)S(1)} %get-tuple-element.115), channel_id=1, source_target_pairs={{0,1},{1,0},{4,5},{5,4},{8,9},{9,8},{12,13},{13,12},{2,3},{3,2},{6... | collective-permute-start | bytes 98312 | tf_op jit(solution)/shard_map/ppermute | solution.py:696
  18.3 3.9 %collective-permute-start.5 = (bf16[128,128]{1,0:T(8,128)(2,1)S(1)}, bf16[128,128]{1,0:T(8,128)(2,1)S(1)}, u32[]{:S(2)}, u32[]{:S(2)}) collective-permute-start(bf16[128,128]{1,0:T(8,128)(2,1)S(1)} %get-tuple-element.113.unused_ref), channel_id=1, source_target_pairs={{1,4},{4,1},{5,8},{8,5},{9,12},{12,9},{0,2},{13,15},{3,6},{6,3},{7... | collective-permute-start | bytes 98312 | tf_op jit(solution)/shard_map/ppermute | solution.py:697
  25.4 1.4 %collective-permute-start.6 = (bf16[464,128]{1,0:T(8,128)(2,1)S(1)}, bf16[464,128]{1,0:T(8,128)(2,1)S(1)}, u32[]{:S(2)}, u32[]{:S(2)}) collective-permute-start(bf16[464,128]{1,0:T(8,128)(2,1)S(1)} %get-tuple-element.129), channel_id=1, source_target_pairs={{0,1},{1,0},{2,3},{3,2},{4,5},{5,4},{6,7},{7,6},{8,9},{9,8},{10,11... | collective-permute-start | bytes 356360 | tf_op jit(solution)/shard_map/ppermute | solution.py:911
  26.8 6.1 %collective-permute-start.7 = (bf16[464,128]{1,0:T(8,128)(2,1)S(1)}, bf16[464,128]{1,0:T(8,128)(2,1)S(1)}, u32[]{:S(2)}, u32[]{:S(2)}) collective-permute-start(bf16[464,128]{1,0:T(8,128)(2,1)S(1)} %shard_map.317.own_ref), channel_id=1, source_target_pairs={{0,2},{2,0},{1,3},{3,1},{4,6},{6,4},{5,7},{7,5},{8,10},{10,8},{9,1... | collective-permute-start | bytes 356360 | tf_op jit(solution)/shard_map/ppermute | solution.py:925
  28.8 1.4 %collective-permute-start.8 = (bf16[128,128]{1,0:T(8,128)(2,1)S(1)}, bf16[128,128]{1,0:T(8,128)(2,1)S(1)}, u32[]{:S(2)}, u32[]{:S(2)}) collective-permute-start(bf16[128,128]{1,0:T(8,128)(2,1)S(1)} %get-tuple-element.130), channel_id=1, source_target_pairs={{0,1},{1,0},{4,5},{5,4},{8,9},{9,8},{12,13},{13,12},{2,3},{3,2},{6... | collective-permute-start | bytes 98312 | tf_op jit(solution)/shard_map/ppermute | solution.py:696
  29.4 3.6 %collective-permute-start.9 = (bf16[128,128]{1,0:T(8,128)(2,1)S(1)}, bf16[128,128]{1,0:T(8,128)(2,1)S(1)}, u32[]{:S(2)}, u32[]{:S(2)}) collective-permute-start(bf16[128,128]{1,0:T(8,128)(2,1)S(1)} %get-tuple-element.131), channel_id=1, source_target_pairs={{1,4},{4,1},{5,8},{8,5},{9,12},{12,9},{0,2},{13,15},{3,6},{6,3},{7... | collective-permute-start | bytes 98312 | tf_op jit(solution)/shard_map/ppermute | solution.py:697
  33.0 8.5 %collective-permute-start.10 = (bf16[464,128]{1,0:T(8,128)(2,1)S(1)}, bf16[464,128]{1,0:T(8,128)(2,1)S(1)}, u32[]{:S(2)}, u32[]{:S(2)}) collective-permute-start(bf16[464,128]{1,0:T(8,128)(2,1)S(1)} %get-tuple-element.138.own_ref), channel_id=1, source_target_pairs={{0,8},{4,12},{8,0},{12,4},{1,9},{5,13},{9,1},{13,5},{2,10},{6,14},... | collective-permute-start | bytes 356360 | tf_op jit(solution)/shard_map/ppermute | solution.py:925
  41.5 4.2 %collective-permute-start.11 = (bf16[464,128]{1,0:T(8,128)(2,1)S(1)}, bf16[464,128]{1,0:T(8,128)(2,1)S(1)}, u32[]{:S(2)}, u32[]{:S(2)}) collective-permute-start(bf16[464,128]{1,0:T(8,128)(2,1)S(1)} %get-tuple-element.141.own_ref), channel_id=1, source_target_pairs={{0,4},{4,0},{8,12},{12,8},{1,5},{5,1},{9,13},{13,9},{2,6},{6,2},{1... | collective-permute-start | bytes 356360 | tf_op jit(solution)/shard_map/ppermute | solution.py:925
  45.7 2.6 %collective-permute-start.12 = (bf16[464,128]{1,0:T(8,128)(2,1)S(1)}, bf16[464,128]{1,0:T(8,128)(2,1)S(1)}, u32[]{:S(2)}, u32[]{:S(2)}) collective-permute-start(bf16[464,128]{1,0:T(8,128)(2,1)S(1)} %shard_map.325.own_ref), channel_id=1, source_target_pairs={{0,1},{1,0},{2,3},{3,2},{4,5},{5,4},{6,7},{7,6},{8,9},{9,8},{10,11... | collective-permute-start | bytes 356360 | tf_op jit(solution)/shard_map/ppermute | solution.py:981

commit v14 on v13

--- a/solution.py
+++ b/solution.py
@@ -211,6 +211,7 @@
     turned_weights,
     snd_low,
     snd_table,
+    sent_rows,
     sems,
 ):
     copies = started([(edge_cot_hbm, edge_cot_ref), (node_cot_hbm, node_cot_ref)], sems)
@@ -239,12 +240,17 @@
 
     def tile(i):
         rows = pl.ds(pl.multiple_of(i * edge_tile, edge_tile), edge_tile)
-        x = edge_ref[rows, :]
-        sent = pick(snd_column[rows, :], snd_low[rows, :], half, snd_table[...]).astype(bf16)
-        z_ref[rows, :] = dot(jnp.concatenate([x, sent], axis=1), w1) + b1
+        sent = pick(snd_column[rows, :], snd_low[rows, :], half, snd_table[...])
+        sent_rows[rows, :] = sent.astype(bf16)
+
+    def rest(i):
+        rows = pl.ds(pl.multiple_of(i * edge_tile, edge_tile), edge_tile)
+        sent = sent_rows[rows, :]
+        z_ref[rows, :] = dot(jnp.concatenate([edge_ref[rows, :], sent], axis=1), w1) + b1
         turned_ref[:, rows] = sent.T
 
     each_tile(edge_ref.shape[0], tile)
+    each_tile(edge_ref.shape[0], rest)
     for copy in copies:
         copy.wait()
 
@@ -475,6 +481,9 @@
         rows = pl.ds(pl.multiple_of(i * edge_tile, edge_tile), edge_tile)
         local = pick(rcv_column[rows, :], rcv_low[rows, :], half, table[...])
         up_ref[rows, :] = cot_ref[rows, :].astype(f32) + local
+
+    def rest(i):
+        rows = pl.ds(pl.multiple_of(i * edge_tile, edge_tile), edge_tile)
         z = z_ref[rows, :]
         sig = sigmoid(z)
         slope_ref[rows, :] = sig * (1.0 + z * (1.0 - sig))
@@ -482,6 +491,7 @@
         turned_ref[lane:, rows] = (z * sig).astype(bf16).T
 
     each_tile(cot_ref.shape[0], tile)
+    each_tile(cot_ref.shape[0], rest)
 
 
 def edge_backward_kernel(
@@ -781,7 +791,7 @@
             ((2 * lane, 2 * lane), bf16),
             ((7 * lane, lane), bf16),
         ],
-        [((edges, lane), jnp.int16), ((snd_half, 2 * lane), bf16)],
+        [((edges, lane), jnp.int16), ((snd_half, 2 * lane), bf16), edge_shape],
         ids,
         node,
         weights,

time: 49.8 us -> 49.8 us (level)
  no operation moved by 1% of the time
where the time goes in v14:
time: 49.8 us; the launch traced here: 49.4 us
  Pallas kernels  24.7 us (50%)
  starting transfers between devices  11.9 us (24%)
  waiting for transfers between devices  11.8 us (24%)
  between operations  0.96 us (2%)
    pallas_call x21, Pallas kernels, call(): pl.pallas_call(kernel, out_shape=[jax.ShapeDtypeStruct(shape, dtype) for...  24.7 us
    ppermute x3, waiting for transfers between devices, on_device(): other = lax.ppermute(grads, axis, partners)  6.87 us
    ppermute x4, starting transfers between devices, exchange(): return (near, lax.ppermute(far, ('dom', 'sample', 'sub'), outer), far)  6.09 us
    ppermute x4, waiting for transfers between devices, exchange(): return (near, lax.ppermute(far, ('dom', 'sample', 'sub'), outer), far)  2.75 us
    ppermute x3, starting transfers between devices, on_device(): other = lax.ppermute(grads, axis, partners)  2.34 us
    ppermute x1, starting transfers between devices, on_device(): others = lax.ppermute(grads, 'sub', core_pairs)  1.62 us
    ppermute x4, starting transfers between devices, exchange(): near = lax.ppermute(near, chain, inner)  1.46 us
    ppermute x1, waiting for transfers between devices, on_device(): other = lax.ppermute(grads_sent, 'sub', core_pairs)  1.02 us
  transfers between devices with their start and end apart: 13, of which 6 were waited for; matrix products, arithmetic and copies ran while one was open for 0% of the time, Pallas kernels for 27%

profile of v14, /device:TPU:1, one launch (start us, length us, event | category | flops | bytes accessed | tf_op | source)
XLA Modules:
  0.0 49.4 jit_solution(17384978370299835573)
XLA Ops:
  0.7 1.6 %shard_map.306 = (bf16[1024,128]{1,0:T(8,128)(2,1)S(1)}, bf16[256,128]{1,0:T(8,128)(2,1)S(1)}, s32[50,128]{1,0:T(8,128)S(1)}, bf16[3072,128]{1,0:T(8,128)(2,1)S(...) custom-call(bf16[1024,128]{1,0:T(8,128)(2,1)} %bitcast.33, s32[2,128]{1,0:T(2,128)} %bitcast.36, ...), custom_call_target="tpu_custom_call" | custom-call | bytes 1307648 | tf_op jit(solution)/shard_map/pallas_call | solution.py:682
  2.4 2.7 %collective-permute-start.1 = (bf16[128,128]{1,0:T(8,128)(2,1)S(1)}, bf16[128,128]{1,0:T(8,128)(2,1)S(1)}, u32[]{:S(2)}, u32[]{:S(2)}) collective-permute-start(bf16[128,128]{1,0:T(8,128)(2,1)S(1)} %get-tuple-element.87.unused_ref), channel_id=1, source_target_pairs={{1,4},{4,1},{5,8},{8,5},{9,12},{12,9},{0,2},{13,15},{3,6},{6,3},{7... | collective-permute-start | bytes 98312 | tf_op jit(solution)/shard_map/ppermute | solution.py:707
  5.1 3.0 %shard_map.308 = (bf16[3072,128]{1,0:T(8,128)(2,1)S(1)}, bf16[1024,128]{1,0:T(8,128)(2,1)S(1)}, s32[3072,128]{1,0:T(8,128)S(1)}, s32[3072,128]{1,0:T(8,128)S(1)}...) custom-call(s32[50,128]{1,0:T(8,128)S(1)} %get-tuple-element.88.ids_, ...), custom_call_target="tpu_custom_call" | custom-call | bytes 2388992 | tf_op jit(solution)/shard_map/pallas_call | solution.py:682
  8.1 3.9 %shard_map.309 = (f32[3072,128]{1,0:T(8,128)S(1)}, f32[3072,128]{1,0:T(8,128)S(1)}, f32[3072,128]{1,0:T(8,128)S(1)}, bf16[3072,128]{1,0:T(8,128)(2,1)S(1)}, bf16[256,128]{1,0:T(8,128)(2,1)S(1)}) custom-call(bf16[128,128]{1,0:T(8,128)(2,1)S(1)} %collective-permute-done.near_ref, bf16[128,128]{1,0:T(8,128)(2,1)S(1)} %collective-permute-done.1.far_ref, ...), custom_call_target="tpu_custom_call" | custom-call | bytes 4781056 | tf_op jit(solution)/shard_map/pallas_call | solution.py:682
  12.4 1.4 %collective-permute-start.3 = (bf16[128,128]{1,0:T(8,128)(2,1)S(1)}, bf16[128,128]{1,0:T(8,128)(2,1)S(1)}, u32[]{:S(2)}, u32[]{:S(2)}) collective-permute-start(bf16[128,128]{1,0:T(8,128)(2,1)S(1)} %get-tuple-element.101.unused_ref), channel_id=1, source_target_pairs={{1,4},{4,1},{5,8},{8,5},{9,12},{12,9},{0,2},{13,15},{3,6},{6,3},{7... | collective-permute-start | bytes 98312 | tf_op jit(solution)/shard_map/ppermute | solution.py:707
  13.8 2.3 %shard_map.311 = (f32[1024,128]{1,0:T(8,128)S(1)}, bf16[128,3072]{1,0:T(8,128)(2,1)S(1)}) custom-call(s32[50,128]{1,0:T(8,128)S(1)} %get-tuple-element.88.ids_ref.refs_0_, s32[3072,128]{1,0:T(8,128)S(1)} %get-tuple-element.93.rcv_column, s16[3072,128]{1,0:T(8,128)(2,1)S(1)} %get-tuple-element.94.rcv_low, ...), custom_call_target="tpu_custom_call" | custom-call | bytes 3531776 | tf_op jit(solution)/shard_map/pallas_call | solution.py:682
  16.2 1.6 %shard_map.312 = (bf16[1024,256]{1,0:T(8,128)(2,1)S(1)}, bf16[1024,128]{1,0:T(8,128)(2,1)S(1)}, f32[1024,128]{1,0:T(8,128)S(1)}, bf16[1024,128]{1,0:T(8,128)(2,1...) custom-call(bf16[128,128]{1,0:T(8,128)(2,1)S(1)} %collective-permute, ...), custom_call_target="tpu_custom_call" | custom-call | bytes 1864704 | tf_op jit(solution)/shard_map/pallas_call | solution.py:682
  18.2 1.3 %collective-permute-start.5 = (bf16[128,128]{1,0:T(8,128)(2,1)S(1)}, bf16[128,128]{1,0:T(8,128)(2,1)S(1)}, u32[]{:S(2)}, u32[]{:S(2)}) collective-permute-start(bf16[128,128]{1,0:T(8,128)(2,1)S(1)} %get-tuple-element.113.unused_ref), channel_id=1, source_target_pairs={{1,4},{4,1},{5,8},{8,5},{9,12},{12,9},{0,2},{13,15},{3,6},{6,3},{7... | collective-permute-start | bytes 98312 | tf_op jit(solution)/shard_map/ppermute | solution.py:707
  19.5 1.6 %shard_map.315 = (f32[3072,128]{1,0:T(8,128)S(1)}, f32[3072,128]{1,0:T(8,128)S(1)}, bf16[256,3072]{1,0:T(8,128)(2,1)S(1)}) custom-call(s32[3072,128]{1,0:T(8,128)S(1)} %get-tuple-element.93.rcv_column, s16[3072,128]{1,0:T(8,128)(2,1)S(1)} %get-tuple-element.94.rcv_low, bf16[1024,128]{1,0:T(8,128)(2,1)S(1)} %get-tuple-element.116.dagg_ref, ...), custom_call_target="tpu_custom_call" | custom-call | bytes 5799936 | tf_op jit(solution)/shard_map/pallas_call | solution.py:682
  21.1 1.0 %shard_map.314 = (bf16[1024,128]{1,0:T(8,128)(2,1)}, f32[1024,128]{1,0:T(8,128)S(1)}, f32[400,128]{1,0:T(8,128)S(1)}) custom-call(bf16[1024,256]{1,0:T(8,128)(2,1)S(1)} %get-tuple-element.106.x_ref, bf16[1024,128]{1,0:T(8,128)(2,1)S(1)} %get-tuple-element.107.act_ref, f32[1024,128]{1,0:T(8,128)S(1)} %get-tuple-element.108.normed_ref, ...), custom_call_target="tpu_custom_call" | custom-call | bytes 2371584 | tf_op jit(solution)/shard_map/pallas_call | solution.py:682
  22.1 3.4 %shard_map.316 = (bf16[3072,128]{1,0:T(8,128)(2,1)S(1)}, f32[464,128]{1,0:T(8,128)S(1)}, bf16[464,128]{1,0:T(8,128)(2,1)S(1)}) custom-call(bf16[128,128]{1,0:T(8,128)(2,1)S(1)} %collective-permute-done.4.dagg_near_ref, bf16[128,128]{1,0:T(8,128)(2,1)S(1)} %collective-permute-done.5.dagg_far_ref, f32[3072,128]{1,0:T(8,128)S(1)} %get-tuple-element.119.up_ref, ...), custom_call_target="tpu_custom_call" | custom-call | bytes 10858496 | tf_op jit(solution)/shard_map/pallas_call | solution.py:682
  25.9 1.0 %collective-permute-done.6.other_ref = bf16[464,128]{1,0:T(8,128)(2,1)S(1)} collective-permute-done((bf16[464,128]{1,0:T(8,128)(2,1)S(1)}, bf16[464,128]{1,0:T(8,128)(2,1)S(1)}, u32[]{:S(2)}, u32[]{:S(2)}) %collective-permute-start.6) | collective-permute-done | bytes 118816 | tf_op jit(solution)/shard_map/ppermute | solution.py:921
  26.9 1.3 %collective-permute-start.7 = (bf16[464,128]{1,0:T(8,128)(2,1)S(1)}, bf16[464,128]{1,0:T(8,128)(2,1)S(1)}, u32[]{:S(2)}, u32[]{:S(2)}) collective-permute-start(bf16[464,128]{1,0:T(8,128)(2,1)S(1)} %shard_map.317.own_ref), channel_id=1, source_target_pairs={{0,2},{2,0},{1,3},{3,1},{4,6},{6,4},{5,7},{7,5},{8,10},{10,8},{9,1... | collective-permute-start | bytes 356360 | tf_op jit(solution)/shard_map/ppermute | solution.py:935
  28.2 0.7 %shard_map.318.message_ref = bf16[256,128]{1,0:T(8,128)(2,1)S(1)} custom-call(s32[50,128]{1,0:T(8,128)S(1)} %get-tuple-element.88.ids_ref.refs_0_, bf16[3072,128]{1,0:T(8,128)(2,1)S(1)} %get-tuple-element.127.dz_ref, bf16[896,128]{1,0:T(8,128)(2,1)S(1)} %get-tuple-element.105.turned_weights), custom_call_target="tpu_custom_call" | custom-call | bytes 1041408 | tf_op jit(solution)/shard_map/pallas_call | solution.py:682
  30.3 2.7 %collective-permute-done.9.refs_2_.far_ref = bf16[128,128]{1,0:T(8,128)(2,1)S(1)} collective-permute-done((bf16[128,128]{1,0:T(8,128)(2,1)S(1)}, bf16[128,128]{1,0:T(8,128)(2,1)S(1)}, u32[]{:S(2)}, u32[]{:S(2)}) %collective-permute-start.9) | collective-permute-done | bytes 32800 | tf_op jit(solution)/shard_map/ppermute | solution.py:707
  33.1 1.0 %collective-permute-start.10 = (bf16[464,128]{1,0:T(8,128)(2,1)S(1)}, bf16[464,128]{1,0:T(8,128)(2,1)S(1)}, u32[]{:S(2)}, u32[]{:S(2)}) collective-permute-start(bf16[464,128]{1,0:T(8,128)(2,1)S(1)} %get-tuple-element.138.own_ref), channel_id=1, source_target_pairs={{0,8},{4,12},{8,0},{12,4},{1,9},{5,13},{9,1},{13,5},{2,10},{6,14},... | collective-permute-start | bytes 356360 | tf_op jit(solution)/shard_map/ppermute | solution.py:935
  34.1 1.5 %shard_map.321 = (bf16[3072,128]{1,0:T(8,128)(2,1)}, bf16[3072,128]{1,0:T(8,128)(2,1)}) custom-call(bf16[3072,128]{1,0:T(8,128)(2,1)S(1)} %get-tuple-element.127.dz_ref, bf16[3072,128]{1,0:T(8,128)(2,1)S(1)} %get-tuple-element.117.cot_ref, bf16[3072,128]{1,0:T(8,128)(2,1)S(1)} %get-tuple-element.92.edge_ref, f32[3072,128]{1,0:T(8,128)S(1)} %get-tuple-element.120.normed_ref, ...), custom_call_target="tpu_custom_call" | custom-call | bytes 4165632 | tf_op jit(solution)/shard_map/pallas_call | solution.py:682
  35.6 2.0 %shard_map.322 = (bf16[1024,128]{1,0:T(8,128)(2,1)S(1)}, bf16[1024,128]{1,0:T(8,128)(2,1)S(1)}) custom-call(s32[50,128]{1,0:T(8,128)S(1)} %get-tuple-element.88.ids_ref.refs_0_, bf16[3072,128]{1,0:T(8,128)(2,1)S(1)} %get-tuple-element.127.dz_ref, s32[3072,128]{1,0:T(8,128)S(1)} %get-tuple-element.135.snd_column, ...), custom_call_target="tpu_custom_call" | custom-call | bytes 3961856 | tf_op jit(solution)/shard_map/pallas_call | solution.py:682
  37.6 3.9 %collective-permute-done.10.other_ref = bf16[464,128]{1,0:T(8,128)(2,1)S(1)} collective-permute-done((bf16[464,128]{1,0:T(8,128)(2,1)S(1)}, bf16[464,128]{1,0:T(8,128)(2,1)S(1)}, u32[]{:S(2)}, u32[]{:S(2)}) %collective-permute-start.10) | collective-permute-done | bytes 118816 | tf_op jit(solution)/shard_map/ppermute | solution.py:935
  41.7 1.1 %shard_map.324.refs_0_ = bf16[1024,128]{1,0:T(8,128)(2,1)} custom-call(bf16[128,128]{1,0:T(8,128)(2,1)S(1)} %collective-permute-done.8.refs_1_.near_ref, bf16[128,128]{1,0:T(8,128)(2,1)S(1)} %collective-permute-done.9.refs_2_.far_ref, f32[1024,128]{1,0:T(8,128)S(1)} %get-tuple-element.134.base_ref, ...), custom_call_target="tpu_custom_call" | custom-call | bytes 1369088 | tf_op jit(solution)/shard_map/pallas_call | solution.py:682
  42.8 3.0 %collective-permute-done.11.other_ref = bf16[464,128]{1,0:T(8,128)(2,1)S(1)} collective-permute-done((bf16[464,128]{1,0:T(8,128)(2,1)S(1)}, bf16[464,128]{1,0:T(8,128)(2,1)S(1)}, u32[]{:S(2)}, u32[]{:S(2)}) %collective-permute-start.11) | collective-permute-done | bytes 118816 | tf_op jit(solution)/shard_map/ppermute | solution.py:935
  45.8 1.6 %collective-permute-start.12 = (bf16[464,128]{1,0:T(8,128)(2,1)S(1)}, bf16[464,128]{1,0:T(8,128)(2,1)S(1)}, u32[]{:S(2)}, u32[]{:S(2)}) collective-permute-start(bf16[464,128]{1,0:T(8,128)(2,1)S(1)} %shard_map.325.own_ref), channel_id=1, source_target_pairs={{0,1},{1,0},{2,3},{3,2},{4,5},{5,4},{6,7},{7,6},{8,9},{9,8},{10,11... | collective-permute-start | bytes 356360 | tf_op jit(solution)/shard_map/ppermute | solution.py:991
  47.4 1.0 %collective-permute-done.12.other_ref = bf16[464,128]{1,0:T(8,128)(2,1)S(1)} collective-permute-done((bf16[464,128]{1,0:T(8,128)(2,1)S(1)}, bf16[464,128]{1,0:T(8,128)(2,1)S(1)}, u32[]{:S(2)}, u32[]{:S(2)}) %collective-permute-start.12) | collective-permute-done | bytes 118816 | tf_op jit(solution)/shard_map/ppermute | solution.py:991
  48.4 0.8 %shard_map.326 = (f32[384,128]{1,0:T(8,128)}, f32[128,128]{1,0:T(8,128)}, f32[256,128]{1,0:T(8,128)}, f32[128,128]{1,0:T(8,128)}, f32[1,128]{1,0:T(1,128)}, /*in...) custom-call(bf16[464,128]{1,0:T(8,128)(2,1)S(1)} %shard_map.325.own_, ...), custom_call_target="tpu_custom_call" | custom-call | bytes 237568 | tf_op jit(solution)/shard_map/pallas_call | solution.py:682
  (23 shorter events, 2.9 us)
Async XLA Ops:
  2.3 5.8 %collective-permute-start = (bf16[128,128]{1,0:T(8,128)(2,1)S(1)}, bf16[128,128]{1,0:T(8,128)(2,1)S(1)}, u32[]{:S(2)}, u32[]{:S(2)}) collective-permute-start(bf16[128,128]{1,0:T(8,128)(2,1)S(1)} %get-tuple-element.86), channel_id=1, source_target_pairs={{0,1},{1,0},{4,5},{5,4},{8,9},{9,8},{12,13},{13,12},{2,3},{3,2},{6... | collective-permute-start | bytes 98312 | tf_op jit(solution)/shard_map/ppermute | solution.py:706
  2.4 5.7 %collective-permute-start.1 = (bf16[128,128]{1,0:T(8,128)(2,1)S(1)}, bf16[128,128]{1,0:T(8,128)(2,1)S(1)}, u32[]{:S(2)}, u32[]{:S(2)}) collective-permute-start(bf16[128,128]{1,0:T(8,128)(2,1)S(1)} %get-tuple-element.87.unused_ref), channel_id=1, source_target_pairs={{1,4},{4,1},{5,8},{8,5},{9,12},{12,9},{0,2},{13,15},{3,6},{6,3},{7... | collective-permute-start | bytes 98312 | tf_op jit(solution)/shard_map/ppermute | solution.py:707
  12.0 4.1 %collective-permute-start.2 = (bf16[128,128]{1,0:T(8,128)(2,1)S(1)}, bf16[128,128]{1,0:T(8,128)(2,1)S(1)}, u32[]{:S(2)}, u32[]{:S(2)}) collective-permute-start(bf16[128,128]{1,0:T(8,128)(2,1)S(1)} %get-tuple-element.100), channel_id=1, source_target_pairs={{0,1},{1,0},{4,5},{5,4},{8,9},{9,8},{12,13},{13,12},{2,3},{3,2},{6... | collective-permute-start | bytes 98312 | tf_op jit(solution)/shard_map/ppermute | solution.py:706
  12.4 3.7 %collective-permute-start.3 = (bf16[128,128]{1,0:T(8,128)(2,1)S(1)}, bf16[128,128]{1,0:T(8,128)(2,1)S(1)}, u32[]{:S(2)}, u32[]{:S(2)}) collective-permute-start(bf16[128,128]{1,0:T(8,128)(2,1)S(1)} %get-tuple-element.101.unused_ref), channel_id=1, source_target_pairs={{1,4},{4,1},{5,8},{8,5},{9,12},{12,9},{0,2},{13,15},{3,6},{6,3},{7... | collective-permute-start | bytes 98312 | tf_op jit(solution)/shard_map/ppermute | solution.py:707
  17.8 4.3 %collective-permute-start.4 = (bf16[128,128]{1,0:T(8,128)(2,1)S(1)}, bf16[128,128]{1,0:T(8,128)(2,1)S(1)}, u32[]{:S(2)}, u32[]{:S(2)}) collective-permute-start(bf16[128,128]{1,0:T(8,128)(2,1)S(1)} %get-tuple-element.115), channel_id=1, source_target_pairs={{0,1},{1,0},{4,5},{5,4},{8,9},{9,8},{12,13},{13,12},{2,3},{3,2},{6... | collective-permute-start | bytes 98312 | tf_op jit(solution)/shard_map/ppermute | solution.py:706
  18.2 3.9 %collective-permute-start.5 = (bf16[128,128]{1,0:T(8,128)(2,1)S(1)}, bf16[128,128]{1,0:T(8,128)(2,1)S(1)}, u32[]{:S(2)}, u32[]{:S(2)}) collective-permute-start(bf16[128,128]{1,0:T(8,128)(2,1)S(1)} %get-tuple-element.113.unused_ref), channel_id=1, source_target_pairs={{1,4},{4,1},{5,8},{8,5},{9,12},{12,9},{0,2},{13,15},{3,6},{6,3},{7... | collective-permute-start | bytes 98312 | tf_op jit(solution)/shard_map/ppermute | solution.py:707
  25.5 1.4 %collective-permute-start.6 = (bf16[464,128]{1,0:T(8,128)(2,1)S(1)}, bf16[464,128]{1,0:T(8,128)(2,1)S(1)}, u32[]{:S(2)}, u32[]{:S(2)}) collective-permute-start(bf16[464,128]{1,0:T(8,128)(2,1)S(1)} %get-tuple-element.129), channel_id=1, source_target_pairs={{0,1},{1,0},{2,3},{3,2},{4,5},{5,4},{6,7},{7,6},{8,9},{9,8},{10,11... | collective-permute-start | bytes 356360 | tf_op jit(solution)/shard_map/ppermute | solution.py:921
  26.9 6.1 %collective-permute-start.7 = (bf16[464,128]{1,0:T(8,128)(2,1)S(1)}, bf16[464,128]{1,0:T(8,128)(2,1)S(1)}, u32[]{:S(2)}, u32[]{:S(2)}) collective-permute-start(bf16[464,128]{1,0:T(8,128)(2,1)S(1)} %shard_map.317.own_ref), channel_id=1, source_target_pairs={{0,2},{2,0},{1,3},{3,1},{4,6},{6,4},{5,7},{7,5},{8,10},{10,8},{9,1... | collective-permute-start | bytes 356360 | tf_op jit(solution)/shard_map/ppermute | solution.py:935
  28.9 1.4 %collective-permute-start.8 = (bf16[128,128]{1,0:T(8,128)(2,1)S(1)}, bf16[128,128]{1,0:T(8,128)(2,1)S(1)}, u32[]{:S(2)}, u32[]{:S(2)}) collective-permute-start(bf16[128,128]{1,0:T(8,128)(2,1)S(1)} %get-tuple-element.130), channel_id=1, source_target_pairs={{0,1},{1,0},{4,5},{5,4},{8,9},{9,8},{12,13},{13,12},{2,3},{3,2},{6... | collective-permute-start | bytes 98312 | tf_op jit(solution)/shard_map/ppermute | solution.py:706
  29.4 3.6 %collective-permute-start.9 = (bf16[128,128]{1,0:T(8,128)(2,1)S(1)}, bf16[128,128]{1,0:T(8,128)(2,1)S(1)}, u32[]{:S(2)}, u32[]{:S(2)}) collective-permute-start(bf16[128,128]{1,0:T(8,128)(2,1)S(1)} %get-tuple-element.131), channel_id=1, source_target_pairs={{1,4},{4,1},{5,8},{8,5},{9,12},{12,9},{0,2},{13,15},{3,6},{6,3},{7... | collective-permute-start | bytes 98312 | tf_op jit(solution)/shard_map/ppermute | solution.py:707
  33.1 8.5 %collective-permute-start.10 = (bf16[464,128]{1,0:T(8,128)(2,1)S(1)}, bf16[464,128]{1,0:T(8,128)(2,1)S(1)}, u32[]{:S(2)}, u32[]{:S(2)}) collective-permute-start(bf16[464,128]{1,0:T(8,128)(2,1)S(1)} %get-tuple-element.138.own_ref), channel_id=1, source_target_pairs={{0,8},{4,12},{8,0},{12,4},{1,9},{5,13},{9,1},{13,5},{2,10},{6,14},... | collective-permute-start | bytes 356360 | tf_op jit(solution)/shard_map/ppermute | solution.py:935
  41.6 4.2 %collective-permute-start.11 = (bf16[464,128]{1,0:T(8,128)(2,1)S(1)}, bf16[464,128]{1,0:T(8,128)(2,1)S(1)}, u32[]{:S(2)}, u32[]{:S(2)}) collective-permute-start(bf16[464,128]{1,0:T(8,128)(2,1)S(1)} %get-tuple-element.141.own_ref), channel_id=1, source_target_pairs={{0,4},{4,0},{8,12},{12,8},{1,5},{5,1},{9,13},{13,9},{2,6},{6,2},{1... | collective-permute-start | bytes 356360 | tf_op jit(solution)/shard_map/ppermute | solution.py:935
  45.8 2.6 %collective-permute-start.12 = (bf16[464,128]{1,0:T(8,128)(2,1)S(1)}, bf16[464,128]{1,0:T(8,128)(2,1)S(1)}, u32[]{:S(2)}, u32[]{:S(2)}) collective-permute-start(bf16[464,128]{1,0:T(8,128)(2,1)S(1)} %shard_map.325.own_ref), channel_id=1, source_target_pairs={{0,1},{1,0},{2,3},{3,2},{4,5},{5,4},{6,7},{7,6},{8,9},{9,8},{10,11... | collective-permute-start | bytes 356360 | tf_op jit(solution)/shard_map/ppermute | solution.py:991
